TPU v7x, 256 devices: a whole 4x4x8 slice. The times are simulated.
256 devices in a mesh: dp: 16 (over x_lo, z), ctx: 16 (over y, x_hi, core).
Axes of the slice: x: 4 (x_hi: 2, x_lo: 2; x = x_hi * 2 + x_lo), y: 4, z: 8, core: 2. Of those that a mesh axis runs over, the one named last changes fastest.
Arguments:
- queries: bfloat16 [32768, 3072], P(('dp', 'ctx')), may hold values from -6 to 6
- keys: bfloat16 [32768, 512], P(('dp', 'ctx')), may hold values from -6 to 6
- values: bfloat16 [32768, 512], P(('dp', 'ctx')), may hold values from -6 to 6
- d_out: bfloat16 [32768, 3072], P(('dp', 'ctx')), may hold values from -6 to 6
- features: bfloat16 [32768, 6144], P(('dp', 'ctx')), may hold values from -6 to 6
- doc_start: int32 [32768], P(('dp', 'ctx')), may hold values from 0 to 2047, as said below
- error: float32 [16, 6144, 512], P('dp', 'ctx'), may hold values from -6 to 6
- q_init: float32 [512, 128], replicated, may hold values from -6 to 6
Outputs:
- d_query: bfloat16 [32768, 3072], P(('dp', 'ctx'))
- d_key: bfloat16 [32768, 512], P(('dp', 'ctx'))
- d_value: bfloat16 [32768, 512], P(('dp', 'ctx'))
- compressed: float32 [6144, 512], P('ctx')
- q_factor: float32 [512, 128], replicated
- new_error: float32 [16, 6144, 512], P('dp', 'ctx')
Inputs may be any that keep to these rules, and one draw needn't show every extreme that they name: Within each sequence doc_start never falls, equals the position at each document's first token and is at most the token's own position; the first document starts at 0. In the first sequence the last token begins a document of its own.
All inputs are finite; a program needn't handle non-finite values.
Results may differ from a plain program's by a relative error of at most 0.015.
Values may be sent and summed in bfloat16 or wider, within the bound.
No kernel may reach another device: no remote copies, remote signals or barrier semaphores. Data moves between devices by JAX's collectives and lax.ppermute only.
A program may use at most 128 MiB of HBM per device.

v0:
```python
import math

import jax
import jax.numpy as jnp
from jax import lax
from jax.sharding import PartitionSpec as P

HEAD_DIM = 128


NEG_FILL = -1e30


def body(queries, keys, values, d_out, features, doc_start, error, q_init):
    tokens_here = queries.shape[0]
    width_kv = keys.shape[1]
    kv_count = width_kv // HEAD_DIM
    q_count = queries.shape[1] // HEAD_DIM
    group_size = q_count // kv_count
    ctx_size = lax.axis_size("ctx")
    length = tokens_here * ctx_size
    block = math.gcd(512, length)
    softmax_scale = 1.0 / math.sqrt(HEAD_DIM)
    offset = lax.axis_index("ctx") * tokens_here
    highest = lax.Precision.HIGHEST
    contract = (((0,), (0,)), ((), ()))
    key_all, value_all = (
        lax.all_gather(keys, "ctx", axis=0, tiled=True),
        lax.all_gather(values, "ctx", axis=0, tiled=True),
    )
    query_grid = queries.reshape(tokens_here, kv_count, group_size, HEAD_DIM)
    dout_grid = d_out.reshape(tokens_here, kv_count, group_size, HEAD_DIM)
    query_pos = offset + jnp.arange(tokens_here, dtype=jnp.int32)
    first_block = jnp.min(doc_start) // block
    end_block = (offset + tokens_here - 1) // block + 1

    def block_scores(block_id):
        key_block = lax.dynamic_slice_in_dim(key_all, block_id * block, block, 0).reshape(
            block, kv_count, HEAD_DIM
        )
        scores = (
            jnp.einsum("qghd,kgd->ghqk", query_grid, key_block, preferred_element_type=jnp.float32)
            * softmax_scale
        )
        key_pos = block_id * block + jnp.arange(block, dtype=jnp.int32)
        allowed = (key_pos[None, :] <= query_pos[:, None]) & (
            key_pos[None, :] >= doc_start[:, None]
        )
        return (jnp.where(allowed, scores, NEG_FILL), allowed, key_block)

    def stats_step(block_id, carry):
        top, total = carry
        scores, allowed, key_block = block_scores(block_id)
        new_top = jnp.maximum(top, jnp.max(scores, axis=3))
        fresh = jnp.sum(jnp.where(allowed, jnp.exp(scores - new_top[..., None]), 0.0), axis=3)
        return (new_top, total * jnp.exp(top - new_top) + fresh)

    stat_shape = (kv_count, group_size, tokens_here)
    top, total = lax.fori_loop(
        first_block,
        end_block,
        stats_step,
        (jnp.full(stat_shape, NEG_FILL, jnp.float32), jnp.zeros(stat_shape, jnp.float32)),
    )

    def block_probs(block_id):
        scores, allowed, key_block = block_scores(block_id)
        probs = jnp.where(allowed, jnp.exp(scores - top[..., None]), 0.0) / total[..., None]
        value_block = lax.dynamic_slice_in_dim(value_all, block_id * block, block, 0).reshape(
            block, kv_count, HEAD_DIM
        )
        dprob = jnp.einsum(
            "qghd,kgd->ghqk", dout_grid, value_block, preferred_element_type=jnp.float32
        )
        return (probs, dprob, key_block)

    def value_step(block_id, carry):
        mix, value_grad = carry
        probs, dprob, key_block = block_probs(block_id)
        probs_low = probs.astype(jnp.bfloat16)
        mix = mix + jnp.sum(probs_low.astype(jnp.float32) * dprob, axis=3)
        piece = jnp.einsum(
            "ghqk,qghd->kgd", probs_low, dout_grid, preferred_element_type=jnp.float32
        )
        value_grad = lax.dynamic_update_slice_in_dim(
            value_grad, piece.reshape(block, width_kv), block_id * block, 0
        )
        return (mix, value_grad)

    mix, value_grad = lax.fori_loop(
        first_block,
        end_block,
        value_step,
        (jnp.zeros(stat_shape, jnp.float32), jnp.zeros((length, width_kv), jnp.float32)),
    )

    def key_step(block_id, carry):
        query_acc, key_grad = carry
        probs, dprob, key_block = block_probs(block_id)
        dscore = (probs * (dprob - mix[..., None])).astype(jnp.bfloat16)
        query_acc = query_acc + jnp.einsum(
            "ghqk,kgd->qghd", dscore, key_block, preferred_element_type=jnp.float32
        )
        piece = (
            jnp.einsum("ghqk,qghd->kgd", dscore, query_grid, preferred_element_type=jnp.float32)
            * softmax_scale
        )
        key_grad = lax.dynamic_update_slice_in_dim(
            key_grad, piece.reshape(block, width_kv), block_id * block, 0
        )
        return (query_acc, key_grad)

    query_acc, key_grad = lax.fori_loop(
        first_block,
        end_block,
        key_step,
        (jnp.zeros(query_grid.shape, jnp.float32), jnp.zeros((length, width_kv), jnp.float32)),
    )
    d_query = (
        (query_acc * softmax_scale).reshape(tokens_here, q_count * HEAD_DIM).astype(jnp.bfloat16)
    )
    key_own, value_own = (
        lax.psum_scatter(
            key_grad.astype(jnp.bfloat16), "ctx", scatter_dimension=0, tiled=True
        ).astype(jnp.float32),
        lax.psum_scatter(
            value_grad.astype(jnp.bfloat16), "ctx", scatter_dimension=0, tiled=True
        ).astype(jnp.float32),
    )
    d_key = key_own.astype(jnp.bfloat16)
    d_value = value_own.astype(jnp.bfloat16)
    rows = features.shape[1] // ctx_size
    grad_rows = lax.psum_scatter(
        lax.dot_general(features, d_key, contract, preferred_element_type=jnp.float32),
        "ctx",
        scatter_dimension=0,
        tiled=True,
    )
    combined = grad_rows + error.reshape(rows, width_kv)
    p_local = jnp.dot(combined, q_init, precision=highest, preferred_element_type=jnp.float32)
    rank_size = q_init.shape[1]
    padded = jnp.zeros((rows * ctx_size, rank_size), jnp.float32)
    padded = lax.dynamic_update_slice_in_dim(padded, p_local, lax.axis_index("ctx") * rows, 0)
    padded = lax.psum(padded, ("dp", "ctx"))
    gram = lax.dot_general(padded, padded, contract, precision=highest)
    p_own = lax.dynamic_slice_in_dim(padded, lax.axis_index("ctx") * rows, rows, 0)
    lower = jnp.linalg.cholesky(gram)
    p_hat = jax.scipy.linalg.solve_triangular(lower, p_own.T, lower=True).T
    q_part = lax.dot_general(combined, p_hat, contract, precision=highest)
    q_factor = lax.psum(q_part, ("dp", "ctx")) / lax.axis_size("dp")
    compressed = jnp.dot(p_hat, q_factor.T, precision=highest)
    new_error = (combined - compressed).reshape(1, rows, width_kv)
    return (d_query, d_key, d_value, compressed, q_factor, new_error)


def solution(mesh):
    in_specs = (
        P(("dp", "ctx"), None),
        P(("dp", "ctx"), None),
        P(("dp", "ctx"), None),
        P(("dp", "ctx"), None),
        P(("dp", "ctx"), None),
        P(("dp", "ctx")),
        P("dp", "ctx", None),
        P(),
    )
    out_specs = (
        P(("dp", "ctx"), None),
        P(("dp", "ctx"), None),
        P(("dp", "ctx"), None),
        P("ctx", None),
        P(),
        P("dp", "ctx", None),
    )
    return jax.shard_map(body, mesh=mesh, in_specs=in_specs, out_specs=out_specs, check_vma=False)
```

profile of v0, /device:TPU:1, one launch (start us, length us, event | category | flops | bytes accessed | tf_op | source)
XLA Modules:
  0.0 1058.1 jit_solution(15491944939785829700)
XLA Ops:
  7.2 1.8 copy.41
  9.0 0.0 all-gather.5.cloned.1.call-start
  9.1 1.7 copy.44
  10.8 1.3 reduce_min.9
  14.7 1.5 copy.42
  16.3 0.4 copy.43
  16.7 2.3 copy.45
  18.9 2.3 copy.47
  21.2 46.3 %all-gather.3.cloned.1.call-done = bf16[2048,512]{0,1:T(8,128)(2,1)} async-done(((bf16[128,512]{0,1:T(8,128)(2,1)}), bf16[2048,512]{0,1:T(8,128)(2,1)}) %all-gather.3.cloned.1.call-update) | async-done | bytes 2097168 | tf_op jit(solution)/shard_map/all_gather | solution.py:28
  67.5 4.0 while.39
  67.6 0.1 compare_and_fusion.6
  67.7 1.1 constant_dynamic-slice_fusion.8
  68.8 1.2 fusion.80
  70.0 1.5 select_reduce_fusion.3
  71.5 49.5 %all-gather.5.cloned.1.call-done = bf16[2048,512]{0,1:T(8,128)(2,1)} async-done(((bf16[128,512]{0,1:T(8,128)(2,1)}), bf16[2048,512]{0,1:T(8,128)(2,1)}) %all-gather.5.cloned.1.call-update) | async-done | bytes 2097168 | tf_op jit(solution)/shard_map/all_gather | solution.py:29
  121.0 1.5 broadcast.106.clone2
  122.5 7.2 while.40
  122.5 0.1 compare_and_fusion.7
  122.7 1.3 constant_dynamic-slice_fusion.9
  124.0 2.4 fusion.87
  126.4 1.0 fusion.88
  127.4 1.2 fusion.89
  128.6 0.2 copy.85
  128.8 0.9 constant_dynamic-update-slice_fusion.4
  129.7 0.2 broadcast_in_dim.61
  129.9 1.5 broadcast.106.clone
  131.3 13.3 %while.41 = (s32[]{:T(128)}, f32[128,4,6,128]{0,3,2,1:T(8,128)S(1)}, bf16[2048,512]{1,0:T(8,128)(2,1)}, s32[]{:T(128)}, bf16[2048,512]{0,1:T(8,128)(2,1)}, /*ind...) while((s32[]{:T(128)}, ...), condition=%wide.region_9.10_spmd.clone, body=%wide.region_8.9_spmd.clone.sunk | while | flops 1624310400 | bytes 40281876 | solution.py:113
  131.3 0.1 compare_and_fusion.8
  131.5 1.3 constant_dynamic-slice_fusion.10
  132.8 2.2 fusion.98
  135.0 2.8 fusion.99
  137.8 1.9 fusion.100
  139.7 0.9 bitcast_add_fusion.6
  140.7 2.1 copy.86
  142.7 1.9 constant_dynamic-update-slice_fusion.5
  144.7 134.3 %reduce-scatter.4.cloned.1.call-done = bf16[128,512]{1,0:T(8,128)(2,1)} async-done(((bf16[2048,512]{1,0:T(8,128)(2,1)}), bf16[128,512]{1,0:T(8,128)(2,1)}) %reduce-scatter.4.cloned.1.call-update) | async-done | bytes 131088 | tf_op jit(solution)/shard_map/reduce_scatter | solution.py:123
  279.0 7.3 convolution_bitcast_fusion.1
  286.3 0.0 all-reduce.3.cloned.1.call-start
  286.3 2.3 copy.50
  288.7 128.1 %reduce-scatter.8.cloned.1.call-done = f32[384,512]{0,1:T(8,128)} async-done(((f32[6144,512]{0,1:T(8,128)}), f32[384,512]{0,1:T(8,128)}) %reduce-scatter.8.cloned.1.call-update) | async-done | bytes 786448 | tf_op jit(solution)/shard_map/reduce_scatter | solution.py:133
  416.7 1.9 broadcast_in_dim.63
  418.6 0.1 copy-done.5
  418.7 2.1 convolution_dynamic-update-slice_fusion
  420.8 0.3 all-reduce.5.cloned.1.call-start
  421.1 263.9 %all-reduce.3.cloned.1.call-done = f32[6144,128]{1,0:T(8,128)} async-done(((f32[6144,128]{1,0:T(8,128)}), f32[6144,128]{1,0:T(8,128)}) %all-reduce.3.cloned.1.call-update) | async-done | bytes 3145744 | tf_op jit(solution)/shard_map/psum | solution.py:144
  685.0 7.9 fusion.29
  692.9 0.1 copy.51
  693.1 11.7 %cholesky.16 = f32[128,128]{1,0:T(8,128)S(1)} custom-call(f32[128,128]{1,0:T(8,128)S(1)} %fusion.24), custom_call_target="Cholesky" | custom-call | tf_op jit(solution)/shard_map/jit(cholesky)/cholesky | solution.py:147
  704.8 0.6 compare_reduce_fusion
  705.4 0.7 fusion.22
  706.1 9.8 custom-call.7
  715.9 1.3 fusion.20
  717.3 3.2 fusion.26
  720.5 0.7 reduce-scatter.6.cloned.1.call-update
  721.2 1.1 multiply_convert_fusion
  722.3 2.4 copy.53
  724.7 244.9 %all-reduce.5.cloned.1.call-done = f32[512,128]{1,0:T(8,128)} async-done(((f32[512,128]{1,0:T(8,128)}), f32[512,128]{1,0:T(8,128)}) %all-reduce.5.cloned.1.call-update) | async-done | bytes 262160 | tf_op jit(solution)/shard_map/psum | solution.py:150
  969.7 1.0 broadcast_multiply_fusion
  970.6 0.7 copy-done.8
  971.3 1.7 fusion.30
  973.0 2.3 copy.52
  975.3 2.1 subtract_bitcast_fusion
  977.5 2.3 copy.54
  979.8 71.5 %reduce-scatter.6.cloned.1.call-done = bf16[128,512]{1,0:T(8,128)(2,1)} async-done(((bf16[2048,512]{1,0:T(8,128)(2,1)}), bf16[128,512]{1,0:T(8,128)(2,1)}) %reduce-scatter.6.cloned.1.call-update) | async-done | bytes 131088 | tf_op jit(solution)/shard_map/reduce_scatter | solution.py:126
  (47 shorter events, 0.4 us)
Async XLA Ops:
  7.2 271.8 %copy-start = (bf16[128,6144]{1,0:T(8,128)(2,1)S(1)}, bf16[128,6144]{1,0:T(8,128)(2,1)}, u32[]{:S(2)}) copy-start(bf16[128,6144]{1,0:T(8,128)(2,1)} %param.18) | copy-start | bytes 4718596
  7.2 60.3 %all-gather.3.cloned.1.call-start = ((), (), s32[]{:S(2)}) async-start(), calls=%async_computation.3 | async-start | bytes 2228224 | tf_op jit(solution)/shard_map/all_gather | solution.py:28
  9.0 112.0 %all-gather.5.cloned.1.call-start = ((), (), s32[]{:S(2)}) async-start(), calls=%async_computation.4 | async-start | bytes 2228224 | tf_op jit(solution)/shard_map/all_gather | solution.py:29
  10.8 268.2 %reduce-scatter.4.cloned.1.call-start = ((), (), s32[]{:S(2)}) async-start(), calls=%async_computation.5 | async-start | bytes 2228224 | tf_op jit(solution)/shard_map/reduce_scatter | solution.py:123
  14.7 52.8 %copy-start.11 = (s32[128]{0:T(128)S(1)}, s32[128]{0:T(128)}, u32[]{:S(2)}) copy-start(s32[128]{0:T(128)} %param.19) | copy-start | bytes 1540
  16.3 51.3 %copy-start.1 = (bf16[128,3072]{0,1:T(8,128)(2,1)}, bf16[128,3072]{0,1:T(8,128)(2,1)S(1)}, u32[]{:S(2)}) copy-start(bf16[128,3072]{0,1:T(8,128)(2,1)S(1)} %copy.42) | copy-start | bytes 2359300
  123.9 2.4 copy-start.7
  132.7 2.2 copy-start.9
  135.0 2.8 copy-start.2
  144.6 272.1 %reduce-scatter.8.cloned.1.call-start = ((), (), s32[]{:S(2)}) async-start(), calls=%async_computation.7 | async-start | bytes 13369344 | tf_op jit(solution)/shard_map/reduce_scatter | solution.py:133
  286.3 132.3 %copy-start.10 = (f32[512,128]{1,0:T(8,128)S(1)}, f32[512,128]{1,0:T(8,128)}, u32[]{:S(2)}) copy-start(f32[512,128]{1,0:T(8,128)} %param.21) | copy-start | bytes 786436
  286.3 398.7 %all-reduce.3.cloned.1.call-start = ((), (), s32[]{:S(2)}) async-start(), calls=%async_computation.8 | async-start | bytes 6291456 | tf_op jit(solution)/shard_map/psum | solution.py:144
  416.7 1.9 copy-start.3
  416.7 2.0 copy-start.5
  420.8 548.8 %all-reduce.5.cloned.1.call-start = ((), (), s32[]{:S(2)}) async-start(), calls=%async_computation.9 | async-start | bytes 524288 | tf_op jit(solution)/shard_map/psum | solution.py:150
  720.5 330.8 %reduce-scatter.6.cloned.1.call-start = ((), (), s32[]{:S(2)}) async-start(), calls=%async_computation.6 | async-start | bytes 2228224 | tf_op jit(solution)/shard_map/reduce_scatter | solution.py:126
  722.3 253.0 %copy-start.4 = (f32[1,384,512]{1,2,0:T(8,128)S(1)}, f32[1,384,512]{1,2,0:T(8,128)}, u32[]{:S(2)}) copy-start(f32[1,384,512]{1,2,0:T(8,128)} %copy.50) | copy-start | bytes 2359300
  722.3 253.0 %copy-start.6 = (f32[384,512]{0,1:T(8,128)S(1)}, f32[384,512]{0,1:T(8,128)}, u32[]{:S(2)}) copy-start(f32[384,512]{0,1:T(8,128)} %reduce-scatter.8.cloned.1.call-done) | copy-start | bytes 2359300
  970.6 0.7 copy-start.8
Sparse Core Ops, SparseCore 0:
  11.2 56.2 all-gather.2
  70.7 50.2 all-gather.4
  144.8 134.1 reduce-scatter.3
  286.4 130.2 reduce-scatter.7
  422.9 262.0 all-reduce.2
  720.6 249.0 all-reduce.4
  974.4 76.8 reduce-scatter.5
where the time goes:
time: 1060 us
  waiting for transfers between devices  939 us (89%)
  matrix products  37.1 us (4%)
  local copies, waits for them, and re-layouts  33.8 us (3%)
  other arithmetic  30.3 us (3%)
  between operations  16.9 us (2%)
    psum x1, waiting for transfers between devices, body(): padded = lax.psum(padded, ('dp', 'ctx'))  264 us
    psum x1, waiting for transfers between devices, body(): q_factor = lax.psum(q_part, ('dp', 'ctx')) / lax.axis_size('dp')  245 us
    reduce_scatter x1, waiting for transfers between devices, body(): lax.psum_scatter(key_grad.astype(jnp.bfloat16), 'ctx', scatter_dimension=...  134 us
    reduce_scatter x1, waiting for transfers between devices, body(): lax.psum_scatter(lax.dot_general(features, d_key, contract, preferred_ele...  128 us
    reduce_scatter x1, waiting for transfers between devices, body(): lax.psum_scatter(value_grad.astype(jnp.bfloat16), 'ctx', scatter_dimensio...  71.5 us
    all_gather x1, waiting for transfers between devices, body(): lax.all_gather(values, 'ctx', axis=0, tiled=True)  49.5 us
    all_gather x1, waiting for transfers between devices, body(): lax.all_gather(keys, 'ctx', axis=0, tiled=True)  46.3 us
  transfers between devices with their start and end apart: 7, of which 7 were waited for; matrix products, arithmetic and copies ran while one was open for 3% of the time, Pallas kernels for 0%

commit v1 on v0

v1 whole, which is shorter than its diff:
```python
import math

import jax
import jax.numpy as jnp
from jax import lax
from jax.experimental import pallas as pl
from jax.experimental.pallas import tpu as pltpu
from jax.sharding import Mesh
from jax.sharding import PartitionSpec as P

HEAD = 128
NEG_FILL = -1e30
LOG2E = 1.4426950408889634
HIGHEST = lax.Precision.HIGHEST
TN = (((0,), (0,)), ((), ()))
NT = (((1,), (1,)), ((), ()))
HEADS_AT_ONCE = 2


def attention(where, queries, q_peer, d_out, do_peer, kv, doc, group_size):
    tokens = queries.shape[0]
    block = 2 * tokens
    length = kv.shape[0]
    slots = length // block
    width_kv = kv.shape[1] // 2
    heads = q_peer.shape[1] // HEAD
    steps = heads // HEADS_AT_ONCE
    per_group = group_size // HEADS_AT_ONCE
    groups = width_kv // HEAD
    wide = HEADS_AT_ONCE * HEAD
    columns = HEADS_AT_ONCE * block
    scale = 1.0 / math.sqrt(HEAD)
    power = scale * LOG2E

    def kernel(
        at, qo, qp, do, dp_, k_ref, v_ref, doc_ref, dqo, dqp, dk_ref, dv_ref,
        s_scr, d_scr, bias, k_turned, dq_acc, dk_acc, dv_acc,
    ):
        step = pl.program_id(0)
        core, chip = at[0], at[1]
        first = (jnp.min(doc_ref[...].astype(jnp.float32)).astype(jnp.int32)) // block

        def place(index):
            return jnp.where(index < tokens, index + core * tokens, index - core * tokens)

        @pl.when(step == 0)
        def _():
            q_pos = chip * block + place(lax.broadcasted_iota(jnp.int32, (block, block), 1))
            k_off = place(lax.broadcasted_iota(jnp.int32, (block, block), 0))
            start = doc_ref[...]

            def fill(j, _):
                slot = jnp.bitwise_xor(j, chip)
                k_pos = j * block + k_off
                ok = (k_pos <= q_pos) & (k_pos >= start)
                bias[pl.ds(pl.multiple_of(slot * block, block), block), :] = jnp.where(
                    ok, 0.0, NEG_FILL
                )
                return 0

            lax.fori_loop(first, chip + 1, fill, 0)

        @pl.when(lax.rem(step, per_group) == 0)
        def _():
            dk_acc[...] = jnp.zeros_like(dk_acc)
            dv_acc[...] = jnp.zeros_like(dv_acc)
            for slot in range(slots):
                k_turned[slot] = (
                    k_ref[slot * block : (slot + 1) * block, :].astype(jnp.float32).T
                ).astype(jnp.bfloat16)

        def rows_of(own, peer):
            parts = []
            for n in range(HEADS_AT_ONCE):
                parts.append(own[:, n * HEAD : (n + 1) * HEAD])
                parts.append(peer[:, n * HEAD : (n + 1) * HEAD])
            return jnp.concatenate(parts, axis=0)

        q = rows_of(qo, qp)
        g = rows_of(do, dp_)

        def fold(x):
            return x.reshape(block // 8, 8, columns)

        def here(j):
            slot = jnp.bitwise_xor(j, chip)
            return slot, pl.ds(pl.multiple_of(slot * block, block), block)

        def score_step(j, top):
            _, span = here(j)
            s = lax.dot_general(k_ref[span, :], q, NT, preferred_element_type=jnp.float32)
            b = bias[span, :]
            s = s + jnp.concatenate([b] * HEADS_AT_ONCE, axis=1)
            s_scr[span, :] = s
            return jnp.maximum(top, jnp.max(fold(s), axis=0))

        top = lax.fori_loop(
            first, chip + 1, score_step, jnp.full((8, columns), NEG_FILL, jnp.float32)
        )
        top = jnp.max(top, axis=0, keepdims=True)

        def prob_step(j, carry):
            total, mix = carry
            _, span = here(j)
            p = jnp.exp2((s_scr[span, :] - top) * power)
            d = lax.dot_general(v_ref[span, :], g, NT, preferred_element_type=jnp.float32)
            s_scr[span, :] = p
            d_scr[span, :] = d
            return (total + jnp.sum(fold(p), axis=0), mix + jnp.sum(fold(p * d), axis=0))

        zero = jnp.zeros((8, columns), jnp.float32)
        total, mix = lax.fori_loop(first, chip + 1, prob_step, (zero, zero))
        inverse = 1.0 / jnp.sum(total, axis=0, keepdims=True)
        mix = jnp.sum(mix, axis=0, keepdims=True) * inverse
        dq_acc[...] = jnp.zeros_like(dq_acc)

        def grad_step(j, _):
            slot, span = here(j)
            p = s_scr[span, :] * inverse
            ds = (p * (d_scr[span, :] - mix)).astype(jnp.bfloat16)
            low = p.astype(jnp.bfloat16)
            dv_acc[span, :] += jnp.dot(low, g, preferred_element_type=jnp.float32)
            dk_acc[span, :] += jnp.dot(ds, q, preferred_element_type=jnp.float32)
            dq_acc[...] += jnp.dot(k_turned[slot], ds, preferred_element_type=jnp.float32)
            return 0

        lax.fori_loop(first, chip + 1, grad_step, 0)
        dq = (dq_acc[...] * scale).T.astype(jnp.bfloat16)
        for n in range(HEADS_AT_ONCE):
            at_row = n * block
            dqo[:, n * HEAD : (n + 1) * HEAD] = dq[at_row : at_row + tokens]
            dqp[:, n * HEAD : (n + 1) * HEAD] = dq[at_row + tokens : at_row + block]

        @pl.when(lax.rem(step, per_group) == per_group - 1)
        def _():
            dk_ref[...] = (dk_acc[...] * scale).astype(jnp.bfloat16)
            dv_ref[...] = dv_acc[...].astype(jnp.bfloat16)

    own = pl.BlockSpec((tokens, wide), lambda s, at: (0, at[0] * steps + s))
    peer = pl.BlockSpec((tokens, wide), lambda s, at: (0, s))
    part = pl.BlockSpec((length, HEAD), lambda s, at: (0, s // per_group))
    flops = 5 * 2 * length * block * heads * HEAD
    return pl.pallas_call(
        kernel,
        grid_spec=pltpu.PrefetchScalarGridSpec(
            num_scalar_prefetch=1,
            grid=(steps,),
            in_specs=[
                own,
                peer,
                own,
                peer,
                part,
                pl.BlockSpec((length, HEAD), lambda s, at: (0, groups + s // per_group)),
                pl.BlockSpec((1, block), lambda s, at: (0, 0)),
            ],
            out_specs=[peer, peer, part, part],
            scratch_shapes=[
                pltpu.VMEM((length, columns), jnp.float32),
                pltpu.VMEM((length, columns), jnp.float32),
                pltpu.VMEM((length, block), jnp.float32),
                pltpu.VMEM((slots, HEAD, block), jnp.bfloat16),
                pltpu.VMEM((HEAD, columns), jnp.float32),
                pltpu.VMEM((length, HEAD), jnp.float32),
                pltpu.VMEM((length, HEAD), jnp.float32),
            ],
        ),
        out_shape=[
            jax.ShapeDtypeStruct((tokens, heads * HEAD), jnp.bfloat16),
            jax.ShapeDtypeStruct((tokens, heads * HEAD), jnp.bfloat16),
            jax.ShapeDtypeStruct((length, width_kv), jnp.bfloat16),
            jax.ShapeDtypeStruct((length, width_kv), jnp.bfloat16),
        ],
        compiler_params=pltpu.CompilerParams(
            dimension_semantics=("arbitrary",), vmem_limit_bytes=40 * 1024 * 1024
        ),
        cost_estimate=pl.CostEstimate(
            flops=4 * flops, bytes_accessed=8 * 1024 * 1024, transcendentals=0
        ),
        name="attention",
    )(where, queries, q_peer, d_out, do_peer, kv, kv, doc)


def inverse_factor(gram):
    size = gram.shape[0]
    tiles = size // 8

    def kernel(g_ref, out_ref):
        sub = lax.broadcasted_iota(jnp.int32, (8, 1), 0)
        lane = lax.broadcasted_iota(jnp.int32, (8, size), 1)
        row8 = lax.broadcasted_iota(jnp.int32, (8, size), 0)
        left = [g_ref[8 * t : 8 * t + 8, :] for t in range(tiles)]
        right = [jnp.where(lane == row8 + 8 * t, 1.0, 0.0) for t in range(tiles)]
        for j in range(size):
            t0, r = j // 8, j % 8
            row_l = left[t0][r : r + 1, :]
            row_r = right[t0][r : r + 1, :]
            root = 1.0 / jnp.sqrt(row_l[:, j : j + 1])
            row_l = row_l * root
            row_r = row_r * root
            for t in range(t0, tiles):
                c = left[t][:, j : j + 1] * root
                if t == t0:
                    c = jnp.where(sub > r, c, 0.0)
                    hit = sub == r
                    left[t] = jnp.where(hit, row_l, left[t] - c * row_l)
                    right[t] = jnp.where(hit, row_r, right[t] - c * row_r)
                else:
                    left[t] = left[t] - c * row_l
                    right[t] = right[t] - c * row_r
        for t in range(tiles):
            out_ref[8 * t : 8 * t + 8, :] = right[t]

    return pl.pallas_call(
        kernel,
        out_shape=jax.ShapeDtypeStruct((size, size), jnp.float32),
        in_specs=[pl.BlockSpec(memory_space=pltpu.VMEM)],
        out_specs=pl.BlockSpec(memory_space=pltpu.VMEM),
        name="inverse_factor",
    )(gram)


def body(queries, keys, values, d_out, features, doc_start, error, q_init):
    tokens = queries.shape[0]
    width_kv = keys.shape[1]
    half_kv = width_kv // 2
    half_q = queries.shape[1] // 2
    group_size = queries.shape[1] // width_kv
    chips = lax.axis_size("chip")
    replicas = lax.axis_size("dp")
    core = lax.axis_index("core")
    chip = lax.axis_index("chip")
    other = 1 - core
    f32, bf16 = jnp.float32, jnp.bfloat16

    def swap(x):
        return lax.ppermute(x, "core", [(0, 1), (1, 0)])

    def piece(x, size, index, axis=1):
        return lax.dynamic_slice_in_dim(x, index * size, size, axis)

    def in_order(mine, theirs):
        return jnp.where(
            core == 0,
            jnp.concatenate([mine, theirs], axis=1),
            jnp.concatenate([theirs, mine], axis=1),
        )

    def send(x, k, keep=lambda i, j: True):
        pairs = [(i, i ^ k) for i in range(chips) if keep(i, i ^ k)]
        return lax.ppermute(x, "chip", pairs)

    kv_peer = swap(
        jnp.concatenate([piece(keys, half_kv, other), piece(values, half_kv, other)], axis=1)
    )
    kv_mine = jnp.concatenate([piece(keys, half_kv, core), piece(values, half_kv, core)], axis=1)
    kv_chip = jnp.concatenate([kv_mine, kv_peer], axis=0)
    kv = jnp.concatenate(
        [kv_chip] + [send(kv_chip, k, lambda i, j: i < j) for k in range(1, chips)], axis=0
    )
    q_peer = swap(piece(queries, half_q, other))
    do_peer = swap(piece(d_out, half_q, other))
    doc = jnp.concatenate([doc_start, swap(doc_start)])[None, :]
    where = jnp.stack([core, chip]).astype(jnp.int32)

    kv, features = lax.optimization_barrier((kv, features))
    rows2 = features.shape[1] // chips
    rows = rows2 // 2
    blocks = [piece(features, rows2, chip)]
    for k in range(1, chips):
        blocks.append(send(piece(features, rows2, jnp.bitwise_xor(chip, k)), k))

    dq_own, dq_peer, dk, dv = attention(
        where, queries, q_peer, d_out, do_peer, kv, doc, group_size
    )

    block = 2 * tokens

    def gather_sum(x):
        total = x[:block].astype(f32)
        for k in range(1, chips):
            part = send(x[k * block : (k + 1) * block], k, lambda i, j: i > j)
            total = total + part.astype(f32)
        return total.astype(bf16)

    dk_half = gather_sum(dk)
    dk_mine = jnp.stack([dk_half] + [send(dk_half, k) for k in range(1, chips)])
    dk_theirs = swap(dk_mine)
    d_key = in_order(dk_half[:tokens], dk_theirs[0, tokens:])

    feat = jnp.concatenate(blocks, axis=0)
    feat_own = piece(feat, rows, core)
    feat_peer = swap(piece(feat, rows, other))
    feat = jnp.concatenate([feat_own, feat_peer], axis=0)
    by_token = jnp.concatenate(
        [
            jnp.concatenate([dk_mine[:, :tokens], dk_mine[:, tokens:]], axis=0),
            jnp.concatenate([dk_theirs[:, tokens:], dk_theirs[:, :tokens]], axis=0),
        ],
        axis=2,
    ).reshape(2 * chips * tokens, width_kv)
    grad = lax.dot_general(feat, by_token, TN, preferred_element_type=f32)
    grad = jnp.where(core == 0, grad, jnp.roll(grad, half_kv, axis=1))
    combined = grad + error.reshape(rows, width_kv)

    shares = combined.astype(bf16).reshape(replicas, rows // replicas, width_kv)
    shares = lax.all_to_all(shares, "dp", 0, 0)
    share = jnp.sum(shares.astype(f32), axis=0).astype(bf16)
    total = lax.all_to_all(jnp.broadcast_to(share[None], (replicas,) + share.shape), "dp", 0, 0)
    total = total.reshape(rows, width_kv).astype(f32)

    p_sum = jnp.dot(total, q_init, precision=HIGHEST)
    both = lax.dot_general(
        jnp.concatenate([total, p_sum], axis=1), p_sum, TN, precision=HIGHEST
    )
    rank = q_init.shape[1]
    size = both.shape[0] // 2
    part = piece(both, size, core, 0) + swap(piece(both, size, other, 0))
    part = lax.all_to_all(part.reshape(chips, size // chips, rank), "chip", 0, 0)
    part = jnp.sum(part, axis=0)
    part = lax.all_to_all(jnp.broadcast_to(part[None], (chips,) + part.shape), "chip", 0, 0)
    part = part.reshape(size, rank)
    their = swap(part)
    both = jnp.where(
        core == 0, jnp.concatenate([part, their]), jnp.concatenate([their, part])
    )
    inverse = inverse_factor(both[width_kv:])
    p_hat = lax.dot_general(p_sum, inverse, NT, precision=HIGHEST)
    q_factor = lax.dot_general(both[:width_kv], inverse, NT, precision=HIGHEST) / replicas
    compressed = lax.dot_general(p_hat, q_factor, NT, precision=HIGHEST)
    new_error = (combined - compressed).reshape(1, rows, width_kv)

    dv_half = gather_sum(dv)
    d_value = in_order(dv_half[:tokens], swap(dv_half[tokens:]))
    d_query = in_order(dq_own, swap(dq_peer))
    return (d_query, d_key, d_value, compressed, q_factor, new_error)


def solution(mesh):
    replicas, ctx = mesh.devices.shape
    parts = Mesh(mesh.devices.reshape(replicas, ctx // 2, 2), ("dp", "chip", "core"))
    everywhere = ("dp", "chip", "core")
    tokens = P(everywhere, None)
    in_specs = (
        tokens, tokens, tokens, tokens, tokens, P(everywhere), P("dp", ("chip", "core"), None), P(),
    )
    out_specs = (
        tokens, tokens, tokens, P(("chip", "core"), None), P(), P("dp", ("chip", "core"), None),
    )
    return jax.shard_map(body, mesh=parts, in_specs=in_specs, out_specs=out_specs, check_vma=False)
```

time: 1060 us -> 296 us (0.28)
  waiting for transfers between devices: 939 us -> 84.7 us
  starting transfers between devices: 0.51 us -> 120 us
  matrix products: 37.1 us -> 7.79 us
  blocking collectives: 0 us -> 25.8 us
  Pallas kernels: 0 us -> 23.7 us
  other arithmetic: 30.3 us -> 11.4 us
  between operations: 16.9 us -> 1.47 us
  local copies, waits for them, and re-layouts: 33.8 us -> 20.7 us
    psum x2 -> x0, waiting for transfers between devices: 509 us -> none  [the longest x1 264 us: body(): padded = lax.psum(padded, ('dp', 'ctx'))]
    reduce_scatter x3 -> x0, waiting for transfers between devices: 334 us -> none  [the longest x1 134 us: body(): lax.psum_scatter(key_grad.astype(jnp.bfloat16), 'ctx', scatter_dimension=...]
    ppermute x0 -> x45, starting transfers between devices: none -> 107 us  [the longest x35 75.8 us: send(): return lax.ppermute(x, 'chip', pairs)]
    all_gather x2 -> x0, waiting for transfers between devices: 95.8 us -> none  [the longest x1 49.5 us: body(): lax.all_gather(values, 'ctx', axis=0, tiled=True)]
    ppermute x0 -> x45, waiting for transfers between devices: none -> 73.4 us  [the longest x35 71.5 us: send(): return lax.ppermute(x, 'chip', pairs)]
    dot_general x13 -> x6, matrix products: 35.8 us -> 7.79 us  [the longest x1 2.13 us: body(): grad = lax.dot_general(feat, by_token, TN, preferred_element_type=f32)]
    all_to_all x0 -> x1, blocking collectives: none -> 25.8 us  [body(): shares = lax.all_to_all(shares, 'dp', 0, 0)]
    pallas_call x0 -> x2, Pallas kernels: none -> 23.7 us  [the longest x1 14.1 us: inverse_factor(): pl.pallas_call(kernel, out_shape=jax.ShapeDtypeStruct((size, size), jnp.f...]
  transfers between devices with their start and end apart: 7 -> 48, of which waited for: 7 -> 20; matrix products, arithmetic and copies ran while one was open for 3% -> 8% of each run, Pallas kernels for 0% -> 0%
where the time goes in v1:
time: 296 us; the launch traced here: 295 us
  starting transfers between devices  120 us (41%)
  waiting for transfers between devices  84.7 us (29%)
  blocking collectives  25.8 us (9%)
  Pallas kernels  23.7 us (8%)
  local copies, waits for them, and re-layouts  20.7 us (7%)
  other arithmetic  11.4 us (4%)
  matrix products  7.79 us (3%)
    ppermute x35, starting transfers between devices, send(): return lax.ppermute(x, 'chip', pairs)  75.8 us
    ppermute x35, waiting for transfers between devices, send(): return lax.ppermute(x, 'chip', pairs)  71.5 us
    ppermute x10, starting transfers between devices, swap(): return lax.ppermute(x, 'core', [(0, 1), (1, 0)])  31.1 us
    all_to_all x1, blocking collectives, body(): shares = lax.all_to_all(shares, 'dp', 0, 0)  25.8 us
    pallas_call x1, Pallas kernels, inverse_factor(): pl.pallas_call(kernel, out_shape=jax.ShapeDtypeStruct((size, size), jnp.f...  14.1 us
    pallas_call x1, Pallas kernels, attention(): pl.pallas_call(kernel, grid_spec=pltpu.PrefetchScalarGridSpec(num_scalar_...  9.57 us
    unnamed x51, local copies, waits for them, and re-layouts  7.92 us
    all_to_all x1, waiting for transfers between devices, body(): lax.all_to_all(part.reshape(chips, size // chips, rank), 'chip', 0, 0)  6.4 us
  transfers between devices with their start and end apart: 48, of which 20 were waited for; matrix products, arithmetic and copies ran while one was open for 8% of the time, Pallas kernels for 0%

profile of v1, /device:TPU:1, one launch (start us, length us, event | category | flops | bytes accessed | tf_op | source)
XLA Modules:
  0.0 295.4 jit_solution(18190827081495235636)
XLA Ops:
  1.7 3.3 %collective-permute-start = (bf16[128,1536]{1,0:T(8,128)(2,1)S(1)}, bf16[128,1536]{1,0:T(8,128)(2,1)S(1)}, u32[]{:S(2)}, u32[]{:S(2)}) collective-permute-start(bf16[128,1536]{1,0:T(8,128)(2,1)S(1)} %constant_dynamic-slice_fusion.15), channel_id=1, source_target_pairs={{0,1},{1,0},{2,3},{3,2},{4,5},{5,4},{6,7},{7,6},{8,9},{9,8},{10,11... | collective-permute-start | bytes 1179656 | tf_op jit(solution)/shard_map/ppermute | solution.py:237
  7.9 3.1 %collective-permute-start.3 = (bf16[256,512]{1,0:T(8,128)(2,1)S(1)}, bf16[256,512]{1,0:T(8,128)(2,1)S(1)}, u32[]{:S(2)}, u32[]{:S(2)}) collective-permute-start(bf16[256,512]{1,0:T(8,128)(2,1)S(1)} %pad_maximum_fusion), channel_id=1, source_target_pairs={{0,2},{4,6},{8,10},{12,14},{1,3},{5,7},{9,11},{13,15},{16,18},{20,... | collective-permute-start | bytes 786440 | tf_op jit(solution)/shard_map/ppermute | solution.py:251
  11.1 3.2 %collective-permute-start.4 = (bf16[256,512]{1,0:T(8,128)(2,1)S(1)}, bf16[256,512]{1,0:T(8,128)(2,1)S(1)}, u32[]{:S(2)}, u32[]{:S(2)}) collective-permute-start(bf16[256,512]{1,0:T(8,128)(2,1)S(1)} %pad_maximum_fusion), channel_id=1, source_target_pairs={{0,4},{2,6},{8,12},{10,14},{1,5},{3,7},{9,13},{11,15},{16,20},{18,... | collective-permute-start | bytes 786440 | tf_op jit(solution)/shard_map/ppermute | solution.py:251
  14.3 1.3 collective-permute-start.5
  16.2 4.8 %collective-permute-start.6 = (bf16[256,512]{1,0:T(8,128)(2,1)S(1)}, bf16[256,512]{1,0:T(8,128)(2,1)S(1)}, u32[]{:S(2)}, u32[]{:S(2)}) collective-permute-start(bf16[256,512]{1,0:T(8,128)(2,1)S(1)} %pad_maximum_fusion), channel_id=1, source_target_pairs={{0,8},{2,10},{4,12},{6,14},{1,9},{3,11},{5,13},{7,15},{16,24},{18,... | collective-permute-start | bytes 786440 | tf_op jit(solution)/shard_map/ppermute | solution.py:251
  21.1 3.6 %collective-permute-done.4 = bf16[256,512]{1,0:T(8,128)(2,1)S(1)} collective-permute-done((bf16[256,512]{1,0:T(8,128)(2,1)S(1)}, bf16[256,512]{1,0:T(8,128)(2,1)S(1)}, u32[]{:S(2)}, u32[]{:S(2)}) %collective-permute-start.4) | collective-permute-done | bytes 262176 | tf_op jit(solution)/shard_map/ppermute | solution.py:251
  24.7 1.3 collective-permute-start.7
  26.0 5.7 %collective-permute-start.8 = (bf16[256,512]{1,0:T(8,128)(2,1)S(1)}, bf16[256,512]{1,0:T(8,128)(2,1)S(1)}, u32[]{:S(2)}, u32[]{:S(2)}) collective-permute-start(bf16[256,512]{1,0:T(8,128)(2,1)S(1)} %pad_maximum_fusion), channel_id=1, source_target_pairs={{0,12},{2,14},{4,8},{6,10},{1,13},{3,15},{5,9},{7,11},{16,28},{18,... | collective-permute-start | bytes 786440 | tf_op jit(solution)/shard_map/ppermute | solution.py:251
  31.8 2.5 collective-permute-start.9
  34.3 13.2 %collective-permute-done.8 = bf16[256,512]{1,0:T(8,128)(2,1)S(1)} collective-permute-done((bf16[256,512]{1,0:T(8,128)(2,1)S(1)}, bf16[256,512]{1,0:T(8,128)(2,1)S(1)}, u32[]{:S(2)}, u32[]{:S(2)}) %collective-permute-start.8) | collective-permute-done | bytes 262176 | tf_op jit(solution)/shard_map/ppermute | solution.py:251
  49.4 9.6 %attention.1 = (bf16[128,1536]{1,0:T(8,128)(2,1)S(1)}, bf16[128,1536]{1,0:T(8,128)(2,1)S(1)}, bf16[2048,256]{1,0:T(8,128)(2,1)S(1)}, bf16[2048,256]{1,0:T(8,128)(2,1)S(1)}) custom-call(s32[2]{0:T(128)S(1)} %pad_add_fusion.1.at, bf16[128,3072]{1,0:T(8,128)(2,1)S(1)} %copy-done.1, bf16[128,1536]{1,0:T(8,128)(2,1)S(1)} %collective-permute-done.qp, ...), custom_call_target="tpu_custom_call" | custom-call | flops 32212254720 | bytes 8388608 | tf_op jit(solution)/shard_map/attention/pallas_call | solution.py:143
  62.4 1.3 collective-permute-start.16
  63.7 1.3 collective-permute-start.15
  65.0 1.3 collective-permute-start.14
  66.3 11.5 %collective-permute-done.18 = bf16[256,256]{1,0:T(8,128)(2,1)} collective-permute-done((bf16[256,256]{1,0:T(8,128)(2,1)}, bf16[256,256]{1,0:T(8,128)(2,1)}, u32[]{:S(2)}, u32[]{:S(2)}) %collective-permute-start.18) | collective-permute-done | bytes 131104 | tf_op jit(solution)/shard_map/ppermute | solution.py:251
  79.1 1.3 collective-permute-start.12
  80.4 1.6 constant_dynamic-slice_fusion.3
  82.0 11.7 %collective-permute-done.16 = bf16[256,256]{1,0:T(8,128)(2,1)S(1)} collective-permute-done((bf16[256,256]{1,0:T(8,128)(2,1)}, bf16[256,256]{1,0:T(8,128)(2,1)S(1)}, u32[]{:S(2)}, u32[]{:S(2)}) %collective-permute-start.16) | collective-permute-done | bytes 131104 | tf_op jit(solution)/shard_map/ppermute | solution.py:251
  93.7 1.4 collective-permute-start.35
  95.1 1.4 collective-permute-done.15
  96.5 3.9 %collective-permute-start.36 = (bf16[128,768]{1,0:T(8,128)(2,1)S(1)}, bf16[128,768]{1,0:T(8,128)(2,1)S(1)}, u32[]{:S(2)}, u32[]{:S(2)}) collective-permute-start(bf16[128,768]{1,0:T(8,128)(2,1)S(1)} %get-tuple-element.29), channel_id=1, source_target_pairs={{0,4},{2,6},{4,0},{6,2},{8,12},{10,14},{12,8},{14,10},{1,5},{3,7},... | collective-permute-start | bytes 589832 | tf_op jit(solution)/shard_map/ppermute | solution.py:251
  100.4 2.2 collective-permute-start.38
  102.6 3.3 %collective-permute-start.39 = (bf16[128,768]{1,0:T(8,128)(2,1)S(1)}, bf16[128,768]{1,0:T(8,128)(2,1)S(1)}, u32[]{:S(2)}, u32[]{:S(2)}) collective-permute-start(bf16[128,768]{1,0:T(8,128)(2,1)S(1)} %get-tuple-element.26), channel_id=1, source_target_pairs={{0,10},{2,8},{4,14},{6,12},{8,2},{10,0},{12,6},{14,4},{1,11},{3,9}... | collective-permute-start | bytes 589832 | tf_op jit(solution)/shard_map/ppermute | solution.py:251
  105.9 1.8 bitcast_dynamic-update-slice_fusion.7
  108.0 2.2 collective-permute-start.40
  110.2 4.5 %collective-permute-done.19 = bf16[256,256]{1,0:T(8,128)(2,1)S(1)} collective-permute-done((bf16[256,256]{1,0:T(8,128)(2,1)S(1)}, bf16[256,256]{1,0:T(8,128)(2,1)S(1)}, u32[]{:S(2)}, u32[]{:S(2)}) %collective-permute-start.19) | collective-permute-done | bytes 131104 | tf_op jit(solution)/shard_map/ppermute | solution.py:251
  114.7 2.4 collective-permute-start.20
  117.8 2.2 collective-permute-done.20
  120.0 1.5 collective-permute-start.21
  122.1 4.1 %collective-permute-done.21 = bf16[256,256]{1,0:T(8,128)(2,1)S(1)} collective-permute-done((bf16[256,256]{1,0:T(8,128)(2,1)S(1)}, bf16[256,256]{1,0:T(8,128)(2,1)S(1)}, u32[]{:S(2)}, u32[]{:S(2)}) %collective-permute-start.21) | collective-permute-done | bytes 131104 | tf_op jit(solution)/shard_map/ppermute | solution.py:251
  126.2 2.4 collective-permute-start.22
  129.3 2.2 collective-permute-done.22
  131.5 3.9 %collective-permute-start.23 = (bf16[256,256]{1,0:T(8,128)(2,1)S(1)}, bf16[256,256]{1,0:T(8,128)(2,1)S(1)}, u32[]{:S(2)}, u32[]{:S(2)}) collective-permute-start(bf16[256,256]{1,0:T(8,128)(2,1)S(1)} %get-tuple-element.21), channel_id=1, source_target_pairs={{0,10},{2,8},{4,14},{6,12},{8,2},{10,0},{12,6},{14,4},{1,11},{3,9}... | collective-permute-start | bytes 393224 | tf_op jit(solution)/shard_map/ppermute | solution.py:251
  136.0 3.2 %collective-permute-done.23 = bf16[256,256]{1,0:T(8,128)(2,1)S(1)} collective-permute-done((bf16[256,256]{1,0:T(8,128)(2,1)S(1)}, bf16[256,256]{1,0:T(8,128)(2,1)S(1)}, u32[]{:S(2)}, u32[]{:S(2)}) %collective-permute-start.23) | collective-permute-done | bytes 131104 | tf_op jit(solution)/shard_map/ppermute | solution.py:251
  139.2 3.4 %collective-permute-start.24 = (bf16[256,256]{1,0:T(8,128)(2,1)S(1)}, bf16[256,256]{1,0:T(8,128)(2,1)S(1)}, u32[]{:S(2)}, u32[]{:S(2)}) collective-permute-start(bf16[256,256]{1,0:T(8,128)(2,1)S(1)} %get-tuple-element.21), channel_id=1, source_target_pairs={{0,12},{2,14},{4,8},{6,10},{8,4},{10,6},{12,0},{14,2},{1,13},{3,15... | collective-permute-start | bytes 393224 | tf_op jit(solution)/shard_map/ppermute | solution.py:251
  143.3 2.0 collective-permute-done.24
  145.3 4.6 %collective-permute-start.25 = (bf16[256,256]{1,0:T(8,128)(2,1)S(1)}, bf16[256,256]{1,0:T(8,128)(2,1)S(1)}, u32[]{:S(2)}, u32[]{:S(2)}) collective-permute-start(bf16[256,256]{1,0:T(8,128)(2,1)S(1)} %get-tuple-element.21), channel_id=1, source_target_pairs={{0,14},{2,12},{4,10},{6,8},{8,6},{10,4},{12,2},{14,0},{1,15},{3,13... | collective-permute-start | bytes 393224 | tf_op jit(solution)/shard_map/ppermute | solution.py:251
  150.5 2.3 collective-permute-done.25
  152.8 4.5 %collective-permute-start.41 = (bf16[128,768]{1,0:T(8,128)(2,1)S(1)}, bf16[128,768]{1,0:T(8,128)(2,1)S(1)}, u32[]{:S(2)}, u32[]{:S(2)}) collective-permute-start(bf16[128,768]{1,0:T(8,128)(2,1)S(1)} %get-tuple-element.24), channel_id=1, source_target_pairs={{0,14},{2,12},{4,10},{6,8},{8,6},{10,4},{12,2},{14,0},{1,15},{3,13... | collective-permute-start | bytes 589832 | tf_op jit(solution)/shard_map/ppermute | solution.py:251
  158.0 7.6 %collective-permute-start.26 = (bf16[8,256,256]{2,1,0:T(8,128)(2,1)}, bf16[8,256,256]{2,1,0:T(8,128)(2,1)S(1)}, u32[]{:S(2)}, u32[]{:S(2)}) collective-permute-start(bf16[8,256,256]{2,1,0:T(8,128)(2,1)} %bitcast_dynamic-update-slice_fusion), channel_id=1, source_target_pairs={{0,1},{1,0},{2,3},{3,2},{4,5},{5,4},{6,7},{7,6},{8,9},{9,8},{10,11... | collective-permute-start | bytes 3145736 | tf_op jit(solution)/shard_map/ppermute | solution.py:237
  165.7 1.4 constant_dynamic-slice_fusion.2
  167.1 6.9 %collective-permute-start.42 = (bf16[1024,384]{1,0:T(8,128)(2,1)}, bf16[1024,384]{1,0:T(8,128)(2,1)}, u32[]{:S(2)}, u32[]{:S(2)}) collective-permute-start(bf16[1024,384]{1,0:T(8,128)(2,1)} %get-tuple-element.23), channel_id=1, source_target_pairs={{0,1},{1,0},{2,3},{3,2},{4,5},{5,4},{6,7},{7,6},{8,9},{9,8},{10,11... | collective-permute-start | bytes 2359304 | tf_op jit(solution)/shard_map/ppermute | solution.py:237
  176.5 2.1 fusion
  180.9 25.8 %all_to_all.20 = bf16[16,24,512]{2,1,0:T(8,128)(2,1)S(1)} all-to-all(bf16[16,24,512]{2,1,0:T(8,128)(2,1)S(1)} %bitcast.44), channel_id=1, replica_groups=mesh['dp'=16,'chip'=8,'core'=2] {'dp'}, dimensions={0} | all-to-all | bytes 786432 | tf_op jit(solution)/shard_map/all_to_all | solution.py:307
  207.3 1.5 broadcast_in_dim.7
  208.9 6.3 %all-to-all-start.1 = ((bf16[16,24,512]{2,1,0:T(8,128)(2,1)}), bf16[16,24,512]{2,1,0:T(8,128)(2,1)S(1)}, u32[]{:S(2)}, u32[]{:S(2)}) async-start(bf16[16,24,512]{2,1,0:T(8,128)(2,1)} %broadcast_in_dim.7), calls=%async_computation.1 | async-start | bytes 786432 | tf_op jit(solution)/shard_map/all_to_all | solution.py:309
  217.3 1.3 collective-permute-start.32
  218.6 1.3 collective-permute-start.31
  219.9 1.3 collective-permute-start.30
  221.2 1.3 collective-permute-start.29
  222.5 5.5 %collective-permute-done.33 = bf16[256,256]{1,0:T(8,128)(2,1)S(1)} collective-permute-done((bf16[256,256]{1,0:T(8,128)(2,1)S(1)}, bf16[256,256]{1,0:T(8,128)(2,1)S(1)}, u32[]{:S(2)}, u32[]{:S(2)}) %collective-permute-start.33) | collective-permute-done | bytes 131104 | tf_op jit(solution)/shard_map/ppermute | solution.py:251
  231.2 5.7 %collective-permute-start.11 = (bf16[128,1536]{1,0:T(8,128)(2,1)S(1)}, bf16[128,1536]{1,0:T(8,128)(2,1)}, u32[]{:S(2)}, u32[]{:S(2)}) collective-permute-start(bf16[128,1536]{1,0:T(8,128)(2,1)S(1)} %get-tuple-element.14), channel_id=1, source_target_pairs={{0,1},{1,0},{2,3},{3,2},{4,5},{5,4},{6,7},{7,6},{8,9},{9,8},{10,11... | collective-permute-start | bytes 1179656 | tf_op jit(solution)/shard_map/ppermute | solution.py:237
  236.9 3.4 %collective-permute-done.27 = bf16[256,256]{1,0:T(8,128)(2,1)} collective-permute-done((bf16[256,256]{1,0:T(8,128)(2,1)}, bf16[256,256]{1,0:T(8,128)(2,1)}, u32[]{:S(2)}, u32[]{:S(2)}) %collective-permute-start.27) | collective-permute-done | bytes 131104 | tf_op jit(solution)/shard_map/ppermute | solution.py:251
  240.4 2.0 add_convert_fusion
  243.2 1.8 fusion.4
  245.1 3.9 %collective-permute-start.43 = (f32[320,128]{1,0:T(8,128)S(1)}, f32[320,128]{1,0:T(8,128)S(1)}, u32[]{:S(2)}, u32[]{:S(2)}) collective-permute-start(f32[320,128]{1,0:T(8,128)S(1)} %constant_dynamic-slice_fusion), channel_id=1, source_target_pairs={{0,1},{1,0},{2,3},{3,2},{4,5},{5,4},{6,7},{7,6},{8,9},{9,8},{10,11... | collective-permute-start | bytes 491528 | tf_op jit(solution)/shard_map/ppermute | solution.py:237
  250.7 3.4 %all-to-all-start.2 = ((f32[8,40,128]{2,1,0:T(8,128)}), f32[8,40,128]{2,1,0:T(8,128)S(1)}, u32[]{:S(2)}, u32[]{:S(2)}) async-start(f32[8,40,128]{2,1,0:T(8,128)} %bitcast.16), calls=%async_computation.2 | async-start | bytes 327680 | tf_op jit(solution)/shard_map/all_to_all | solution.py:319
  254.8 6.4 %all-to-all-done.2 = f32[8,40,128]{2,1,0:T(8,128)S(1)} async-done(((f32[8,40,128]{2,1,0:T(8,128)}), f32[8,40,128]{2,1,0:T(8,128)S(1)}, u32[]{:S(2)}, u32[]{:S(2)}) %all-to-all-start.2) | async-done | bytes 163872 | tf_op jit(solution)/shard_map/all_to_all | solution.py:319
  261.9 3.4 %all-to-all-start.3 = ((f32[8,40,128]{2,1,0:T(8,128)}), f32[8,40,128]{2,1,0:T(8,128)S(1)}, u32[]{:S(2)}, u32[]{:S(2)}) async-start(f32[8,40,128]{2,1,0:T(8,128)} %broadcast_in_dim.8), calls=%async_computation.3 | async-start | bytes 327680 | tf_op jit(solution)/shard_map/all_to_all | solution.py:321
  265.3 2.2 maximum_select_fusion
  267.5 4.9 %all-to-all-done.3 = f32[8,40,128]{2,1,0:T(8,128)S(1)} async-done(((f32[8,40,128]{2,1,0:T(8,128)}), f32[8,40,128]{2,1,0:T(8,128)S(1)}, u32[]{:S(2)}, u32[]{:S(2)}) %all-to-all-start.3) | async-done | bytes 163872 | tf_op jit(solution)/shard_map/all_to_all | solution.py:321
  272.4 2.7 collective-permute-start.44
  276.8 14.1 %inverse_factor.1 = f32[128,128]{1,0:T(8,128)} custom-call(f32[128,128]{1,0:T(8,128)} %slice.124.g_ref), custom_call_target="tpu_custom_call" | custom-call | tf_op jit(solution)/shard_map/inverse_factor/pallas_call | solution.py:214
  290.9 1.3 fusion.21
  (131 shorter events, 35.6 us)
Async XLA Ops:
  0.6 241.8 %copy-start = (f32[512,128]{1,0:T(8,128)S(1)}, f32[512,128]{1,0:T(8,128)}, u32[]{:S(2)}) copy-start(f32[512,128]{1,0:T(8,128)} %param.15) | copy-start | bytes 786436
  0.6 7.1 %copy-start.15 = (s32[128]{0:T(128)S(1)}, s32[128]{0:T(128)}, u32[]{:S(2)}) copy-start(s32[128]{0:T(128)} %param.13) | copy-start | bytes 1540
  1.7 45.9 %collective-permute-start = (bf16[128,1536]{1,0:T(8,128)(2,1)S(1)}, bf16[128,1536]{1,0:T(8,128)(2,1)S(1)}, u32[]{:S(2)}, u32[]{:S(2)}) collective-permute-start(bf16[128,1536]{1,0:T(8,128)(2,1)S(1)} %constant_dynamic-slice_fusion.15), channel_id=1, source_target_pairs={{0,1},{1,0},{2,3},{3,2},{4,5},{5,4},{6,7},{7,6},{8,9},{9,8},{10,11... | collective-permute-start | bytes 1179656 | tf_op jit(solution)/shard_map/ppermute | solution.py:237
  6.0 1.8 collective-permute-start.2
  7.2 40.4 %collective-permute-start.1 = (bf16[128,1536]{1,0:T(8,128)(2,1)S(1)}, bf16[128,1536]{1,0:T(8,128)(2,1)S(1)}, u32[]{:S(2)}, u32[]{:S(2)}) collective-permute-start(bf16[128,1536]{1,0:T(8,128)(2,1)S(1)} %constant_dynamic-slice_fusion.14), channel_id=1, source_target_pairs={{0,1},{1,0},{2,3},{3,2},{4,5},{5,4},{6,7},{7,6},{8,9},{9,8},{10,11... | collective-permute-start | bytes 1179656 | tf_op jit(solution)/shard_map/ppermute | solution.py:237
  7.7 6.5 %collective-permute-start.10 = (s32[128]{0:T(128)S(1)}, s32[128]{0:T(128)S(1)}, u32[]{:S(2)}, u32[]{:S(2)}) collective-permute-start(s32[128]{0:T(128)S(1)} %copy-done.15), channel_id=1, source_target_pairs={{0,1},{1,0},{2,3},{3,2},{4,5},{5,4},{6,7},{7,6},{8,9},{9,8},{10,11... | collective-permute-start | bytes 1544 | tf_op jit(solution)/shard_map/ppermute | solution.py:237
  7.9 40.5 %copy-start.1 = (bf16[128,3072]{1,0:T(8,128)(2,1)S(1)}, bf16[128,3072]{1,0:T(8,128)(2,1)}, u32[]{:S(2)}) copy-start(bf16[128,3072]{1,0:T(8,128)(2,1)} %qo.1) | copy-start | bytes 2359300
  7.9 40.4 %copy-start.2 = (bf16[128,3072]{1,0:T(8,128)(2,1)S(1)}, bf16[128,3072]{1,0:T(8,128)(2,1)}, u32[]{:S(2)}) copy-start(bf16[128,3072]{1,0:T(8,128)(2,1)} %do.1) | copy-start | bytes 2359300
  7.9 8.3 %collective-permute-start.3 = (bf16[256,512]{1,0:T(8,128)(2,1)S(1)}, bf16[256,512]{1,0:T(8,128)(2,1)S(1)}, u32[]{:S(2)}, u32[]{:S(2)}) collective-permute-start(bf16[256,512]{1,0:T(8,128)(2,1)S(1)} %pad_maximum_fusion), channel_id=1, source_target_pairs={{0,2},{4,6},{8,10},{12,14},{1,3},{5,7},{9,11},{13,15},{16,18},{20,... | collective-permute-start | bytes 786440 | tf_op jit(solution)/shard_map/ppermute | solution.py:251
  11.1 13.6 %collective-permute-start.4 = (bf16[256,512]{1,0:T(8,128)(2,1)S(1)}, bf16[256,512]{1,0:T(8,128)(2,1)S(1)}, u32[]{:S(2)}, u32[]{:S(2)}) collective-permute-start(bf16[256,512]{1,0:T(8,128)(2,1)S(1)} %pad_maximum_fusion), channel_id=1, source_target_pairs={{0,4},{2,6},{8,12},{10,14},{1,5},{3,7},{9,13},{11,15},{16,20},{18,... | collective-permute-start | bytes 786440 | tf_op jit(solution)/shard_map/ppermute | solution.py:251
  14.3 11.7 %collective-permute-start.5 = (bf16[256,512]{1,0:T(8,128)(2,1)S(1)}, bf16[256,512]{1,0:T(8,128)(2,1)S(1)}, u32[]{:S(2)}, u32[]{:S(2)}) collective-permute-start(bf16[256,512]{1,0:T(8,128)(2,1)S(1)} %pad_maximum_fusion), channel_id=1, source_target_pairs={{0,6},{2,4},{8,14},{10,12},{1,7},{3,5},{9,15},{11,13},{16,22},{18,... | collective-permute-start | bytes 786440 | tf_op jit(solution)/shard_map/ppermute | solution.py:251
  16.2 15.5 %collective-permute-start.6 = (bf16[256,512]{1,0:T(8,128)(2,1)S(1)}, bf16[256,512]{1,0:T(8,128)(2,1)S(1)}, u32[]{:S(2)}, u32[]{:S(2)}) collective-permute-start(bf16[256,512]{1,0:T(8,128)(2,1)S(1)} %pad_maximum_fusion), channel_id=1, source_target_pairs={{0,8},{2,10},{4,12},{6,14},{1,9},{3,11},{5,13},{7,15},{16,24},{18,... | collective-permute-start | bytes 786440 | tf_op jit(solution)/shard_map/ppermute | solution.py:251
  24.7 9.6 %collective-permute-start.7 = (bf16[256,512]{1,0:T(8,128)(2,1)S(1)}, bf16[256,512]{1,0:T(8,128)(2,1)S(1)}, u32[]{:S(2)}, u32[]{:S(2)}) collective-permute-start(bf16[256,512]{1,0:T(8,128)(2,1)S(1)} %pad_maximum_fusion), channel_id=1, source_target_pairs={{0,10},{2,8},{4,14},{6,12},{1,11},{3,9},{5,15},{7,13},{16,26},{18,... | collective-permute-start | bytes 786440 | tf_op jit(solution)/shard_map/ppermute | solution.py:251
  26.0 21.5 %collective-permute-start.8 = (bf16[256,512]{1,0:T(8,128)(2,1)S(1)}, bf16[256,512]{1,0:T(8,128)(2,1)S(1)}, u32[]{:S(2)}, u32[]{:S(2)}) collective-permute-start(bf16[256,512]{1,0:T(8,128)(2,1)S(1)} %pad_maximum_fusion), channel_id=1, source_target_pairs={{0,12},{2,14},{4,8},{6,10},{1,13},{3,15},{5,9},{7,11},{16,28},{18,... | collective-permute-start | bytes 786440 | tf_op jit(solution)/shard_map/ppermute | solution.py:251
  31.8 15.8 %collective-permute-start.9 = (bf16[256,512]{1,0:T(8,128)(2,1)S(1)}, bf16[256,512]{1,0:T(8,128)(2,1)S(1)}, u32[]{:S(2)}, u32[]{:S(2)}) collective-permute-start(bf16[256,512]{1,0:T(8,128)(2,1)S(1)} %pad_maximum_fusion), channel_id=1, source_target_pairs={{0,14},{2,12},{4,10},{6,8},{1,15},{3,13},{5,11},{7,9},{16,30},{18,... | collective-permute-start | bytes 786440 | tf_op jit(solution)/shard_map/ppermute | solution.py:251
  47.6 0.7 copy-start.3
  48.4 1.0 copy-start.4
  59.7 18.1 %collective-permute-start.18 = (bf16[256,256]{1,0:T(8,128)(2,1)}, bf16[256,256]{1,0:T(8,128)(2,1)}, u32[]{:S(2)}, u32[]{:S(2)}) collective-permute-start(bf16[256,256]{1,0:T(8,128)(2,1)} %get-tuple-element.44), channel_id=1, source_target_pairs={{8,6},{10,4},{12,2},{14,0},{9,7},{11,5},{13,3},{15,1},{24,22},{26,... | collective-permute-start | bytes 393224 | tf_op jit(solution)/shard_map/ppermute | solution.py:251
  61.0 18.1 %collective-permute-start.17 = (bf16[256,256]{1,0:T(8,128)(2,1)}, bf16[256,256]{1,0:T(8,128)(2,1)}, u32[]{:S(2)}, u32[]{:S(2)}) collective-permute-start(bf16[256,256]{1,0:T(8,128)(2,1)} %get-tuple-element.45), channel_id=1, source_target_pairs={{8,4},{10,6},{12,0},{14,2},{9,5},{11,7},{13,1},{15,3},{24,20},{26,... | collective-permute-start | bytes 393224 | tf_op jit(solution)/shard_map/ppermute | solution.py:251
  62.4 31.3 %collective-permute-start.16 = (bf16[256,256]{1,0:T(8,128)(2,1)}, bf16[256,256]{1,0:T(8,128)(2,1)S(1)}, u32[]{:S(2)}, u32[]{:S(2)}) collective-permute-start(bf16[256,256]{1,0:T(8,128)(2,1)} %get-tuple-element.46), channel_id=1, source_target_pairs={{8,2},{10,0},{12,6},{14,4},{9,3},{11,1},{13,7},{15,5},{24,18},{26,... | collective-permute-start | bytes 393224 | tf_op jit(solution)/shard_map/ppermute | solution.py:251
  63.7 32.9 %collective-permute-start.15 = (bf16[256,256]{1,0:T(8,128)(2,1)}, bf16[256,256]{1,0:T(8,128)(2,1)S(1)}, u32[]{:S(2)}, u32[]{:S(2)}) collective-permute-start(bf16[256,256]{1,0:T(8,128)(2,1)} %get-tuple-element.47), channel_id=1, source_target_pairs={{8,0},{10,2},{12,4},{14,6},{9,1},{11,3},{13,5},{15,7},{24,16},{26,... | collective-permute-start | bytes 393224 | tf_op jit(solution)/shard_map/ppermute | solution.py:251
  65.0 35.4 %collective-permute-start.14 = (bf16[256,256]{1,0:T(8,128)(2,1)S(1)}, bf16[256,256]{1,0:T(8,128)(2,1)S(1)}, u32[]{:S(2)}, u32[]{:S(2)}) collective-permute-start(bf16[256,256]{1,0:T(8,128)(2,1)S(1)} %get-tuple-element.48), channel_id=1, source_target_pairs={{4,2},{6,0},{12,10},{14,8},{5,3},{7,1},{13,11},{15,9},{20,18},{22,... | collective-permute-start | bytes 393224 | tf_op jit(solution)/shard_map/ppermute | solution.py:251
  77.8 22.6 %collective-permute-start.13 = (bf16[256,256]{1,0:T(8,128)(2,1)S(1)}, bf16[256,256]{1,0:T(8,128)(2,1)S(1)}, u32[]{:S(2)}, u32[]{:S(2)}) collective-permute-start(bf16[256,256]{1,0:T(8,128)(2,1)S(1)} %get-tuple-element.49), channel_id=1, source_target_pairs={{4,0},{6,2},{12,8},{14,10},{5,1},{7,3},{13,9},{15,11},{20,16},{22,... | collective-permute-start | bytes 393224 | tf_op jit(solution)/shard_map/ppermute | solution.py:251
  79.1 23.5 %collective-permute-start.12 = (bf16[256,256]{1,0:T(8,128)(2,1)S(1)}, bf16[256,256]{1,0:T(8,128)(2,1)S(1)}, u32[]{:S(2)}, u32[]{:S(2)}) collective-permute-start(bf16[256,256]{1,0:T(8,128)(2,1)S(1)} %get-tuple-element.43), channel_id=1, source_target_pairs={{2,0},{6,4},{10,8},{14,12},{3,1},{7,5},{11,9},{15,13},{18,16},{22,... | collective-permute-start | bytes 393224 | tf_op jit(solution)/shard_map/ppermute | solution.py:251
  93.7 14.0 %collective-permute-start.35 = (bf16[128,768]{1,0:T(8,128)(2,1)S(1)}, bf16[128,768]{1,0:T(8,128)(2,1)S(1)}, u32[]{:S(2)}, u32[]{:S(2)}) collective-permute-start(bf16[128,768]{1,0:T(8,128)(2,1)S(1)} %get-tuple-element.30), channel_id=1, source_target_pairs={{0,2},{2,0},{4,6},{6,4},{8,10},{10,8},{12,14},{14,12},{1,3},{3,1},... | collective-permute-start | bytes 589832 | tf_op jit(solution)/shard_map/ppermute | solution.py:251
  96.5 11.4 %collective-permute-start.36 = (bf16[128,768]{1,0:T(8,128)(2,1)S(1)}, bf16[128,768]{1,0:T(8,128)(2,1)S(1)}, u32[]{:S(2)}, u32[]{:S(2)}) collective-permute-start(bf16[128,768]{1,0:T(8,128)(2,1)S(1)} %get-tuple-element.29), channel_id=1, source_target_pairs={{0,4},{2,6},{4,0},{6,2},{8,12},{10,14},{12,8},{14,10},{1,5},{3,7},... | collective-permute-start | bytes 589832 | tf_op jit(solution)/shard_map/ppermute | solution.py:251
  100.4 57.5 %collective-permute-start.37 = (bf16[128,768]{1,0:T(8,128)(2,1)S(1)}, bf16[128,768]{1,0:T(8,128)(2,1)S(1)}, u32[]{:S(2)}, u32[]{:S(2)}) collective-permute-start(bf16[128,768]{1,0:T(8,128)(2,1)S(1)} %get-tuple-element.28), channel_id=1, source_target_pairs={{0,6},{2,4},{4,2},{6,0},{8,14},{10,12},{12,10},{14,8},{1,7},{3,5},... | collective-permute-start | bytes 589832 | tf_op jit(solution)/shard_map/ppermute | solution.py:251
  100.4 65.2 %collective-permute-start.38 = (bf16[128,768]{1,0:T(8,128)(2,1)S(1)}, bf16[128,768]{1,0:T(8,128)(2,1)S(1)}, u32[]{:S(2)}, u32[]{:S(2)}) collective-permute-start(bf16[128,768]{1,0:T(8,128)(2,1)S(1)} %get-tuple-element.27), channel_id=1, source_target_pairs={{0,8},{2,10},{4,12},{6,14},{8,0},{10,2},{12,4},{14,6},{1,9},{3,11}... | collective-permute-start | bytes 589832 | tf_op jit(solution)/shard_map/ppermute | solution.py:251
  102.6 63.0 %collective-permute-start.39 = (bf16[128,768]{1,0:T(8,128)(2,1)S(1)}, bf16[128,768]{1,0:T(8,128)(2,1)S(1)}, u32[]{:S(2)}, u32[]{:S(2)}) collective-permute-start(bf16[128,768]{1,0:T(8,128)(2,1)S(1)} %get-tuple-element.26), channel_id=1, source_target_pairs={{0,10},{2,8},{4,14},{6,12},{8,2},{10,0},{12,6},{14,4},{1,11},{3,9}... | collective-permute-start | bytes 589832 | tf_op jit(solution)/shard_map/ppermute | solution.py:251
  107.7 58.0 %copy-start.11 = (bf16[256,256]{1,0:T(8,128)(2,1)}, bf16[256,256]{1,0:T(8,128)(2,1)S(1)}, u32[]{:S(2)}) copy-start(bf16[256,256]{1,0:T(8,128)(2,1)S(1)} %get-tuple-element.21) | copy-start | bytes 393220
  107.7 7.0 %collective-permute-start.19 = (bf16[256,256]{1,0:T(8,128)(2,1)S(1)}, bf16[256,256]{1,0:T(8,128)(2,1)S(1)}, u32[]{:S(2)}, u32[]{:S(2)}) collective-permute-start(bf16[256,256]{1,0:T(8,128)(2,1)S(1)} %get-tuple-element.21), channel_id=1, source_target_pairs={{0,2},{2,0},{4,6},{6,4},{8,10},{10,8},{12,14},{14,12},{1,3},{3,1},... | collective-permute-start | bytes 393224 | tf_op jit(solution)/shard_map/ppermute | solution.py:251
  108.0 57.7 %collective-permute-start.40 = (bf16[128,768]{1,0:T(8,128)(2,1)S(1)}, bf16[128,768]{1,0:T(8,128)(2,1)S(1)}, u32[]{:S(2)}, u32[]{:S(2)}) collective-permute-start(bf16[128,768]{1,0:T(8,128)(2,1)S(1)} %get-tuple-element.25), channel_id=1, source_target_pairs={{0,12},{2,14},{4,8},{6,10},{8,4},{10,6},{12,0},{14,2},{1,13},{3,15... | collective-permute-start | bytes 589832 | tf_op jit(solution)/shard_map/ppermute | solution.py:251
  114.7 5.3 %collective-permute-start.20 = (bf16[256,256]{1,0:T(8,128)(2,1)S(1)}, bf16[256,256]{1,0:T(8,128)(2,1)S(1)}, u32[]{:S(2)}, u32[]{:S(2)}) collective-permute-start(bf16[256,256]{1,0:T(8,128)(2,1)S(1)} %get-tuple-element.21), channel_id=1, source_target_pairs={{0,4},{2,6},{4,0},{6,2},{8,12},{10,14},{12,8},{14,10},{1,5},{3,7},... | collective-permute-start | bytes 393224 | tf_op jit(solution)/shard_map/ppermute | solution.py:251
  120.0 6.2 %collective-permute-start.21 = (bf16[256,256]{1,0:T(8,128)(2,1)S(1)}, bf16[256,256]{1,0:T(8,128)(2,1)S(1)}, u32[]{:S(2)}, u32[]{:S(2)}) collective-permute-start(bf16[256,256]{1,0:T(8,128)(2,1)S(1)} %get-tuple-element.21), channel_id=1, source_target_pairs={{0,6},{2,4},{4,2},{6,0},{8,14},{10,12},{12,10},{14,8},{1,7},{3,5},... | collective-permute-start | bytes 393224 | tf_op jit(solution)/shard_map/ppermute | solution.py:251
  126.2 5.3 %collective-permute-start.22 = (bf16[256,256]{1,0:T(8,128)(2,1)S(1)}, bf16[256,256]{1,0:T(8,128)(2,1)S(1)}, u32[]{:S(2)}, u32[]{:S(2)}) collective-permute-start(bf16[256,256]{1,0:T(8,128)(2,1)S(1)} %get-tuple-element.21), channel_id=1, source_target_pairs={{0,8},{2,10},{4,12},{6,14},{8,0},{10,2},{12,4},{14,6},{1,9},{3,11}... | collective-permute-start | bytes 393224 | tf_op jit(solution)/shard_map/ppermute | solution.py:251
  131.5 7.7 %collective-permute-start.23 = (bf16[256,256]{1,0:T(8,128)(2,1)S(1)}, bf16[256,256]{1,0:T(8,128)(2,1)S(1)}, u32[]{:S(2)}, u32[]{:S(2)}) collective-permute-start(bf16[256,256]{1,0:T(8,128)(2,1)S(1)} %get-tuple-element.21), channel_id=1, source_target_pairs={{0,10},{2,8},{4,14},{6,12},{8,2},{10,0},{12,6},{14,4},{1,11},{3,9}... | collective-permute-start | bytes 393224 | tf_op jit(solution)/shard_map/ppermute | solution.py:251
  139.2 6.1 %collective-permute-start.24 = (bf16[256,256]{1,0:T(8,128)(2,1)S(1)}, bf16[256,256]{1,0:T(8,128)(2,1)S(1)}, u32[]{:S(2)}, u32[]{:S(2)}) collective-permute-start(bf16[256,256]{1,0:T(8,128)(2,1)S(1)} %get-tuple-element.21), channel_id=1, source_target_pairs={{0,12},{2,14},{4,8},{6,10},{8,4},{10,6},{12,0},{14,2},{1,13},{3,15... | collective-permute-start | bytes 393224 | tf_op jit(solution)/shard_map/ppermute | solution.py:251
  145.3 7.5 %collective-permute-start.25 = (bf16[256,256]{1,0:T(8,128)(2,1)S(1)}, bf16[256,256]{1,0:T(8,128)(2,1)S(1)}, u32[]{:S(2)}, u32[]{:S(2)}) collective-permute-start(bf16[256,256]{1,0:T(8,128)(2,1)S(1)} %get-tuple-element.21), channel_id=1, source_target_pairs={{0,14},{2,12},{4,10},{6,8},{8,6},{10,4},{12,2},{14,0},{1,15},{3,13... | collective-permute-start | bytes 393224 | tf_op jit(solution)/shard_map/ppermute | solution.py:251
  152.8 12.9 %collective-permute-start.41 = (bf16[128,768]{1,0:T(8,128)(2,1)S(1)}, bf16[128,768]{1,0:T(8,128)(2,1)S(1)}, u32[]{:S(2)}, u32[]{:S(2)}) collective-permute-start(bf16[128,768]{1,0:T(8,128)(2,1)S(1)} %get-tuple-element.24), channel_id=1, source_target_pairs={{0,14},{2,12},{4,10},{6,8},{8,6},{10,4},{12,2},{14,0},{1,15},{3,13... | collective-permute-start | bytes 589832 | tf_op jit(solution)/shard_map/ppermute | solution.py:251
  158.0 17.4 %collective-permute-start.26 = (bf16[8,256,256]{2,1,0:T(8,128)(2,1)}, bf16[8,256,256]{2,1,0:T(8,128)(2,1)S(1)}, u32[]{:S(2)}, u32[]{:S(2)}) collective-permute-start(bf16[8,256,256]{2,1,0:T(8,128)(2,1)} %bitcast_dynamic-update-slice_fusion), channel_id=1, source_target_pairs={{0,1},{1,0},{2,3},{3,2},{4,5},{5,4},{6,7},{7,6},{8,9},{9,8},{10,11... | collective-permute-start | bytes 3145736 | tf_op jit(solution)/shard_map/ppermute | solution.py:237
  167.1 9.2 %collective-permute-start.42 = (bf16[1024,384]{1,0:T(8,128)(2,1)}, bf16[1024,384]{1,0:T(8,128)(2,1)}, u32[]{:S(2)}, u32[]{:S(2)}) collective-permute-start(bf16[1024,384]{1,0:T(8,128)(2,1)} %get-tuple-element.23), channel_id=1, source_target_pairs={{0,1},{1,0},{2,3},{3,2},{4,5},{5,4},{6,7},{7,6},{8,9},{9,8},{10,11... | collective-permute-start | bytes 2359304 | tf_op jit(solution)/shard_map/ppermute | solution.py:237
  175.4 1.1 copy-start.8
  178.7 1.1 copy-start.9
  208.9 33.6 %all-to-all-start.1 = ((bf16[16,24,512]{2,1,0:T(8,128)(2,1)}), bf16[16,24,512]{2,1,0:T(8,128)(2,1)S(1)}, u32[]{:S(2)}, u32[]{:S(2)}) async-start(bf16[16,24,512]{2,1,0:T(8,128)(2,1)} %broadcast_in_dim.7), calls=%async_computation.1 | async-start | bytes 786432 | tf_op jit(solution)/shard_map/all_to_all | solution.py:309
  216.0 11.9 %collective-permute-start.33 = (bf16[256,256]{1,0:T(8,128)(2,1)S(1)}, bf16[256,256]{1,0:T(8,128)(2,1)S(1)}, u32[]{:S(2)}, u32[]{:S(2)}) collective-permute-start(bf16[256,256]{1,0:T(8,128)(2,1)S(1)} %get-tuple-element.37), channel_id=1, source_target_pairs={{8,6},{10,4},{12,2},{14,0},{9,7},{11,5},{13,3},{15,1},{24,22},{26,... | collective-permute-start | bytes 393224 | tf_op jit(solution)/shard_map/ppermute | solution.py:251
  217.3 12.0 %collective-permute-start.32 = (bf16[256,256]{1,0:T(8,128)(2,1)S(1)}, bf16[256,256]{1,0:T(8,128)(2,1)S(1)}, u32[]{:S(2)}, u32[]{:S(2)}) collective-permute-start(bf16[256,256]{1,0:T(8,128)(2,1)S(1)} %get-tuple-element.38), channel_id=1, source_target_pairs={{8,4},{10,6},{12,0},{14,2},{9,5},{11,7},{13,1},{15,3},{24,20},{26,... | collective-permute-start | bytes 393224 | tf_op jit(solution)/shard_map/ppermute | solution.py:251
  218.6 12.6 %collective-permute-start.31 = (bf16[256,256]{1,0:T(8,128)(2,1)}, bf16[256,256]{1,0:T(8,128)(2,1)}, u32[]{:S(2)}, u32[]{:S(2)}) collective-permute-start(bf16[256,256]{1,0:T(8,128)(2,1)} %get-tuple-element.39), channel_id=1, source_target_pairs={{8,2},{10,0},{12,6},{14,4},{9,3},{11,1},{13,7},{15,5},{24,18},{26,... | collective-permute-start | bytes 393224 | tf_op jit(solution)/shard_map/ppermute | solution.py:251
  219.9 17.1 %collective-permute-start.30 = (bf16[256,256]{1,0:T(8,128)(2,1)}, bf16[256,256]{1,0:T(8,128)(2,1)}, u32[]{:S(2)}, u32[]{:S(2)}) collective-permute-start(bf16[256,256]{1,0:T(8,128)(2,1)} %get-tuple-element.40), channel_id=1, source_target_pairs={{8,0},{10,2},{12,4},{14,6},{9,1},{11,3},{13,5},{15,7},{24,16},{26,... | collective-permute-start | bytes 393224 | tf_op jit(solution)/shard_map/ppermute | solution.py:251
  221.2 15.8 %collective-permute-start.29 = (bf16[256,256]{1,0:T(8,128)(2,1)}, bf16[256,256]{1,0:T(8,128)(2,1)}, u32[]{:S(2)}, u32[]{:S(2)}) collective-permute-start(bf16[256,256]{1,0:T(8,128)(2,1)} %get-tuple-element.41), channel_id=1, source_target_pairs={{4,2},{6,0},{12,10},{14,8},{5,3},{7,1},{13,11},{15,9},{20,18},{22,... | collective-permute-start | bytes 393224 | tf_op jit(solution)/shard_map/ppermute | solution.py:251
  227.9 1.3 copy-start.13
  227.9 9.0 %collective-permute-start.28 = (bf16[256,256]{1,0:T(8,128)(2,1)}, bf16[256,256]{1,0:T(8,128)(2,1)}, u32[]{:S(2)}, u32[]{:S(2)}) collective-permute-start(bf16[256,256]{1,0:T(8,128)(2,1)} %get-tuple-element.42), channel_id=1, source_target_pairs={{4,0},{6,2},{12,8},{14,10},{5,1},{7,3},{13,9},{15,11},{20,16},{22,... | collective-permute-start | bytes 393224 | tf_op jit(solution)/shard_map/ppermute | solution.py:251
  229.2 0.6 copy-start.14
  229.9 10.5 %collective-permute-start.27 = (bf16[256,256]{1,0:T(8,128)(2,1)}, bf16[256,256]{1,0:T(8,128)(2,1)}, u32[]{:S(2)}, u32[]{:S(2)}) collective-permute-start(bf16[256,256]{1,0:T(8,128)(2,1)} %get-tuple-element.36), channel_id=1, source_target_pairs={{2,0},{6,4},{10,8},{14,12},{3,1},{7,5},{11,9},{15,13},{18,16},{22,... | collective-permute-start | bytes 393224 | tf_op jit(solution)/shard_map/ppermute | solution.py:251
  231.2 34.1 %collective-permute-start.11 = (bf16[128,1536]{1,0:T(8,128)(2,1)S(1)}, bf16[128,1536]{1,0:T(8,128)(2,1)}, u32[]{:S(2)}, u32[]{:S(2)}) collective-permute-start(bf16[128,1536]{1,0:T(8,128)(2,1)S(1)} %get-tuple-element.14), channel_id=1, source_target_pairs={{0,1},{1,0},{2,3},{3,2},{4,5},{5,4},{6,7},{7,6},{8,9},{9,8},{10,11... | collective-permute-start | bytes 1179656 | tf_op jit(solution)/shard_map/ppermute | solution.py:237
  242.4 6.6 %copy-start.10 = (bf16[256,256]{1,0:T(8,128)(2,1)S(1)}, bf16[256,256]{1,0:T(8,128)(2,1)}, u32[]{:S(2)}) copy-start(bf16[256,256]{1,0:T(8,128)(2,1)} %add_convert_fusion) | copy-start | bytes 393220
  243.1 11.0 %copy-start.12 = (bf16[256,256]{1,0:T(8,128)(2,1)S(1)}, bf16[256,256]{1,0:T(8,128)(2,1)}, u32[]{:S(2)}) copy-start(bf16[256,256]{1,0:T(8,128)(2,1)} %copy-done.11) | copy-start | bytes 393220
  245.1 4.9 %collective-permute-start.43 = (f32[320,128]{1,0:T(8,128)S(1)}, f32[320,128]{1,0:T(8,128)S(1)}, u32[]{:S(2)}, u32[]{:S(2)}) collective-permute-start(f32[320,128]{1,0:T(8,128)S(1)} %constant_dynamic-slice_fusion), channel_id=1, source_target_pairs={{0,1},{1,0},{2,3},{3,2},{4,5},{5,4},{6,7},{7,6},{8,9},{9,8},{10,11... | collective-permute-start | bytes 491528 | tf_op jit(solution)/shard_map/ppermute | solution.py:237
  249.0 5.1 %collective-permute-start.34 = (bf16[128,256]{1,0:T(8,128)(2,1)S(1)}, bf16[128,256]{1,0:T(8,128)(2,1)S(1)}, u32[]{:S(2)}, u32[]{:S(2)}) collective-permute-start(bf16[128,256]{1,0:T(8,128)(2,1)S(1)} %get-tuple-element.53), channel_id=1, source_target_pairs={{0,1},{1,0},{2,3},{3,2},{4,5},{5,4},{6,7},{7,6},{8,9},{9,8},{10,11... | collective-permute-start | bytes 196616 | tf_op jit(solution)/shard_map/ppermute | solution.py:237
  250.7 10.5 %all-to-all-start.2 = ((f32[8,40,128]{2,1,0:T(8,128)}), f32[8,40,128]{2,1,0:T(8,128)S(1)}, u32[]{:S(2)}, u32[]{:S(2)}) async-start(f32[8,40,128]{2,1,0:T(8,128)} %bitcast.16), calls=%async_computation.2 | async-start | bytes 327680 | tf_op jit(solution)/shard_map/all_to_all | solution.py:319
  261.9 10.5 %all-to-all-start.3 = ((f32[8,40,128]{2,1,0:T(8,128)}), f32[8,40,128]{2,1,0:T(8,128)S(1)}, u32[]{:S(2)}, u32[]{:S(2)}) async-start(f32[8,40,128]{2,1,0:T(8,128)} %broadcast_in_dim.8), calls=%async_computation.3 | async-start | bytes 327680 | tf_op jit(solution)/shard_map/all_to_all | solution.py:321
  267.5 26.7 %copy-start.6 = (f32[384,512]{1,0:T(8,128)S(1)}, f32[384,512]{1,0:T(8,128)}, u32[]{:S(2)}) copy-start(f32[384,512]{1,0:T(8,128)} %get-tuple-element.19) | copy-start | bytes 2359300
  272.4 3.7 %collective-permute-start.44 = (f32[320,128]{1,0:T(8,128)S(1)}, f32[320,128]{1,0:T(8,128)S(1)}, u32[]{:S(2)}, u32[]{:S(2)}) collective-permute-start(f32[320,128]{1,0:T(8,128)S(1)} %bitcast.45), channel_id=1, source_target_pairs={{0,1},{1,0},{2,3},{3,2},{4,5},{5,4},{6,7},{7,6},{8,9},{9,8},{10,11... | collective-permute-start | bytes 491528 | tf_op jit(solution)/shard_map/ppermute | solution.py:237
  293.4 1.9 copy-start.7
  294.2 1.1 copy-start.5

commit v2 on v1

v2 whole, which is shorter than its diff:
```python
import math

import jax
import jax.numpy as jnp
from jax import lax
from jax.experimental import pallas as pl
from jax.experimental.pallas import tpu as pltpu
from jax.sharding import Mesh
from jax.sharding import PartitionSpec as P

HEAD = 128
NEG_FILL = -1e30
LOG2E = 1.4426950408889634
HIGHEST = lax.Precision.HIGHEST
TN = (((0,), (0,)), ((), ()))
NT = (((1,), (1,)), ((), ()))
HEADS_AT_ONCE = 2


def attention(where, qg, kv):
    devices, padded, _ = kv.shape
    tokens = HEAD
    block = 2 * tokens
    chips = devices // 2
    length = devices * tokens
    heads = qg.shape[1] // (2 * HEAD)
    steps = heads // HEADS_AT_ONCE
    wide = HEADS_AT_ONCE * HEAD
    columns = HEADS_AT_ONCE * block
    scale = 1.0 / math.sqrt(HEAD)
    power = scale * LOG2E

    def kernel(
        at, q_ref, g_ref, k_ref, v_ref, dq_ref, dk_ref, dv_ref,
        s_scr, d_scr, bias, k_turned, dq_acc, dk_acc, dv_acc,
    ):
        step = pl.program_id(0)
        core = at[0]
        chip = at[1 + step // steps]

        def place(index):
            return jnp.where(index < tokens, index + core * tokens, index - core * tokens)

        def starts(device):
            high = k_ref[device, tokens : tokens + 1, :].astype(jnp.float32)
            low = v_ref[device, tokens : tokens + 1, :].astype(jnp.float32)
            return high * 64.0 + low

        start = jnp.concatenate(
            [starts(2 * chip + core), starts(2 * chip + 1 - core)], axis=1
        )
        first = jnp.min(start).astype(jnp.int32) // block

        def span_of(j):
            return pl.ds(pl.multiple_of(j * block, block), block)

        def rows_of(ref, j):
            return ref[pl.ds(2 * j, 2), :tokens, :].reshape(block, HEAD)

        @pl.when(lax.rem(step, steps) == 0)
        def _():
            q_pos = chip * block + place(lax.broadcasted_iota(jnp.int32, (block, block), 1))
            k_off = lax.broadcasted_iota(jnp.int32, (block, block), 0)
            begin = start.astype(jnp.int32)

            def fill(j, _):
                k_pos = j * block + k_off
                ok = (k_pos <= q_pos) & (k_pos >= begin)
                bias[span_of(j), :] = jnp.where(ok, 0.0, NEG_FILL)
                return 0

            lax.fori_loop(first, chip + 1, fill, 0)

        @pl.when(step == 0)
        def _():
            dk_acc[...] = jnp.zeros_like(dk_acc)
            dv_acc[...] = jnp.zeros_like(dv_acc)
            for j in range(chips):
                k_turned[j] = (
                    k_ref[2 * j : 2 * j + 2, :tokens, :].reshape(block, HEAD).astype(jnp.float32).T
                ).astype(jnp.bfloat16)

        def stacked(ref):
            x = ref[...]
            return jnp.concatenate(
                [x[:, n * HEAD : (n + 1) * HEAD] for n in range(HEADS_AT_ONCE)], axis=0
            )

        q = stacked(q_ref)
        g = stacked(g_ref)

        def fold(x):
            return x.reshape(block // 8, 8, columns)

        def score_step(j, top):
            s = lax.dot_general(rows_of(k_ref, j), q, NT, preferred_element_type=jnp.float32)
            b = bias[span_of(j), :]
            s = s + jnp.concatenate([b] * HEADS_AT_ONCE, axis=1)
            s_scr[span_of(j), :] = s
            return jnp.maximum(top, jnp.max(fold(s), axis=0))

        top = lax.fori_loop(
            first, chip + 1, score_step, jnp.full((8, columns), NEG_FILL, jnp.float32)
        )
        top = jnp.max(top, axis=0, keepdims=True)

        def prob_step(j, carry):
            total, mix = carry
            span = span_of(j)
            p = jnp.exp2((s_scr[span, :] - top) * power)
            d = lax.dot_general(rows_of(v_ref, j), g, NT, preferred_element_type=jnp.float32)
            s_scr[span, :] = p
            d_scr[span, :] = d
            return (total + jnp.sum(fold(p), axis=0), mix + jnp.sum(fold(p * d), axis=0))

        zero = jnp.zeros((8, columns), jnp.float32)
        total, mix = lax.fori_loop(first, chip + 1, prob_step, (zero, zero))
        inverse = 1.0 / jnp.sum(total, axis=0, keepdims=True)
        mix = jnp.sum(mix, axis=0, keepdims=True) * inverse
        dq_acc[...] = jnp.zeros_like(dq_acc)

        def grad_step(j, _):
            span = span_of(j)
            p = s_scr[span, :] * inverse
            ds = (p * (d_scr[span, :] - mix)).astype(jnp.bfloat16)
            low = p.astype(jnp.bfloat16)
            dv_acc[span, :] += jnp.dot(low, g, preferred_element_type=jnp.float32)
            dk_acc[span, :] += jnp.dot(ds, q, preferred_element_type=jnp.float32)
            dq_acc[...] += jnp.dot(k_turned[j], ds, preferred_element_type=jnp.float32)
            return 0

        lax.fori_loop(first, chip + 1, grad_step, 0)
        dq = (dq_acc[...] * scale).T.astype(jnp.bfloat16)
        for n in range(HEADS_AT_ONCE):
            dq_ref[:, n * HEAD : (n + 1) * HEAD] = dq[n * block : (n + 1) * block]

        @pl.when(step == 2 * steps - 1)
        def _():
            dk_ref[...] = (dk_acc[...] * scale).astype(jnp.bfloat16)
            dv_ref[...] = dv_acc[...].astype(jnp.bfloat16)

    whole = pl.BlockSpec((length, HEAD), lambda s, at: (0, 0))
    queries_at = pl.BlockSpec((block, wide), lambda s, at: (s // steps, s % steps))
    flops = 5 * 2 * length * block * heads * HEAD
    return pl.pallas_call(
        kernel,
        grid_spec=pltpu.PrefetchScalarGridSpec(
            num_scalar_prefetch=1,
            grid=(2 * steps,),
            in_specs=[
                queries_at,
                pl.BlockSpec((block, wide), lambda s, at: (s // steps, steps + s % steps)),
                pl.BlockSpec((devices, padded, HEAD), lambda s, at: (0, 0, 0)),
                pl.BlockSpec((devices, padded, HEAD), lambda s, at: (0, 0, 1)),
            ],
            out_specs=[queries_at, whole, whole],
            scratch_shapes=[
                pltpu.VMEM((length, columns), jnp.float32),
                pltpu.VMEM((length, columns), jnp.float32),
                pltpu.VMEM((length, block), jnp.float32),
                pltpu.VMEM((chips, HEAD, block), jnp.bfloat16),
                pltpu.VMEM((HEAD, columns), jnp.float32),
                pltpu.VMEM((length, HEAD), jnp.float32),
                pltpu.VMEM((length, HEAD), jnp.float32),
            ],
        ),
        out_shape=[
            jax.ShapeDtypeStruct((2 * block, heads * HEAD), jnp.bfloat16),
            jax.ShapeDtypeStruct((length, HEAD), jnp.bfloat16),
            jax.ShapeDtypeStruct((length, HEAD), jnp.bfloat16),
        ],
        compiler_params=pltpu.CompilerParams(
            dimension_semantics=("arbitrary",), vmem_limit_bytes=40 * 1024 * 1024
        ),
        cost_estimate=pl.CostEstimate(
            flops=8 * flops, bytes_accessed=8 * 1024 * 1024, transcendentals=0
        ),
        name="attention",
    )(where, qg, qg, kv, kv)


def inverse_factor(gram):
    size = gram.shape[0]
    tiles = size // 8

    def kernel(g_ref, out_ref):
        sub = lax.broadcasted_iota(jnp.int32, (8, 1), 0)
        lane = lax.broadcasted_iota(jnp.int32, (8, size), 1)
        row8 = lax.broadcasted_iota(jnp.int32, (8, size), 0)
        left = [g_ref[8 * t : 8 * t + 8, :] for t in range(tiles)]
        right = [jnp.where(lane == row8 + 8 * t, 1.0, 0.0) for t in range(tiles)]
        for j in range(size):
            t0, r = j // 8, j % 8
            row_l = left[t0][r : r + 1, :]
            row_r = right[t0][r : r + 1, :]
            root = 1.0 / jnp.sqrt(row_l[:, j : j + 1])
            row_l = row_l * root
            row_r = row_r * root
            for t in range(t0, tiles):
                c = left[t][:, j : j + 1] * root
                if t == t0:
                    c = jnp.where(sub > r, c, 0.0)
                    hit = sub == r
                    left[t] = jnp.where(hit, row_l, left[t] - c * row_l)
                    right[t] = jnp.where(hit, row_r, right[t] - c * row_r)
                else:
                    left[t] = left[t] - c * row_l
                    right[t] = right[t] - c * row_r
        for t in range(tiles):
            out_ref[8 * t : 8 * t + 8, :] = right[t]

    return pl.pallas_call(
        kernel,
        out_shape=jax.ShapeDtypeStruct((size, size), jnp.float32),
        in_specs=[pl.BlockSpec(memory_space=pltpu.VMEM)],
        out_specs=pl.BlockSpec(memory_space=pltpu.VMEM),
        name="inverse_factor",
    )(gram)


def body(queries, keys, values, d_out, features, doc_start, error, q_init):
    tokens = queries.shape[0]
    width_kv = keys.shape[1]
    group = queries.shape[1] // (width_kv // HEAD)
    chips = lax.axis_size("chip")
    devices = 2 * chips
    replicas = lax.axis_size("dp")
    core = lax.axis_index("core")
    chip = lax.axis_index("chip")
    upper = (chip >= chips // 2).astype(jnp.int32)
    f32, bf16 = jnp.float32, jnp.bfloat16
    ctx = ("chip", "core")

    def swap(x):
        return lax.ppermute(x, "core", [(0, 1), (1, 0)])

    def piece(x, size, index, axis=1):
        return lax.dynamic_slice_in_dim(x, index * size, size, axis)

    def move(x, cross, turn):
        pairs = []
        for c in range(chips):
            for h in range(2):
                to = (chips - 1 - c if cross else c) * 2 + (1 - h if turn else h)
                pairs.append((2 * c + h, to))
        return lax.ppermute(x, ctx, pairs)

    def exchange(x, axis):
        return lax.all_to_all(x, axis, 0, 0)

    def spread(x, axis, size):
        return exchange(jnp.broadcast_to(x[None], (size,) + x.shape), axis)

    def head_of(cross, turn):
        return 2 * (1 - core if turn else core) + (1 - upper if cross else upper)

    ways = [(False, False), (False, True), (True, False), (True, True)]
    start_row = jnp.concatenate([doc_start // 64, doc_start % 64]).astype(bf16)[None, :]
    start_rows = jnp.concatenate([start_row, jnp.zeros((15, 2 * tokens), bf16)], axis=0)
    per_head = [
        jnp.concatenate(
            [
                jnp.concatenate(
                    [keys[:, h * HEAD : (h + 1) * HEAD], values[:, h * HEAD : (h + 1) * HEAD]],
                    axis=1,
                ),
                start_rows,
            ],
            axis=0,
        )
        for h in range(width_kv // HEAD)
    ]
    per_half = [jnp.stack([per_head[u], per_head[2 + u]]) for u in range(2)]
    kv_send = jnp.concatenate([per_half[0]] * (chips // 2) + [per_half[1]] * (chips // 2), axis=0)
    kv = exchange(kv_send, ctx)

    def both_of(head):
        return jnp.concatenate([piece(queries, group, head), piece(d_out, group, head)], axis=1)

    qg = [both_of(head_of(False, False))]
    for cross, turn in ways[1:]:
        qg.append(move(both_of(head_of(cross, turn)), cross, turn))
    qg = jnp.concatenate(qg, axis=0)

    rows = features.shape[1] // devices
    feat_send = jnp.transpose(features.reshape(tokens, devices, rows), (1, 0, 2))
    kv, feat_send = lax.optimization_barrier((kv, feat_send))
    feat = exchange(feat_send, ctx)

    where = jnp.stack([core, chip, chips - 1 - chip]).astype(jnp.int32)
    dq, dk, dv = attention(where, qg, kv)
    dk, feat = lax.optimization_barrier((dk, feat))

    def to_owner(x):
        x = exchange(x.reshape(devices, tokens, HEAD), ctx)
        x = x.reshape(2, chips // 2, 2, tokens, HEAD).astype(f32)
        x = jnp.sum(x, axis=1).astype(bf16)
        return jnp.concatenate([x[0, 0], x[1, 0], x[0, 1], x[1, 1]], axis=1)

    d_key = to_owner(dk)
    dk_mine = spread(d_key, "chip", chips)
    dk_theirs = swap(dk_mine)
    by_token = jnp.where(
        core == 0,
        jnp.stack([dk_mine, dk_theirs], axis=1),
        jnp.stack([dk_theirs, dk_mine], axis=1),
    ).reshape(devices * tokens, width_kv)
    grad = lax.dot_general(
        feat.reshape(devices * tokens, rows), by_token, TN, preferred_element_type=f32
    )
    combined = grad + error.reshape(rows, width_kv)

    shares = combined.astype(bf16).reshape(replicas, rows // replicas, width_kv)
    shares, dv, dq = lax.optimization_barrier((shares, dv, dq))
    shares = exchange(shares, "dp")
    d_value = to_owner(dv)
    share = jnp.sum(shares.astype(f32), axis=0).astype(bf16)
    total = spread(share, "dp", replicas).reshape(rows, width_kv).astype(f32)

    d_query = jnp.zeros((tokens, queries.shape[1]), bf16)
    for n, (cross, turn) in enumerate(ways):
        back = dq[n * tokens : (n + 1) * tokens]
        if n:
            back = move(back, cross, turn)
        d_query = lax.dynamic_update_slice_in_dim(d_query, back, head_of(cross, turn) * group, 1)

    p_sum = jnp.dot(total, q_init, precision=HIGHEST)
    gram = lax.dot_general(p_sum, p_sum, TN, precision=HIGHEST)
    gram = jnp.sum(spread(gram + swap(gram), "chip", chips), axis=0)
    moment = lax.dot_general(total, p_sum, TN, precision=HIGHEST)
    size = width_kv // 2
    moment = piece(moment, size, core, 0) + swap(piece(moment, size, 1 - core, 0))
    moment, gram = lax.optimization_barrier((moment.astype(bf16), gram))
    moment = jnp.sum(spread(moment, "chip", chips).astype(f32), axis=0)
    inverse = inverse_factor(gram)
    q_mine = lax.dot_general(moment, inverse, NT, precision=HIGHEST) / replicas
    q_theirs = swap(q_mine)
    q_factor = jnp.where(
        core == 0, jnp.concatenate([q_mine, q_theirs]), jnp.concatenate([q_theirs, q_mine])
    )
    p_hat = lax.dot_general(p_sum, inverse, NT, precision=HIGHEST)
    compressed = lax.dot_general(p_hat, q_factor, NT, precision=HIGHEST)
    new_error = (combined - compressed).reshape(1, rows, width_kv)
    return (d_query, d_key, d_value, compressed, q_factor, new_error)


def solution(mesh):
    replicas, ctx = mesh.devices.shape
    parts = Mesh(mesh.devices.reshape(replicas, ctx // 2, 2), ("dp", "chip", "core"))
    everywhere = ("dp", "chip", "core")
    tokens = P(everywhere, None)
    in_specs = (
        tokens, tokens, tokens, tokens, tokens, P(everywhere), P("dp", ("chip", "core"), None), P(),
    )
    out_specs = (
        tokens, tokens, tokens, P(("chip", "core"), None), P(), P("dp", ("chip", "core"), None),
    )
    return jax.shard_map(body, mesh=parts, in_specs=in_specs, out_specs=out_specs, check_vma=False)
```

time: 296 us -> 231 us (0.78)
  starting transfers between devices: 120 us -> 45.1 us
  waiting for transfers between devices: 84.7 us -> 29.4 us
  blocking collectives: 25.8 us -> 73.2 us
  Pallas kernels: 23.7 us -> 40.5 us
  other arithmetic: 11.4 us -> 22 us
  local copies, waits for them, and re-layouts: 20.7 us -> 12.7 us
    ppermute x35 -> x6, starting transfers between devices: 75.8 us -> 17.8 us  [move(): return lax.ppermute(x, ctx, pairs)]
    ppermute x35 -> x6, waiting for transfers between devices: 71.5 us -> 16.2 us  [move(): return lax.ppermute(x, ctx, pairs)]
    all_to_all x1 -> x4, blocking collectives: 25.8 us -> 73.2 us  [exchange(): return lax.all_to_all(x, axis, 0, 0)]
    ppermute x10 -> x4, starting transfers between devices: 31.1 us -> 5.96 us  [swap(): return lax.ppermute(x, 'core', [(0, 1), (1, 0)])]
    pallas_call x1, Pallas kernels: 9.57 us -> 26.4 us  [attention(): pl.pallas_call(kernel, grid_spec=pltpu.PrefetchScalarGridSpec(num_scalar_...]
    unnamed x2 -> x15, other arithmetic: 1.79 us -> 10.7 us
    all_to_all x3 -> x5, starting transfers between devices: 13 us -> 21.3 us  [exchange(): return lax.all_to_all(x, axis, 0, 0)]
    concatenate x4 -> x8, other arithmetic: 0.22 us -> 7.24 us  [the longest x3 4.48 us: both_of(): jnp.concatenate([piece(queries, group, head), piece(d_out, group, head)],...]
  transfers between devices with their start and end apart: 48 -> 15, of which waited for: 20 -> 5; matrix products, arithmetic and copies ran while one was open for 8% -> 12% of each run, Pallas kernels for 0% -> 18%
where the time goes in v2:
time: 231 us; the launch traced here: 230 us
  blocking collectives  73.2 us (32%)
  starting transfers between devices  45.1 us (20%)
  Pallas kernels  40.5 us (18%)
  waiting for transfers between devices  29.4 us (13%)
  other arithmetic  22 us (10%)
  local copies, waits for them, and re-layouts  12.7 us (5%)
  matrix products  5.64 us (2%)
    all_to_all x4, blocking collectives, exchange(): return lax.all_to_all(x, axis, 0, 0)  73.2 us
    pallas_call x1, Pallas kernels, attention(): pl.pallas_call(kernel, grid_spec=pltpu.PrefetchScalarGridSpec(num_scalar_...  26.4 us
    all_to_all x5, starting transfers between devices, exchange(): return lax.all_to_all(x, axis, 0, 0)  21.3 us
    ppermute x6, starting transfers between devices, move(): return lax.ppermute(x, ctx, pairs)  17.8 us
    ppermute x6, waiting for transfers between devices, move(): return lax.ppermute(x, ctx, pairs)  16.2 us
    pallas_call x1, Pallas kernels, inverse_factor(): pl.pallas_call(kernel, out_shape=jax.ShapeDtypeStruct((size, size), jnp.f...  14.1 us
    all_to_all x5, waiting for transfers between devices, exchange(): return lax.all_to_all(x, axis, 0, 0)  11.8 us
    unnamed x15, other arithmetic  10.7 us
  transfers between devices with their start and end apart: 15, of which 5 were waited for; matrix products, arithmetic and copies ran while one was open for 12% of the time, Pallas kernels for 18%

profile of v2, /device:TPU:1, one launch (start us, length us, event | category | flops | bytes accessed | tf_op | source)
XLA Modules:
  0.0 229.6 jit_solution(7938164571830020943)
XLA Ops:
  0.7 2.5 %constant_dynamic-slice_fusion.7 = (bf16[128,768]{1,0:T(8,128)(2,1)S(1)}, bf16[128,768]{1,0:T(8,128)(2,1)}, bf16[128,768]{1,0:T(8,128)(2,1)S(1)}, bf16[128,768]{...) fusion(bf16[128,3072]{1,0:T(8,128)(2,1)} %param.11, ...), kind=kLoop, calls=%fused_computation.59 | loop fusion | bytes 3145744 | tf_op jit(solution)/shard_map/dynamic_slice | solution.py:238
  3.2 0.8 pad_maximum_fusion.3
  3.9 6.6 %collective-permute-start.2 = (bf16[128,1536]{1,0:T(8,128)(2,1)}, bf16[128,1536]{1,0:T(8,128)(2,1)}, u32[]{:S(2)}, u32[]{:S(2)}) collective-permute-start(bf16[128,1536]{1,0:T(8,128)(2,1)} %pad_maximum_fusion.3), channel_id=1, source_target_pairs={{0,15},{1,14},{2,13},{3,12},{4,11},{5,10},{6,9},{7,8},{8,7},{9,6},... | collective-permute-start | bytes 1179656 | tf_op jit(solution)/shard_map/ppermute | solution.py:246
  10.7 0.7 constant_dynamic-update-slice_fusion.15
  11.4 0.7 constant_dynamic-update-slice_fusion.14
  12.1 0.7 constant_dynamic-update-slice_fusion.13
  12.8 0.7 constant_dynamic-update-slice_fusion.12
  13.5 0.7 constant_dynamic-update-slice_fusion.11
  14.2 0.7 constant_dynamic-update-slice_fusion.10
  15.0 0.7 constant_dynamic-update-slice_fusion.9
  15.7 0.7 constant_dynamic-update-slice_fusion.8
  16.4 0.7 constant_dynamic-update-slice_fusion.7
  17.1 0.7 constant_dynamic-update-slice_fusion.6
  17.8 0.7 constant_dynamic-update-slice_fusion.5
  18.5 0.7 constant_dynamic-update-slice_fusion.4
  19.3 0.7 constant_dynamic-update-slice_fusion.3
  20.0 0.7 constant_dynamic-update-slice_fusion.2
  20.7 0.7 constant_dynamic-update-slice_fusion.1
  21.4 0.7 constant_dynamic-update-slice_fusion
  22.1 3.6 %all-to-all-start = ((bf16[16,144,256]{2,1,0:T(8,128)(2,1)}), bf16[16,144,256]{2,1,0:T(8,128)(2,1)S(1)}, u32[]{:S(2)}, u32[]{:S(2)}) async-start(bf16[16,144,256]{2,1,0:T(8,128)(2,1)} %constant_dynamic-update-slice_fusion), calls=%async_computation | async-start | bytes 2359296 | tf_op jit(solution)/shard_map/all_to_all | solution.py:249
  25.7 1.9 pad_maximum_fusion.2
  27.7 4.8 %collective-permute-start.1 = (bf16[128,1536]{1,0:T(8,128)(2,1)}, bf16[128,1536]{1,0:T(8,128)(2,1)}, u32[]{:S(2)}, u32[]{:S(2)}) collective-permute-start(bf16[128,1536]{1,0:T(8,128)(2,1)} %pad_maximum_fusion.2), channel_id=1, source_target_pairs={{0,14},{1,15},{2,12},{3,13},{4,10},{5,11},{6,8},{7,9},{8,6},{9,7},... | collective-permute-start | bytes 1179656 | tf_op jit(solution)/shard_map/ppermute | solution.py:246
  32.5 1.8 pad_maximum_fusion.1
  34.2 0.6 collective-permute-start
  34.9 1.6 copy.16
  36.6 16.1 %collective-permute-done.1 = bf16[128,1536]{1,0:T(8,128)(2,1)} collective-permute-done((bf16[128,1536]{1,0:T(8,128)(2,1)}, bf16[128,1536]{1,0:T(8,128)(2,1)}, u32[]{:S(2)}, u32[]{:S(2)}) %collective-permute-start.1) | collective-permute-done | bytes 393248 | tf_op jit(solution)/shard_map/ppermute | solution.py:246
  52.7 1.3 pad_maximum_fusion.q_ref.g_ref
  54.1 5.1 %all-to-all-start.1 = ((bf16[16,128,384]{1,2,0:T(8,128)(2,1)}), bf16[16,128,384]{1,2,0:T(8,128)(2,1)}, u32[]{:S(2)}, u32[]{:S(2)}) async-start(bf16[16,128,384]{1,2,0:T(8,128)(2,1)} %bitcast.96), calls=%async_computation.1 | async-start | bytes 3145728 | tf_op jit(solution)/shard_map/all_to_all | solution.py:249
  59.2 26.4 %attention.1 = (bf16[512,768]{1,0:T(8,128)(2,1)S(1)}, bf16[2048,128]{1,0:T(8,128)(2,1)S(1)}, bf16[2048,128]{1,0:T(8,128)(2,1)}) custom-call(s32[3]{0:T(128)S(1)} %pad_add_fusion.at, bf16[512,1536]{1,0:T(8,128)(2,1)S(1)} %pad_maximum_fusion.q_ref.g_ref, bf16[512,1536]{1,0:T(8,128)(2,1)S(1)} %pad_maximum_fusion.q_ref.g_ref, ...), custom_call_target="tpu_custom_call" | custom-call | flops 32212254720 | bytes 8388608 | tf_op jit(solution)/shard_map/attention/pallas_call | solution.py:145
  85.6 0.9 copy-done.1
  86.5 18.4 %all_to_all.45 = bf16[16,128,128]{2,1,0:T(8,128)(2,1)S(1)} all-to-all(bf16[16,128,128]{2,1,0:T(8,128)(2,1)S(1)} %bitcast.94), channel_id=1, replica_groups=mesh['dp'=16,'chip'=8,'core'=2] {'chip','core'}, dimensions={0} | all-to-all | bytes 1048576 | tf_op jit(solution)/shard_map/all_to_all | solution.py:249
  105.1 19.0 %all_to_all.46 = bf16[8,128,512]{2,1,0:T(8,128)(2,1)S(1)} all-to-all(bf16[8,128,512]{2,1,0:T(8,128)(2,1)S(1)} %broadcast_in_dim.14), channel_id=1, replica_groups=mesh['dp'=16,'chip'=8,'core'=2] {'chip'}, dimensions={0} | all-to-all | bytes 2097152 | tf_op jit(solution)/shard_map/all_to_all | solution.py:249
  124.1 1.8 collective-permute-start.3
  126.0 1.9 copy.17
  127.9 0.5 collective-permute-done.3
  128.4 1.9 maximum_select_fusion
  130.3 1.0 fusion.14
  131.3 18.9 %all_to_all.47 = bf16[16,24,512]{2,1,0:T(8,128)(2,1)S(1)} all-to-all(bf16[16,24,512]{2,1,0:T(8,128)(2,1)S(1)} %bitcast.103), channel_id=1, replica_groups=mesh['dp'=16,'chip'=8,'core'=2] {'dp'}, dimensions={0} | all-to-all | bytes 786432 | tf_op jit(solution)/shard_map/all_to_all | solution.py:249
  150.3 16.9 %all_to_all.48 = bf16[16,24,512]{2,1,0:T(8,128)(2,1)S(1)} all-to-all(bf16[16,24,512]{2,1,0:T(8,128)(2,1)S(1)} %broadcast_in_dim.15), channel_id=1, replica_groups=mesh['dp'=16,'chip'=8,'core'=2] {'dp'}, dimensions={0} | all-to-all | bytes 786432 | tf_op jit(solution)/shard_map/all_to_all | solution.py:249
  167.2 0.5 fusion.15
  168.2 2.5 %collective-permute-start.8 = (f32[128,128]{1,0:T(8,128)S(1)}, f32[128,128]{1,0:T(8,128)S(1)}, u32[]{:S(2)}, u32[]{:S(2)}) collective-permute-start(f32[128,128]{1,0:T(8,128)S(1)} %fusion.17), channel_id=1, source_target_pairs={{0,1},{1,0},{2,3},{3,2},{4,5},{5,4},{6,7},{7,6},{8,9},{9,8},{10,11... | collective-permute-start | bytes 196616 | tf_op jit(solution)/shard_map/ppermute | solution.py:235
  170.7 0.9 collective-permute-done.8
  171.7 0.8 broadcast_in_dim.16
  172.5 3.5 %all-to-all-start.7 = ((f32[8,128,128]{2,1,0:T(8,128)}), f32[8,128,128]{2,1,0:T(8,128)S(1)}, u32[]{:S(2)}, u32[]{:S(2)}) async-start(f32[8,128,128]{2,1,0:T(8,128)} %broadcast_in_dim.16), calls=%async_computation.7 | async-start | bytes 1048576 | tf_op jit(solution)/shard_map/all_to_all | solution.py:249
  176.0 1.0 broadcast_in_dim.12
  177.0 0.9 fusion.11
  178.2 5.3 %collective-permute-start.5 = (bf16[128,768]{1,0:T(8,128)(2,1)}, bf16[128,768]{1,0:T(8,128)(2,1)S(1)}, u32[]{:S(2)}, u32[]{:S(2)}) collective-permute-start(bf16[128,768]{1,0:T(8,128)(2,1)} %get-tuple-element.31), channel_id=1, source_target_pairs={{0,14},{1,15},{2,12},{3,13},{4,10},{5,11},{6,8},{7,9},{8,6},{9,7},... | collective-permute-start | bytes 589832 | tf_op jit(solution)/shard_map/ppermute | solution.py:246
  183.7 0.6 fusion.16
  184.2 2.8 %all-to-all-done.7 = f32[8,128,128]{2,1,0:T(8,128)S(1)} async-done(((f32[8,128,128]{2,1,0:T(8,128)}), f32[8,128,128]{2,1,0:T(8,128)S(1)}, u32[]{:S(2)}, u32[]{:S(2)}) %all-to-all-start.7) | async-done | bytes 524320 | tf_op jit(solution)/shard_map/all_to_all | solution.py:249
  187.0 5.6 %all-to-all-start.4 = ((bf16[16,128,128]{2,1,0:T(8,128)(2,1)}), bf16[16,128,128]{2,1,0:T(8,128)(2,1)S(1)}, u32[]{:S(2)}, u32[]{:S(2)}) async-start(bf16[16,128,128]{2,1,0:T(8,128)(2,1)} %bitcast.23), calls=%async_computation.4 | async-start | bytes 1048576 | tf_op jit(solution)/shard_map/all_to_all | solution.py:249
  193.0 0.7 constant_dynamic-update-slice_fusion.18
  193.7 0.7 constant_dynamic-update-slice_fusion.17
  194.4 0.7 reduce_sum.57.g_ref
  195.0 9.0 %all-to-all-done.4 = bf16[16,128,128]{2,1,0:T(8,128)(2,1)S(1)} async-done(((bf16[16,128,128]{2,1,0:T(8,128)(2,1)}), bf16[16,128,128]{2,1,0:T(8,128)(2,1)S(1)}, u32[]{:S(2)}, u32[]{:S(2)}) %all-to-all-start.4) | async-done | bytes 524320 | tf_op jit(solution)/shard_map/all_to_all | solution.py:249
  204.0 0.9 broadcast_in_dim.17
  204.9 3.5 %all-to-all-start.8 = ((bf16[8,256,128]{2,1,0:T(8,128)(2,1)}), bf16[8,256,128]{2,1,0:T(8,128)(2,1)S(1)}, u32[]{:S(2)}, u32[]{:S(2)}) async-start(bf16[8,256,128]{2,1,0:T(8,128)(2,1)} %broadcast_in_dim.17), calls=%async_computation.8 | async-start | bytes 1048576 | tf_op jit(solution)/shard_map/all_to_all | solution.py:249
  208.4 0.7 constant_dynamic-update-slice_fusion.16
  209.2 0.7 pad_maximum_fusion.5
  209.9 14.1 %inverse_factor.1 = f32[128,128]{1,0:T(8,128)} custom-call(f32[128,128]{1,0:T(8,128)} %reduce_sum.57.g_ref), custom_call_target="tpu_custom_call" | custom-call | tf_op jit(solution)/shard_map/inverse_factor/pallas_call | solution.py:212
  224.0 1.1 convolution_multiply_fusion
  225.2 1.2 collective-permute-start.9
  226.4 1.2 fusion.18
  227.6 0.8 fusion.19
  228.4 1.1 subtract_bitcast_fusion
  (53 shorter events, 2.1 us)
Async XLA Ops:
  0.6 166.6 %copy-start = (f32[512,128]{1,0:T(8,128)S(1)}, f32[512,128]{1,0:T(8,128)}, u32[]{:S(2)}) copy-start(f32[512,128]{1,0:T(8,128)} %param.15) | copy-start | bytes 786436
  0.7 9.8 %copy-start.10 = (s32[128]{0:T(128)S(1)}, s32[128]{0:T(128)}, u32[]{:S(2)}) copy-start(s32[128]{0:T(128)} %param.13) | copy-start | bytes 1540
  0.7 9.9 %copy-start.8 = (bf16[128,512]{1,0:T(8,128)(2,1)S(1)}, bf16[128,512]{1,0:T(8,128)(2,1)}, u32[]{:S(2)}) copy-start(bf16[128,512]{1,0:T(8,128)(2,1)} %param.9) | copy-start | bytes 393220
  0.7 9.9 %copy-start.9 = (bf16[128,512]{1,0:T(8,128)(2,1)S(1)}, bf16[128,512]{1,0:T(8,128)(2,1)}, u32[]{:S(2)}) copy-start(bf16[128,512]{1,0:T(8,128)(2,1)} %param.10) | copy-start | bytes 393220
  3.9 32.6 %collective-permute-start.2 = (bf16[128,1536]{1,0:T(8,128)(2,1)}, bf16[128,1536]{1,0:T(8,128)(2,1)}, u32[]{:S(2)}, u32[]{:S(2)}) collective-permute-start(bf16[128,1536]{1,0:T(8,128)(2,1)} %pad_maximum_fusion.3), channel_id=1, source_target_pairs={{0,15},{1,14},{2,13},{3,12},{4,11},{5,10},{6,9},{7,8},{8,7},{9,6},... | collective-permute-start | bytes 1179656 | tf_op jit(solution)/shard_map/ppermute | solution.py:246
  22.1 31.9 %all-to-all-start = ((bf16[16,144,256]{2,1,0:T(8,128)(2,1)}), bf16[16,144,256]{2,1,0:T(8,128)(2,1)S(1)}, u32[]{:S(2)}, u32[]{:S(2)}) async-start(bf16[16,144,256]{2,1,0:T(8,128)(2,1)} %constant_dynamic-update-slice_fusion), calls=%async_computation | async-start | bytes 2359296 | tf_op jit(solution)/shard_map/all_to_all | solution.py:249
  25.7 9.2 %copy-start.4 = (bf16[128,6144]{1,0:T(8,128)(2,1)S(1)}, bf16[128,6144]{1,0:T(8,128)(2,1)}, u32[]{:S(2)}) copy-start(bf16[128,6144]{1,0:T(8,128)(2,1)} %param.12) | copy-start | bytes 4718596
  27.7 25.1 %collective-permute-start.1 = (bf16[128,1536]{1,0:T(8,128)(2,1)}, bf16[128,1536]{1,0:T(8,128)(2,1)}, u32[]{:S(2)}, u32[]{:S(2)}) collective-permute-start(bf16[128,1536]{1,0:T(8,128)(2,1)} %pad_maximum_fusion.2), channel_id=1, source_target_pairs={{0,14},{1,15},{2,12},{3,13},{4,10},{5,11},{6,8},{7,9},{8,6},{9,7},... | collective-permute-start | bytes 1179656 | tf_op jit(solution)/shard_map/ppermute | solution.py:246
  34.2 18.5 %collective-permute-start = (bf16[128,1536]{1,0:T(8,128)(2,1)}, bf16[128,1536]{1,0:T(8,128)(2,1)}, u32[]{:S(2)}, u32[]{:S(2)}) collective-permute-start(bf16[128,1536]{1,0:T(8,128)(2,1)} %pad_maximum_fusion.1), channel_id=1, source_target_pairs={{0,1},{1,0},{2,3},{3,2},{4,5},{5,4},{6,7},{7,6},{8,9},{9,8},{10,11... | collective-permute-start | bytes 1179656 | tf_op jit(solution)/shard_map/ppermute | solution.py:246
  54.1 32.4 %all-to-all-start.1 = ((bf16[16,128,384]{1,2,0:T(8,128)(2,1)}), bf16[16,128,384]{1,2,0:T(8,128)(2,1)}, u32[]{:S(2)}, u32[]{:S(2)}) async-start(bf16[16,128,384]{1,2,0:T(8,128)(2,1)} %bitcast.96), calls=%async_computation.1 | async-start | bytes 3145728 | tf_op jit(solution)/shard_map/all_to_all | solution.py:249
  85.6 0.9 copy-start.1
  105.0 19.2 %copy-start.7 = (bf16[128,512]{1,0:T(8,128)(2,1)}, bf16[128,512]{1,0:T(8,128)(2,1)S(1)}, u32[]{:S(2)}) copy-start(bf16[128,512]{1,0:T(8,128)(2,1)S(1)} %pad_maximum_fusion.4) | copy-start | bytes 393220
  124.1 4.3 %collective-permute-start.3 = (bf16[8,128,512]{2,1,0:T(8,128)(2,1)S(1)}, bf16[8,128,512]{2,1,0:T(8,128)(2,1)}, u32[]{:S(2)}, u32[]{:S(2)}) collective-permute-start(bf16[8,128,512]{2,1,0:T(8,128)(2,1)S(1)} %all_to_all.46), channel_id=1, source_target_pairs={{0,1},{1,0},{2,3},{3,2},{4,5},{5,4},{6,7},{7,6},{8,9},{9,8},{10,11... | collective-permute-start | bytes 3145736 | tf_op jit(solution)/shard_map/ppermute | solution.py:235
  128.4 1.9 copy-start.6
  168.2 3.4 %collective-permute-start.8 = (f32[128,128]{1,0:T(8,128)S(1)}, f32[128,128]{1,0:T(8,128)S(1)}, u32[]{:S(2)}, u32[]{:S(2)}) collective-permute-start(f32[128,128]{1,0:T(8,128)S(1)} %fusion.17), channel_id=1, source_target_pairs={{0,1},{1,0},{2,3},{3,2},{4,5},{5,4},{6,7},{7,6},{8,9},{9,8},{10,11... | collective-permute-start | bytes 196616 | tf_op jit(solution)/shard_map/ppermute | solution.py:235
  171.7 5.3 %copy-start.2 = (bf16[512,768]{1,0:T(8,128)(2,1)S(1)}, bf16[512,768]{1,0:T(8,128)(2,1)}, u32[]{:S(2)}) copy-start(bf16[512,768]{1,0:T(8,128)(2,1)} %copy-done.1) | copy-start | bytes 2359300
  172.5 14.5 %all-to-all-start.7 = ((f32[8,128,128]{2,1,0:T(8,128)}), f32[8,128,128]{2,1,0:T(8,128)S(1)}, u32[]{:S(2)}, u32[]{:S(2)}) async-start(f32[8,128,128]{2,1,0:T(8,128)} %broadcast_in_dim.16), calls=%async_computation.7 | async-start | bytes 1048576 | tf_op jit(solution)/shard_map/all_to_all | solution.py:249
  177.9 15.1 %collective-permute-start.4 = (bf16[128,768]{1,0:T(8,128)(2,1)}, bf16[128,768]{1,0:T(8,128)(2,1)S(1)}, u32[]{:S(2)}, u32[]{:S(2)}) collective-permute-start(bf16[128,768]{1,0:T(8,128)(2,1)} %get-tuple-element.32), channel_id=1, source_target_pairs={{0,1},{1,0},{2,3},{3,2},{4,5},{5,4},{6,7},{7,6},{8,9},{9,8},{10,11... | collective-permute-start | bytes 589832 | tf_op jit(solution)/shard_map/ppermute | solution.py:246
  178.2 15.5 %collective-permute-start.5 = (bf16[128,768]{1,0:T(8,128)(2,1)}, bf16[128,768]{1,0:T(8,128)(2,1)S(1)}, u32[]{:S(2)}, u32[]{:S(2)}) collective-permute-start(bf16[128,768]{1,0:T(8,128)(2,1)} %get-tuple-element.31), channel_id=1, source_target_pairs={{0,14},{1,15},{2,12},{3,13},{4,10},{5,11},{6,8},{7,9},{8,6},{9,7},... | collective-permute-start | bytes 589832 | tf_op jit(solution)/shard_map/ppermute | solution.py:246
  183.5 24.9 %collective-permute-start.6 = (bf16[128,768]{1,0:T(8,128)(2,1)}, bf16[128,768]{1,0:T(8,128)(2,1)S(1)}, u32[]{:S(2)}, u32[]{:S(2)}) collective-permute-start(bf16[128,768]{1,0:T(8,128)(2,1)} %get-tuple-element.30), channel_id=1, source_target_pairs={{0,15},{1,14},{2,13},{3,12},{4,11},{5,10},{6,9},{7,8},{8,7},{9,6},... | collective-permute-start | bytes 589832 | tf_op jit(solution)/shard_map/ppermute | solution.py:246
  187.0 17.0 %all-to-all-start.4 = ((bf16[16,128,128]{2,1,0:T(8,128)(2,1)}), bf16[16,128,128]{2,1,0:T(8,128)(2,1)S(1)}, u32[]{:S(2)}, u32[]{:S(2)}) async-start(bf16[16,128,128]{2,1,0:T(8,128)(2,1)} %bitcast.23), calls=%async_computation.4 | async-start | bytes 1048576 | tf_op jit(solution)/shard_map/all_to_all | solution.py:249
  192.7 1.7 collective-permute-start.7
  204.9 19.1 %all-to-all-start.8 = ((bf16[8,256,128]{2,1,0:T(8,128)(2,1)}), bf16[8,256,128]{2,1,0:T(8,128)(2,1)S(1)}, u32[]{:S(2)}, u32[]{:S(2)}) async-start(bf16[8,256,128]{2,1,0:T(8,128)(2,1)} %broadcast_in_dim.17), calls=%async_computation.8 | async-start | bytes 1048576 | tf_op jit(solution)/shard_map/all_to_all | solution.py:249
  225.2 2.4 %collective-permute-start.9 = (f32[256,128]{1,0:T(8,128)S(1)}, f32[256,128]{1,0:T(8,128)S(1)}, u32[]{:S(2)}, u32[]{:S(2)}) collective-permute-start(f32[256,128]{1,0:T(8,128)S(1)} %convolution_multiply_fusion), channel_id=1, source_target_pairs={{0,1},{1,0},{2,3},{3,2},{4,5},{5,4},{6,7},{7,6},{8,9},{9,8},{10,11... | collective-permute-start | bytes 393224 | tf_op jit(solution)/shard_map/ppermute | solution.py:235
  227.6 1.9 copy-start.5
  228.4 1.1 copy-start.3

commit v3 on v2

--- a/solution.py
+++ b/solution.py
@@ -17,13 +17,13 @@
 HEADS_AT_ONCE = 2
 
 
-def attention(where, qg, kv):
+def attention(where, parts, kv):
     devices, padded, _ = kv.shape
     tokens = HEAD
     block = 2 * tokens
     chips = devices // 2
     length = devices * tokens
-    heads = qg.shape[1] // (2 * HEAD)
+    heads = parts[0].shape[1] // (2 * HEAD)
     steps = heads // HEADS_AT_ONCE
     wide = HEADS_AT_ONCE * HEAD
     columns = HEADS_AT_ONCE * block
@@ -31,7 +31,7 @@
     power = scale * LOG2E
 
     def kernel(
-        at, q_ref, g_ref, k_ref, v_ref, dq_ref, dk_ref, dv_ref,
+        at, q0, q1, q2, q3, g0, g1, g2, g3, k_ref, v_ref, dq_ref, dk_ref, dv_ref,
         s_scr, d_scr, bias, k_turned, dq_acc, dk_acc, dv_acc,
     ):
         step = pl.program_id(0)
@@ -80,14 +80,16 @@
                     k_ref[2 * j : 2 * j + 2, :tokens, :].reshape(block, HEAD).astype(jnp.float32).T
                 ).astype(jnp.bfloat16)
 
-        def stacked(ref):
-            x = ref[...]
-            return jnp.concatenate(
-                [x[:, n * HEAD : (n + 1) * HEAD] for n in range(HEADS_AT_ONCE)], axis=0
-            )
-
-        q = stacked(q_ref)
-        g = stacked(g_ref)
+        def stacked(a, b, c, d):
+            x = jnp.where(step < steps, a[...], c[...])
+            y = jnp.where(step < steps, b[...], d[...])
+            rows = []
+            for n in range(HEADS_AT_ONCE):
+                rows += [x[:, n * HEAD : (n + 1) * HEAD], y[:, n * HEAD : (n + 1) * HEAD]]
+            return jnp.concatenate(rows, axis=0)
+
+        q = stacked(q0, q1, q2, q3)
+        g = stacked(g0, g1, g2, g3)
 
         def fold(x):
             return x.reshape(block // 8, 8, columns)
@@ -148,8 +150,8 @@
             num_scalar_prefetch=1,
             grid=(2 * steps,),
             in_specs=[
-                queries_at,
-                pl.BlockSpec((block, wide), lambda s, at: (s // steps, steps + s % steps)),
+                *[pl.BlockSpec((tokens, wide), lambda s, at: (0, s % steps))] * 4,
+                *[pl.BlockSpec((tokens, wide), lambda s, at: (0, steps + s % steps))] * 4,
                 pl.BlockSpec((devices, padded, HEAD), lambda s, at: (0, 0, 0)),
                 pl.BlockSpec((devices, padded, HEAD), lambda s, at: (0, 0, 1)),
             ],
@@ -176,46 +178,190 @@
             flops=8 * flops, bytes_accessed=8 * 1024 * 1024, transcendentals=0
         ),
         name="attention",
-    )(where, qg, qg, kv, kv)
-
-
-def inverse_factor(gram):
-    size = gram.shape[0]
+    )(where, *parts, *parts, kv, kv)
+
+
+VMEM = pl.BlockSpec(memory_space=pltpu.VMEM)
+SMEM = pl.BlockSpec(memory_space=pltpu.SMEM)
+
+
+def pack_keys(keys, values, starts, devices):
+    tokens = keys.shape[0]
+
+    def kernel(k_ref, v_ref, s_ref, out_ref):
+        start = s_ref[...]
+        high = jnp.right_shift(start, 6).astype(jnp.float32)
+        low = jnp.bitwise_and(start, 63).astype(jnp.float32)
+        row = jnp.concatenate([high, low], axis=1)
+        first = lax.broadcasted_iota(jnp.int32, (16, 2 * tokens), 0) == 0
+        extra = jnp.where(first, row, 0.0).astype(jnp.bfloat16)
+        for n in range(devices):
+            h = 2 * (n % 2) + (n >= devices // 2)
+            out_ref[n, :tokens, :HEAD] = k_ref[:, h * HEAD : (h + 1) * HEAD]
+            out_ref[n, :tokens, HEAD:] = v_ref[:, h * HEAD : (h + 1) * HEAD]
+            out_ref[n, tokens:, :] = extra
+
+    return pl.pallas_call(
+        kernel,
+        out_shape=jax.ShapeDtypeStruct((devices, tokens + 16, 2 * HEAD), jnp.bfloat16),
+        in_specs=[VMEM] * 3,
+        out_specs=VMEM,
+        name="pack_keys",
+    )(keys, values, starts)
+
+
+def pack_queries(heads, queries, d_out, group):
+    tokens = queries.shape[0]
+
+    def kernel(h_ref, q_ref, g_ref, *outs):
+        for n, out in enumerate(outs):
+            span = pl.ds(pl.multiple_of(h_ref[n] * group, group), group)
+            out[:, :group] = q_ref[:, span]
+            out[:, group:] = g_ref[:, span]
+
+    return pl.pallas_call(
+        kernel,
+        out_shape=[jax.ShapeDtypeStruct((tokens, 2 * group), jnp.bfloat16)] * 4,
+        in_specs=[SMEM, VMEM, VMEM],
+        out_specs=[VMEM] * 4,
+        name="pack_queries",
+    )(heads, queries, d_out)
+
+
+def unpack_queries(heads, parts, group):
+    tokens = parts[0].shape[0]
+
+    def kernel(h_ref, *refs):
+        for n in range(4):
+            span = pl.ds(pl.multiple_of(h_ref[n] * group, group), group)
+            refs[4][:, span] = refs[n][...]
+
+    return pl.pallas_call(
+        kernel,
+        out_shape=jax.ShapeDtypeStruct((tokens, 4 * group), jnp.bfloat16),
+        in_specs=[SMEM] + [VMEM] * 4,
+        out_specs=VMEM,
+        name="unpack_queries",
+    )(heads, *parts)
+
+
+def gradient(where, turned, mine, theirs, error):
+    devices, rows, tokens = turned.shape
+    width = mine.shape[2]
+
+    def kernel(at, f_ref, m_ref, t_ref, e_ref, out_ref, low_ref):
+        core = at[0]
+        total = e_ref[...]
+        for c in range(devices // 2):
+            total = total + jnp.dot(
+                f_ref[2 * c + core], m_ref[c], preferred_element_type=jnp.float32
+            )
+            total = total + jnp.dot(
+                f_ref[2 * c + 1 - core], t_ref[c], preferred_element_type=jnp.float32
+            )
+        out_ref[...] = total
+        low_ref[...] = total.astype(jnp.bfloat16)
+
+    return pl.pallas_call(
+        kernel,
+        out_shape=[
+            jax.ShapeDtypeStruct((rows, width), jnp.float32),
+            jax.ShapeDtypeStruct((rows, width), jnp.bfloat16),
+        ],
+        in_specs=[SMEM] + [VMEM] * 4,
+        out_specs=[VMEM] * 2,
+        compiler_params=pltpu.CompilerParams(vmem_limit_bytes=32 * 1024 * 1024),
+        name="gradient",
+    )(where, turned, mine, theirs, error)
+
+
+def inverse_factor(parts):
+    count, size, _ = parts.shape
     tiles = size // 8
 
     def kernel(g_ref, out_ref):
         sub = lax.broadcasted_iota(jnp.int32, (8, 1), 0)
         lane = lax.broadcasted_iota(jnp.int32, (8, size), 1)
         row8 = lax.broadcasted_iota(jnp.int32, (8, size), 0)
-        left = [g_ref[8 * t : 8 * t + 8, :] for t in range(tiles)]
-        right = [jnp.where(lane == row8 + 8 * t, 1.0, 0.0) for t in range(tiles)]
-        for j in range(size):
+        left, right = [], []
+        for t in range(tiles):
+            total = g_ref[0, 8 * t : 8 * t + 8, :]
+            for n in range(1, count):
+                total = total + g_ref[n, 8 * t : 8 * t + 8, :]
+            left.append(total)
+            right.append(jnp.where(lane == row8 + 8 * t, 1.0, 0.0))
+        for j in range(0, size, 2):
             t0, r = j // 8, j % 8
-            row_l = left[t0][r : r + 1, :]
-            row_r = right[t0][r : r + 1, :]
-            root = 1.0 / jnp.sqrt(row_l[:, j : j + 1])
-            row_l = row_l * root
-            row_r = row_r * root
+            l0, l1 = left[t0][r : r + 1, :], left[t0][r + 1 : r + 2, :]
+            r0, r1 = right[t0][r : r + 1, :], right[t0][r + 1 : r + 2, :]
+            a, b, c = l0[:, j : j + 1], l0[:, j + 1 : j + 2], l1[:, j + 1 : j + 2]
+            det = a * c - b * b
+            inv = 1.0 / det
+            ai, bi, ci = a * inv, b * inv, c * inv
+            ul, vl = ci * l0 - bi * l1, ai * l1 - bi * l0
+            ur, vr = ci * r0 - bi * r1, ai * r1 - bi * r0
+            over = 1.0 / a
+            out_ref[j : j + 1, :] = r0 * jnp.sqrt(over)
+            out_ref[j + 1 : j + 2, :] = (r1 - (b * over) * r0) * jnp.sqrt(ai)
             for t in range(t0, tiles):
-                c = left[t][:, j : j + 1] * root
+                x, y = left[t][:, j : j + 1], left[t][:, j + 1 : j + 2]
                 if t == t0:
-                    c = jnp.where(sub > r, c, 0.0)
-                    hit = sub == r
-                    left[t] = jnp.where(hit, row_l, left[t] - c * row_l)
-                    right[t] = jnp.where(hit, row_r, right[t] - c * row_r)
-                else:
-                    left[t] = left[t] - c * row_l
-                    right[t] = right[t] - c * row_r
-        for t in range(tiles):
-            out_ref[8 * t : 8 * t + 8, :] = right[t]
+                    if r == 6:
+                        continue
+                    x = jnp.where(sub > r + 1, x, 0.0)
+                    y = jnp.where(sub > r + 1, y, 0.0)
+                left[t] = left[t] - (x * ul + y * vl)
+                right[t] = right[t] - (x * ur + y * vr)
 
     return pl.pallas_call(
         kernel,
         out_shape=jax.ShapeDtypeStruct((size, size), jnp.float32),
-        in_specs=[pl.BlockSpec(memory_space=pltpu.VMEM)],
-        out_specs=pl.BlockSpec(memory_space=pltpu.VMEM),
+        in_specs=[VMEM],
+        out_specs=VMEM,
+        cost_estimate=pl.CostEstimate(
+            flops=8 * 10**9, bytes_accessed=10**6, transcendentals=0
+        ),
         name="inverse_factor",
-    )(gram)
+    )(parts)
+
+
+def finish(where, p_sum, inverse, moment, their_moment, combined, replicas):
+    rows, width = combined.shape
+    rank = p_sum.shape[1]
+    half = moment.shape[0]
+
+    def kernel(at, p_ref, i_ref, m_ref, t_ref, c_ref, comp_ref, q_ref, new_ref):
+        core = at[0]
+        inv = i_ref[...]
+
+        def product(x, y):
+            return lax.dot_general(
+                x, y, NT, precision=HIGHEST, preferred_element_type=jnp.float32
+            )
+
+        q_ref[pl.ds(pl.multiple_of(core * half, half), half), :] = (
+            product(m_ref[...], inv) * (1.0 / replicas)
+        )
+        q_ref[pl.ds(pl.multiple_of((1 - core) * half, half), half), :] = (
+            product(t_ref[...], inv) * (1.0 / replicas)
+        )
+        p_hat = product(p_ref[...], inv)
+        out = product(p_hat, q_ref[...])
+        comp_ref[...] = out
+        new_ref[0] = c_ref[...] - out
+
+    return pl.pallas_call(
+        kernel,
+        out_shape=[
+            jax.ShapeDtypeStruct((rows, width), jnp.float32),
+            jax.ShapeDtypeStruct((width, rank), jnp.float32),
+            jax.ShapeDtypeStruct((1, rows, width), jnp.float32),
+        ],
+        in_specs=[SMEM] + [VMEM] * 5,
+        out_specs=[VMEM] * 3,
+        compiler_params=pltpu.CompilerParams(vmem_limit_bytes=32 * 1024 * 1024),
+        name="finish",
+    )(where, p_sum, inverse, moment, their_moment, combined)
 
 
 def body(queries, keys, values, d_out, features, doc_start, error, q_init):
@@ -255,40 +401,18 @@
         return 2 * (1 - core if turn else core) + (1 - upper if cross else upper)
 
     ways = [(False, False), (False, True), (True, False), (True, True)]
-    start_row = jnp.concatenate([doc_start // 64, doc_start % 64]).astype(bf16)[None, :]
-    start_rows = jnp.concatenate([start_row, jnp.zeros((15, 2 * tokens), bf16)], axis=0)
-    per_head = [
-        jnp.concatenate(
-            [
-                jnp.concatenate(
-                    [keys[:, h * HEAD : (h + 1) * HEAD], values[:, h * HEAD : (h + 1) * HEAD]],
-                    axis=1,
-                ),
-                start_rows,
-            ],
-            axis=0,
-        )
-        for h in range(width_kv // HEAD)
-    ]
-    per_half = [jnp.stack([per_head[u], per_head[2 + u]]) for u in range(2)]
-    kv_send = jnp.concatenate([per_half[0]] * (chips // 2) + [per_half[1]] * (chips // 2), axis=0)
-    kv = exchange(kv_send, ctx)
-
-    def both_of(head):
-        return jnp.concatenate([piece(queries, group, head), piece(d_out, group, head)], axis=1)
-
-    qg = [both_of(head_of(False, False))]
-    for cross, turn in ways[1:]:
-        qg.append(move(both_of(head_of(cross, turn)), cross, turn))
-    qg = jnp.concatenate(qg, axis=0)
+    heads = jnp.stack([head_of(*way) for way in ways]).astype(jnp.int32)
+    kv = exchange(pack_keys(keys, values, doc_start[None, :], devices), ctx)
+    parts = pack_queries(heads, queries, d_out, group)
+    parts = [parts[0]] + [move(x, *way) for x, way in zip(parts[1:], ways[1:])]
 
     rows = features.shape[1] // devices
-    feat_send = jnp.transpose(features.reshape(tokens, devices, rows), (1, 0, 2))
-    kv, feat_send = lax.optimization_barrier((kv, feat_send))
-    feat = exchange(feat_send, ctx)
+    feat = jnp.transpose(features).reshape(devices, rows, tokens)
+    kv, feat = lax.optimization_barrier((kv, feat))
+    feat = exchange(feat, ctx)
 
     where = jnp.stack([core, chip, chips - 1 - chip]).astype(jnp.int32)
-    dq, dk, dv = attention(where, qg, kv)
+    dq, dk, dv = attention(where, parts, kv)
     dk, feat = lax.optimization_barrier((dk, feat))
 
     def to_owner(x):
@@ -300,47 +424,57 @@
     d_key = to_owner(dk)
     dk_mine = spread(d_key, "chip", chips)
     dk_theirs = swap(dk_mine)
-    by_token = jnp.where(
-        core == 0,
-        jnp.stack([dk_mine, dk_theirs], axis=1),
-        jnp.stack([dk_theirs, dk_mine], axis=1),
-    ).reshape(devices * tokens, width_kv)
-    grad = lax.dot_general(
-        feat.reshape(devices * tokens, rows), by_token, TN, preferred_element_type=f32
-    )
-    combined = grad + error.reshape(rows, width_kv)
-
-    shares = combined.astype(bf16).reshape(replicas, rows // replicas, width_kv)
+    combined, low = gradient(where, feat, dk_mine, dk_theirs, error.reshape(rows, width_kv))
+
+    shares = low.reshape(replicas, rows // replicas, width_kv)
     shares, dv, dq = lax.optimization_barrier((shares, dv, dq))
     shares = exchange(shares, "dp")
-    d_value = to_owner(dv)
+    dv = dv.reshape(chips, 2 * tokens, HEAD)
+    sums = []
+    for low_k in (0, chips // 2):
+        total = None
+        for k in range(low_k, low_k + chips // 2):
+            x = piece(dv, 1, jnp.bitwise_xor(chip, k), 0)[0]
+            if k:
+                x = lax.ppermute(x, "chip", [(i, i ^ k) for i in range(chips)])
+            x = x.astype(f32)
+            total = x if total is None else total + x
+        sums.append(total.astype(bf16))
     share = jnp.sum(shares.astype(f32), axis=0).astype(bf16)
-    total = spread(share, "dp", replicas).reshape(rows, width_kv).astype(f32)
-
-    d_query = jnp.zeros((tokens, queries.shape[1]), bf16)
-    for n, (cross, turn) in enumerate(ways):
-        back = dq[n * tokens : (n + 1) * tokens]
-        if n:
-            back = move(back, cross, turn)
-        d_query = lax.dynamic_update_slice_in_dim(d_query, back, head_of(cross, turn) * group, 1)
-
+    share, *sums = lax.optimization_barrier((share, *sums))
+    total = spread(share, "dp", replicas).reshape(rows, width_kv)
+    dv_half = jnp.where(
+        upper == 0,
+        jnp.concatenate(sums, axis=1),
+        jnp.concatenate(sums[::-1], axis=1),
+    )
+    dv_mine = piece(dv_half, tokens, core, 0)
+    dv_theirs = swap(piece(dv_half, tokens, 1 - core, 0))
+    d_value = jnp.where(
+        core == 0,
+        jnp.concatenate([dv_mine, dv_theirs], axis=1),
+        jnp.concatenate([dv_theirs, dv_mine], axis=1),
+    )
+    back = [dq[:tokens]] + [
+        move(dq[n * tokens : (n + 1) * tokens], *ways[n]) for n in range(1, 4)
+    ]
+    total, *back = lax.optimization_barrier((total, *back))
+    d_query = unpack_queries(heads, back, group)
+
+    total = total.astype(f32)
     p_sum = jnp.dot(total, q_init, precision=HIGHEST)
     gram = lax.dot_general(p_sum, p_sum, TN, precision=HIGHEST)
-    gram = jnp.sum(spread(gram + swap(gram), "chip", chips), axis=0)
+    gram = spread(gram + swap(gram), "chip", chips)
     moment = lax.dot_general(total, p_sum, TN, precision=HIGHEST)
     size = width_kv // 2
     moment = piece(moment, size, core, 0) + swap(piece(moment, size, 1 - core, 0))
     moment, gram = lax.optimization_barrier((moment.astype(bf16), gram))
     moment = jnp.sum(spread(moment, "chip", chips).astype(f32), axis=0)
+    their_moment = swap(moment)
     inverse = inverse_factor(gram)
-    q_mine = lax.dot_general(moment, inverse, NT, precision=HIGHEST) / replicas
-    q_theirs = swap(q_mine)
-    q_factor = jnp.where(
-        core == 0, jnp.concatenate([q_mine, q_theirs]), jnp.concatenate([q_theirs, q_mine])
+    compressed, q_factor, new_error = finish(
+        where, p_sum, inverse, moment, their_moment, combined, replicas
     )
-    p_hat = lax.dot_general(p_sum, inverse, NT, precision=HIGHEST)
-    compressed = lax.dot_general(p_hat, q_factor, NT, precision=HIGHEST)
-    new_error = (combined - compressed).reshape(1, rows, width_kv)
     return (d_query, d_key, d_value, compressed, q_factor, new_error)
 
 

time: 231 us -> 238 us (1.030)
  starting transfers between devices: 45.1 us -> 73.5 us
  blocking collectives: 73.2 us -> 45.2 us
  waiting for transfers between devices: 29.4 us -> 55.9 us
  other arithmetic: 22 us -> 2.34 us
  Pallas kernels: 40.5 us -> 46.3 us
  matrix products: 5.64 us -> 1.57 us
    all_to_all x4 -> x2, blocking collectives: 73.2 us -> 45.2 us  [exchange(): return lax.all_to_all(x, axis, 0, 0)]
    all_to_all x5 -> x6, starting transfers between devices: 21.3 us -> 39 us  [exchange(): return lax.all_to_all(x, axis, 0, 0)]
    pallas_call x0 -> x5, Pallas kernels: none -> 13.2 us  [the longest x1 3.13 us: finish(): pl.pallas_call(kernel, out_shape=[jax.ShapeDtypeStruct((rows, width), jnp...]
    ppermute x0 -> x7, starting transfers between devices: none -> 12.3 us  [body(): x = lax.ppermute(x, 'chip', [(i, i ^ k) for i in range(chips)])]
    pallas_call x1, Pallas kernels: 26.4 us -> 14.3 us  [attention(): pl.pallas_call(kernel, grid_spec=pltpu.PrefetchScalarGridSpec(num_scalar_...]
    ppermute x6, waiting for transfers between devices: 16.2 us -> 27.5 us  [move(): return lax.ppermute(x, ctx, pairs)]
    unnamed x15 -> x0, other arithmetic: 10.7 us -> none
    all_to_all x5 -> x6, waiting for transfers between devices: 11.8 us -> 21.6 us  [exchange(): return lax.all_to_all(x, axis, 0, 0)]
  transfers between devices with their start and end apart: 15 -> 24, of which waited for: 5 -> 13; matrix products, arithmetic and copies ran while one was open for 12% -> 2% of each run, Pallas kernels for 18% -> 16%
where the time goes in v3:
time: 238 us; the launch traced here: 237 us
  starting transfers between devices  73.5 us (31%)
  waiting for transfers between devices  55.9 us (23%)
  Pallas kernels  46.3 us (19%)
  blocking collectives  45.2 us (19%)
  local copies, waits for them, and re-layouts  11 us (5%)
    all_to_all x2, blocking collectives, exchange(): return lax.all_to_all(x, axis, 0, 0)  45.2 us
    all_to_all x6, starting transfers between devices, exchange(): return lax.all_to_all(x, axis, 0, 0)  39 us
    ppermute x6, waiting for transfers between devices, move(): return lax.ppermute(x, ctx, pairs)  27.5 us
    all_to_all x6, waiting for transfers between devices, exchange(): return lax.all_to_all(x, axis, 0, 0)  21.6 us
    pallas_call x1, Pallas kernels, inverse_factor(): pl.pallas_call(kernel, out_shape=jax.ShapeDtypeStruct((size, size), jnp.f...  18.9 us
    ppermute x6, starting transfers between devices, move(): return lax.ppermute(x, ctx, pairs)  14.8 us
    pallas_call x1, Pallas kernels, attention(): pl.pallas_call(kernel, grid_spec=pltpu.PrefetchScalarGridSpec(num_scalar_...  14.3 us
    ppermute x7, starting transfers between devices, body(): x = lax.ppermute(x, 'chip', [(i, i ^ k) for i in range(chips)])  12.3 us
  transfers between devices with their start and end apart: 24, of which 13 were waited for; matrix products, arithmetic and copies ran while one was open for 2% of the time, Pallas kernels for 16%

profile of v3, /device:TPU:1, one launch (start us, length us, event | category | flops | bytes accessed | tf_op | source)
XLA Modules:
  0.0 236.7 jit_solution(3107786073055162259)
XLA Ops:
  0.6 2.2 pack_keys.1
  2.8 8.6 %all-to-all-start = ((bf16[16,144,256]{2,1,0:T(8,128)(2,1)}), bf16[16,144,256]{2,1,0:T(8,128)(2,1)S(1)}, u32[]{:S(2)}, u32[]{:S(2)}) async-start(bf16[16,144,256]{2,1,0:T(8,128)(2,1)} %pack_keys.1), calls=%async_computation | async-start | bytes 2359296 | tf_op jit(solution)/shard_map/all_to_all | solution.py:395
  11.4 0.6 pad_add_fusion.h_ref
  12.0 2.6 %pack_queries.1 = (bf16[128,1536]{1,0:T(8,128)(2,1)}, bf16[128,1536]{1,0:T(8,128)(2,1)}, bf16[128,1536]{1,0:T(8,128)(2,1)}, bf16[128,1536]{1,0:T(8,128)(2,1)}) custom-call(s32[4]{0:T(128)} %pad_add_fusion.h_ref, bf16[128,3072]{1,0:T(8,128)(2,1)} %q_ref.1, bf16[128,3072]{1,0:T(8,128)(2,1)} %g_ref.1), custom_call_target="tpu_custom_call" | custom-call | tf_op jit(solution)/shard_map/pack_queries/pallas_call | solution.py:222
  14.6 0.1 collective-permute-start
  14.7 5.2 %collective-permute-start.1 = (bf16[128,1536]{1,0:T(8,128)(2,1)}, bf16[128,1536]{1,0:T(8,128)(2,1)}, u32[]{:S(2)}, u32[]{:S(2)}) collective-permute-start(bf16[128,1536]{1,0:T(8,128)(2,1)} %get-tuple-element.37), channel_id=1, source_target_pairs={{0,14},{1,15},{2,12},{3,13},{4,10},{5,11},{6,8},{7,9},{8,6},{9,7},... | collective-permute-start | bytes 1179656 | tf_op jit(solution)/shard_map/ppermute | solution.py:392
  20.0 0.4 collective-permute-start.2
  20.4 1.6 copy.15
  22.0 8.0 %all-to-all-done.k_ref.v_ref = bf16[16,144,256]{2,1,0:T(8,128)(2,1)S(1)} async-done(((bf16[16,144,256]{2,1,0:T(8,128)(2,1)}), bf16[16,144,256]{2,1,0:T(8,128)(2,1)S(1)}, u32[]{:S(2)}, u32[]{:S(2)}) %all-to-all-start) | async-done | bytes 1179680 | tf_op jit(solution)/shard_map/all_to_all | solution.py:395
  30.0 4.9 %all-to-all-start.1 = ((bf16[16,384,128]{2,1,0:T(8,128)(2,1)}), bf16[16,384,128]{2,1,0:T(8,128)(2,1)S(1)}, u32[]{:S(2)}, u32[]{:S(2)}) async-start(bf16[16,384,128]{2,1,0:T(8,128)(2,1)} %bitcast.51), calls=%async_computation.1 | async-start | bytes 3145728 | tf_op jit(solution)/shard_map/all_to_all | solution.py:395
  35.0 0.7 copy-done.7
  35.7 2.9 %collective-permute-done.1.q2.g2 = bf16[128,1536]{1,0:T(8,128)(2,1)} collective-permute-done((bf16[128,1536]{1,0:T(8,128)(2,1)}, bf16[128,1536]{1,0:T(8,128)(2,1)}, u32[]{:S(2)}, u32[]{:S(2)}) %collective-permute-start.1) | collective-permute-done | bytes 393248 | tf_op jit(solution)/shard_map/ppermute | solution.py:392
  38.6 12.8 %collective-permute-done.2.q3.g3 = bf16[128,1536]{1,0:T(8,128)(2,1)} collective-permute-done((bf16[128,1536]{1,0:T(8,128)(2,1)}, bf16[128,1536]{1,0:T(8,128)(2,1)}, u32[]{:S(2)}, u32[]{:S(2)}) %collective-permute-start.2) | collective-permute-done | bytes 393248 | tf_op jit(solution)/shard_map/ppermute | solution.py:392
  51.4 1.0 copy-done.6
  52.4 1.0 copy-done.8
  53.3 14.3 %attention.1 = (bf16[512,768]{1,0:T(8,128)(2,1)S(1)}, bf16[2048,128]{1,0:T(8,128)(2,1)S(1)}, bf16[2048,128]{1,0:T(8,128)(2,1)S(1)}) custom-call(s32[3]{0:T(128)S(1)} %pad_add_fusion.1.at, bf16[128,1536]{1,0:T(8,128)(2,1)S(1)} %copy-done.6, bf16[128,1536]{1,0:T(8,128)(2,1)S(1)} %copy-done.8, bf16[128,1536]{1,0:T(8,128)(2,1)} %collective-permute-done.1.q2.g2, ...), custom_call_target="tpu_custom_call" | custom-call | flops 32212254720 | bytes 8388608 | tf_op jit(solution)/shard_map/attention/pallas_call | solution.py:147
  67.7 0.9 copy-done.2
  68.5 0.8 copy-done.4
  69.3 26.0 %all_to_all.40 = bf16[16,128,128]{2,1,0:T(8,128)(2,1)S(1)} all-to-all(bf16[16,128,128]{2,1,0:T(8,128)(2,1)} %bitcast.50), channel_id=1, replica_groups=mesh['dp'=16,'chip'=8,'core'=2] {'chip','core'}, dimensions={0} | all-to-all | bytes 1048576 | tf_op jit(solution)/shard_map/all_to_all | solution.py:395
  95.6 19.2 %all_to_all.41.m_ref = bf16[8,128,512]{2,1,0:T(8,128)(2,1)S(1)} all-to-all(bf16[8,128,512]{2,1,0:T(8,128)(2,1)S(1)} %broadcast_in_dim.11), channel_id=1, replica_groups=mesh['dp'=16,'chip'=8,'core'=2] {'chip'}, dimensions={0} | all-to-all | bytes 2097152 | tf_op jit(solution)/shard_map/all_to_all | solution.py:395
  114.7 1.8 collective-permute-start.3
  116.6 2.3 collective-permute-done.3.t_ref
  118.9 3.1 %gradient.1 = (f32[384,512]{1,0:T(8,128)S(1)}, bf16[384,512]{1,0:T(8,128)(2,1)}) custom-call(s32[3]{0:T(128)S(1)} %pad_add_fusion.1.at, bf16[16,384,128]{2,1,0:T(8,128)(2,1)S(1)} %all-to-all-done.1.f_ref, bf16[8,128,512]{2,1,0:T(8,128)(2,1)S(1)} %all_to_all.41.m_ref, bf16[8,128,512]{2,1,0:T(8,128)(2,1)S(1)} %collective-permute-done.3.t_ref, ...), custom_call_target="tpu_custom_call" | custom-call | tf_op jit(solution)/shard_map/gradient/pallas_call | solution.py:265
  121.9 11.6 %all-to-all-start.4 = ((bf16[16,24,512]{2,1,0:T(8,128)(2,1)}), bf16[16,24,512]{2,1,0:T(8,128)(2,1)S(1)}, u32[]{:S(2)}, u32[]{:S(2)}) async-start(bf16[16,24,512]{2,1,0:T(8,128)(2,1)} %bitcast.17), calls=%async_computation.4 | async-start | bytes 786432 | tf_op jit(solution)/shard_map/all_to_all | solution.py:395
  133.6 1.2 collective-permute-start.4
  134.8 0.3 collective-permute-start.5
  135.1 2.7 %collective-permute-start.6 = (bf16[256,128]{1,0:T(8,128)(2,1)S(1)}, bf16[256,128]{1,0:T(8,128)(2,1)S(1)}, u32[]{:S(2)}, u32[]{:S(2)}) collective-permute-start(bf16[256,128]{1,0:T(8,128)(2,1)S(1)} %get-tuple-element.72), channel_id=1, source_target_pairs={{0,6},{2,4},{4,2},{6,0},{8,14},{10,12},{12,10},{14,8},{1,7},{3,5},... | collective-permute-start | bytes 196616 | tf_op jit(solution)/shard_map/ppermute | solution.py:439
  137.8 1.8 collective-permute-start.10
  139.6 1.1 collective-permute-start.7
  140.8 2.9 %collective-permute-start.8 = (bf16[256,128]{1,0:T(8,128)(2,1)S(1)}, bf16[256,128]{1,0:T(8,128)(2,1)S(1)}, u32[]{:S(2)}, u32[]{:S(2)}) collective-permute-start(bf16[256,128]{1,0:T(8,128)(2,1)S(1)} %get-tuple-element.71), channel_id=1, source_target_pairs={{0,10},{2,8},{4,14},{6,12},{8,2},{10,0},{12,6},{14,4},{1,11},{3,9}... | collective-permute-start | bytes 196616 | tf_op jit(solution)/shard_map/ppermute | solution.py:439
  143.7 2.2 collective-permute-start.9
  145.9 0.7 fusion.2
  146.6 1.4 collective-permute-done.8
  148.0 0.9 collective-permute-done.9
  149.0 0.8 broadcast_in_dim.12
  149.8 6.9 %all-to-all-start.5 = ((bf16[16,24,512]{2,1,0:T(8,128)(2,1)}), bf16[16,24,512]{2,1,0:T(8,128)(2,1)S(1)}, u32[]{:S(2)}, u32[]{:S(2)}) async-start(bf16[16,24,512]{2,1,0:T(8,128)(2,1)} %broadcast_in_dim.12), calls=%async_computation.5 | async-start | bytes 786432 | tf_op jit(solution)/shard_map/all_to_all | solution.py:395
  156.7 0.7 fusion.3
  157.4 3.8 %collective-permute-start.11 = (bf16[128,768]{1,0:T(8,128)(2,1)S(1)}, bf16[128,768]{1,0:T(8,128)(2,1)S(1)}, u32[]{:S(2)}, u32[]{:S(2)}) collective-permute-start(bf16[128,768]{1,0:T(8,128)(2,1)S(1)} %get-tuple-element.66), channel_id=1, source_target_pairs={{0,1},{1,0},{2,3},{3,2},{4,5},{5,4},{6,7},{7,6},{8,9},{9,8},{10,11... | collective-permute-start | bytes 589832 | tf_op jit(solution)/shard_map/ppermute | solution.py:392
  161.2 3.2 %collective-permute-start.12 = (bf16[128,768]{1,0:T(8,128)(2,1)S(1)}, bf16[128,768]{1,0:T(8,128)(2,1)S(1)}, u32[]{:S(2)}, u32[]{:S(2)}) collective-permute-start(bf16[128,768]{1,0:T(8,128)(2,1)S(1)} %get-tuple-element.65), channel_id=1, source_target_pairs={{0,14},{1,15},{2,12},{3,13},{4,10},{5,11},{6,8},{7,9},{8,6},{9,7},... | collective-permute-start | bytes 589832 | tf_op jit(solution)/shard_map/ppermute | solution.py:392
  164.4 2.1 collective-permute-start.13
  166.5 7.6 %collective-permute-done.12.refs_2_ = bf16[128,768]{1,0:T(8,128)(2,1)S(1)} collective-permute-done((bf16[128,768]{1,0:T(8,128)(2,1)S(1)}, bf16[128,768]{1,0:T(8,128)(2,1)S(1)}, u32[]{:S(2)}, u32[]{:S(2)}) %collective-permute-start.12) | collective-permute-done | bytes 196640 | tf_op jit(solution)/shard_map/ppermute | solution.py:392
  174.1 4.2 %collective-permute-done.13.refs_3_ = bf16[128,768]{1,0:T(8,128)(2,1)S(1)} collective-permute-done((bf16[128,768]{1,0:T(8,128)(2,1)S(1)}, bf16[128,768]{1,0:T(8,128)(2,1)S(1)}, u32[]{:S(2)}, u32[]{:S(2)}) %collective-permute-start.13) | collective-permute-done | bytes 196640 | tf_op jit(solution)/shard_map/ppermute | solution.py:392
  178.3 0.7 copy-done.15
  179.0 0.5 fusion.4.p_ref
  179.5 0.5 fusion.6
  180.0 0.5 collective-permute-start.16
  180.4 0.6 fusion.5
  181.0 0.3 collective-permute-done.16
  181.4 0.8 broadcast_in_dim.13
  182.2 3.6 %all-to-all-start.6 = ((f32[8,128,128]{2,1,0:T(8,128)}), f32[8,128,128]{2,1,0:T(8,128)S(1)}, u32[]{:S(2)}, u32[]{:S(2)}) async-start(f32[8,128,128]{2,1,0:T(8,128)} %broadcast_in_dim.13), calls=%async_computation.6 | async-start | bytes 1048576 | tf_op jit(solution)/shard_map/all_to_all | solution.py:395
  185.9 0.5 collective-permute-start.15
  186.3 1.0 collective-permute-done.15
  187.3 9.4 %all-to-all-done.6.g_ref = f32[8,128,128]{2,1,0:T(8,128)S(1)} async-done(((f32[8,128,128]{2,1,0:T(8,128)}), f32[8,128,128]{2,1,0:T(8,128)S(1)}, u32[]{:S(2)}, u32[]{:S(2)}) %all-to-all-start.6) | async-done | bytes 524320 | tf_op jit(solution)/shard_map/all_to_all | solution.py:395
  196.7 0.9 broadcast_in_dim.14
  197.7 3.5 %all-to-all-start.7 = ((bf16[8,256,128]{2,1,0:T(8,128)(2,1)}), bf16[8,256,128]{2,1,0:T(8,128)(2,1)S(1)}, u32[]{:S(2)}, u32[]{:S(2)}) async-start(bf16[8,256,128]{2,1,0:T(8,128)(2,1)} %broadcast_in_dim.14), calls=%async_computation.7 | async-start | bytes 1048576 | tf_op jit(solution)/shard_map/all_to_all | solution.py:395
  201.3 1.7 collective-permute-start.14
  202.9 0.9 collective-permute-done.14
  203.8 0.7 maximum_select_fusion.1
  204.5 2.2 unpack_queries.1
  206.7 4.2 %all-to-all-done.7 = bf16[8,256,128]{2,1,0:T(8,128)(2,1)S(1)} async-done(((bf16[8,256,128]{2,1,0:T(8,128)(2,1)}), bf16[8,256,128]{2,1,0:T(8,128)(2,1)S(1)}, u32[]{:S(2)}, u32[]{:S(2)}) %all-to-all-start.7) | async-done | bytes 524320 | tf_op jit(solution)/shard_map/all_to_all | solution.py:395
  210.9 2.9 %collective-permute-start.17 = (f32[256,128]{1,0:T(8,128)S(1)}, f32[256,128]{1,0:T(8,128)S(1)}, u32[]{:S(2)}, u32[]{:S(2)}) collective-permute-start(f32[256,128]{1,0:T(8,128)S(1)} %convert_reduce_fusion.m_ref), channel_id=1, source_target_pairs={{0,1},{1,0},{2,3},{3,2},{4,5},{5,4},{6,7},{7,6},{8,9},{9,8},{10,11... | collective-permute-start | bytes 393224 | tf_op jit(solution)/shard_map/ppermute | solution.py:381
  213.8 18.9 %inverse_factor.1.i_ref = f32[128,128]{1,0:T(8,128)} custom-call(f32[8,128,128]{2,1,0:T(8,128)} %copy-done.11), custom_call_target="tpu_custom_call" | custom-call | flops 8000000000 | bytes 1000000 | tf_op jit(solution)/shard_map/inverse_factor/pallas_call | solution.py:316
  232.7 0.8 copy-done.5
  233.5 3.1 %finish.1 = (f32[384,512]{1,0:T(8,128)}, f32[512,128]{1,0:T(8,128)}, f32[1,384,512]{2,1,0:T(8,128)}) custom-call(s32[3]{0:T(128)S(1)} %pad_add_fusion.1.at, f32[384,128]{1,0:T(8,128)S(1)} %fusion.4.p_ref, f32[128,128]{1,0:T(8,128)S(1)} %copy-done.5, f32[256,128]{1,0:T(8,128)S(1)} %convert_reduce_fusion.m_ref, f32[256,128]{1,0:T(8,128)S(1)} %collective-permute-done.17.t_ref, ...), custom_call_target="tpu_custom_call" | custom-call | tf_op jit(solution)/shard_map/finish/pallas_call | solution.py:353
  (50 shorter events, 0.7 us)
Async XLA Ops:
  0.6 178.3 %copy-start = (f32[512,128]{1,0:T(8,128)S(1)}, f32[512,128]{1,0:T(8,128)}, u32[]{:S(2)}) copy-start(f32[512,128]{1,0:T(8,128)} %param.15) | copy-start | bytes 786436
  2.8 17.6 %copy-start.9 = (bf16[128,6144]{1,0:T(8,128)(2,1)S(1)}, bf16[128,6144]{1,0:T(8,128)(2,1)}, u32[]{:S(2)}) copy-start(bf16[128,6144]{1,0:T(8,128)(2,1)} %param.12) | copy-start | bytes 4718596
  2.8 27.2 %all-to-all-start = ((bf16[16,144,256]{2,1,0:T(8,128)(2,1)}), bf16[16,144,256]{2,1,0:T(8,128)(2,1)S(1)}, u32[]{:S(2)}, u32[]{:S(2)}) async-start(bf16[16,144,256]{2,1,0:T(8,128)(2,1)} %pack_keys.1), calls=%async_computation | async-start | bytes 2359296 | tf_op jit(solution)/shard_map/all_to_all | solution.py:395
  14.6 20.3 %collective-permute-start = (bf16[128,1536]{1,0:T(8,128)(2,1)}, bf16[128,1536]{1,0:T(8,128)(2,1)S(1)}, u32[]{:S(2)}, u32[]{:S(2)}) collective-permute-start(bf16[128,1536]{1,0:T(8,128)(2,1)} %get-tuple-element.36), channel_id=1, source_target_pairs={{0,1},{1,0},{2,3},{3,2},{4,5},{5,4},{6,7},{7,6},{8,9},{9,8},{10,11... | collective-permute-start | bytes 1179656 | tf_op jit(solution)/shard_map/ppermute | solution.py:392
  14.7 23.8 %collective-permute-start.1 = (bf16[128,1536]{1,0:T(8,128)(2,1)}, bf16[128,1536]{1,0:T(8,128)(2,1)}, u32[]{:S(2)}, u32[]{:S(2)}) collective-permute-start(bf16[128,1536]{1,0:T(8,128)(2,1)} %get-tuple-element.37), channel_id=1, source_target_pairs={{0,14},{1,15},{2,12},{3,13},{4,10},{5,11},{6,8},{7,9},{8,6},{9,7},... | collective-permute-start | bytes 1179656 | tf_op jit(solution)/shard_map/ppermute | solution.py:392
  20.0 31.4 %collective-permute-start.2 = (bf16[128,1536]{1,0:T(8,128)(2,1)}, bf16[128,1536]{1,0:T(8,128)(2,1)}, u32[]{:S(2)}, u32[]{:S(2)}) collective-permute-start(bf16[128,1536]{1,0:T(8,128)(2,1)} %get-tuple-element.38), channel_id=1, source_target_pairs={{0,15},{1,14},{2,13},{3,12},{4,11},{5,10},{6,9},{7,8},{8,7},{9,6},... | collective-permute-start | bytes 1179656 | tf_op jit(solution)/shard_map/ppermute | solution.py:392
  30.0 39.3 %all-to-all-start.1 = ((bf16[16,384,128]{2,1,0:T(8,128)(2,1)}), bf16[16,384,128]{2,1,0:T(8,128)(2,1)S(1)}, u32[]{:S(2)}, u32[]{:S(2)}) async-start(bf16[16,384,128]{2,1,0:T(8,128)(2,1)} %bitcast.51), calls=%async_computation.1 | async-start | bytes 3145728 | tf_op jit(solution)/shard_map/all_to_all | solution.py:395
  34.9 0.7 copy-start.7
  51.4 1.0 copy-start.6
  52.4 1.0 copy-start.8
  67.7 0.9 copy-start.2
  68.5 0.8 copy-start.4
  95.4 19.3 %copy-start.10 = (bf16[128,512]{1,0:T(8,128)(2,1)}, bf16[128,512]{1,0:T(8,128)(2,1)S(1)}, u32[]{:S(2)}) copy-start(bf16[128,512]{1,0:T(8,128)(2,1)S(1)} %pad_maximum_fusion) | copy-start | bytes 393220
  95.5 23.4 %copy-start.1 = (f32[1,384,512]{2,1,0:T(8,128)S(1)}, f32[1,384,512]{2,1,0:T(8,128)}, u32[]{:S(2)}) copy-start(f32[1,384,512]{2,1,0:T(8,128)} %param.14) | copy-start | bytes 2359300
  114.7 4.1 %collective-permute-start.3 = (bf16[8,128,512]{2,1,0:T(8,128)(2,1)S(1)}, bf16[8,128,512]{2,1,0:T(8,128)(2,1)S(1)}, u32[]{:S(2)}, u32[]{:S(2)}) collective-permute-start(bf16[8,128,512]{2,1,0:T(8,128)(2,1)S(1)} %all_to_all.41.m_ref), channel_id=1, source_target_pairs={{0,1},{1,0},{2,3},{3,2},{4,5},{5,4},{6,7},{7,6},{8,9},{9,8},{10,11... | collective-permute-start | bytes 3145736 | tf_op jit(solution)/shard_map/ppermute | solution.py:381
  121.9 27.0 %all-to-all-start.4 = ((bf16[16,24,512]{2,1,0:T(8,128)(2,1)}), bf16[16,24,512]{2,1,0:T(8,128)(2,1)S(1)}, u32[]{:S(2)}, u32[]{:S(2)}) async-start(bf16[16,24,512]{2,1,0:T(8,128)(2,1)} %bitcast.17), calls=%async_computation.4 | async-start | bytes 786432 | tf_op jit(solution)/shard_map/all_to_all | solution.py:395
  133.5 23.2 %copy-start.3 = (bf16[512,768]{1,0:T(8,128)(2,1)S(1)}, bf16[512,768]{1,0:T(8,128)(2,1)}, u32[]{:S(2)}) copy-start(bf16[512,768]{1,0:T(8,128)(2,1)} %copy-done.2) | copy-start | bytes 2359300
  133.6 7.2 %collective-permute-start.4 = (bf16[256,128]{1,0:T(8,128)(2,1)S(1)}, bf16[256,128]{1,0:T(8,128)(2,1)S(1)}, u32[]{:S(2)}, u32[]{:S(2)}) collective-permute-start(bf16[256,128]{1,0:T(8,128)(2,1)S(1)} %get-tuple-element.74), channel_id=1, source_target_pairs={{0,2},{2,0},{4,6},{6,4},{8,10},{10,8},{12,14},{14,12},{1,3},{3,1},... | collective-permute-start | bytes 196616 | tf_op jit(solution)/shard_map/ppermute | solution.py:439
  134.8 8.9 %collective-permute-start.5 = (bf16[256,128]{1,0:T(8,128)(2,1)S(1)}, bf16[256,128]{1,0:T(8,128)(2,1)S(1)}, u32[]{:S(2)}, u32[]{:S(2)}) collective-permute-start(bf16[256,128]{1,0:T(8,128)(2,1)S(1)} %get-tuple-element.73), channel_id=1, source_target_pairs={{0,4},{2,6},{4,0},{6,2},{8,12},{10,14},{12,8},{14,10},{1,5},{3,7},... | collective-permute-start | bytes 196616 | tf_op jit(solution)/shard_map/ppermute | solution.py:439
  135.1 10.8 %collective-permute-start.6 = (bf16[256,128]{1,0:T(8,128)(2,1)S(1)}, bf16[256,128]{1,0:T(8,128)(2,1)S(1)}, u32[]{:S(2)}, u32[]{:S(2)}) collective-permute-start(bf16[256,128]{1,0:T(8,128)(2,1)S(1)} %get-tuple-element.72), channel_id=1, source_target_pairs={{0,6},{2,4},{4,2},{6,0},{8,14},{10,12},{12,10},{14,8},{1,7},{3,5},... | collective-permute-start | bytes 196616 | tf_op jit(solution)/shard_map/ppermute | solution.py:439
  137.8 8.7 %collective-permute-start.10 = (bf16[256,128]{1,0:T(8,128)(2,1)S(1)}, bf16[256,128]{1,0:T(8,128)(2,1)S(1)}, u32[]{:S(2)}, u32[]{:S(2)}) collective-permute-start(bf16[256,128]{1,0:T(8,128)(2,1)S(1)} %get-tuple-element.69), channel_id=1, source_target_pairs={{0,14},{2,12},{4,10},{6,8},{8,6},{10,4},{12,2},{14,0},{1,15},{3,13... | collective-permute-start | bytes 196616 | tf_op jit(solution)/shard_map/ppermute | solution.py:439
  139.6 6.9 %collective-permute-start.7 = (bf16[256,128]{1,0:T(8,128)(2,1)S(1)}, bf16[256,128]{1,0:T(8,128)(2,1)S(1)}, u32[]{:S(2)}, u32[]{:S(2)}) collective-permute-start(bf16[256,128]{1,0:T(8,128)(2,1)S(1)} %get-tuple-element.68), channel_id=1, source_target_pairs={{0,8},{2,10},{4,12},{6,14},{8,0},{10,2},{12,4},{14,6},{1,9},{3,11}... | collective-permute-start | bytes 196616 | tf_op jit(solution)/shard_map/ppermute | solution.py:439
  140.8 7.2 %collective-permute-start.8 = (bf16[256,128]{1,0:T(8,128)(2,1)S(1)}, bf16[256,128]{1,0:T(8,128)(2,1)S(1)}, u32[]{:S(2)}, u32[]{:S(2)}) collective-permute-start(bf16[256,128]{1,0:T(8,128)(2,1)S(1)} %get-tuple-element.71), channel_id=1, source_target_pairs={{0,10},{2,8},{4,14},{6,12},{8,2},{10,0},{12,6},{14,4},{1,11},{3,9}... | collective-permute-start | bytes 196616 | tf_op jit(solution)/shard_map/ppermute | solution.py:439
  143.7 5.2 %collective-permute-start.9 = (bf16[256,128]{1,0:T(8,128)(2,1)S(1)}, bf16[256,128]{1,0:T(8,128)(2,1)S(1)}, u32[]{:S(2)}, u32[]{:S(2)}) collective-permute-start(bf16[256,128]{1,0:T(8,128)(2,1)S(1)} %get-tuple-element.70), channel_id=1, source_target_pairs={{0,12},{2,14},{4,8},{6,10},{8,4},{10,6},{12,0},{14,2},{1,13},{3,15... | collective-permute-start | bytes 196616 | tf_op jit(solution)/shard_map/ppermute | solution.py:439
  149.8 28.5 %all-to-all-start.5 = ((bf16[16,24,512]{2,1,0:T(8,128)(2,1)}), bf16[16,24,512]{2,1,0:T(8,128)(2,1)S(1)}, u32[]{:S(2)}, u32[]{:S(2)}) async-start(bf16[16,24,512]{2,1,0:T(8,128)(2,1)} %broadcast_in_dim.12), calls=%async_computation.5 | async-start | bytes 786432 | tf_op jit(solution)/shard_map/all_to_all | solution.py:395
  157.4 9.0 %collective-permute-start.11 = (bf16[128,768]{1,0:T(8,128)(2,1)S(1)}, bf16[128,768]{1,0:T(8,128)(2,1)S(1)}, u32[]{:S(2)}, u32[]{:S(2)}) collective-permute-start(bf16[128,768]{1,0:T(8,128)(2,1)S(1)} %get-tuple-element.66), channel_id=1, source_target_pairs={{0,1},{1,0},{2,3},{3,2},{4,5},{5,4},{6,7},{7,6},{8,9},{9,8},{10,11... | collective-permute-start | bytes 589832 | tf_op jit(solution)/shard_map/ppermute | solution.py:392
  161.2 12.8 %collective-permute-start.12 = (bf16[128,768]{1,0:T(8,128)(2,1)S(1)}, bf16[128,768]{1,0:T(8,128)(2,1)S(1)}, u32[]{:S(2)}, u32[]{:S(2)}) collective-permute-start(bf16[128,768]{1,0:T(8,128)(2,1)S(1)} %get-tuple-element.65), channel_id=1, source_target_pairs={{0,14},{1,15},{2,12},{3,13},{4,10},{5,11},{6,8},{7,9},{8,6},{9,7},... | collective-permute-start | bytes 589832 | tf_op jit(solution)/shard_map/ppermute | solution.py:392
  164.4 13.9 %collective-permute-start.13 = (bf16[128,768]{1,0:T(8,128)(2,1)S(1)}, bf16[128,768]{1,0:T(8,128)(2,1)S(1)}, u32[]{:S(2)}, u32[]{:S(2)}) collective-permute-start(bf16[128,768]{1,0:T(8,128)(2,1)S(1)} %get-tuple-element.64), channel_id=1, source_target_pairs={{0,15},{1,14},{2,13},{3,12},{4,11},{5,10},{6,9},{7,8},{8,7},{9,6},... | collective-permute-start | bytes 589832 | tf_op jit(solution)/shard_map/ppermute | solution.py:392
  166.5 15.7 %copy-start.13 = (bf16[128,768]{1,0:T(8,128)(2,1)}, bf16[128,768]{1,0:T(8,128)(2,1)S(1)}, u32[]{:S(2)}) copy-start(bf16[128,768]{1,0:T(8,128)(2,1)S(1)} %collective-permute-done.11.refs_1_) | copy-start | bytes 589828
  174.1 8.1 %copy-start.14 = (bf16[128,768]{1,0:T(8,128)(2,1)}, bf16[128,768]{1,0:T(8,128)(2,1)S(1)}, u32[]{:S(2)}) copy-start(bf16[128,768]{1,0:T(8,128)(2,1)S(1)} %collective-permute-done.12.refs_2_) | copy-start | bytes 589828
  178.3 0.7 copy-start.15
  180.0 1.4 collective-permute-start.16
  182.2 19.0 %copy-start.12 = (bf16[256,128]{1,0:T(8,128)(2,1)S(1)}, bf16[256,128]{1,0:T(8,128)(2,1)}, u32[]{:S(2)}) copy-start(bf16[256,128]{1,0:T(8,128)(2,1)} %fusion.2) | copy-start | bytes 196612
  182.2 14.5 %all-to-all-start.6 = ((f32[8,128,128]{2,1,0:T(8,128)}), f32[8,128,128]{2,1,0:T(8,128)S(1)}, u32[]{:S(2)}, u32[]{:S(2)}) async-start(f32[8,128,128]{2,1,0:T(8,128)} %broadcast_in_dim.13), calls=%async_computation.6 | async-start | bytes 1048576 | tf_op jit(solution)/shard_map/all_to_all | solution.py:395
  185.9 1.4 collective-permute-start.15
  196.7 10.0 %copy-start.11 = (f32[8,128,128]{2,1,0:T(8,128)}, f32[8,128,128]{2,1,0:T(8,128)S(1)}, u32[]{:S(2)}) copy-start(f32[8,128,128]{2,1,0:T(8,128)S(1)} %all-to-all-done.6.g_ref) | copy-start | bytes 1572868
  197.7 13.2 %all-to-all-start.7 = ((bf16[8,256,128]{2,1,0:T(8,128)(2,1)}), bf16[8,256,128]{2,1,0:T(8,128)(2,1)S(1)}, u32[]{:S(2)}, u32[]{:S(2)}) async-start(bf16[8,256,128]{2,1,0:T(8,128)(2,1)} %broadcast_in_dim.14), calls=%async_computation.7 | async-start | bytes 1048576 | tf_op jit(solution)/shard_map/all_to_all | solution.py:395
  201.3 2.6 %collective-permute-start.14 = (bf16[128,256]{1,0:T(8,128)(2,1)S(1)}, bf16[128,256]{1,0:T(8,128)(2,1)S(1)}, u32[]{:S(2)}, u32[]{:S(2)}) collective-permute-start(bf16[128,256]{1,0:T(8,128)(2,1)S(1)} %get-tuple-element.76), channel_id=1, source_target_pairs={{0,1},{1,0},{2,3},{3,2},{4,5},{5,4},{6,7},{7,6},{8,9},{9,8},{10,11... | collective-permute-start | bytes 196616 | tf_op jit(solution)/shard_map/ppermute | solution.py:381
  210.9 21.8 %collective-permute-start.17 = (f32[256,128]{1,0:T(8,128)S(1)}, f32[256,128]{1,0:T(8,128)S(1)}, u32[]{:S(2)}, u32[]{:S(2)}) collective-permute-start(f32[256,128]{1,0:T(8,128)S(1)} %convert_reduce_fusion.m_ref), channel_id=1, source_target_pairs={{0,1},{1,0},{2,3},{3,2},{4,5},{5,4},{6,7},{7,6},{8,9},{9,8},{10,11... | collective-permute-start | bytes 393224 | tf_op jit(solution)/shard_map/ppermute | solution.py:381
  232.7 0.8 copy-start.5

commit v4 on v3

--- a/solution.py
+++ b/solution.py
@@ -14,7 +14,7 @@
 HIGHEST = lax.Precision.HIGHEST
 TN = (((0,), (0,)), ((), ()))
 NT = (((1,), (1,)), ((), ()))
-HEADS_AT_ONCE = 2
+HEADS_AT_ONCE = 6
 
 
 def attention(where, parts, kv):
@@ -31,7 +31,7 @@
     power = scale * LOG2E
 
     def kernel(
-        at, q0, q1, q2, q3, g0, g1, g2, g3, k_ref, v_ref, dq_ref, dk_ref, dv_ref,
+        at, q0, q1, q2, q3, g0, g1, g2, g3, k_ref, v_ref, dq_ref, dkv_ref,
         s_scr, d_scr, bias, k_turned, dq_acc, dk_acc, dv_acc,
     ):
         step = pl.program_id(0)
@@ -138,10 +138,10 @@
 
         @pl.when(step == 2 * steps - 1)
         def _():
-            dk_ref[...] = (dk_acc[...] * scale).astype(jnp.bfloat16)
-            dv_ref[...] = dv_acc[...].astype(jnp.bfloat16)
-
-    whole = pl.BlockSpec((length, HEAD), lambda s, at: (0, 0))
+            dkv_ref[:, :HEAD] = (dk_acc[...] * scale).astype(jnp.bfloat16)
+            dkv_ref[:, HEAD:] = dv_acc[...].astype(jnp.bfloat16)
+
+    whole = pl.BlockSpec((length, 2 * HEAD), lambda s, at: (0, 0))
     queries_at = pl.BlockSpec((block, wide), lambda s, at: (s // steps, s % steps))
     flops = 5 * 2 * length * block * heads * HEAD
     return pl.pallas_call(
@@ -155,7 +155,7 @@
                 pl.BlockSpec((devices, padded, HEAD), lambda s, at: (0, 0, 0)),
                 pl.BlockSpec((devices, padded, HEAD), lambda s, at: (0, 0, 1)),
             ],
-            out_specs=[queries_at, whole, whole],
+            out_specs=[queries_at, whole],
             scratch_shapes=[
                 pltpu.VMEM((length, columns), jnp.float32),
                 pltpu.VMEM((length, columns), jnp.float32),
@@ -168,8 +168,7 @@
         ),
         out_shape=[
             jax.ShapeDtypeStruct((2 * block, heads * HEAD), jnp.bfloat16),
-            jax.ShapeDtypeStruct((length, HEAD), jnp.bfloat16),
-            jax.ShapeDtypeStruct((length, HEAD), jnp.bfloat16),
+            jax.ShapeDtypeStruct((length, 2 * HEAD), jnp.bfloat16),
         ],
         compiler_params=pltpu.CompilerParams(
             dimension_semantics=("arbitrary",), vmem_limit_bytes=40 * 1024 * 1024
@@ -278,40 +277,43 @@
 def inverse_factor(parts):
     count, size, _ = parts.shape
     tiles = size // 8
+    shape = (8, size)
 
     def kernel(g_ref, out_ref):
-        sub = lax.broadcasted_iota(jnp.int32, (8, 1), 0)
-        lane = lax.broadcasted_iota(jnp.int32, (8, size), 1)
-        row8 = lax.broadcasted_iota(jnp.int32, (8, size), 0)
+        lane = lax.broadcasted_iota(jnp.int32, shape, 1)
+        sub = lax.broadcasted_iota(jnp.int32, shape, 0)
         left, right = [], []
         for t in range(tiles):
             total = g_ref[0, 8 * t : 8 * t + 8, :]
             for n in range(1, count):
                 total = total + g_ref[n, 8 * t : 8 * t + 8, :]
             left.append(total)
-            right.append(jnp.where(lane == row8 + 8 * t, 1.0, 0.0))
-        for j in range(0, size, 2):
-            t0, r = j // 8, j % 8
-            l0, l1 = left[t0][r : r + 1, :], left[t0][r + 1 : r + 2, :]
-            r0, r1 = right[t0][r : r + 1, :], right[t0][r + 1 : r + 2, :]
-            a, b, c = l0[:, j : j + 1], l0[:, j + 1 : j + 2], l1[:, j + 1 : j + 2]
-            det = a * c - b * b
-            inv = 1.0 / det
-            ai, bi, ci = a * inv, b * inv, c * inv
-            ul, vl = ci * l0 - bi * l1, ai * l1 - bi * l0
-            ur, vr = ci * r0 - bi * r1, ai * r1 - bi * r0
-            over = 1.0 / a
-            out_ref[j : j + 1, :] = r0 * jnp.sqrt(over)
-            out_ref[j + 1 : j + 2, :] = (r1 - (b * over) * r0) * jnp.sqrt(ai)
-            for t in range(t0, tiles):
-                x, y = left[t][:, j : j + 1], left[t][:, j + 1 : j + 2]
-                if t == t0:
-                    if r == 6:
-                        continue
-                    x = jnp.where(sub > r + 1, x, 0.0)
-                    y = jnp.where(sub > r + 1, y, 0.0)
-                left[t] = left[t] - (x * ul + y * vl)
-                right[t] = right[t] - (x * ur + y * vr)
+            right.append(jnp.where(lane == sub + 8 * t, 1.0, 0.0))
+
+        def row(x, r):
+            return jnp.broadcast_to(x[r : r + 1, :], shape)
+
+        for p in range(tiles):
+            spread = [
+                [
+                    jnp.broadcast_to(left[t][:, 8 * p + k : 8 * p + k + 1], shape)
+                    for k in range(8)
+                ]
+                for t in range(p, tiles)
+            ]
+            for k in range(8):
+                pivot = spread[0][k]
+                root = lax.rsqrt(row(pivot, k))
+                row_l = row(left[p], k) * root
+                row_r = row(right[p], k) * root
+                out_ref[8 * p + k : 8 * p + k + 1, :] = row_r[0:1]
+                factors = [row(pivot, m) * root for m in range(k + 1, 8)]
+                for t in range(p, tiles):
+                    x = spread[t - p][k] * root
+                    for m in range(k + 1, 8):
+                        spread[t - p][m] = spread[t - p][m] - x * factors[m - k - 1]
+                    left[t] = left[t] - x * row_l
+                    right[t] = right[t] - x * row_r
 
     return pl.pallas_call(
         kernel,
@@ -325,28 +327,16 @@
     )(parts)
 
 
-def finish(where, p_sum, inverse, moment, their_moment, combined, replicas):
+def finish(p_sum, inverse, q_factor, combined):
     rows, width = combined.shape
-    rank = p_sum.shape[1]
-    half = moment.shape[0]
-
-    def kernel(at, p_ref, i_ref, m_ref, t_ref, c_ref, comp_ref, q_ref, new_ref):
-        core = at[0]
-        inv = i_ref[...]
-
+
+    def kernel(p_ref, i_ref, q_ref, c_ref, comp_ref, new_ref):
         def product(x, y):
             return lax.dot_general(
                 x, y, NT, precision=HIGHEST, preferred_element_type=jnp.float32
             )
 
-        q_ref[pl.ds(pl.multiple_of(core * half, half), half), :] = (
-            product(m_ref[...], inv) * (1.0 / replicas)
-        )
-        q_ref[pl.ds(pl.multiple_of((1 - core) * half, half), half), :] = (
-            product(t_ref[...], inv) * (1.0 / replicas)
-        )
-        p_hat = product(p_ref[...], inv)
-        out = product(p_hat, q_ref[...])
+        out = product(product(p_ref[...], i_ref[...]), q_ref[...])
         comp_ref[...] = out
         new_ref[0] = c_ref[...] - out
 
@@ -354,14 +344,13 @@
         kernel,
         out_shape=[
             jax.ShapeDtypeStruct((rows, width), jnp.float32),
-            jax.ShapeDtypeStruct((width, rank), jnp.float32),
             jax.ShapeDtypeStruct((1, rows, width), jnp.float32),
         ],
-        in_specs=[SMEM] + [VMEM] * 5,
-        out_specs=[VMEM] * 3,
+        in_specs=[VMEM] * 4,
+        out_specs=[VMEM] * 2,
         compiler_params=pltpu.CompilerParams(vmem_limit_bytes=32 * 1024 * 1024),
         name="finish",
-    )(where, p_sum, inverse, moment, their_moment, combined)
+    )(p_sum, inverse, q_factor, combined)
 
 
 def body(queries, keys, values, d_out, features, doc_start, error, q_init):
@@ -412,53 +401,26 @@
     feat = exchange(feat, ctx)
 
     where = jnp.stack([core, chip, chips - 1 - chip]).astype(jnp.int32)
-    dq, dk, dv = attention(where, parts, kv)
-    dk, feat = lax.optimization_barrier((dk, feat))
-
-    def to_owner(x):
-        x = exchange(x.reshape(devices, tokens, HEAD), ctx)
-        x = x.reshape(2, chips // 2, 2, tokens, HEAD).astype(f32)
-        x = jnp.sum(x, axis=1).astype(bf16)
-        return jnp.concatenate([x[0, 0], x[1, 0], x[0, 1], x[1, 1]], axis=1)
-
-    d_key = to_owner(dk)
+    dq, dkv = attention(where, parts, kv)
+    dkv, feat = lax.optimization_barrier((dkv, feat))
+
+    home = exchange(dkv.reshape(devices, tokens, 2 * HEAD), ctx)
+    home = home.reshape(2, chips // 2, 2, tokens, 2 * HEAD).astype(f32)
+    home = jnp.sum(home, axis=1).astype(bf16)
+    home = [home[0, 0], home[1, 0], home[0, 1], home[1, 1]]
+    d_key = jnp.concatenate([x[:, :HEAD] for x in home], axis=1)
+    d_value = jnp.concatenate([x[:, HEAD:] for x in home], axis=1)
     dk_mine = spread(d_key, "chip", chips)
     dk_theirs = swap(dk_mine)
     combined, low = gradient(where, feat, dk_mine, dk_theirs, error.reshape(rows, width_kv))
 
-    shares = low.reshape(replicas, rows // replicas, width_kv)
-    shares, dv, dq = lax.optimization_barrier((shares, dv, dq))
-    shares = exchange(shares, "dp")
-    dv = dv.reshape(chips, 2 * tokens, HEAD)
-    sums = []
-    for low_k in (0, chips // 2):
-        total = None
-        for k in range(low_k, low_k + chips // 2):
-            x = piece(dv, 1, jnp.bitwise_xor(chip, k), 0)[0]
-            if k:
-                x = lax.ppermute(x, "chip", [(i, i ^ k) for i in range(chips)])
-            x = x.astype(f32)
-            total = x if total is None else total + x
-        sums.append(total.astype(bf16))
+    shares = exchange(low.reshape(replicas, rows // replicas, width_kv), "dp")
     share = jnp.sum(shares.astype(f32), axis=0).astype(bf16)
-    share, *sums = lax.optimization_barrier((share, *sums))
     total = spread(share, "dp", replicas).reshape(rows, width_kv)
-    dv_half = jnp.where(
-        upper == 0,
-        jnp.concatenate(sums, axis=1),
-        jnp.concatenate(sums[::-1], axis=1),
-    )
-    dv_mine = piece(dv_half, tokens, core, 0)
-    dv_theirs = swap(piece(dv_half, tokens, 1 - core, 0))
-    d_value = jnp.where(
-        core == 0,
-        jnp.concatenate([dv_mine, dv_theirs], axis=1),
-        jnp.concatenate([dv_theirs, dv_mine], axis=1),
-    )
+
     back = [dq[:tokens]] + [
         move(dq[n * tokens : (n + 1) * tokens], *ways[n]) for n in range(1, 4)
     ]
-    total, *back = lax.optimization_barrier((total, *back))
     d_query = unpack_queries(heads, back, group)
 
     total = total.astype(f32)
@@ -470,11 +432,13 @@
     moment = piece(moment, size, core, 0) + swap(piece(moment, size, 1 - core, 0))
     moment, gram = lax.optimization_barrier((moment.astype(bf16), gram))
     moment = jnp.sum(spread(moment, "chip", chips).astype(f32), axis=0)
-    their_moment = swap(moment)
     inverse = inverse_factor(gram)
-    compressed, q_factor, new_error = finish(
-        where, p_sum, inverse, moment, their_moment, combined, replicas
+    q_mine = lax.dot_general(moment, inverse, NT, precision=HIGHEST) / replicas
+    q_theirs = swap(q_mine)
+    q_factor = jnp.where(
+        core == 0, jnp.concatenate([q_mine, q_theirs]), jnp.concatenate([q_theirs, q_mine])
     )
+    compressed, new_error = finish(p_sum, inverse, q_factor, combined)
     return (d_query, d_key, d_value, compressed, q_factor, new_error)
 
 

time: 238 us -> 204 us (0.86)
  starting transfers between devices: 73.5 us -> 45.8 us
  Pallas kernels: 46.3 us -> 26.7 us
  blocking collectives: 45.2 us -> 64.7 us
  waiting for transfers between devices: 55.9 us -> 50.6 us
    all_to_all x2 -> x3, blocking collectives: 45.2 us -> 64.7 us  [exchange(): return lax.all_to_all(x, axis, 0, 0)]
    pallas_call x1, Pallas kernels: 18.9 us -> 5.55 us  [inverse_factor(): pl.pallas_call(kernel, out_shape=jax.ShapeDtypeStruct((size, size), jnp.f...]
    all_to_all x6 -> x5, starting transfers between devices: 39 us -> 26.7 us  [exchange(): return lax.all_to_all(x, axis, 0, 0)]
    ppermute x7 -> x0, starting transfers between devices: 12.3 us -> none  [body(): x = lax.ppermute(x, 'chip', [(i, i ^ k) for i in range(chips)])]
    ppermute x6, waiting for transfers between devices: 27.5 us -> 16.2 us  [move(): return lax.ppermute(x, ctx, pairs)]
    all_to_all x6 -> x5, waiting for transfers between devices: 21.6 us -> 31.9 us  [exchange(): return lax.all_to_all(x, axis, 0, 0)]
    pallas_call x1, Pallas kernels: 14.3 us -> 9.51 us  [attention(): pl.pallas_call(kernel, grid_spec=pltpu.PrefetchScalarGridSpec(num_scalar_...]
    unnamed x32, local copies, waits for them, and re-layouts: 5.96 us -> 2.59 us
  transfers between devices with their start and end apart: 24 -> 15, of which waited for: 13 -> 9; matrix products, arithmetic and copies ran while one was open for 2% -> 4% of each run, Pallas kernels for 16% -> 10%
where the time goes in v4:
time: 204 us; the launch traced here: 203 us
  blocking collectives  64.7 us (32%)
  waiting for transfers between devices  50.6 us (25%)
  starting transfers between devices  45.8 us (22%)
  Pallas kernels  26.7 us (13%)
  local copies, waits for them, and re-layouts  9.5 us (5%)
  matrix products  2.69 us (1%)
    all_to_all x3, blocking collectives, exchange(): return lax.all_to_all(x, axis, 0, 0)  64.7 us
    all_to_all x5, waiting for transfers between devices, exchange(): return lax.all_to_all(x, axis, 0, 0)  31.9 us
    all_to_all x5, starting transfers between devices, exchange(): return lax.all_to_all(x, axis, 0, 0)  26.7 us
    ppermute x6, waiting for transfers between devices, move(): return lax.ppermute(x, ctx, pairs)  16.2 us
    ppermute x6, starting transfers between devices, move(): return lax.ppermute(x, ctx, pairs)  11.5 us
    pallas_call x1, Pallas kernels, attention(): pl.pallas_call(kernel, grid_spec=pltpu.PrefetchScalarGridSpec(num_scalar_...  9.51 us
    ppermute x4, starting transfers between devices, swap(): return lax.ppermute(x, 'core', [(0, 1), (1, 0)])  7.6 us
    pallas_call x1, Pallas kernels, inverse_factor(): pl.pallas_call(kernel, out_shape=jax.ShapeDtypeStruct((size, size), jnp.f...  5.55 us
  transfers between devices with their start and end apart: 15, of which 9 were waited for; matrix products, arithmetic and copies ran while one was open for 4% of the time, Pallas kernels for 10%

profile of v4, /device:TPU:1, one launch (start us, length us, event | category | flops | bytes accessed | tf_op | source)
XLA Modules:
  0.0 202.7 jit_solution(2700021978013392983)
XLA Ops:
  0.6 0.0 copy-start
  0.6 2.2 %pack_keys.1 = bf16[16,144,256]{2,1,0:T(8,128)(2,1)} custom-call(bf16[128,512]{1,0:T(8,128)(2,1)} %k_ref.1, bf16[128,512]{1,0:T(8,128)(2,1)} %v_ref.1, s32[1,128]{1,0:T(1,128)} %bitcast.39), custom_call_target="tpu_custom_call" | custom-call | tf_op jit(solution)/shard_map/pack_keys/pallas_call | solution.py:203
  2.8 8.6 %all-to-all-start = ((bf16[16,144,256]{2,1,0:T(8,128)(2,1)}), bf16[16,144,256]{2,1,0:T(8,128)(2,1)S(1)}, u32[]{:S(2)}, u32[]{:S(2)}) async-start(bf16[16,144,256]{2,1,0:T(8,128)(2,1)} %pack_keys.1), calls=%async_computation | async-start | bytes 2359296 | tf_op jit(solution)/shard_map/all_to_all | solution.py:384
  11.4 0.7 pad_add_fusion.h_ref
  12.1 2.6 %pack_queries.1 = (bf16[128,1536]{1,0:T(8,128)(2,1)}, bf16[128,1536]{1,0:T(8,128)(2,1)}, bf16[128,1536]{1,0:T(8,128)(2,1)}, bf16[128,1536]{1,0:T(8,128)(2,1)}) custom-call(s32[4]{0:T(128)} %pad_add_fusion.h_ref, bf16[128,3072]{1,0:T(8,128)(2,1)} %q_ref.1, bf16[128,3072]{1,0:T(8,128)(2,1)} %g_ref.1), custom_call_target="tpu_custom_call" | custom-call | tf_op jit(solution)/shard_map/pack_queries/pallas_call | solution.py:221
  14.7 0.1 collective-permute-start
  14.8 5.3 %collective-permute-start.1 = (bf16[128,1536]{1,0:T(8,128)(2,1)}, bf16[128,1536]{1,0:T(8,128)(2,1)}, u32[]{:S(2)}, u32[]{:S(2)}) collective-permute-start(bf16[128,1536]{1,0:T(8,128)(2,1)} %get-tuple-element.24), channel_id=1, source_target_pairs={{0,14},{1,15},{2,12},{3,13},{4,10},{5,11},{6,8},{7,9},{8,6},{9,7},... | collective-permute-start | bytes 1179656 | tf_op jit(solution)/shard_map/ppermute | solution.py:381
  20.1 0.4 collective-permute-start.2
  20.5 1.6 copy.15
  22.1 0.1 pad_add_fusion.1.at
  22.1 7.9 %all-to-all-done.k_ref.v_ref = bf16[16,144,256]{2,1,0:T(8,128)(2,1)S(1)} async-done(((bf16[16,144,256]{2,1,0:T(8,128)(2,1)}), bf16[16,144,256]{2,1,0:T(8,128)(2,1)S(1)}, u32[]{:S(2)}, u32[]{:S(2)}) %all-to-all-start) | async-done | bytes 1179680 | tf_op jit(solution)/shard_map/all_to_all | solution.py:384
  30.1 5.0 %all-to-all-start.1 = ((bf16[16,384,128]{2,1,0:T(8,128)(2,1)}), bf16[16,384,128]{2,1,0:T(8,128)(2,1)S(1)}, u32[]{:S(2)}, u32[]{:S(2)}) async-start(bf16[16,384,128]{2,1,0:T(8,128)(2,1)} %bitcast.34), calls=%async_computation.1 | async-start | bytes 3145728 | tf_op jit(solution)/shard_map/all_to_all | solution.py:384
  35.1 3.5 %collective-permute-done.1.q2.g2 = bf16[128,1536]{1,0:T(8,128)(2,1)} collective-permute-done((bf16[128,1536]{1,0:T(8,128)(2,1)}, bf16[128,1536]{1,0:T(8,128)(2,1)}, u32[]{:S(2)}, u32[]{:S(2)}) %collective-permute-start.1) | collective-permute-done | bytes 393248 | tf_op jit(solution)/shard_map/ppermute | solution.py:381
  38.6 12.7 %collective-permute-done.2.q3.g3 = bf16[128,1536]{1,0:T(8,128)(2,1)} collective-permute-done((bf16[128,1536]{1,0:T(8,128)(2,1)}, bf16[128,1536]{1,0:T(8,128)(2,1)}, u32[]{:S(2)}, u32[]{:S(2)}) %collective-permute-start.2) | collective-permute-done | bytes 393248 | tf_op jit(solution)/shard_map/ppermute | solution.py:381
  51.3 9.5 %attention.1 = (bf16[512,768]{1,0:T(8,128)(2,1)S(1)}, bf16[2048,256]{1,0:T(8,128)(2,1)S(1)}) custom-call(s32[3]{0:T(128)S(1)} %pad_add_fusion.1.at, bf16[128,1536]{1,0:T(8,128)(2,1)S(1)} %copy-done.7, bf16[128,1536]{1,0:T(8,128)(2,1)} %collective-permute-done.q1.g1, bf16[128,1536]{1,0:T(8,128)(2,1)} %collective-permute-done.1.q2.g2, ...), custom_call_target="tpu_custom_call" | custom-call | flops 32212254720 | bytes 8388608 | tf_op jit(solution)/shard_map/attention/pallas_call | solution.py:147
  60.9 1.0 copy-done.2
  61.9 0.9 copy-done.4
  62.7 4.5 %all-to-all-done.1.f_ref = bf16[16,384,128]{2,1,0:T(8,128)(2,1)S(1)} async-done(((bf16[16,384,128]{2,1,0:T(8,128)(2,1)}), bf16[16,384,128]{2,1,0:T(8,128)(2,1)S(1)}, u32[]{:S(2)}, u32[]{:S(2)}) %all-to-all-start.1) | async-done | bytes 1572896 | tf_op jit(solution)/shard_map/all_to_all | solution.py:384
  67.3 22.4 %all_to_all.40 = bf16[16,128,256]{2,1,0:T(8,128)(2,1)S(1)} all-to-all(bf16[16,128,256]{2,1,0:T(8,128)(2,1)} %bitcast.31), channel_id=1, replica_groups=mesh['dp'=16,'chip'=8,'core'=2] {'chip','core'}, dimensions={0} | all-to-all | bytes 2097152 | tf_op jit(solution)/shard_map/all_to_all | solution.py:384
  89.7 0.2 reduce_sum.33
  89.9 0.6 fusion.1
  90.6 0.6 fusion.3
  91.2 0.0 copy-start.9
  91.2 0.0 copy-start.3
  91.2 0.1 broadcast_in_dim.11
  91.3 19.2 %all_to_all.41.m_ref = bf16[8,128,512]{2,1,0:T(8,128)(2,1)S(1)} all-to-all(bf16[8,128,512]{2,1,0:T(8,128)(2,1)S(1)} %broadcast_in_dim.11), channel_id=1, replica_groups=mesh['dp'=16,'chip'=8,'core'=2] {'chip'}, dimensions={0} | all-to-all | bytes 2097152 | tf_op jit(solution)/shard_map/all_to_all | solution.py:384
  110.5 1.8 collective-permute-start.6
  112.4 2.3 %collective-permute-done.6.t_ref = bf16[8,128,512]{2,1,0:T(8,128)(2,1)S(1)} collective-permute-done((bf16[8,128,512]{2,1,0:T(8,128)(2,1)S(1)}, bf16[8,128,512]{2,1,0:T(8,128)(2,1)S(1)}, u32[]{:S(2)}, u32[]{:S(2)}) %collective-permute-start.6) | collective-permute-done | bytes 1048608 | tf_op jit(solution)/shard_map/ppermute | solution.py:370
  114.7 2.3 %gradient.1 = (f32[384,512]{1,0:T(8,128)S(1)}, bf16[384,512]{1,0:T(8,128)(2,1)S(1)}) custom-call(s32[3]{0:T(128)S(1)} %pad_add_fusion.1.at, bf16[16,384,128]{2,1,0:T(8,128)(2,1)S(1)} %all-to-all-done.1.f_ref, bf16[8,128,512]{2,1,0:T(8,128)(2,1)S(1)} %all_to_all.41.m_ref, bf16[8,128,512]{2,1,0:T(8,128)(2,1)S(1)} %collective-permute-done.6.t_ref, ...), custom_call_target="tpu_custom_call" | custom-call | tf_op jit(solution)/shard_map/gradient/pallas_call | solution.py:264
  117.0 23.1 %all_to_all.42 = bf16[16,24,512]{2,1,0:T(8,128)(2,1)S(1)} all-to-all(bf16[16,24,512]{2,1,0:T(8,128)(2,1)S(1)} %bitcast.33), channel_id=1, replica_groups=mesh['dp'=16,'chip'=8,'core'=2] {'dp'}, dimensions={0} | all-to-all | bytes 786432 | tf_op jit(solution)/shard_map/all_to_all | solution.py:384
  140.1 0.1 reduce_sum.34
  140.1 0.8 broadcast_in_dim.12
  140.9 6.1 %all-to-all-start.5 = ((bf16[16,24,512]{2,1,0:T(8,128)(2,1)}), bf16[16,24,512]{2,1,0:T(8,128)(2,1)S(1)}, u32[]{:S(2)}, u32[]{:S(2)}) async-start(bf16[16,24,512]{2,1,0:T(8,128)(2,1)} %broadcast_in_dim.12), calls=%async_computation.5 | async-start | bytes 786432 | tf_op jit(solution)/shard_map/all_to_all | solution.py:384
  147.0 11.1 %all-to-all-done.5 = bf16[16,24,512]{2,1,0:T(8,128)(2,1)S(1)} async-done(((bf16[16,24,512]{2,1,0:T(8,128)(2,1)}), bf16[16,24,512]{2,1,0:T(8,128)(2,1)S(1)}, u32[]{:S(2)}, u32[]{:S(2)}) %all-to-all-start.5) | async-done | bytes 393248 | tf_op jit(solution)/shard_map/all_to_all | solution.py:384
  158.0 0.5 fusion.5.p_ref
  158.5 0.5 fusion.7
  159.0 0.0 copy-start.5
  159.1 0.6 fusion.6
  159.6 2.5 %collective-permute-start.8 = (f32[128,128]{1,0:T(8,128)S(1)}, f32[128,128]{1,0:T(8,128)S(1)}, u32[]{:S(2)}, u32[]{:S(2)}) collective-permute-start(f32[128,128]{1,0:T(8,128)S(1)} %fusion.7), channel_id=1, source_target_pairs={{0,1},{1,0},{2,3},{3,2},{4,5},{5,4},{6,7},{7,6},{8,9},{9,8},{10,11... | collective-permute-start | bytes 196616 | tf_op jit(solution)/shard_map/ppermute | solution.py:370
  162.2 0.7 constant_dynamic-slice_fusion
  162.9 0.0 collective-permute-start.7
  162.9 0.2 collective-permute-done.8
  163.1 0.8 broadcast_in_dim.13
  163.9 3.5 %all-to-all-start.6 = ((f32[8,128,128]{2,1,0:T(8,128)}), f32[8,128,128]{2,1,0:T(8,128)S(1)}, u32[]{:S(2)}, u32[]{:S(2)}) async-start(f32[8,128,128]{2,1,0:T(8,128)} %broadcast_in_dim.13), calls=%async_computation.6 | async-start | bytes 1048576 | tf_op jit(solution)/shard_map/all_to_all | solution.py:384
  167.4 0.7 fusion
  168.2 0.4 collective-permute-start.3
  168.5 5.3 %collective-permute-start.4 = (bf16[128,768]{1,0:T(8,128)(2,1)S(1)}, bf16[128,768]{1,0:T(8,128)(2,1)}, u32[]{:S(2)}, u32[]{:S(2)}) collective-permute-start(bf16[128,768]{1,0:T(8,128)(2,1)S(1)} %get-tuple-element.39), channel_id=1, source_target_pairs={{0,14},{1,15},{2,12},{3,13},{4,10},{5,11},{6,8},{7,9},{8,6},{9,7},... | collective-permute-start | bytes 589832 | tf_op jit(solution)/shard_map/ppermute | solution.py:381
  173.8 0.1 collective-permute-start.5
  174.0 4.5 %all-to-all-done.6.g_ref = f32[8,128,128]{2,1,0:T(8,128)S(1)} async-done(((f32[8,128,128]{2,1,0:T(8,128)}), f32[8,128,128]{2,1,0:T(8,128)S(1)}, u32[]{:S(2)}, u32[]{:S(2)}) %all-to-all-start.6) | async-done | bytes 524320 | tf_op jit(solution)/shard_map/all_to_all | solution.py:384
  178.4 0.9 broadcast_in_dim.14
  179.4 3.5 %all-to-all-start.7 = ((bf16[8,256,128]{2,1,0:T(8,128)(2,1)}), bf16[8,256,128]{2,1,0:T(8,128)(2,1)S(1)}, u32[]{:S(2)}, u32[]{:S(2)}) async-start(bf16[8,256,128]{2,1,0:T(8,128)(2,1)} %broadcast_in_dim.14), calls=%async_computation.7 | async-start | bytes 1048576 | tf_op jit(solution)/shard_map/all_to_all | solution.py:384
  182.9 5.5 %inverse_factor.1.i_ref = f32[128,128]{1,0:T(8,128)} custom-call(f32[8,128,128]{2,1,0:T(8,128)} %copy-done.10), custom_call_target="tpu_custom_call" | custom-call | flops 8000000000 | bytes 1000000 | tf_op jit(solution)/shard_map/inverse_factor/pallas_call | solution.py:318
  188.5 3.9 %all-to-all-done.7 = bf16[8,256,128]{2,1,0:T(8,128)(2,1)S(1)} async-done(((bf16[8,256,128]{2,1,0:T(8,128)(2,1)}), bf16[8,256,128]{2,1,0:T(8,128)(2,1)S(1)}, u32[]{:S(2)}, u32[]{:S(2)}) %all-to-all-start.7) | async-done | bytes 524320 | tf_op jit(solution)/shard_map/all_to_all | solution.py:384
  192.3 0.1 convert_reduce_fusion
  192.4 1.1 convolution_multiply_fusion
  193.5 3.2 %collective-permute-start.9 = (f32[256,128]{1,0:T(8,128)S(1)}, f32[256,128]{1,0:T(8,128)S(1)}, u32[]{:S(2)}, u32[]{:S(2)}) collective-permute-start(f32[256,128]{1,0:T(8,128)S(1)} %convolution_multiply_fusion), channel_id=1, source_target_pairs={{0,1},{1,0},{2,3},{3,2},{4,5},{5,4},{6,7},{7,6},{8,9},{9,8},{10,11... | collective-permute-start | bytes 393224 | tf_op jit(solution)/shard_map/ppermute | solution.py:370
  196.7 0.0 collective-permute-done.3.refs_1_
  196.7 0.0 collective-permute-done.4.refs_2_
  196.7 0.0 collective-permute-done.5.refs_3_
  196.7 0.7 copy-done.11
  197.4 2.2 %unpack_queries.1 = bf16[128,3072]{1,0:T(8,128)(2,1)} custom-call(s32[4]{0:T(128)} %pad_add_fusion.h_ref, bf16[128,768]{1,0:T(8,128)(2,1)} %get-tuple-element.41.refs_0_, bf16[128,768]{1,0:T(8,128)(2,1)} %copy-done.11, bf16[128,768]{1,0:T(8,128)(2,1)} %collective-permute-done.4.refs_2_, bf16[128,768]{1,0:T(8,128)(2,1)} %collective-permute-done.5.refs_3_), custom_call_target="tpu_custom_call" | custom-call | tf_op jit(solution)/shard_map/unpack_queries/pallas_call | solution.py:238
  199.6 0.7 pad_maximum_fusion.1
  200.3 0.0 copy-start.1
  200.3 2.4 %finish.1 = (f32[384,512]{1,0:T(8,128)}, f32[1,384,512]{2,1,0:T(8,128)}) custom-call(f32[384,128]{1,0:T(8,128)S(1)} %fusion.5.p_ref, f32[128,128]{1,0:T(8,128)S(1)} %copy-done.6, f32[512,128]{1,0:T(8,128)S(1)} %maximum_select_fusion.q_ref, f32[384,512]{1,0:T(8,128)S(1)} %get-tuple-element.35.c_ref), custom_call_target="tpu_custom_call" | custom-call | tf_op jit(solution)/shard_map/finish/pallas_call | solution.py:343
  (32 shorter events, 0.1 us)
Async XLA Ops:
  0.6 157.4 %copy-start = (f32[512,128]{1,0:T(8,128)S(1)}, f32[512,128]{1,0:T(8,128)}, u32[]{:S(2)}) copy-start(f32[512,128]{1,0:T(8,128)} %param.15) | copy-start | bytes 786436
  2.8 17.6 %copy-start.8 = (bf16[128,6144]{1,0:T(8,128)(2,1)S(1)}, bf16[128,6144]{1,0:T(8,128)(2,1)}, u32[]{:S(2)}) copy-start(bf16[128,6144]{1,0:T(8,128)(2,1)} %param.12) | copy-start | bytes 4718596
  2.8 27.2 %all-to-all-start = ((bf16[16,144,256]{2,1,0:T(8,128)(2,1)}), bf16[16,144,256]{2,1,0:T(8,128)(2,1)S(1)}, u32[]{:S(2)}, u32[]{:S(2)}) async-start(bf16[16,144,256]{2,1,0:T(8,128)(2,1)} %pack_keys.1), calls=%async_computation | async-start | bytes 2359296 | tf_op jit(solution)/shard_map/all_to_all | solution.py:384
  14.7 20.4 %collective-permute-start = (bf16[128,1536]{1,0:T(8,128)(2,1)}, bf16[128,1536]{1,0:T(8,128)(2,1)}, u32[]{:S(2)}, u32[]{:S(2)}) collective-permute-start(bf16[128,1536]{1,0:T(8,128)(2,1)} %get-tuple-element.23), channel_id=1, source_target_pairs={{0,1},{1,0},{2,3},{3,2},{4,5},{5,4},{6,7},{7,6},{8,9},{9,8},{10,11... | collective-permute-start | bytes 1179656 | tf_op jit(solution)/shard_map/ppermute | solution.py:381
  14.8 23.8 %collective-permute-start.1 = (bf16[128,1536]{1,0:T(8,128)(2,1)}, bf16[128,1536]{1,0:T(8,128)(2,1)}, u32[]{:S(2)}, u32[]{:S(2)}) collective-permute-start(bf16[128,1536]{1,0:T(8,128)(2,1)} %get-tuple-element.24), channel_id=1, source_target_pairs={{0,14},{1,15},{2,12},{3,13},{4,10},{5,11},{6,8},{7,9},{8,6},{9,7},... | collective-permute-start | bytes 1179656 | tf_op jit(solution)/shard_map/ppermute | solution.py:381
  20.1 31.3 %collective-permute-start.2 = (bf16[128,1536]{1,0:T(8,128)(2,1)}, bf16[128,1536]{1,0:T(8,128)(2,1)}, u32[]{:S(2)}, u32[]{:S(2)}) collective-permute-start(bf16[128,1536]{1,0:T(8,128)(2,1)} %get-tuple-element.25), channel_id=1, source_target_pairs={{0,15},{1,14},{2,13},{3,12},{4,11},{5,10},{6,9},{7,8},{8,7},{9,6},... | collective-permute-start | bytes 1179656 | tf_op jit(solution)/shard_map/ppermute | solution.py:381
  30.1 21.3 %copy-start.7 = (bf16[128,1536]{1,0:T(8,128)(2,1)S(1)}, bf16[128,1536]{1,0:T(8,128)(2,1)}, u32[]{:S(2)}) copy-start(bf16[128,1536]{1,0:T(8,128)(2,1)} %get-tuple-element.22.q0.g0) | copy-start | bytes 1179652
  30.1 37.2 %all-to-all-start.1 = ((bf16[16,384,128]{2,1,0:T(8,128)(2,1)}), bf16[16,384,128]{2,1,0:T(8,128)(2,1)S(1)}, u32[]{:S(2)}, u32[]{:S(2)}) async-start(bf16[16,384,128]{2,1,0:T(8,128)(2,1)} %bitcast.34), calls=%async_computation.1 | async-start | bytes 3145728 | tf_op jit(solution)/shard_map/all_to_all | solution.py:384
  60.9 1.0 copy-start.2
  61.9 0.9 copy-start.4
  91.2 19.3 %copy-start.9 = (bf16[128,512]{1,0:T(8,128)(2,1)}, bf16[128,512]{1,0:T(8,128)(2,1)S(1)}, u32[]{:S(2)}) copy-start(bf16[128,512]{1,0:T(8,128)(2,1)S(1)} %pad_maximum_fusion) | copy-start | bytes 393220
  91.2 23.4 %copy-start.3 = (f32[1,384,512]{2,1,0:T(8,128)S(1)}, f32[1,384,512]{2,1,0:T(8,128)}, u32[]{:S(2)}) copy-start(f32[1,384,512]{2,1,0:T(8,128)} %param.14) | copy-start | bytes 2359300
  110.5 4.1 %collective-permute-start.6 = (bf16[8,128,512]{2,1,0:T(8,128)(2,1)S(1)}, bf16[8,128,512]{2,1,0:T(8,128)(2,1)S(1)}, u32[]{:S(2)}, u32[]{:S(2)}) collective-permute-start(bf16[8,128,512]{2,1,0:T(8,128)(2,1)S(1)} %all_to_all.41.m_ref), channel_id=1, source_target_pairs={{0,1},{1,0},{2,3},{3,2},{4,5},{5,4},{6,7},{7,6},{8,9},{9,8},{10,11... | collective-permute-start | bytes 3145736 | tf_op jit(solution)/shard_map/ppermute | solution.py:370
  140.9 17.2 %all-to-all-start.5 = ((bf16[16,24,512]{2,1,0:T(8,128)(2,1)}), bf16[16,24,512]{2,1,0:T(8,128)(2,1)S(1)}, u32[]{:S(2)}, u32[]{:S(2)}) async-start(bf16[16,24,512]{2,1,0:T(8,128)(2,1)} %broadcast_in_dim.12), calls=%async_computation.5 | async-start | bytes 786432 | tf_op jit(solution)/shard_map/all_to_all | solution.py:384
  159.0 8.4 %copy-start.5 = (bf16[512,768]{1,0:T(8,128)(2,1)S(1)}, bf16[512,768]{1,0:T(8,128)(2,1)}, u32[]{:S(2)}) copy-start(bf16[512,768]{1,0:T(8,128)(2,1)} %copy-done.4) | copy-start | bytes 2359300
  159.6 3.4 %collective-permute-start.8 = (f32[128,128]{1,0:T(8,128)S(1)}, f32[128,128]{1,0:T(8,128)S(1)}, u32[]{:S(2)}, u32[]{:S(2)}) collective-permute-start(f32[128,128]{1,0:T(8,128)S(1)} %fusion.7), channel_id=1, source_target_pairs={{0,1},{1,0},{2,3},{3,2},{4,5},{5,4},{6,7},{7,6},{8,9},{9,8},{10,11... | collective-permute-start | bytes 196616 | tf_op jit(solution)/shard_map/ppermute | solution.py:370
  162.9 11.1 %collective-permute-start.7 = (f32[256,128]{1,0:T(8,128)}, f32[256,128]{1,0:T(8,128)S(1)}, u32[]{:S(2)}, u32[]{:S(2)}) collective-permute-start(f32[256,128]{1,0:T(8,128)} %constant_dynamic-slice_fusion), channel_id=1, source_target_pairs={{0,1},{1,0},{2,3},{3,2},{4,5},{5,4},{6,7},{7,6},{8,9},{9,8},{10,11... | collective-permute-start | bytes 393224 | tf_op jit(solution)/shard_map/ppermute | solution.py:370
  163.9 14.5 %all-to-all-start.6 = ((f32[8,128,128]{2,1,0:T(8,128)}), f32[8,128,128]{2,1,0:T(8,128)S(1)}, u32[]{:S(2)}, u32[]{:S(2)}) async-start(f32[8,128,128]{2,1,0:T(8,128)} %broadcast_in_dim.13), calls=%async_computation.6 | async-start | bytes 1048576 | tf_op jit(solution)/shard_map/all_to_all | solution.py:384
  168.2 28.5 %collective-permute-start.3 = (bf16[128,768]{1,0:T(8,128)(2,1)S(1)}, bf16[128,768]{1,0:T(8,128)(2,1)S(1)}, u32[]{:S(2)}, u32[]{:S(2)}) collective-permute-start(bf16[128,768]{1,0:T(8,128)(2,1)S(1)} %get-tuple-element.40), channel_id=1, source_target_pairs={{0,1},{1,0},{2,3},{3,2},{4,5},{5,4},{6,7},{7,6},{8,9},{9,8},{10,11... | collective-permute-start | bytes 589832 | tf_op jit(solution)/shard_map/ppermute | solution.py:381
  168.5 28.2 %collective-permute-start.4 = (bf16[128,768]{1,0:T(8,128)(2,1)S(1)}, bf16[128,768]{1,0:T(8,128)(2,1)}, u32[]{:S(2)}, u32[]{:S(2)}) collective-permute-start(bf16[128,768]{1,0:T(8,128)(2,1)S(1)} %get-tuple-element.39), channel_id=1, source_target_pairs={{0,14},{1,15},{2,12},{3,13},{4,10},{5,11},{6,8},{7,9},{8,6},{9,7},... | collective-permute-start | bytes 589832 | tf_op jit(solution)/shard_map/ppermute | solution.py:381
  173.8 22.9 %collective-permute-start.5 = (bf16[128,768]{1,0:T(8,128)(2,1)S(1)}, bf16[128,768]{1,0:T(8,128)(2,1)}, u32[]{:S(2)}, u32[]{:S(2)}) collective-permute-start(bf16[128,768]{1,0:T(8,128)(2,1)S(1)} %get-tuple-element.38), channel_id=1, source_target_pairs={{0,15},{1,14},{2,13},{3,12},{4,11},{5,10},{6,9},{7,8},{8,7},{9,6},... | collective-permute-start | bytes 589832 | tf_op jit(solution)/shard_map/ppermute | solution.py:381
  178.4 4.5 %copy-start.10 = (f32[8,128,128]{2,1,0:T(8,128)}, f32[8,128,128]{2,1,0:T(8,128)S(1)}, u32[]{:S(2)}) copy-start(f32[8,128,128]{2,1,0:T(8,128)S(1)} %all-to-all-done.6.g_ref) | copy-start | bytes 1572868
  179.4 12.9 %all-to-all-start.7 = ((bf16[8,256,128]{2,1,0:T(8,128)(2,1)}), bf16[8,256,128]{2,1,0:T(8,128)(2,1)S(1)}, u32[]{:S(2)}, u32[]{:S(2)}) async-start(bf16[8,256,128]{2,1,0:T(8,128)(2,1)} %broadcast_in_dim.14), calls=%async_computation.7 | async-start | bytes 1048576 | tf_op jit(solution)/shard_map/all_to_all | solution.py:384
  188.4 11.1 %copy-start.12 = (bf16[128,128]{1,0:T(8,128)(2,1)S(1)}, bf16[128,128]{1,0:T(8,128)(2,1)}, u32[]{:S(2)}) copy-start(bf16[128,128]{1,0:T(8,128)(2,1)} %get-tuple-element.46) | copy-start | bytes 98308
  188.4 11.1 %copy-start.13 = (bf16[128,128]{1,0:T(8,128)(2,1)S(1)}, bf16[128,128]{1,0:T(8,128)(2,1)}, u32[]{:S(2)}) copy-start(bf16[128,128]{1,0:T(8,128)(2,1)} %get-tuple-element.55) | copy-start | bytes 98308
  188.4 11.1 %copy-start.14 = (bf16[128,128]{1,0:T(8,128)(2,1)S(1)}, bf16[128,128]{1,0:T(8,128)(2,1)}, u32[]{:S(2)}) copy-start(bf16[128,128]{1,0:T(8,128)(2,1)} %get-tuple-element.50) | copy-start | bytes 98308
  188.4 11.1 %copy-start.15 = (bf16[128,128]{1,0:T(8,128)(2,1)S(1)}, bf16[128,128]{1,0:T(8,128)(2,1)}, u32[]{:S(2)}) copy-start(bf16[128,128]{1,0:T(8,128)(2,1)} %get-tuple-element.57) | copy-start | bytes 98308
  188.5 11.8 %copy-start.6 = (f32[128,128]{1,0:T(8,128)S(1)}, f32[128,128]{1,0:T(8,128)}, u32[]{:S(2)}) copy-start(f32[128,128]{1,0:T(8,128)} %inverse_factor.1.i_ref) | copy-start | bytes 196612
  193.5 6.7 %collective-permute-start.9 = (f32[256,128]{1,0:T(8,128)S(1)}, f32[256,128]{1,0:T(8,128)S(1)}, u32[]{:S(2)}, u32[]{:S(2)}) collective-permute-start(f32[256,128]{1,0:T(8,128)S(1)} %convolution_multiply_fusion), channel_id=1, source_target_pairs={{0,1},{1,0},{2,3},{3,2},{4,5},{5,4},{6,7},{7,6},{8,9},{9,8},{10,11... | collective-permute-start | bytes 393224 | tf_op jit(solution)/shard_map/ppermute | solution.py:370
  196.7 0.7 copy-start.11
  200.3 2.4 %copy-start.1 = (f32[512,128]{1,0:T(8,128)}, f32[512,128]{1,0:T(8,128)S(1)}, u32[]{:S(2)}) copy-start(f32[512,128]{1,0:T(8,128)S(1)} %maximum_select_fusion.q_ref) | copy-start | bytes 786436

commit v5 on v4

--- a/solution.py
+++ b/solution.py
@@ -15,9 +15,10 @@
 TN = (((0,), (0,)), ((), ()))
 NT = (((1,), (1,)), ((), ()))
 HEADS_AT_ONCE = 6
-
-
-def attention(where, parts, kv):
+EARLY = 160
+
+
+def attention(where, parts, kv, extra):
     devices, padded, _ = kv.shape
     tokens = HEAD
     block = 2 * tokens
@@ -31,7 +32,7 @@
     power = scale * LOG2E
 
     def kernel(
-        at, q0, q1, q2, q3, g0, g1, g2, g3, k_ref, v_ref, dq_ref, dkv_ref,
+        at, q0, q1, q2, q3, g0, g1, g2, g3, k_ref, v_ref, e_ref, dq_ref, out_ref,
         s_scr, d_scr, bias, k_turned, dq_acc, dk_acc, dv_acc,
     ):
         step = pl.program_id(0)
@@ -138,10 +139,14 @@
 
         @pl.when(step == 2 * steps - 1)
         def _():
-            dkv_ref[:, :HEAD] = (dk_acc[...] * scale).astype(jnp.bfloat16)
-            dkv_ref[:, HEAD:] = dv_acc[...].astype(jnp.bfloat16)
-
-    whole = pl.BlockSpec((length, 2 * HEAD), lambda s, at: (0, 0))
+            dk = (dk_acc[...] * scale).astype(jnp.bfloat16)
+            out_ref[:, :tokens, :] = dk.reshape(devices, tokens, HEAD)
+            dv = dv_acc[...].astype(jnp.bfloat16)
+            out_ref[:, tokens:block, :] = dv.reshape(devices, tokens, HEAD)
+            out_ref[:, block:, :] = e_ref[...]
+
+    more = extra.shape[1]
+    whole = pl.BlockSpec((devices, block + more, HEAD), lambda s, at: (0, 0, 0))
     queries_at = pl.BlockSpec((block, wide), lambda s, at: (s // steps, s % steps))
     flops = 5 * 2 * length * block * heads * HEAD
     return pl.pallas_call(
@@ -154,6 +159,7 @@
                 *[pl.BlockSpec((tokens, wide), lambda s, at: (0, steps + s % steps))] * 4,
                 pl.BlockSpec((devices, padded, HEAD), lambda s, at: (0, 0, 0)),
                 pl.BlockSpec((devices, padded, HEAD), lambda s, at: (0, 0, 1)),
+                pl.BlockSpec((devices, more, HEAD), lambda s, at: (0, 0, 0)),
             ],
             out_specs=[queries_at, whole],
             scratch_shapes=[
@@ -168,16 +174,16 @@
         ),
         out_shape=[
             jax.ShapeDtypeStruct((2 * block, heads * HEAD), jnp.bfloat16),
-            jax.ShapeDtypeStruct((length, 2 * HEAD), jnp.bfloat16),
+            jax.ShapeDtypeStruct((devices, block + more, HEAD), jnp.bfloat16),
         ],
         compiler_params=pltpu.CompilerParams(
-            dimension_semantics=("arbitrary",), vmem_limit_bytes=40 * 1024 * 1024
+            dimension_semantics=("arbitrary",), vmem_limit_bytes=44 * 1024 * 1024
         ),
         cost_estimate=pl.CostEstimate(
             flops=8 * flops, bytes_accessed=8 * 1024 * 1024, transcendentals=0
         ),
         name="attention",
-    )(where, *parts, *parts, kv, kv)
+    )(where, *parts, *parts, kv, kv, extra)
 
 
 VMEM = pl.BlockSpec(memory_space=pltpu.VMEM)
@@ -244,22 +250,24 @@
     )(heads, *parts)
 
 
-def gradient(where, turned, mine, theirs, error):
-    devices, rows, tokens = turned.shape
-    width = mine.shape[2]
-
-    def kernel(at, f_ref, m_ref, t_ref, e_ref, out_ref, low_ref):
+def gradient(where, first, later, skip, mine, theirs, error):
+    devices, early, _ = first.shape
+    rows, width = error.shape
+
+    def kernel(at, f_ref, l_ref, m_ref, t_ref, e_ref, out_ref, low_ref):
         core = at[0]
-        total = e_ref[...]
+        top, rest = e_ref[:early, :], e_ref[early:, :]
         for c in range(devices // 2):
-            total = total + jnp.dot(
-                f_ref[2 * c + core], m_ref[c], preferred_element_type=jnp.float32
-            )
-            total = total + jnp.dot(
-                f_ref[2 * c + 1 - core], t_ref[c], preferred_element_type=jnp.float32
-            )
-        out_ref[...] = total
-        low_ref[...] = total.astype(jnp.bfloat16)
+            for n, d_ref in ((2 * c + core, m_ref), (2 * c + 1 - core, t_ref)):
+                d = d_ref[c]
+                top = top + jnp.dot(f_ref[n], d, preferred_element_type=jnp.float32)
+                rest = rest + jnp.dot(
+                    l_ref[n, skip:, :], d, preferred_element_type=jnp.float32
+                )
+        out_ref[:early, :] = top
+        out_ref[early:, :] = rest
+        low_ref[:early, :] = top.astype(jnp.bfloat16)
+        low_ref[early:, :] = rest.astype(jnp.bfloat16)
 
     return pl.pallas_call(
         kernel,
@@ -267,29 +275,115 @@
             jax.ShapeDtypeStruct((rows, width), jnp.float32),
             jax.ShapeDtypeStruct((rows, width), jnp.bfloat16),
         ],
-        in_specs=[SMEM] + [VMEM] * 4,
+        in_specs=[SMEM] + [VMEM] * 5,
         out_specs=[VMEM] * 2,
         compiler_params=pltpu.CompilerParams(vmem_limit_bytes=32 * 1024 * 1024),
         name="gradient",
-    )(where, turned, mine, theirs, error)
-
-
-def inverse_factor(parts):
-    count, size, _ = parts.shape
+    )(where, first, later, mine, theirs, error)
+
+
+def moments(where, total, q_init):
+    rows, width = total.shape
+    rank = q_init.shape[1]
+    half, part = width // 2, rank // 2
+
+    def kernel(at, t_ref, q_ref, p_ref, mine_ref, other_ref, all_ref, gram_ref):
+        core = at[0]
+        x = t_ref[...].astype(jnp.float32)
+        p = jnp.dot(x, q_ref[...], precision=HIGHEST, preferred_element_type=jnp.float32)
+        p_ref[...] = p
+        p_turned = p.T
+        gram_ref[...] = jnp.dot(
+            p_turned, p, precision=HIGHEST, preferred_element_type=jnp.float32
+        )
+        all_ref[...] = jnp.dot(
+            p_turned, x, precision=HIGHEST, preferred_element_type=jnp.float32
+        ).T
+        for out, who in ((mine_ref, core), (other_ref, 1 - core)):
+            out[:half, :] = all_ref[pl.ds(pl.multiple_of(who * half, half), half), :]
+            out[half:, :] = gram_ref[pl.ds(pl.multiple_of(who * part, part), part), :]
+
+    return pl.pallas_call(
+        kernel,
+        out_shape=[
+            jax.ShapeDtypeStruct((rows, rank), jnp.float32),
+            jax.ShapeDtypeStruct((half + part, rank), jnp.float32),
+            jax.ShapeDtypeStruct((half + part, rank), jnp.float32),
+        ],
+        in_specs=[SMEM, VMEM, VMEM],
+        out_specs=[VMEM] * 3,
+        scratch_shapes=[
+            pltpu.VMEM((width, rank), jnp.float32),
+            pltpu.VMEM((rank, rank), jnp.float32),
+        ],
+        name="moments",
+    )(where, total, q_init)
+
+
+def pack_moments(mine, theirs, copies, half):
+    count, rank = mine.shape
+    part = count - half
+
+    def kernel(m_ref, t_ref, out_ref):
+        total = m_ref[...] + t_ref[...]
+        gram = total[half:, :]
+        high = gram.astype(jnp.bfloat16)
+        gram = gram - high.astype(jnp.float32)
+        mid = gram.astype(jnp.bfloat16)
+        low = (gram - mid.astype(jnp.float32)).astype(jnp.bfloat16)
+        whole = jnp.concatenate([total[:half, :].astype(jnp.bfloat16), high, mid, low], axis=0)
+        for n in range(copies):
+            out_ref[n] = whole
+
+    return pl.pallas_call(
+        kernel,
+        out_shape=jax.ShapeDtypeStruct((copies, half + 3 * part, rank), jnp.bfloat16),
+        in_specs=[VMEM] * 2,
+        out_specs=VMEM,
+        name="pack_moments",
+    )(mine, theirs)
+
+
+def sum_moments(parts, half):
+    copies, count, rank = parts.shape
+    part = (count - half) // 3
+
+    def kernel(x_ref, out_ref):
+        total = x_ref[0].astype(jnp.float32)
+        for n in range(1, copies):
+            total = total + x_ref[n].astype(jnp.float32)
+        out_ref[:half, :] = total[:half, :]
+        out_ref[half:, :] = (
+            total[half : half + part, :]
+            + total[half + part : half + 2 * part, :]
+            + total[half + 2 * part :, :]
+        )
+
+    return pl.pallas_call(
+        kernel,
+        out_shape=jax.ShapeDtypeStruct((half + part, rank), jnp.float32),
+        in_specs=[VMEM],
+        out_specs=VMEM,
+        name="sum_moments",
+    )(parts)
+
+
+def finish(where, p_sum, mine, theirs, combined, replicas):
+    rows, width = combined.shape
+    size = p_sum.shape[1]
+    half, part = width // 2, size // 2
     tiles = size // 8
     shape = (8, size)
 
-    def kernel(g_ref, out_ref):
+    def kernel(at, p_ref, m_ref, t_ref, c_ref, comp_ref, q_ref, new_ref, gram_ref, inv_ref, all_ref):
+        core = at[0]
+        for x, who in ((m_ref, core), (t_ref, 1 - core)):
+            all_ref[pl.ds(pl.multiple_of(who * half, half), half), :] = x[:half, :]
+            gram_ref[pl.ds(pl.multiple_of(who * part, part), part), :] = x[half:, :]
         lane = lax.broadcasted_iota(jnp.int32, shape, 1)
         sub = lax.broadcasted_iota(jnp.int32, shape, 0)
-        left, right = [], []
-        for t in range(tiles):
-            total = g_ref[0, 8 * t : 8 * t + 8, :]
-            for n in range(1, count):
-                total = total + g_ref[n, 8 * t : 8 * t + 8, :]
-            left.append(total)
-            right.append(jnp.where(lane == sub + 8 * t, 1.0, 0.0))
-
+        left = [gram_ref[8 * t : 8 * t + 8, :] for t in range(tiles)]
+        right = [jnp.where(lane == sub + 8 * t, 1.0, 0.0) for t in range(tiles)]
         def row(x, r):
             return jnp.broadcast_to(x[r : r + 1, :], shape)
 
@@ -306,7 +400,7 @@
                 root = lax.rsqrt(row(pivot, k))
                 row_l = row(left[p], k) * root
                 row_r = row(right[p], k) * root
-                out_ref[8 * p + k : 8 * p + k + 1, :] = row_r[0:1]
+                inv_ref[8 * p + k : 8 * p + k + 1, :] = row_r[0:1]
                 factors = [row(pivot, m) * root for m in range(k + 1, 8)]
                 for t in range(p, tiles):
                     x = spread[t - p][k] * root
@@ -315,28 +409,15 @@
                     left[t] = left[t] - x * row_l
                     right[t] = right[t] - x * row_r
 
-    return pl.pallas_call(
-        kernel,
-        out_shape=jax.ShapeDtypeStruct((size, size), jnp.float32),
-        in_specs=[VMEM],
-        out_specs=VMEM,
-        cost_estimate=pl.CostEstimate(
-            flops=8 * 10**9, bytes_accessed=10**6, transcendentals=0
-        ),
-        name="inverse_factor",
-    )(parts)
-
-
-def finish(p_sum, inverse, q_factor, combined):
-    rows, width = combined.shape
-
-    def kernel(p_ref, i_ref, q_ref, c_ref, comp_ref, new_ref):
         def product(x, y):
             return lax.dot_general(
                 x, y, NT, precision=HIGHEST, preferred_element_type=jnp.float32
             )
 
-        out = product(product(p_ref[...], i_ref[...]), q_ref[...])
+        inv = inv_ref[...]
+        q = product(all_ref[...], inv) * (1.0 / replicas)
+        q_ref[...] = q
+        out = product(product(p_ref[...], inv), q)
         comp_ref[...] = out
         new_ref[0] = c_ref[...] - out
 
@@ -344,13 +425,19 @@
         kernel,
         out_shape=[
             jax.ShapeDtypeStruct((rows, width), jnp.float32),
+            jax.ShapeDtypeStruct((width, size), jnp.float32),
             jax.ShapeDtypeStruct((1, rows, width), jnp.float32),
         ],
-        in_specs=[VMEM] * 4,
-        out_specs=[VMEM] * 2,
+        in_specs=[SMEM] + [VMEM] * 4,
+        out_specs=[VMEM] * 3,
+        scratch_shapes=[
+            pltpu.VMEM((size, size), jnp.float32),
+            pltpu.VMEM((size, size), jnp.float32),
+            pltpu.VMEM((width, size), jnp.float32),
+        ],
         compiler_params=pltpu.CompilerParams(vmem_limit_bytes=32 * 1024 * 1024),
         name="finish",
-    )(p_sum, inverse, q_factor, combined)
+    )(where, p_sum, mine, theirs, combined)
 
 
 def body(queries, keys, values, d_out, features, doc_start, error, q_init):
@@ -396,23 +483,27 @@
     parts = [parts[0]] + [move(x, *way) for x, way in zip(parts[1:], ways[1:])]
 
     rows = features.shape[1] // devices
-    feat = jnp.transpose(features).reshape(devices, rows, tokens)
-    kv, feat = lax.optimization_barrier((kv, feat))
-    feat = exchange(feat, ctx)
+    turned = jnp.transpose(features).reshape(devices, rows, tokens)
+    first, later = turned[:, :EARLY], turned[:, EARLY:]
+    kv, first = lax.optimization_barrier((kv, first))
+    first = exchange(first, ctx)
 
     where = jnp.stack([core, chip, chips - 1 - chip]).astype(jnp.int32)
-    dq, dkv = attention(where, parts, kv)
-    dkv, feat = lax.optimization_barrier((dkv, feat))
-
-    home = exchange(dkv.reshape(devices, tokens, 2 * HEAD), ctx)
-    home = home.reshape(2, chips // 2, 2, tokens, 2 * HEAD).astype(f32)
+    dq, home = attention(where, parts, kv, later)
+    home, first = lax.optimization_barrier((home, first))
+
+    later = exchange(home, ctx)
+    home = later[:, : 2 * tokens, :]
+    home = home.reshape(2, chips // 2, 2, 2 * tokens, HEAD).astype(f32)
     home = jnp.sum(home, axis=1).astype(bf16)
     home = [home[0, 0], home[1, 0], home[0, 1], home[1, 1]]
-    d_key = jnp.concatenate([x[:, :HEAD] for x in home], axis=1)
-    d_value = jnp.concatenate([x[:, HEAD:] for x in home], axis=1)
+    d_key = jnp.concatenate([x[:tokens] for x in home], axis=1)
+    d_value = jnp.concatenate([x[tokens:] for x in home], axis=1)
     dk_mine = spread(d_key, "chip", chips)
     dk_theirs = swap(dk_mine)
-    combined, low = gradient(where, feat, dk_mine, dk_theirs, error.reshape(rows, width_kv))
+    combined, low = gradient(
+        where, first, later, 2 * tokens, dk_mine, dk_theirs, error.reshape(rows, width_kv)
+    )
 
     shares = exchange(low.reshape(replicas, rows // replicas, width_kv), "dp")
     share = jnp.sum(shares.astype(f32), axis=0).astype(bf16)
@@ -423,22 +514,10 @@
     ]
     d_query = unpack_queries(heads, back, group)
 
-    total = total.astype(f32)
-    p_sum = jnp.dot(total, q_init, precision=HIGHEST)
-    gram = lax.dot_general(p_sum, p_sum, TN, precision=HIGHEST)
-    gram = spread(gram + swap(gram), "chip", chips)
-    moment = lax.dot_general(total, p_sum, TN, precision=HIGHEST)
-    size = width_kv // 2
-    moment = piece(moment, size, core, 0) + swap(piece(moment, size, 1 - core, 0))
-    moment, gram = lax.optimization_barrier((moment.astype(bf16), gram))
-    moment = jnp.sum(spread(moment, "chip", chips).astype(f32), axis=0)
-    inverse = inverse_factor(gram)
-    q_mine = lax.dot_general(moment, inverse, NT, precision=HIGHEST) / replicas
-    q_theirs = swap(q_mine)
-    q_factor = jnp.where(
-        core == 0, jnp.concatenate([q_mine, q_theirs]), jnp.concatenate([q_theirs, q_mine])
-    )
-    compressed, new_error = finish(p_sum, inverse, q_factor, combined)
+    half = width_kv // 2
+    p_sum, mine, other = moments(where, total, q_init)
+    part = sum_moments(exchange(pack_moments(mine, swap(other), chips, half), "chip"), half)
+    compressed, q_factor, new_error = finish(where, p_sum, part, swap(part), combined, replicas)
     return (d_query, d_key, d_value, compressed, q_factor, new_error)
 
 

time: 204 us -> 217 us (1.064)
  blocking collectives: 64.7 us -> 95 us
  waiting for transfers between devices: 50.6 us -> 34.9 us
  starting transfers between devices: 45.8 us -> 35.3 us
  Pallas kernels: 26.7 us -> 35.7 us
  matrix products: 2.69 us -> 0 us
  local copies, waits for them, and re-layouts: 9.5 us -> 11.9 us
    all_to_all x3 -> x4, blocking collectives: 64.7 us -> 95 us  [exchange(): return lax.all_to_all(x, axis, 0, 0)]
    all_to_all x5 -> x3, waiting for transfers between devices: 31.9 us -> 13.1 us  [exchange(): return lax.all_to_all(x, axis, 0, 0)]
    all_to_all x5 -> x3, starting transfers between devices: 26.7 us -> 16.9 us  [exchange(): return lax.all_to_all(x, axis, 0, 0)]
    pallas_call x1, Pallas kernels: 2.36 us -> 7.01 us  [finish(): pl.pallas_call(kernel, out_shape=[jax.ShapeDtypeStruct((rows, width), jnp...]
    slice x2 -> x4, local copies, waits for them, and re-layouts: 1.28 us -> 5 us  [the longest x2 3.26 us: body(): first, later = (turned[:, :EARLY], turned[:, EARLY:])]
    pallas_call x1 -> x3, Pallas kernels: 5.55 us -> 8.41 us  [the longest x1 4.45 us: moments(): pl.pallas_call(kernel, out_shape=[jax.ShapeDtypeStruct((rows, rank), jnp....]
    dot_general x4 -> x0, matrix products: 2.69 us -> none  [the longest x1 1.11 us: body(): q_mine = lax.dot_general(moment, inverse, NT, precision=HIGHEST) / replicas]
    broadcast_in_dim x4 -> x2, local copies, waits for them, and re-layouts: 2.62 us -> 0.11 us  [spread(): return exchange(jnp.broadcast_to(x[None], (size,) + x.shape), axis)]
  transfers between devices with their start and end apart: 15 -> 12, of which waited for: 9 -> 8; matrix products, arithmetic and copies ran while one was open for 4% -> 3% of each run, Pallas kernels for 10% -> 8%
where the time goes in v5:
time: 217 us; the launch traced here: 216 us
  blocking collectives  95 us (44%)
  Pallas kernels  35.7 us (16%)
  starting transfers between devices  35.3 us (16%)
  waiting for transfers between devices  34.9 us (16%)
  local copies, waits for them, and re-layouts  11.9 us (5%)
  other arithmetic  2.86 us (1%)
    all_to_all x4, blocking collectives, exchange(): return lax.all_to_all(x, axis, 0, 0)  95 us
    ppermute x6, waiting for transfers between devices, move(): return lax.ppermute(x, ctx, pairs)  18.3 us
    all_to_all x3, starting transfers between devices, exchange(): return lax.all_to_all(x, axis, 0, 0)  16.9 us
    all_to_all x3, waiting for transfers between devices, exchange(): return lax.all_to_all(x, axis, 0, 0)  13.1 us
    ppermute x6, starting transfers between devices, move(): return lax.ppermute(x, ctx, pairs)  12.1 us
    pallas_call x1, Pallas kernels, attention(): pl.pallas_call(kernel, grid_spec=pltpu.PrefetchScalarGridSpec(num_scalar_...  11 us
    pallas_call x1, Pallas kernels, finish(): pl.pallas_call(kernel, out_shape=[jax.ShapeDtypeStruct((rows, width), jnp...  7.01 us
    ppermute x3, starting transfers between devices, swap(): return lax.ppermute(x, 'core', [(0, 1), (1, 0)])  6.31 us
  transfers between devices with their start and end apart: 12, of which 8 were waited for; matrix products, arithmetic and copies ran while one was open for 3% of the time, Pallas kernels for 8%

profile of v5, /device:TPU:1, one launch (start us, length us, event | category | flops | bytes accessed | tf_op | source)
XLA Modules:
  0.0 216.5 jit_solution(17502780733950125671)
XLA Ops:
  0.6 2.1 pack_keys.1
  2.8 8.6 %all-to-all-start = ((bf16[16,144,256]{2,1,0:T(8,128)(2,1)}), bf16[16,144,256]{2,1,0:T(8,128)(2,1)S(1)}, u32[]{:S(2)}, u32[]{:S(2)}) async-start(bf16[16,144,256]{2,1,0:T(8,128)(2,1)} %pack_keys.1), calls=%async_computation | async-start | bytes 2359296 | tf_op jit(solution)/shard_map/all_to_all | solution.py:471
  11.4 0.6 pad_add_fusion.h_ref
  12.0 2.6 %pack_queries.1 = (bf16[128,1536]{1,0:T(8,128)(2,1)}, bf16[128,1536]{1,0:T(8,128)(2,1)}, bf16[128,1536]{1,0:T(8,128)(2,1)}, bf16[128,1536]{1,0:T(8,128)(2,1)}) custom-call(s32[4]{0:T(128)} %pad_add_fusion.h_ref, bf16[128,3072]{1,0:T(8,128)(2,1)} %q_ref.2, bf16[128,3072]{1,0:T(8,128)(2,1)} %g_ref.1), custom_call_target="tpu_custom_call" | custom-call | tf_op jit(solution)/shard_map/pack_queries/pallas_call | solution.py:227
  14.6 0.1 collective-permute-start
  14.7 5.2 %collective-permute-start.1 = (bf16[128,1536]{1,0:T(8,128)(2,1)}, bf16[128,1536]{1,0:T(8,128)(2,1)}, u32[]{:S(2)}, u32[]{:S(2)}) collective-permute-start(bf16[128,1536]{1,0:T(8,128)(2,1)} %get-tuple-element.26), channel_id=1, source_target_pairs={{0,14},{1,15},{2,12},{3,13},{4,10},{5,11},{6,8},{7,9},{8,6},{9,7},... | collective-permute-start | bytes 1179656 | tf_op jit(solution)/shard_map/ppermute | solution.py:468
  20.0 0.4 collective-permute-start.2
  20.4 0.0 copy-done.10
  20.4 1.6 copy.14
  22.0 2.0 slice.104
  23.9 1.3 slice.105.e_ref
  25.2 0.1 pad_add_fusion.1.at
  25.3 4.7 %all-to-all-done.k_ref.v_ref = bf16[16,144,256]{2,1,0:T(8,128)(2,1)S(1)} async-done(((bf16[16,144,256]{2,1,0:T(8,128)(2,1)}), bf16[16,144,256]{2,1,0:T(8,128)(2,1)S(1)}, u32[]{:S(2)}, u32[]{:S(2)}) %all-to-all-start) | async-done | bytes 1179680 | tf_op jit(solution)/shard_map/all_to_all | solution.py:471
  30.0 4.8 %all-to-all-start.1 = ((bf16[16,160,128]{2,1,0:T(8,128)(2,1)}), bf16[16,160,128]{2,1,0:T(8,128)(2,1)S(1)}, u32[]{:S(2)}, u32[]{:S(2)}) async-start(bf16[16,160,128]{2,1,0:T(8,128)(2,1)} %slice.104), calls=%async_computation.1 | async-start | bytes 1310720 | tf_op jit(solution)/shard_map/all_to_all | solution.py:471
  34.8 0.0 collective-permute-done.q1.g1
  34.8 3.7 %collective-permute-done.1.q2.g2 = bf16[128,1536]{1,0:T(8,128)(2,1)} collective-permute-done((bf16[128,1536]{1,0:T(8,128)(2,1)}, bf16[128,1536]{1,0:T(8,128)(2,1)}, u32[]{:S(2)}, u32[]{:S(2)}) %collective-permute-start.1) | collective-permute-done | bytes 393248 | tf_op jit(solution)/shard_map/ppermute | solution.py:468
  38.5 11.0 %collective-permute-done.2.q3.g3 = bf16[128,1536]{1,0:T(8,128)(2,1)} collective-permute-done((bf16[128,1536]{1,0:T(8,128)(2,1)}, bf16[128,1536]{1,0:T(8,128)(2,1)}, u32[]{:S(2)}, u32[]{:S(2)}) %collective-permute-start.2) | collective-permute-done | bytes 393248 | tf_op jit(solution)/shard_map/ppermute | solution.py:468
  49.5 0.0 copy-done.8
  49.5 11.0 %attention.1 = (bf16[512,768]{1,0:T(8,128)(2,1)S(1)}, bf16[16,480,128]{2,1,0:T(8,128)(2,1)S(1)}) custom-call(s32[3]{0:T(128)S(1)} %pad_add_fusion.1.at, bf16[128,1536]{1,0:T(8,128)(2,1)S(1)} %copy-done.8, bf16[128,1536]{1,0:T(8,128)(2,1)} %collective-permute-done.q1.g1, bf16[128,1536]{1,0:T(8,128)(2,1)} %collective-permute-done.1.q2.g2, ...), custom_call_target="tpu_custom_call" | custom-call | flops 32212254720 | bytes 8388608 | tf_op jit(solution)/shard_map/attention/pallas_call | solution.py:152
  60.6 0.0 copy-start
  60.6 1.3 copy-done
  61.9 0.9 copy-done.1
  62.7 0.0 all-to-all-done.1.f_ref
  62.7 35.1 %all_to_all.35.l_ref = bf16[16,480,128]{2,1,0:T(8,128)(2,1)S(1)} all-to-all(bf16[16,480,128]{2,1,0:T(8,128)(2,1)} %copy-done), channel_id=1, replica_groups=mesh['dp'=16,'chip'=8,'core'=2] {'chip','core'}, dimensions={0} | all-to-all | bytes 3932160 | tf_op jit(solution)/shard_map/all_to_all | solution.py:471
  97.8 1.1 slice.106
  98.9 1.4 reduce_sum.24
  100.4 0.7 slice_bitcast_fusion.3
  101.0 0.0 copy-start.11
  101.0 0.0 copy-start.3
  101.1 0.1 broadcast_in_dim.7
  101.1 19.2 %all_to_all.36.m_ref = bf16[8,128,512]{2,1,0:T(8,128)(2,1)S(1)} all-to-all(bf16[8,128,512]{2,1,0:T(8,128)(2,1)S(1)} %broadcast_in_dim.7), channel_id=1, replica_groups=mesh['dp'=16,'chip'=8,'core'=2] {'chip'}, dimensions={0} | all-to-all | bytes 2097152 | tf_op jit(solution)/shard_map/all_to_all | solution.py:471
  120.3 0.0 copy-done.11
  120.3 1.9 collective-permute-start.6
  122.2 2.3 %collective-permute-done.6.t_ref = bf16[8,128,512]{2,1,0:T(8,128)(2,1)S(1)} collective-permute-done((bf16[8,128,512]{2,1,0:T(8,128)(2,1)S(1)}, bf16[8,128,512]{2,1,0:T(8,128)(2,1)S(1)}, u32[]{:S(2)}, u32[]{:S(2)}) %collective-permute-start.6) | collective-permute-done | bytes 1048608 | tf_op jit(solution)/shard_map/ppermute | solution.py:457
  124.5 0.0 copy-done.6
  124.5 0.0 copy-done.3
  124.5 2.3 %gradient.1 = (f32[384,512]{1,0:T(8,128)S(1)}, bf16[384,512]{1,0:T(8,128)(2,1)S(1)}) custom-call(s32[3]{0:T(128)S(1)} %pad_add_fusion.1.at, bf16[16,160,128]{2,1,0:T(8,128)(2,1)S(1)} %all-to-all-done.1.f_ref, bf16[16,480,128]{2,1,0:T(8,128)(2,1)S(1)} %all_to_all.35.l_ref, bf16[8,128,512]{2,1,0:T(8,128)(2,1)S(1)} %all_to_all.36.m_ref, ...), custom_call_target="tpu_custom_call" | custom-call | tf_op jit(solution)/shard_map/gradient/pallas_call | solution.py:272
  126.8 23.7 %all_to_all.37 = bf16[16,24,512]{2,1,0:T(8,128)(2,1)S(1)} all-to-all(bf16[16,24,512]{2,1,0:T(8,128)(2,1)S(1)} %bitcast.31), channel_id=1, replica_groups=mesh['dp'=16,'chip'=8,'core'=2] {'dp'}, dimensions={0} | all-to-all | bytes 786432 | tf_op jit(solution)/shard_map/all_to_all | solution.py:471
  150.5 0.1 reduce_sum.25
  150.6 17.0 %all_to_all.38 = bf16[16,24,512]{2,1,0:T(8,128)(2,1)} all-to-all(bf16[16,24,512]{2,1,0:T(8,128)(2,1)S(1)} %broadcast_in_dim.8), channel_id=1, replica_groups=mesh['dp'=16,'chip'=8,'core'=2] {'dp'}, dimensions={0} | all-to-all | bytes 786432 | tf_op jit(solution)/shard_map/all_to_all | solution.py:471
  167.6 4.5 %moments.1 = (f32[384,128]{1,0:T(8,128)}, f32[320,128]{1,0:T(8,128)}, f32[320,128]{1,0:T(8,128)}) custom-call(s32[3]{0:T(128)} %copy-done.6, bf16[384,512]{1,0:T(8,128)(2,1)} %bitcast.34, f32[512,128]{1,0:T(8,128)} %q_ref.3), custom_call_target="tpu_custom_call" | custom-call | tf_op jit(solution)/shard_map/moments/pallas_call | solution.py:306
  172.1 2.5 %collective-permute-start.7 = (f32[320,128]{1,0:T(8,128)}, f32[320,128]{1,0:T(8,128)S(1)}, u32[]{:S(2)}, u32[]{:S(2)}) collective-permute-start(f32[320,128]{1,0:T(8,128)} %get-tuple-element.37), channel_id=1, source_target_pairs={{0,1},{1,0},{2,3},{3,2},{4,5},{5,4},{6,7},{7,6},{8,9},{9,8},{10,11... | collective-permute-start | bytes 491528 | tf_op jit(solution)/shard_map/ppermute | solution.py:457
  174.6 1.2 collective-permute-done.7.t_ref
  175.8 0.7 copy-done.14
  176.5 2.0 pack_moments.1
  178.5 3.6 %all-to-all-start.6 = ((bf16[8,448,128]{2,1,0:T(8,128)(2,1)}), bf16[8,448,128]{2,1,0:T(8,128)(2,1)S(1)}, u32[]{:S(2)}, u32[]{:S(2)}) async-start(bf16[8,448,128]{2,1,0:T(8,128)(2,1)} %pack_moments.1), calls=%async_computation.6 | async-start | bytes 1835008 | tf_op jit(solution)/shard_map/all_to_all | solution.py:471
  182.0 0.0 copy-done.2
  182.0 0.7 fusion
  182.8 5.6 %collective-permute-start.5 = (bf16[128,768]{1,0:T(8,128)(2,1)S(1)}, bf16[128,768]{1,0:T(8,128)(2,1)S(1)}, u32[]{:S(2)}, u32[]{:S(2)}) collective-permute-start(bf16[128,768]{1,0:T(8,128)(2,1)S(1)} %get-tuple-element.42), channel_id=1, source_target_pairs={{0,15},{1,14},{2,13},{3,12},{4,11},{5,10},{6,9},{7,8},{8,7},{9,6},... | collective-permute-start | bytes 589832 | tf_op jit(solution)/shard_map/ppermute | solution.py:468
  188.4 0.0 collective-permute-start.4
  188.4 0.7 collective-permute-start.3
  189.1 8.4 %all-to-all-done.6.x_ref = bf16[8,448,128]{2,1,0:T(8,128)(2,1)S(1)} async-done(((bf16[8,448,128]{2,1,0:T(8,128)(2,1)}), bf16[8,448,128]{2,1,0:T(8,128)(2,1)S(1)}, u32[]{:S(2)}, u32[]{:S(2)}) %all-to-all-start.6) | async-done | bytes 917536 | tf_op jit(solution)/shard_map/all_to_all | solution.py:471
  197.5 0.9 copy-done.9
  198.4 2.0 sum_moments.1.m_ref
  200.4 2.0 collective-permute-start.8
  202.4 0.6 collective-permute-done.5.refs_3_
  203.0 2.9 %collective-permute-done.4.refs_2_ = bf16[128,768]{1,0:T(8,128)(2,1)S(1)} collective-permute-done((bf16[128,768]{1,0:T(8,128)(2,1)S(1)}, bf16[128,768]{1,0:T(8,128)(2,1)S(1)}, u32[]{:S(2)}, u32[]{:S(2)}) %collective-permute-start.4) | collective-permute-done | bytes 196640 | tf_op jit(solution)/shard_map/ppermute | solution.py:468
  205.9 0.0 collective-permute-done.3.refs_1_
  205.9 0.0 copy-done.12
  205.9 0.7 copy-done.13
  206.6 2.2 unpack_queries.1
  208.8 0.7 pad_maximum_fusion.1
  209.5 0.0 collective-permute-done.8.t_ref
  209.5 7.0 %finish.1 = (f32[384,512]{1,0:T(8,128)}, f32[512,128]{1,0:T(8,128)}, f32[1,384,512]{2,1,0:T(8,128)}) custom-call(s32[3]{0:T(128)S(1)} %copy-done.7, f32[384,128]{1,0:T(8,128)S(1)} %copy-done.5, f32[320,128]{1,0:T(8,128)S(1)} %copy-done.4, f32[320,128]{1,0:T(8,128)S(1)} %collective-permute-done.8.t_ref, f32[384,512]{1,0:T(8,128)S(1)} %get-tuple-element.38.c_ref), custom_call_target="tpu_custom_call" | custom-call | tf_op jit(solution)/shard_map/finish/pallas_call | solution.py:424
  (25 shorter events, 0.1 us)
Async XLA Ops:
  2.8 17.6 %copy-start.10 = (bf16[128,6144]{1,0:T(8,128)(2,1)S(1)}, bf16[128,6144]{1,0:T(8,128)(2,1)}, u32[]{:S(2)}) copy-start(bf16[128,6144]{1,0:T(8,128)(2,1)} %param.12) | copy-start | bytes 4718596
  2.8 27.2 %all-to-all-start = ((bf16[16,144,256]{2,1,0:T(8,128)(2,1)}), bf16[16,144,256]{2,1,0:T(8,128)(2,1)S(1)}, u32[]{:S(2)}, u32[]{:S(2)}) async-start(bf16[16,144,256]{2,1,0:T(8,128)(2,1)} %pack_keys.1), calls=%async_computation | async-start | bytes 2359296 | tf_op jit(solution)/shard_map/all_to_all | solution.py:471
  14.6 20.2 %collective-permute-start = (bf16[128,1536]{1,0:T(8,128)(2,1)}, bf16[128,1536]{1,0:T(8,128)(2,1)}, u32[]{:S(2)}, u32[]{:S(2)}) collective-permute-start(bf16[128,1536]{1,0:T(8,128)(2,1)} %get-tuple-element.25), channel_id=1, source_target_pairs={{0,1},{1,0},{2,3},{3,2},{4,5},{5,4},{6,7},{7,6},{8,9},{9,8},{10,11... | collective-permute-start | bytes 1179656 | tf_op jit(solution)/shard_map/ppermute | solution.py:468
  14.7 23.8 %collective-permute-start.1 = (bf16[128,1536]{1,0:T(8,128)(2,1)}, bf16[128,1536]{1,0:T(8,128)(2,1)}, u32[]{:S(2)}, u32[]{:S(2)}) collective-permute-start(bf16[128,1536]{1,0:T(8,128)(2,1)} %get-tuple-element.26), channel_id=1, source_target_pairs={{0,14},{1,15},{2,12},{3,13},{4,10},{5,11},{6,8},{7,9},{8,6},{9,7},... | collective-permute-start | bytes 1179656 | tf_op jit(solution)/shard_map/ppermute | solution.py:468
  20.0 29.5 %collective-permute-start.2 = (bf16[128,1536]{1,0:T(8,128)(2,1)}, bf16[128,1536]{1,0:T(8,128)(2,1)}, u32[]{:S(2)}, u32[]{:S(2)}) collective-permute-start(bf16[128,1536]{1,0:T(8,128)(2,1)} %get-tuple-element.27), channel_id=1, source_target_pairs={{0,15},{1,14},{2,13},{3,12},{4,11},{5,10},{6,9},{7,8},{8,7},{9,6},... | collective-permute-start | bytes 1179656 | tf_op jit(solution)/shard_map/ppermute | solution.py:468
  23.9 25.6 %copy-start.8 = (bf16[128,1536]{1,0:T(8,128)(2,1)S(1)}, bf16[128,1536]{1,0:T(8,128)(2,1)}, u32[]{:S(2)}) copy-start(bf16[128,1536]{1,0:T(8,128)(2,1)} %get-tuple-element.24.q0.g0) | copy-start | bytes 1179652
  25.3 99.2 %copy-start.6 = (s32[3]{0:T(128)}, s32[3]{0:T(128)S(1)}, u32[]{:S(2)}) copy-start(s32[3]{0:T(128)S(1)} %pad_add_fusion.1.at) | copy-start | bytes 40
  30.0 32.7 %all-to-all-start.1 = ((bf16[16,160,128]{2,1,0:T(8,128)(2,1)}), bf16[16,160,128]{2,1,0:T(8,128)(2,1)S(1)}, u32[]{:S(2)}, u32[]{:S(2)}) async-start(bf16[16,160,128]{2,1,0:T(8,128)(2,1)} %slice.104), calls=%async_computation.1 | async-start | bytes 1310720 | tf_op jit(solution)/shard_map/all_to_all | solution.py:471
  60.6 1.3 copy-start
  61.9 0.9 copy-start.1
  101.0 19.3 %copy-start.11 = (bf16[128,512]{1,0:T(8,128)(2,1)}, bf16[128,512]{1,0:T(8,128)(2,1)S(1)}, u32[]{:S(2)}) copy-start(bf16[128,512]{1,0:T(8,128)(2,1)S(1)} %pad_maximum_fusion) | copy-start | bytes 393220
  101.0 23.4 %copy-start.3 = (f32[1,384,512]{2,1,0:T(8,128)S(1)}, f32[1,384,512]{2,1,0:T(8,128)}, u32[]{:S(2)}) copy-start(f32[1,384,512]{2,1,0:T(8,128)} %param.14) | copy-start | bytes 2359300
  120.3 4.2 %collective-permute-start.6 = (bf16[8,128,512]{2,1,0:T(8,128)(2,1)S(1)}, bf16[8,128,512]{2,1,0:T(8,128)(2,1)S(1)}, u32[]{:S(2)}, u32[]{:S(2)}) collective-permute-start(bf16[8,128,512]{2,1,0:T(8,128)(2,1)S(1)} %all_to_all.36.m_ref), channel_id=1, source_target_pairs={{0,1},{1,0},{2,3},{3,2},{4,5},{5,4},{6,7},{7,6},{8,9},{9,8},{10,11... | collective-permute-start | bytes 3145736 | tf_op jit(solution)/shard_map/ppermute | solution.py:457
  172.1 9.9 %copy-start.2 = (bf16[512,768]{1,0:T(8,128)(2,1)S(1)}, bf16[512,768]{1,0:T(8,128)(2,1)}, u32[]{:S(2)}) copy-start(bf16[512,768]{1,0:T(8,128)(2,1)} %copy-done.1) | copy-start | bytes 2359300
  172.1 3.7 %collective-permute-start.7 = (f32[320,128]{1,0:T(8,128)}, f32[320,128]{1,0:T(8,128)S(1)}, u32[]{:S(2)}, u32[]{:S(2)}) collective-permute-start(f32[320,128]{1,0:T(8,128)} %get-tuple-element.37), channel_id=1, source_target_pairs={{0,1},{1,0},{2,3},{3,2},{4,5},{5,4},{6,7},{7,6},{8,9},{9,8},{10,11... | collective-permute-start | bytes 491528 | tf_op jit(solution)/shard_map/ppermute | solution.py:457
  175.8 0.7 copy-start.14
  178.5 19.1 %all-to-all-start.6 = ((bf16[8,448,128]{2,1,0:T(8,128)(2,1)}), bf16[8,448,128]{2,1,0:T(8,128)(2,1)S(1)}, u32[]{:S(2)}, u32[]{:S(2)}) async-start(bf16[8,448,128]{2,1,0:T(8,128)(2,1)} %pack_moments.1), calls=%async_computation.6 | async-start | bytes 1835008 | tf_op jit(solution)/shard_map/all_to_all | solution.py:471
  182.8 26.0 %copy-start.15 = (bf16[128,128]{1,0:T(8,128)(2,1)S(1)}, bf16[128,128]{1,0:T(8,128)(2,1)}, u32[]{:S(2)}) copy-start(bf16[128,128]{1,0:T(8,128)(2,1)} %get-tuple-element.46) | copy-start | bytes 98308
  182.8 26.0 %copy-start.16 = (bf16[128,128]{1,0:T(8,128)(2,1)S(1)}, bf16[128,128]{1,0:T(8,128)(2,1)}, u32[]{:S(2)}) copy-start(bf16[128,128]{1,0:T(8,128)(2,1)} %get-tuple-element.47) | copy-start | bytes 98308
  182.8 26.0 %copy-start.17 = (bf16[128,128]{1,0:T(8,128)(2,1)S(1)}, bf16[128,128]{1,0:T(8,128)(2,1)}, u32[]{:S(2)}) copy-start(bf16[128,128]{1,0:T(8,128)(2,1)} %get-tuple-element.48) | copy-start | bytes 98308
  182.8 26.0 %copy-start.18 = (bf16[128,128]{1,0:T(8,128)(2,1)S(1)}, bf16[128,128]{1,0:T(8,128)(2,1)}, u32[]{:S(2)}) copy-start(bf16[128,128]{1,0:T(8,128)(2,1)} %get-tuple-element.49) | copy-start | bytes 98308
  182.8 26.7 %copy-start.5 = (f32[384,128]{1,0:T(8,128)S(1)}, f32[384,128]{1,0:T(8,128)}, u32[]{:S(2)}) copy-start(f32[384,128]{1,0:T(8,128)} %get-tuple-element.35.p_ref) | copy-start | bytes 589828
  182.8 26.7 %copy-start.7 = (s32[3]{0:T(128)S(1)}, s32[3]{0:T(128)}, u32[]{:S(2)}) copy-start(s32[3]{0:T(128)} %copy-done.6) | copy-start | bytes 40
  182.8 20.2 %collective-permute-start.5 = (bf16[128,768]{1,0:T(8,128)(2,1)S(1)}, bf16[128,768]{1,0:T(8,128)(2,1)S(1)}, u32[]{:S(2)}, u32[]{:S(2)}) collective-permute-start(bf16[128,768]{1,0:T(8,128)(2,1)S(1)} %get-tuple-element.42), channel_id=1, source_target_pairs={{0,15},{1,14},{2,13},{3,12},{4,11},{5,10},{6,9},{7,8},{8,7},{9,6},... | collective-permute-start | bytes 589832 | tf_op jit(solution)/shard_map/ppermute | solution.py:468
  188.4 17.5 %collective-permute-start.4 = (bf16[128,768]{1,0:T(8,128)(2,1)S(1)}, bf16[128,768]{1,0:T(8,128)(2,1)S(1)}, u32[]{:S(2)}, u32[]{:S(2)}) collective-permute-start(bf16[128,768]{1,0:T(8,128)(2,1)S(1)} %get-tuple-element.43), channel_id=1, source_target_pairs={{0,14},{1,15},{2,12},{3,13},{4,10},{5,11},{6,8},{7,9},{8,6},{9,7},... | collective-permute-start | bytes 589832 | tf_op jit(solution)/shard_map/ppermute | solution.py:468
  188.4 17.5 %collective-permute-start.3 = (bf16[128,768]{1,0:T(8,128)(2,1)S(1)}, bf16[128,768]{1,0:T(8,128)(2,1)}, u32[]{:S(2)}, u32[]{:S(2)}) collective-permute-start(bf16[128,768]{1,0:T(8,128)(2,1)S(1)} %get-tuple-element.44), channel_id=1, source_target_pairs={{0,1},{1,0},{2,3},{3,2},{4,5},{5,4},{6,7},{7,6},{8,9},{9,8},{10,11... | collective-permute-start | bytes 589832 | tf_op jit(solution)/shard_map/ppermute | solution.py:468
  197.5 0.9 copy-start.9
  200.4 9.1 %copy-start.4 = (f32[320,128]{1,0:T(8,128)S(1)}, f32[320,128]{1,0:T(8,128)}, u32[]{:S(2)}) copy-start(f32[320,128]{1,0:T(8,128)} %sum_moments.1.m_ref) | copy-start | bytes 491524
  200.4 9.1 %collective-permute-start.8 = (f32[320,128]{1,0:T(8,128)}, f32[320,128]{1,0:T(8,128)S(1)}, u32[]{:S(2)}, u32[]{:S(2)}) collective-permute-start(f32[320,128]{1,0:T(8,128)} %sum_moments.1.m_ref), channel_id=1, source_target_pairs={{0,1},{1,0},{2,3},{3,2},{4,5},{5,4},{6,7},{7,6},{8,9},{9,8},{10,11... | collective-permute-start | bytes 491528 | tf_op jit(solution)/shard_map/ppermute | solution.py:457
  203.0 2.9 %copy-start.12 = (bf16[128,768]{1,0:T(8,128)(2,1)}, bf16[128,768]{1,0:T(8,128)(2,1)S(1)}, u32[]{:S(2)}) copy-start(bf16[128,768]{1,0:T(8,128)(2,1)S(1)} %collective-permute-done.5.refs_3_) | copy-start | bytes 589828
  205.9 0.7 copy-start.13

commit v6 on v4

--- a/solution.py
+++ b/solution.py
@@ -171,7 +171,7 @@
             jax.ShapeDtypeStruct((length, 2 * HEAD), jnp.bfloat16),
         ],
         compiler_params=pltpu.CompilerParams(
-            dimension_semantics=("arbitrary",), vmem_limit_bytes=40 * 1024 * 1024
+            dimension_semantics=("arbitrary",), vmem_limit_bytes=58 * 1024 * 1024
         ),
         cost_estimate=pl.CostEstimate(
             flops=8 * flops, bytes_accessed=8 * 1024 * 1024, transcendentals=0
@@ -274,22 +274,26 @@
     )(where, turned, mine, theirs, error)
 
 
-def inverse_factor(parts):
-    count, size, _ = parts.shape
+def finish(where, p_sum, mine, theirs, combined, replicas):
+    rows, width = combined.shape
+    size = p_sum.shape[1]
+    half, part = width // 2, size // 2
     tiles = size // 8
     shape = (8, size)
 
-    def kernel(g_ref, out_ref):
+    def kernel(at, p_ref, m_ref, t_ref, c_ref, comp_ref, q_ref, new_ref, gram_ref, inv_ref, all_ref):
+        core = at[0]
+        for x, who in ((m_ref, core), (t_ref, 1 - core)):
+            all_ref[pl.ds(pl.multiple_of(who * half, half), half), :] = x[:half, :]
+            gram_ref[pl.ds(pl.multiple_of(who * part, part), part), :] = (
+                x[half : half + part, :]
+                + x[half + part : half + 2 * part, :]
+                + x[half + 2 * part :, :]
+            )
         lane = lax.broadcasted_iota(jnp.int32, shape, 1)
         sub = lax.broadcasted_iota(jnp.int32, shape, 0)
-        left, right = [], []
-        for t in range(tiles):
-            total = g_ref[0, 8 * t : 8 * t + 8, :]
-            for n in range(1, count):
-                total = total + g_ref[n, 8 * t : 8 * t + 8, :]
-            left.append(total)
-            right.append(jnp.where(lane == sub + 8 * t, 1.0, 0.0))
-
+        left = [gram_ref[8 * t : 8 * t + 8, :] for t in range(tiles)]
+        right = [jnp.where(lane == sub + 8 * t, 1.0, 0.0) for t in range(tiles)]
         def row(x, r):
             return jnp.broadcast_to(x[r : r + 1, :], shape)
 
@@ -306,7 +310,7 @@
                 root = lax.rsqrt(row(pivot, k))
                 row_l = row(left[p], k) * root
                 row_r = row(right[p], k) * root
-                out_ref[8 * p + k : 8 * p + k + 1, :] = row_r[0:1]
+                inv_ref[8 * p + k : 8 * p + k + 1, :] = row_r[0:1]
                 factors = [row(pivot, m) * root for m in range(k + 1, 8)]
                 for t in range(p, tiles):
                     x = spread[t - p][k] * root
@@ -315,28 +319,15 @@
                     left[t] = left[t] - x * row_l
                     right[t] = right[t] - x * row_r
 
-    return pl.pallas_call(
-        kernel,
-        out_shape=jax.ShapeDtypeStruct((size, size), jnp.float32),
-        in_specs=[VMEM],
-        out_specs=VMEM,
-        cost_estimate=pl.CostEstimate(
-            flops=8 * 10**9, bytes_accessed=10**6, transcendentals=0
-        ),
-        name="inverse_factor",
-    )(parts)
-
-
-def finish(p_sum, inverse, q_factor, combined):
-    rows, width = combined.shape
-
-    def kernel(p_ref, i_ref, q_ref, c_ref, comp_ref, new_ref):
         def product(x, y):
             return lax.dot_general(
                 x, y, NT, precision=HIGHEST, preferred_element_type=jnp.float32
             )
 
-        out = product(product(p_ref[...], i_ref[...]), q_ref[...])
+        inv = inv_ref[...]
+        q = product(all_ref[...], inv) * (1.0 / replicas)
+        q_ref[...] = q
+        out = product(product(p_ref[...], inv), q)
         comp_ref[...] = out
         new_ref[0] = c_ref[...] - out
 
@@ -344,13 +335,19 @@
         kernel,
         out_shape=[
             jax.ShapeDtypeStruct((rows, width), jnp.float32),
+            jax.ShapeDtypeStruct((width, size), jnp.float32),
             jax.ShapeDtypeStruct((1, rows, width), jnp.float32),
         ],
-        in_specs=[VMEM] * 4,
-        out_specs=[VMEM] * 2,
+        in_specs=[SMEM] + [VMEM] * 4,
+        out_specs=[VMEM] * 3,
+        scratch_shapes=[
+            pltpu.VMEM((size, size), jnp.float32),
+            pltpu.VMEM((size, size), jnp.float32),
+            pltpu.VMEM((width, size), jnp.float32),
+        ],
         compiler_params=pltpu.CompilerParams(vmem_limit_bytes=32 * 1024 * 1024),
         name="finish",
-    )(p_sum, inverse, q_factor, combined)
+    )(where, p_sum, mine, theirs, combined)
 
 
 def body(queries, keys, values, d_out, features, doc_start, error, q_init):
@@ -426,19 +423,20 @@
     total = total.astype(f32)
     p_sum = jnp.dot(total, q_init, precision=HIGHEST)
     gram = lax.dot_general(p_sum, p_sum, TN, precision=HIGHEST)
-    gram = spread(gram + swap(gram), "chip", chips)
     moment = lax.dot_general(total, p_sum, TN, precision=HIGHEST)
-    size = width_kv // 2
-    moment = piece(moment, size, core, 0) + swap(piece(moment, size, 1 - core, 0))
-    moment, gram = lax.optimization_barrier((moment.astype(bf16), gram))
-    moment = jnp.sum(spread(moment, "chip", chips).astype(f32), axis=0)
-    inverse = inverse_factor(gram)
-    q_mine = lax.dot_general(moment, inverse, NT, precision=HIGHEST) / replicas
-    q_theirs = swap(q_mine)
-    q_factor = jnp.where(
-        core == 0, jnp.concatenate([q_mine, q_theirs]), jnp.concatenate([q_theirs, q_mine])
-    )
-    compressed, new_error = finish(p_sum, inverse, q_factor, combined)
+    half, part = width_kv // 2, q_init.shape[1] // 2
+
+    def share_of(who):
+        return jnp.concatenate([piece(moment, half, who, 0), piece(gram, part, who, 0)], axis=0)
+
+    sums = share_of(core) + swap(share_of(1 - core))
+    gram = sums[half:]
+    high = lax.reduce_precision(gram, 8, 7)
+    mid = lax.reduce_precision(gram - high, 8, 7)
+    low = gram - high - mid
+    sums = jnp.concatenate([sums[:half], high, mid, low], axis=0).astype(bf16)
+    sums = jnp.sum(spread(sums, "chip", chips).astype(f32), axis=0)
+    compressed, q_factor, new_error = finish(where, p_sum, sums, swap(sums), combined, replicas)
     return (d_query, d_key, d_value, compressed, q_factor, new_error)
 
 

time: 204 us -> 204 us (level)
  waiting for transfers between devices: 50.6 us -> 55.8 us
  starting transfers between devices: 45.8 us -> 41.1 us
  local copies, waits for them, and re-layouts: 9.5 us -> 5.93 us
  Pallas kernels: 26.7 us -> 29.4 us
    ppermute x6, waiting for transfers between devices: 16.2 us -> 22.9 us  [move(): return lax.ppermute(x, ctx, pairs)]
    pallas_call x1 -> x0, Pallas kernels: 5.55 us -> none  [inverse_factor(): pl.pallas_call(kernel, out_shape=jax.ShapeDtypeStruct((size, size), jnp.f...]
    pallas_call x1, Pallas kernels: 2.36 us -> 7.01 us  [finish(): pl.pallas_call(kernel, out_shape=[jax.ShapeDtypeStruct((rows, width), jnp...]
    pallas_call x1, Pallas kernels: 9.51 us -> 13.1 us  [attention(): pl.pallas_call(kernel, grid_spec=pltpu.PrefetchScalarGridSpec(num_scalar_...]
    all_to_all x5 -> x4, starting transfers between devices: 26.7 us -> 23.1 us  [exchange(): return lax.all_to_all(x, axis, 0, 0)]
    all_to_all x5 -> x4, waiting for transfers between devices: 31.9 us -> 29.6 us  [exchange(): return lax.all_to_all(x, axis, 0, 0)]
    ppermute x4 -> x3, starting transfers between devices: 7.6 us -> 6.45 us  [swap(): return lax.ppermute(x, 'core', [(0, 1), (1, 0)])]
  transfers between devices with their start and end apart: 15 -> 13, of which waited for: 9 -> 10; matrix products, arithmetic and copies ran while one was open for 4% -> 2% of each run, Pallas kernels for 10% -> 9%
where the time goes in v6:
time: 204 us
  blocking collectives  65.4 us (32%)
  waiting for transfers between devices  55.8 us (27%)
  starting transfers between devices  41.1 us (20%)
  Pallas kernels  29.4 us (14%)
  local copies, waits for them, and re-layouts  5.93 us (3%)
  other arithmetic  3.62 us (2%)
    all_to_all x3, blocking collectives, exchange(): return lax.all_to_all(x, axis, 0, 0)  65.4 us
    all_to_all x4, waiting for transfers between devices, exchange(): return lax.all_to_all(x, axis, 0, 0)  29.6 us
    all_to_all x4, starting transfers between devices, exchange(): return lax.all_to_all(x, axis, 0, 0)  23.1 us
    ppermute x6, waiting for transfers between devices, move(): return lax.ppermute(x, ctx, pairs)  22.9 us
    pallas_call x1, Pallas kernels, attention(): pl.pallas_call(kernel, grid_spec=pltpu.PrefetchScalarGridSpec(num_scalar_...  13.1 us
    ppermute x6, starting transfers between devices, move(): return lax.ppermute(x, ctx, pairs)  11.5 us
    pallas_call x1, Pallas kernels, finish(): pl.pallas_call(kernel, out_shape=[jax.ShapeDtypeStruct((rows, width), jnp...  7.01 us
    ppermute x3, starting transfers between devices, swap(): return lax.ppermute(x, 'core', [(0, 1), (1, 0)])  6.45 us
  transfers between devices with their start and end apart: 13, of which 10 were waited for; matrix products, arithmetic and copies ran while one was open for 2% of the time, Pallas kernels for 9%

profile of v6, /device:TPU:1, one launch (start us, length us, event | category | flops | bytes accessed | tf_op | source)
XLA Modules:
  0.0 203.7 jit_solution(4204083602437065563)
XLA Ops:
  0.6 0.0 copy-start
  0.6 2.2 %pack_keys.1 = bf16[16,144,256]{2,1,0:T(8,128)(2,1)} custom-call(bf16[128,512]{1,0:T(8,128)(2,1)} %k_ref.1, bf16[128,512]{1,0:T(8,128)(2,1)} %v_ref.1, s32[1,128]{1,0:T(1,128)} %bitcast.36), custom_call_target="tpu_custom_call" | custom-call | tf_op jit(solution)/shard_map/pack_keys/pallas_call | solution.py:203
  2.8 8.6 %all-to-all-start = ((bf16[16,144,256]{2,1,0:T(8,128)(2,1)}), bf16[16,144,256]{2,1,0:T(8,128)(2,1)}, u32[]{:S(2)}, u32[]{:S(2)}) async-start(bf16[16,144,256]{2,1,0:T(8,128)(2,1)} %pack_keys.1), calls=%async_computation | async-start | bytes 2359296 | tf_op jit(solution)/shard_map/all_to_all | solution.py:381
  11.4 0.6 pad_add_fusion.h_ref
  12.0 2.6 %pack_queries.1 = (bf16[128,1536]{1,0:T(8,128)(2,1)}, bf16[128,1536]{1,0:T(8,128)(2,1)}, bf16[128,1536]{1,0:T(8,128)(2,1)}, bf16[128,1536]{1,0:T(8,128)(2,1)}) custom-call(s32[4]{0:T(128)} %pad_add_fusion.h_ref, bf16[128,3072]{1,0:T(8,128)(2,1)} %q_ref.1, bf16[128,3072]{1,0:T(8,128)(2,1)} %g_ref.1), custom_call_target="tpu_custom_call" | custom-call | tf_op jit(solution)/shard_map/pack_queries/pallas_call | solution.py:221
  14.7 0.2 collective-permute-start
  14.8 5.2 %collective-permute-start.1 = (bf16[128,1536]{1,0:T(8,128)(2,1)}, bf16[128,1536]{1,0:T(8,128)(2,1)S(1)}, u32[]{:S(2)}, u32[]{:S(2)}) collective-permute-start(bf16[128,1536]{1,0:T(8,128)(2,1)} %get-tuple-element.23), channel_id=1, source_target_pairs={{0,14},{1,15},{2,12},{3,13},{4,10},{5,11},{6,8},{7,9},{8,6},{9,7},... | collective-permute-start | bytes 1179656 | tf_op jit(solution)/shard_map/ppermute | solution.py:378
  20.0 0.4 collective-permute-start.2
  20.4 0.0 copy-done.3
  20.4 1.6 copy.15
  22.0 0.7 pad_add_fusion.1.at
  22.7 7.5 %all-to-all-done.k_ref.v_ref = bf16[16,144,256]{2,1,0:T(8,128)(2,1)} async-done(((bf16[16,144,256]{2,1,0:T(8,128)(2,1)}), bf16[16,144,256]{2,1,0:T(8,128)(2,1)}, u32[]{:S(2)}, u32[]{:S(2)}) %all-to-all-start) | async-done | bytes 1179680 | tf_op jit(solution)/shard_map/all_to_all | solution.py:381
  30.2 4.9 %all-to-all-start.1 = ((bf16[16,384,128]{2,1,0:T(8,128)(2,1)}), bf16[16,384,128]{2,1,0:T(8,128)(2,1)S(1)}, u32[]{:S(2)}, u32[]{:S(2)}) async-start(bf16[16,384,128]{2,1,0:T(8,128)(2,1)} %bitcast.9), calls=%async_computation.1 | async-start | bytes 3145728 | tf_op jit(solution)/shard_map/all_to_all | solution.py:381
  35.1 0.0 collective-permute-done.q1.g1
  35.1 0.0 copy-start.9
  35.1 3.4 %collective-permute-done.1.q2.g2 = bf16[128,1536]{1,0:T(8,128)(2,1)S(1)} collective-permute-done((bf16[128,1536]{1,0:T(8,128)(2,1)}, bf16[128,1536]{1,0:T(8,128)(2,1)S(1)}, u32[]{:S(2)}, u32[]{:S(2)}) %collective-permute-start.1) | collective-permute-done | bytes 393248 | tf_op jit(solution)/shard_map/ppermute | solution.py:378
  38.5 12.7 %collective-permute-done.2.q3.g3 = bf16[128,1536]{1,0:T(8,128)(2,1)S(1)} collective-permute-done((bf16[128,1536]{1,0:T(8,128)(2,1)}, bf16[128,1536]{1,0:T(8,128)(2,1)S(1)}, u32[]{:S(2)}, u32[]{:S(2)}) %collective-permute-start.2) | collective-permute-done | bytes 393248 | tf_op jit(solution)/shard_map/ppermute | solution.py:378
  51.2 0.0 copy-done.9
  51.2 0.0 copy-done.10
  51.3 0.7 copy-done.11
  52.0 13.1 %attention.1 = (bf16[512,768]{1,0:T(8,128)(2,1)}, bf16[2048,256]{1,0:T(8,128)(2,1)}) custom-call(s32[3]{0:T(128)} %pad_add_fusion.1.at, bf16[128,1536]{1,0:T(8,128)(2,1)} %get-tuple-element.21.q0.g0, bf16[128,1536]{1,0:T(8,128)(2,1)} %copy-done.9, bf16[128,1536]{1,0:T(8,128)(2,1)} %copy-done.10, bf16[128,1536]{1,0:T(8,128)(2,1)} %copy-done.11, ...), custom_call_target="tpu_custom_call" | custom-call | flops 32212254720 | bytes 8388608 | tf_op jit(solution)/shard_map/attention/pallas_call | solution.py:147
  65.1 2.2 %all-to-all-done.1.f_ref = bf16[16,384,128]{2,1,0:T(8,128)(2,1)S(1)} async-done(((bf16[16,384,128]{2,1,0:T(8,128)(2,1)}), bf16[16,384,128]{2,1,0:T(8,128)(2,1)S(1)}, u32[]{:S(2)}, u32[]{:S(2)}) %all-to-all-start.1) | async-done | bytes 1572896 | tf_op jit(solution)/shard_map/all_to_all | solution.py:381
  67.3 23.5 %all_to_all.35 = bf16[16,128,256]{2,1,0:T(8,128)(2,1)} all-to-all(bf16[16,128,256]{2,1,0:T(8,128)(2,1)} %bitcast.35), channel_id=1, replica_groups=mesh['dp'=16,'chip'=8,'core'=2] {'chip','core'}, dimensions={0} | all-to-all | bytes 2097152 | tf_op jit(solution)/shard_map/all_to_all | solution.py:381
  90.8 1.4 reduce_sum.33
  92.4 0.0 copy-start.5
  92.4 0.0 copy-start.1
  92.4 0.0 copy-start.2
  92.4 0.1 broadcast_in_dim.9
  92.5 19.2 %all_to_all.36.m_ref = bf16[8,128,512]{2,1,0:T(8,128)(2,1)S(1)} all-to-all(bf16[8,128,512]{2,1,0:T(8,128)(2,1)S(1)} %broadcast_in_dim.9), channel_id=1, replica_groups=mesh['dp'=16,'chip'=8,'core'=2] {'chip'}, dimensions={0} | all-to-all | bytes 2097152 | tf_op jit(solution)/shard_map/all_to_all | solution.py:381
  111.7 0.0 copy-done.5
  111.7 1.8 collective-permute-start.6
  113.5 2.3 %collective-permute-done.6.t_ref = bf16[8,128,512]{2,1,0:T(8,128)(2,1)S(1)} collective-permute-done((bf16[8,128,512]{2,1,0:T(8,128)(2,1)S(1)}, bf16[8,128,512]{2,1,0:T(8,128)(2,1)S(1)}, u32[]{:S(2)}, u32[]{:S(2)}) %collective-permute-start.6) | collective-permute-done | bytes 1048608 | tf_op jit(solution)/shard_map/ppermute | solution.py:367
  115.8 0.0 copy-done.1
  115.8 0.0 copy-done.2
  115.8 2.3 %gradient.1 = (f32[384,512]{1,0:T(8,128)S(1)}, bf16[384,512]{1,0:T(8,128)(2,1)S(1)}) custom-call(s32[3]{0:T(128)S(1)} %copy-done.2, bf16[16,384,128]{2,1,0:T(8,128)(2,1)S(1)} %all-to-all-done.1.f_ref, bf16[8,128,512]{2,1,0:T(8,128)(2,1)S(1)} %all_to_all.36.m_ref, bf16[8,128,512]{2,1,0:T(8,128)(2,1)S(1)} %collective-permute-done.6.t_ref, f32[384,512]{1,0:T(8,128)S(1)} %bitcast.29), custom_call_target="tpu_custom_call" | custom-call | tf_op jit(solution)/shard_map/gradient/pallas_call | solution.py:264
  118.1 22.6 %all_to_all.37 = bf16[16,24,512]{2,1,0:T(8,128)(2,1)S(1)} all-to-all(bf16[16,24,512]{2,1,0:T(8,128)(2,1)S(1)} %bitcast.30), channel_id=1, replica_groups=mesh['dp'=16,'chip'=8,'core'=2] {'dp'}, dimensions={0} | all-to-all | bytes 786432 | tf_op jit(solution)/shard_map/all_to_all | solution.py:381
  140.8 0.1 reduce_sum.34
  140.8 0.8 broadcast_in_dim.10
  141.6 6.1 %all-to-all-start.5 = ((bf16[16,24,512]{2,1,0:T(8,128)(2,1)}), bf16[16,24,512]{2,1,0:T(8,128)(2,1)S(1)}, u32[]{:S(2)}, u32[]{:S(2)}) async-start(bf16[16,24,512]{2,1,0:T(8,128)(2,1)} %broadcast_in_dim.10), calls=%async_computation.5 | async-start | bytes 786432 | tf_op jit(solution)/shard_map/all_to_all | solution.py:381
  147.7 11.1 %all-to-all-done.5 = bf16[16,24,512]{2,1,0:T(8,128)(2,1)S(1)} async-done(((bf16[16,24,512]{2,1,0:T(8,128)(2,1)}), bf16[16,24,512]{2,1,0:T(8,128)(2,1)S(1)}, u32[]{:S(2)}, u32[]{:S(2)}) %all-to-all-start.5) | async-done | bytes 393248 | tf_op jit(solution)/shard_map/all_to_all | solution.py:381
  158.7 0.0 copy-done
  158.8 0.5 fusion.6.p_ref
  159.3 0.6 fusion.7
  159.9 0.5 fusion.8
  160.4 2.5 %collective-permute-start.7 = (f32[320,128]{1,0:T(8,128)S(1)}, f32[320,128]{1,0:T(8,128)S(1)}, u32[]{:S(2)}, u32[]{:S(2)}) collective-permute-start(f32[320,128]{1,0:T(8,128)S(1)} %pad_maximum_fusion), channel_id=1, source_target_pairs={{0,1},{1,0},{2,3},{3,2},{4,5},{5,4},{6,7},{7,6},{8,9},{9,8},{10,11... | collective-permute-start | bytes 491528 | tf_op jit(solution)/shard_map/ppermute | solution.py:367
  163.0 1.0 collective-permute-done.7
  164.0 0.0 copy-start.4
  164.1 1.1 broadcast_in_dim.11
  165.1 3.6 %all-to-all-start.6 = ((bf16[8,448,128]{2,1,0:T(8,128)(2,1)}), bf16[8,448,128]{2,1,0:T(8,128)(2,1)S(1)}, u32[]{:S(2)}, u32[]{:S(2)}) async-start(bf16[8,448,128]{2,1,0:T(8,128)(2,1)} %broadcast_in_dim.11), calls=%async_computation.6 | async-start | bytes 1835008 | tf_op jit(solution)/shard_map/all_to_all | solution.py:381
  168.7 0.8 fusion.1
  169.5 0.4 collective-permute-start.3
  169.9 5.3 %collective-permute-start.4 = (bf16[128,768]{1,0:T(8,128)(2,1)}, bf16[128,768]{1,0:T(8,128)(2,1)S(1)}, u32[]{:S(2)}, u32[]{:S(2)}) collective-permute-start(bf16[128,768]{1,0:T(8,128)(2,1)} %get-tuple-element.37), channel_id=1, source_target_pairs={{0,14},{1,15},{2,12},{3,13},{4,10},{5,11},{6,8},{7,9},{8,6},{9,7},... | collective-permute-start | bytes 589832 | tf_op jit(solution)/shard_map/ppermute | solution.py:378
  175.2 0.1 collective-permute-start.5
  175.3 8.9 %all-to-all-done.6 = bf16[8,448,128]{2,1,0:T(8,128)(2,1)S(1)} async-done(((bf16[8,448,128]{2,1,0:T(8,128)(2,1)}), bf16[8,448,128]{2,1,0:T(8,128)(2,1)S(1)}, u32[]{:S(2)}, u32[]{:S(2)}) %all-to-all-start.6) | async-done | bytes 917536 | tf_op jit(solution)/shard_map/all_to_all | solution.py:381
  184.2 0.1 convert_reduce_fusion.m_ref
  184.3 2.1 %collective-permute-start.8 = (f32[448,128]{1,0:T(8,128)S(1)}, f32[448,128]{1,0:T(8,128)S(1)}, u32[]{:S(2)}, u32[]{:S(2)}) collective-permute-start(f32[448,128]{1,0:T(8,128)S(1)} %convert_reduce_fusion.m_ref), channel_id=1, source_target_pairs={{0,1},{1,0},{2,3},{3,2},{4,5},{5,4},{6,7},{7,6},{8,9},{9,8},{10,11... | collective-permute-start | bytes 688136 | tf_op jit(solution)/shard_map/ppermute | solution.py:367
  186.4 0.0 collective-permute-done.3.refs_1_
  186.4 2.0 collective-permute-done.4.refs_2_
  188.4 4.7 %collective-permute-done.5.refs_3_ = bf16[128,768]{1,0:T(8,128)(2,1)S(1)} collective-permute-done((bf16[128,768]{1,0:T(8,128)(2,1)S(1)}, bf16[128,768]{1,0:T(8,128)(2,1)S(1)}, u32[]{:S(2)}, u32[]{:S(2)}) %collective-permute-start.5) | collective-permute-done | bytes 196640 | tf_op jit(solution)/shard_map/ppermute | solution.py:378
  193.1 0.7 copy-done.8
  193.8 2.2 %unpack_queries.1 = bf16[128,3072]{1,0:T(8,128)(2,1)} custom-call(s32[4]{0:T(128)} %pad_add_fusion.h_ref, bf16[128,768]{1,0:T(8,128)(2,1)} %get-tuple-element.39.refs_0_, bf16[128,768]{1,0:T(8,128)(2,1)} %copy-done.6, bf16[128,768]{1,0:T(8,128)(2,1)} %copy-done.7, bf16[128,768]{1,0:T(8,128)(2,1)} %copy-done.8), custom_call_target="tpu_custom_call" | custom-call | tf_op jit(solution)/shard_map/unpack_queries/pallas_call | solution.py:238
  196.0 0.7 pad_maximum_fusion.2
  196.6 0.0 collective-permute-done.8.t_ref
  196.6 7.0 %finish.1 = (f32[384,512]{1,0:T(8,128)}, f32[512,128]{1,0:T(8,128)}, f32[1,384,512]{2,1,0:T(8,128)}) custom-call(s32[3]{0:T(128)S(1)} %copy-done.2, f32[384,128]{1,0:T(8,128)S(1)} %fusion.6.p_ref, f32[448,128]{1,0:T(8,128)S(1)} %convert_reduce_fusion.m_ref, f32[448,128]{1,0:T(8,128)S(1)} %collective-permute-done.8.t_ref, f32[384,512]{1,0:T(8,128)S(1)} %get-tuple-element.32.c_ref), custom_call_target="tpu_custom_call" | custom-call | tf_op jit(solution)/shard_map/finish/pallas_call | solution.py:334
  (20 shorter events, 0.2 us)
Async XLA Ops:
  0.6 158.1 %copy-start = (f32[512,128]{1,0:T(8,128)S(1)}, f32[512,128]{1,0:T(8,128)}, u32[]{:S(2)}) copy-start(f32[512,128]{1,0:T(8,128)} %param.15) | copy-start | bytes 786436
  2.8 17.6 %copy-start.3 = (bf16[128,6144]{1,0:T(8,128)(2,1)S(1)}, bf16[128,6144]{1,0:T(8,128)(2,1)}, u32[]{:S(2)}) copy-start(bf16[128,6144]{1,0:T(8,128)(2,1)} %param.12) | copy-start | bytes 4718596
  2.8 27.3 %all-to-all-start = ((bf16[16,144,256]{2,1,0:T(8,128)(2,1)}), bf16[16,144,256]{2,1,0:T(8,128)(2,1)}, u32[]{:S(2)}, u32[]{:S(2)}) async-start(bf16[16,144,256]{2,1,0:T(8,128)(2,1)} %pack_keys.1), calls=%async_computation | async-start | bytes 2359296 | tf_op jit(solution)/shard_map/all_to_all | solution.py:381
  14.7 20.4 %collective-permute-start = (bf16[128,1536]{1,0:T(8,128)(2,1)}, bf16[128,1536]{1,0:T(8,128)(2,1)S(1)}, u32[]{:S(2)}, u32[]{:S(2)}) collective-permute-start(bf16[128,1536]{1,0:T(8,128)(2,1)} %get-tuple-element.22), channel_id=1, source_target_pairs={{0,1},{1,0},{2,3},{3,2},{4,5},{5,4},{6,7},{7,6},{8,9},{9,8},{10,11... | collective-permute-start | bytes 1179656 | tf_op jit(solution)/shard_map/ppermute | solution.py:378
  14.8 23.7 %collective-permute-start.1 = (bf16[128,1536]{1,0:T(8,128)(2,1)}, bf16[128,1536]{1,0:T(8,128)(2,1)S(1)}, u32[]{:S(2)}, u32[]{:S(2)}) collective-permute-start(bf16[128,1536]{1,0:T(8,128)(2,1)} %get-tuple-element.23), channel_id=1, source_target_pairs={{0,14},{1,15},{2,12},{3,13},{4,10},{5,11},{6,8},{7,9},{8,6},{9,7},... | collective-permute-start | bytes 1179656 | tf_op jit(solution)/shard_map/ppermute | solution.py:378
  20.0 31.2 %collective-permute-start.2 = (bf16[128,1536]{1,0:T(8,128)(2,1)}, bf16[128,1536]{1,0:T(8,128)(2,1)S(1)}, u32[]{:S(2)}, u32[]{:S(2)}) collective-permute-start(bf16[128,1536]{1,0:T(8,128)(2,1)} %get-tuple-element.24), channel_id=1, source_target_pairs={{0,15},{1,14},{2,13},{3,12},{4,11},{5,10},{6,9},{7,8},{8,7},{9,6},... | collective-permute-start | bytes 1179656 | tf_op jit(solution)/shard_map/ppermute | solution.py:378
  30.2 37.1 %all-to-all-start.1 = ((bf16[16,384,128]{2,1,0:T(8,128)(2,1)}), bf16[16,384,128]{2,1,0:T(8,128)(2,1)S(1)}, u32[]{:S(2)}, u32[]{:S(2)}) async-start(bf16[16,384,128]{2,1,0:T(8,128)(2,1)} %bitcast.9), calls=%async_computation.1 | async-start | bytes 3145728 | tf_op jit(solution)/shard_map/all_to_all | solution.py:381
  35.1 16.2 %copy-start.9 = (bf16[128,1536]{1,0:T(8,128)(2,1)}, bf16[128,1536]{1,0:T(8,128)(2,1)S(1)}, u32[]{:S(2)}) copy-start(bf16[128,1536]{1,0:T(8,128)(2,1)S(1)} %collective-permute-done.q1.g1) | copy-start | bytes 1179652
  38.5 12.8 %copy-start.10 = (bf16[128,1536]{1,0:T(8,128)(2,1)}, bf16[128,1536]{1,0:T(8,128)(2,1)S(1)}, u32[]{:S(2)}) copy-start(bf16[128,1536]{1,0:T(8,128)(2,1)S(1)} %collective-permute-done.1.q2.g2) | copy-start | bytes 1179652
  51.2 0.7 copy-start.11
  92.4 19.3 %copy-start.5 = (bf16[128,512]{1,0:T(8,128)(2,1)}, bf16[128,512]{1,0:T(8,128)(2,1)S(1)}, u32[]{:S(2)}) copy-start(bf16[128,512]{1,0:T(8,128)(2,1)S(1)} %pad_maximum_fusion.1) | copy-start | bytes 393220
  92.4 23.4 %copy-start.1 = (f32[1,384,512]{2,1,0:T(8,128)S(1)}, f32[1,384,512]{2,1,0:T(8,128)}, u32[]{:S(2)}) copy-start(f32[1,384,512]{2,1,0:T(8,128)} %param.14) | copy-start | bytes 2359300
  92.4 23.4 %copy-start.2 = (s32[3]{0:T(128)S(1)}, s32[3]{0:T(128)}, u32[]{:S(2)}) copy-start(s32[3]{0:T(128)} %pad_add_fusion.1.at) | copy-start | bytes 40
  111.7 4.1 %collective-permute-start.6 = (bf16[8,128,512]{2,1,0:T(8,128)(2,1)S(1)}, bf16[8,128,512]{2,1,0:T(8,128)(2,1)S(1)}, u32[]{:S(2)}, u32[]{:S(2)}) collective-permute-start(bf16[8,128,512]{2,1,0:T(8,128)(2,1)S(1)} %all_to_all.36.m_ref), channel_id=1, source_target_pairs={{0,1},{1,0},{2,3},{3,2},{4,5},{5,4},{6,7},{7,6},{8,9},{9,8},{10,11... | collective-permute-start | bytes 3145736 | tf_op jit(solution)/shard_map/ppermute | solution.py:367
  141.6 17.1 %all-to-all-start.5 = ((bf16[16,24,512]{2,1,0:T(8,128)(2,1)}), bf16[16,24,512]{2,1,0:T(8,128)(2,1)S(1)}, u32[]{:S(2)}, u32[]{:S(2)}) async-start(bf16[16,24,512]{2,1,0:T(8,128)(2,1)} %broadcast_in_dim.10), calls=%async_computation.5 | async-start | bytes 786432 | tf_op jit(solution)/shard_map/all_to_all | solution.py:381
  160.4 3.6 %collective-permute-start.7 = (f32[320,128]{1,0:T(8,128)S(1)}, f32[320,128]{1,0:T(8,128)S(1)}, u32[]{:S(2)}, u32[]{:S(2)}) collective-permute-start(f32[320,128]{1,0:T(8,128)S(1)} %pad_maximum_fusion), channel_id=1, source_target_pairs={{0,1},{1,0},{2,3},{3,2},{4,5},{5,4},{6,7},{7,6},{8,9},{9,8},{10,11... | collective-permute-start | bytes 491528 | tf_op jit(solution)/shard_map/ppermute | solution.py:367
  164.0 4.7 %copy-start.4 = (bf16[512,768]{1,0:T(8,128)(2,1)S(1)}, bf16[512,768]{1,0:T(8,128)(2,1)}, u32[]{:S(2)}) copy-start(bf16[512,768]{1,0:T(8,128)(2,1)} %get-tuple-element.26) | copy-start | bytes 2359300
  165.1 19.1 %all-to-all-start.6 = ((bf16[8,448,128]{2,1,0:T(8,128)(2,1)}), bf16[8,448,128]{2,1,0:T(8,128)(2,1)S(1)}, u32[]{:S(2)}, u32[]{:S(2)}) async-start(bf16[8,448,128]{2,1,0:T(8,128)(2,1)} %broadcast_in_dim.11), calls=%async_computation.6 | async-start | bytes 1835008 | tf_op jit(solution)/shard_map/all_to_all | solution.py:381
  169.5 16.9 %collective-permute-start.3 = (bf16[128,768]{1,0:T(8,128)(2,1)}, bf16[128,768]{1,0:T(8,128)(2,1)S(1)}, u32[]{:S(2)}, u32[]{:S(2)}) collective-permute-start(bf16[128,768]{1,0:T(8,128)(2,1)} %get-tuple-element.38), channel_id=1, source_target_pairs={{0,1},{1,0},{2,3},{3,2},{4,5},{5,4},{6,7},{7,6},{8,9},{9,8},{10,11... | collective-permute-start | bytes 589832 | tf_op jit(solution)/shard_map/ppermute | solution.py:378
  169.9 18.5 %collective-permute-start.4 = (bf16[128,768]{1,0:T(8,128)(2,1)}, bf16[128,768]{1,0:T(8,128)(2,1)S(1)}, u32[]{:S(2)}, u32[]{:S(2)}) collective-permute-start(bf16[128,768]{1,0:T(8,128)(2,1)} %get-tuple-element.37), channel_id=1, source_target_pairs={{0,14},{1,15},{2,12},{3,13},{4,10},{5,11},{6,8},{7,9},{8,6},{9,7},... | collective-permute-start | bytes 589832 | tf_op jit(solution)/shard_map/ppermute | solution.py:378
  175.2 17.9 %collective-permute-start.5 = (bf16[128,768]{1,0:T(8,128)(2,1)S(1)}, bf16[128,768]{1,0:T(8,128)(2,1)S(1)}, u32[]{:S(2)}, u32[]{:S(2)}) collective-permute-start(bf16[128,768]{1,0:T(8,128)(2,1)S(1)} %get-tuple-element.36), channel_id=1, source_target_pairs={{0,15},{1,14},{2,13},{3,12},{4,11},{5,10},{6,9},{7,8},{8,7},{9,6},... | collective-permute-start | bytes 589832 | tf_op jit(solution)/shard_map/ppermute | solution.py:378
  184.3 12.3 %collective-permute-start.8 = (f32[448,128]{1,0:T(8,128)S(1)}, f32[448,128]{1,0:T(8,128)S(1)}, u32[]{:S(2)}, u32[]{:S(2)}) collective-permute-start(f32[448,128]{1,0:T(8,128)S(1)} %convert_reduce_fusion.m_ref), channel_id=1, source_target_pairs={{0,1},{1,0},{2,3},{3,2},{4,5},{5,4},{6,7},{7,6},{8,9},{9,8},{10,11... | collective-permute-start | bytes 688136 | tf_op jit(solution)/shard_map/ppermute | solution.py:367
  186.4 6.7 %copy-start.6 = (bf16[128,768]{1,0:T(8,128)(2,1)}, bf16[128,768]{1,0:T(8,128)(2,1)S(1)}, u32[]{:S(2)}) copy-start(bf16[128,768]{1,0:T(8,128)(2,1)S(1)} %collective-permute-done.3.refs_1_) | copy-start | bytes 589828
  188.4 4.7 %copy-start.7 = (bf16[128,768]{1,0:T(8,128)(2,1)}, bf16[128,768]{1,0:T(8,128)(2,1)S(1)}, u32[]{:S(2)}) copy-start(bf16[128,768]{1,0:T(8,128)(2,1)S(1)} %collective-permute-done.4.refs_2_) | copy-start | bytes 589828
  193.1 0.7 copy-start.8

commit v7 on v6

--- a/solution.py
+++ b/solution.py
@@ -171,7 +171,7 @@
             jax.ShapeDtypeStruct((length, 2 * HEAD), jnp.bfloat16),
         ],
         compiler_params=pltpu.CompilerParams(
-            dimension_semantics=("arbitrary",), vmem_limit_bytes=58 * 1024 * 1024
+            dimension_semantics=("arbitrary",), vmem_limit_bytes=40 * 1024 * 1024
         ),
         cost_estimate=pl.CostEstimate(
             flops=8 * flops, bytes_accessed=8 * 1024 * 1024, transcendentals=0
@@ -415,11 +415,6 @@
     share = jnp.sum(shares.astype(f32), axis=0).astype(bf16)
     total = spread(share, "dp", replicas).reshape(rows, width_kv)
 
-    back = [dq[:tokens]] + [
-        move(dq[n * tokens : (n + 1) * tokens], *ways[n]) for n in range(1, 4)
-    ]
-    d_query = unpack_queries(heads, back, group)
-
     total = total.astype(f32)
     p_sum = jnp.dot(total, q_init, precision=HIGHEST)
     gram = lax.dot_general(p_sum, p_sum, TN, precision=HIGHEST)
@@ -437,6 +432,12 @@
     sums = jnp.concatenate([sums[:half], high, mid, low], axis=0).astype(bf16)
     sums = jnp.sum(spread(sums, "chip", chips).astype(f32), axis=0)
     compressed, q_factor, new_error = finish(where, p_sum, sums, swap(sums), combined, replicas)
+
+    back = [dq[:tokens]] + [
+        move(dq[n * tokens : (n + 1) * tokens], *ways[n]) for n in range(1, 4)
+    ]
+    compressed, *back = lax.optimization_barrier((compressed, *back))
+    d_query = unpack_queries(heads, back, group)
     return (d_query, d_key, d_value, compressed, q_factor, new_error)
 
 

time: 204 us -> 201 us (0.985)
  blocking collectives: 65.4 us -> 82.6 us
  waiting for transfers between devices: 55.8 us -> 44.2 us
  Pallas kernels: 29.4 us -> 25.8 us
  starting transfers between devices: 41.1 us -> 37.6 us
    all_to_all x3 -> x4, blocking collectives: 65.4 us -> 82.6 us  [exchange(): return lax.all_to_all(x, axis, 0, 0)]
    all_to_all x4 -> x3, waiting for transfers between devices: 29.6 us -> 23.6 us  [exchange(): return lax.all_to_all(x, axis, 0, 0)]
    ppermute x6, waiting for transfers between devices: 22.9 us -> 17.3 us  [move(): return lax.ppermute(x, ctx, pairs)]
    pallas_call x1, Pallas kernels: 13.1 us -> 9.49 us  [attention(): pl.pallas_call(kernel, grid_spec=pltpu.PrefetchScalarGridSpec(num_scalar_...]
    all_to_all x4 -> x3, starting transfers between devices: 23.1 us -> 19.7 us  [exchange(): return lax.all_to_all(x, axis, 0, 0)]
  transfers between devices with their start and end apart: 13 -> 12, of which waited for: 10 -> 8; matrix products, arithmetic and copies ran while one was open for 2% -> 2% of each run, Pallas kernels for 9% -> 10%
where the time goes in v7:
time: 201 us; the launch traced here: 200 us
  blocking collectives  82.6 us (41%)
  waiting for transfers between devices  44.2 us (22%)
  starting transfers between devices  37.6 us (19%)
  Pallas kernels  25.8 us (13%)
  local copies, waits for them, and re-layouts  6.02 us (3%)
    all_to_all x4, blocking collectives, exchange(): return lax.all_to_all(x, axis, 0, 0)  82.6 us
    all_to_all x3, waiting for transfers between devices, exchange(): return lax.all_to_all(x, axis, 0, 0)  23.6 us
    all_to_all x3, starting transfers between devices, exchange(): return lax.all_to_all(x, axis, 0, 0)  19.7 us
    ppermute x6, waiting for transfers between devices, move(): return lax.ppermute(x, ctx, pairs)  17.3 us
    ppermute x6, starting transfers between devices, move(): return lax.ppermute(x, ctx, pairs)  11.5 us
    pallas_call x1, Pallas kernels, attention(): pl.pallas_call(kernel, grid_spec=pltpu.PrefetchScalarGridSpec(num_scalar_...  9.49 us
    pallas_call x1, Pallas kernels, finish(): pl.pallas_call(kernel, out_shape=[jax.ShapeDtypeStruct((rows, width), jnp...  7.01 us
    ppermute x3, starting transfers between devices, swap(): return lax.ppermute(x, 'core', [(0, 1), (1, 0)])  6.38 us
  transfers between devices with their start and end apart: 12, of which 8 were waited for; matrix products, arithmetic and copies ran while one was open for 2% of the time, Pallas kernels for 10%

profile of v7, /device:TPU:1, one launch (start us, length us, event | category | flops | bytes accessed | tf_op | source)
XLA Modules:
  0.0 200.5 jit_solution(3396567826508698849)
XLA Ops:
  0.6 0.0 copy-start
  0.6 2.2 %pack_keys.1 = bf16[16,144,256]{2,1,0:T(8,128)(2,1)} custom-call(bf16[128,512]{1,0:T(8,128)(2,1)} %k_ref.1, bf16[128,512]{1,0:T(8,128)(2,1)} %v_ref.1, s32[1,128]{1,0:T(1,128)} %bitcast.37), custom_call_target="tpu_custom_call" | custom-call | tf_op jit(solution)/shard_map/pack_keys/pallas_call | solution.py:203
  2.8 8.6 %all-to-all-start = ((bf16[16,144,256]{2,1,0:T(8,128)(2,1)}), bf16[16,144,256]{2,1,0:T(8,128)(2,1)S(1)}, u32[]{:S(2)}, u32[]{:S(2)}) async-start(bf16[16,144,256]{2,1,0:T(8,128)(2,1)} %pack_keys.1), calls=%async_computation | async-start | bytes 2359296 | tf_op jit(solution)/shard_map/all_to_all | solution.py:381
  11.4 0.6 pad_add_fusion.h_ref
  12.0 2.6 %pack_queries.1 = (bf16[128,1536]{1,0:T(8,128)(2,1)}, bf16[128,1536]{1,0:T(8,128)(2,1)}, bf16[128,1536]{1,0:T(8,128)(2,1)}, bf16[128,1536]{1,0:T(8,128)(2,1)}) custom-call(s32[4]{0:T(128)} %pad_add_fusion.h_ref, bf16[128,3072]{1,0:T(8,128)(2,1)} %q_ref.1, bf16[128,3072]{1,0:T(8,128)(2,1)} %g_ref.1), custom_call_target="tpu_custom_call" | custom-call | tf_op jit(solution)/shard_map/pack_queries/pallas_call | solution.py:221
  14.6 0.1 collective-permute-start
  14.8 5.3 %collective-permute-start.1 = (bf16[128,1536]{1,0:T(8,128)(2,1)}, bf16[128,1536]{1,0:T(8,128)(2,1)}, u32[]{:S(2)}, u32[]{:S(2)}) collective-permute-start(bf16[128,1536]{1,0:T(8,128)(2,1)} %get-tuple-element.28), channel_id=1, source_target_pairs={{0,14},{1,15},{2,12},{3,13},{4,10},{5,11},{6,8},{7,9},{8,6},{9,7},... | collective-permute-start | bytes 1179656 | tf_op jit(solution)/shard_map/ppermute | solution.py:378
  20.0 0.4 collective-permute-start.2
  20.4 0.0 copy-done.6
  20.4 1.6 copy.15
  22.0 0.1 pad_add_fusion.1.at
  22.1 8.0 %all-to-all-done.k_ref.v_ref = bf16[16,144,256]{2,1,0:T(8,128)(2,1)S(1)} async-done(((bf16[16,144,256]{2,1,0:T(8,128)(2,1)}), bf16[16,144,256]{2,1,0:T(8,128)(2,1)S(1)}, u32[]{:S(2)}, u32[]{:S(2)}) %all-to-all-start) | async-done | bytes 1179680 | tf_op jit(solution)/shard_map/all_to_all | solution.py:381
  30.1 5.0 %all-to-all-start.1 = ((bf16[16,384,128]{2,1,0:T(8,128)(2,1)}), bf16[16,384,128]{2,1,0:T(8,128)(2,1)S(1)}, u32[]{:S(2)}, u32[]{:S(2)}) async-start(bf16[16,384,128]{2,1,0:T(8,128)(2,1)} %bitcast.32), calls=%async_computation.1 | async-start | bytes 3145728 | tf_op jit(solution)/shard_map/all_to_all | solution.py:381
  35.1 0.0 collective-permute-done.q1.g1
  35.1 3.5 %collective-permute-done.1.q2.g2 = bf16[128,1536]{1,0:T(8,128)(2,1)} collective-permute-done((bf16[128,1536]{1,0:T(8,128)(2,1)}, bf16[128,1536]{1,0:T(8,128)(2,1)}, u32[]{:S(2)}, u32[]{:S(2)}) %collective-permute-start.1) | collective-permute-done | bytes 393248 | tf_op jit(solution)/shard_map/ppermute | solution.py:378
  38.6 12.7 %collective-permute-done.2.q3.g3 = bf16[128,1536]{1,0:T(8,128)(2,1)} collective-permute-done((bf16[128,1536]{1,0:T(8,128)(2,1)}, bf16[128,1536]{1,0:T(8,128)(2,1)}, u32[]{:S(2)}, u32[]{:S(2)}) %collective-permute-start.2) | collective-permute-done | bytes 393248 | tf_op jit(solution)/shard_map/ppermute | solution.py:378
  51.3 0.0 copy-done.5
  51.3 9.5 %attention.1 = (bf16[512,768]{1,0:T(8,128)(2,1)S(1)}, bf16[2048,256]{1,0:T(8,128)(2,1)S(1)}) custom-call(s32[3]{0:T(128)S(1)} %pad_add_fusion.1.at, bf16[128,1536]{1,0:T(8,128)(2,1)S(1)} %copy-done.5, bf16[128,1536]{1,0:T(8,128)(2,1)} %collective-permute-done.q1.g1, bf16[128,1536]{1,0:T(8,128)(2,1)} %collective-permute-done.1.q2.g2, ...), custom_call_target="tpu_custom_call" | custom-call | flops 32212254720 | bytes 8388608 | tf_op jit(solution)/shard_map/attention/pallas_call | solution.py:147
  60.8 0.0 copy-start.1
  60.8 1.0 copy-done.1
  61.8 0.9 copy-done.3
  62.7 4.6 %all-to-all-done.1.f_ref = bf16[16,384,128]{2,1,0:T(8,128)(2,1)S(1)} async-done(((bf16[16,384,128]{2,1,0:T(8,128)(2,1)}), bf16[16,384,128]{2,1,0:T(8,128)(2,1)S(1)}, u32[]{:S(2)}, u32[]{:S(2)}) %all-to-all-start.1) | async-done | bytes 1572896 | tf_op jit(solution)/shard_map/all_to_all | solution.py:381
  67.3 22.4 %all_to_all.35 = bf16[16,128,256]{2,1,0:T(8,128)(2,1)S(1)} all-to-all(bf16[16,128,256]{2,1,0:T(8,128)(2,1)} %bitcast.29), channel_id=1, replica_groups=mesh['dp'=16,'chip'=8,'core'=2] {'chip','core'}, dimensions={0} | all-to-all | bytes 2097152 | tf_op jit(solution)/shard_map/all_to_all | solution.py:381
  89.7 0.2 reduce_sum.33
  90.0 0.0 copy-start.7
  90.0 0.0 copy-start.2
  90.0 0.1 broadcast_in_dim.9
  90.1 19.2 %all_to_all.36.m_ref = bf16[8,128,512]{2,1,0:T(8,128)(2,1)S(1)} all-to-all(bf16[8,128,512]{2,1,0:T(8,128)(2,1)S(1)} %broadcast_in_dim.9), channel_id=1, replica_groups=mesh['dp'=16,'chip'=8,'core'=2] {'chip'}, dimensions={0} | all-to-all | bytes 2097152 | tf_op jit(solution)/shard_map/all_to_all | solution.py:381
  109.3 0.0 copy-done.7
  109.3 1.8 collective-permute-start.3
  111.2 2.3 %collective-permute-done.3.t_ref = bf16[8,128,512]{2,1,0:T(8,128)(2,1)S(1)} collective-permute-done((bf16[8,128,512]{2,1,0:T(8,128)(2,1)S(1)}, bf16[8,128,512]{2,1,0:T(8,128)(2,1)S(1)}, u32[]{:S(2)}, u32[]{:S(2)}) %collective-permute-start.3) | collective-permute-done | bytes 1048608 | tf_op jit(solution)/shard_map/ppermute | solution.py:367
  113.5 0.0 copy-done.2
  113.5 2.3 %gradient.1 = (f32[384,512]{1,0:T(8,128)S(1)}, bf16[384,512]{1,0:T(8,128)(2,1)S(1)}) custom-call(s32[3]{0:T(128)S(1)} %pad_add_fusion.1.at, bf16[16,384,128]{2,1,0:T(8,128)(2,1)S(1)} %all-to-all-done.1.f_ref, bf16[8,128,512]{2,1,0:T(8,128)(2,1)S(1)} %all_to_all.36.m_ref, bf16[8,128,512]{2,1,0:T(8,128)(2,1)S(1)} %collective-permute-done.3.t_ref, ...), custom_call_target="tpu_custom_call" | custom-call | tf_op jit(solution)/shard_map/gradient/pallas_call | solution.py:264
  115.8 23.1 %all_to_all.37 = bf16[16,24,512]{2,1,0:T(8,128)(2,1)S(1)} all-to-all(bf16[16,24,512]{2,1,0:T(8,128)(2,1)S(1)} %bitcast.31), channel_id=1, replica_groups=mesh['dp'=16,'chip'=8,'core'=2] {'dp'}, dimensions={0} | all-to-all | bytes 786432 | tf_op jit(solution)/shard_map/all_to_all | solution.py:381
  138.8 0.1 reduce_sum.34
  138.9 0.8 broadcast_in_dim.10
  139.7 6.1 %all-to-all-start.5 = ((bf16[16,24,512]{2,1,0:T(8,128)(2,1)}), bf16[16,24,512]{2,1,0:T(8,128)(2,1)S(1)}, u32[]{:S(2)}, u32[]{:S(2)}) async-start(bf16[16,24,512]{2,1,0:T(8,128)(2,1)} %broadcast_in_dim.10), calls=%async_computation.5 | async-start | bytes 786432 | tf_op jit(solution)/shard_map/all_to_all | solution.py:381
  145.7 11.1 %all-to-all-done.5 = bf16[16,24,512]{2,1,0:T(8,128)(2,1)S(1)} async-done(((bf16[16,24,512]{2,1,0:T(8,128)(2,1)}), bf16[16,24,512]{2,1,0:T(8,128)(2,1)S(1)}, u32[]{:S(2)}, u32[]{:S(2)}) %all-to-all-start.5) | async-done | bytes 393248 | tf_op jit(solution)/shard_map/all_to_all | solution.py:381
  156.8 0.0 copy-done
  156.8 0.5 fusion.6.p_ref
  157.3 0.6 fusion.7
  157.9 0.5 fusion.8
  158.5 2.5 %collective-permute-start.4 = (f32[320,128]{1,0:T(8,128)S(1)}, f32[320,128]{1,0:T(8,128)S(1)}, u32[]{:S(2)}, u32[]{:S(2)}) collective-permute-start(f32[320,128]{1,0:T(8,128)S(1)} %pad_maximum_fusion), channel_id=1, source_target_pairs={{0,1},{1,0},{2,3},{3,2},{4,5},{5,4},{6,7},{7,6},{8,9},{9,8},{10,11... | collective-permute-start | bytes 491528 | tf_op jit(solution)/shard_map/ppermute | solution.py:367
  161.0 1.0 collective-permute-done.4
  162.2 0.1 broadcast_in_dim.11
  162.3 0.0 copy-start.4
  162.3 18.0 %all_to_all.38 = bf16[8,448,128]{2,1,0:T(8,128)(2,1)S(1)} all-to-all(bf16[8,448,128]{2,1,0:T(8,128)(2,1)S(1)} %broadcast_in_dim.11), channel_id=1, replica_groups=mesh['dp'=16,'chip'=8,'core'=2] {'chip'}, dimensions={0} | all-to-all | bytes 1835008 | tf_op jit(solution)/shard_map/all_to_all | solution.py:381
  180.3 0.1 convert_reduce_fusion.m_ref
  180.4 2.0 collective-permute-start.5
  182.4 0.0 copy-done.4
  182.4 0.7 fusion.1
  183.1 0.0 collective-permute-start.6
  183.2 1.1 collective-permute-start.7
  184.2 4.7 %collective-permute-start.8 = (bf16[128,768]{1,0:T(8,128)(2,1)S(1)}, bf16[128,768]{1,0:T(8,128)(2,1)S(1)}, u32[]{:S(2)}, u32[]{:S(2)}) collective-permute-start(bf16[128,768]{1,0:T(8,128)(2,1)S(1)} %get-tuple-element.46), channel_id=1, source_target_pairs={{0,15},{1,14},{2,13},{3,12},{4,11},{5,10},{6,9},{7,8},{8,7},{9,6},... | collective-permute-start | bytes 589832 | tf_op jit(solution)/shard_map/ppermute | solution.py:378
  188.9 0.7 pad_maximum_fusion.2
  189.6 0.0 collective-permute-done.5.t_ref
  189.6 7.0 %finish.1 = (f32[384,512]{1,0:T(8,128)}, f32[512,128]{1,0:T(8,128)}, f32[1,384,512]{2,1,0:T(8,128)}) custom-call(s32[3]{0:T(128)S(1)} %pad_add_fusion.1.at, f32[384,128]{1,0:T(8,128)S(1)} %fusion.6.p_ref, f32[448,128]{1,0:T(8,128)S(1)} %convert_reduce_fusion.m_ref, f32[448,128]{1,0:T(8,128)S(1)} %collective-permute-done.5.t_ref, ...), custom_call_target="tpu_custom_call" | custom-call | tf_op jit(solution)/shard_map/finish/pallas_call | solution.py:334
  196.6 0.0 collective-permute-done.6.refs_1_
  196.6 0.0 collective-permute-done.7.refs_2_
  196.6 0.0 copy-start.9
  196.6 1.0 collective-permute-done.8.refs_3_
  197.6 0.0 copy-done.9
  197.6 0.7 copy-done.10
  198.3 2.2 %unpack_queries.1 = bf16[128,3072]{1,0:T(8,128)(2,1)} custom-call(s32[4]{0:T(128)} %pad_add_fusion.h_ref, bf16[128,768]{1,0:T(8,128)(2,1)} %get-tuple-element.39.refs_0_, bf16[128,768]{1,0:T(8,128)(2,1)} %copy-done.8, bf16[128,768]{1,0:T(8,128)(2,1)} %copy-done.9, bf16[128,768]{1,0:T(8,128)(2,1)} %copy-done.10), custom_call_target="tpu_custom_call" | custom-call | tf_op jit(solution)/shard_map/unpack_queries/pallas_call | solution.py:238
  (17 shorter events, 0.2 us)
Async XLA Ops:
  0.6 156.2 %copy-start = (f32[512,128]{1,0:T(8,128)S(1)}, f32[512,128]{1,0:T(8,128)}, u32[]{:S(2)}) copy-start(f32[512,128]{1,0:T(8,128)} %param.15) | copy-start | bytes 786436
  2.8 17.6 %copy-start.6 = (bf16[128,6144]{1,0:T(8,128)(2,1)S(1)}, bf16[128,6144]{1,0:T(8,128)(2,1)}, u32[]{:S(2)}) copy-start(bf16[128,6144]{1,0:T(8,128)(2,1)} %param.12) | copy-start | bytes 4718596
  2.8 27.2 %all-to-all-start = ((bf16[16,144,256]{2,1,0:T(8,128)(2,1)}), bf16[16,144,256]{2,1,0:T(8,128)(2,1)S(1)}, u32[]{:S(2)}, u32[]{:S(2)}) async-start(bf16[16,144,256]{2,1,0:T(8,128)(2,1)} %pack_keys.1), calls=%async_computation | async-start | bytes 2359296 | tf_op jit(solution)/shard_map/all_to_all | solution.py:381
  14.6 20.5 %collective-permute-start = (bf16[128,1536]{1,0:T(8,128)(2,1)}, bf16[128,1536]{1,0:T(8,128)(2,1)}, u32[]{:S(2)}, u32[]{:S(2)}) collective-permute-start(bf16[128,1536]{1,0:T(8,128)(2,1)} %get-tuple-element.27), channel_id=1, source_target_pairs={{0,1},{1,0},{2,3},{3,2},{4,5},{5,4},{6,7},{7,6},{8,9},{9,8},{10,11... | collective-permute-start | bytes 1179656 | tf_op jit(solution)/shard_map/ppermute | solution.py:378
  14.8 23.8 %collective-permute-start.1 = (bf16[128,1536]{1,0:T(8,128)(2,1)}, bf16[128,1536]{1,0:T(8,128)(2,1)}, u32[]{:S(2)}, u32[]{:S(2)}) collective-permute-start(bf16[128,1536]{1,0:T(8,128)(2,1)} %get-tuple-element.28), channel_id=1, source_target_pairs={{0,14},{1,15},{2,12},{3,13},{4,10},{5,11},{6,8},{7,9},{8,6},{9,7},... | collective-permute-start | bytes 1179656 | tf_op jit(solution)/shard_map/ppermute | solution.py:378
  20.0 31.3 %collective-permute-start.2 = (bf16[128,1536]{1,0:T(8,128)(2,1)}, bf16[128,1536]{1,0:T(8,128)(2,1)}, u32[]{:S(2)}, u32[]{:S(2)}) collective-permute-start(bf16[128,1536]{1,0:T(8,128)(2,1)} %get-tuple-element.29), channel_id=1, source_target_pairs={{0,15},{1,14},{2,13},{3,12},{4,11},{5,10},{6,9},{7,8},{8,7},{9,6},... | collective-permute-start | bytes 1179656 | tf_op jit(solution)/shard_map/ppermute | solution.py:378
  30.1 21.3 %copy-start.5 = (bf16[128,1536]{1,0:T(8,128)(2,1)S(1)}, bf16[128,1536]{1,0:T(8,128)(2,1)}, u32[]{:S(2)}) copy-start(bf16[128,1536]{1,0:T(8,128)(2,1)} %get-tuple-element.26.q0.g0) | copy-start | bytes 1179652
  30.1 37.2 %all-to-all-start.1 = ((bf16[16,384,128]{2,1,0:T(8,128)(2,1)}), bf16[16,384,128]{2,1,0:T(8,128)(2,1)S(1)}, u32[]{:S(2)}, u32[]{:S(2)}) async-start(bf16[16,384,128]{2,1,0:T(8,128)(2,1)} %bitcast.32), calls=%async_computation.1 | async-start | bytes 3145728 | tf_op jit(solution)/shard_map/all_to_all | solution.py:381
  60.8 1.0 copy-start.1
  61.8 0.9 copy-start.3
  90.0 19.3 %copy-start.7 = (bf16[128,512]{1,0:T(8,128)(2,1)}, bf16[128,512]{1,0:T(8,128)(2,1)S(1)}, u32[]{:S(2)}) copy-start(bf16[128,512]{1,0:T(8,128)(2,1)S(1)} %pad_maximum_fusion.1) | copy-start | bytes 393220
  90.0 23.4 %copy-start.2 = (f32[1,384,512]{2,1,0:T(8,128)S(1)}, f32[1,384,512]{2,1,0:T(8,128)}, u32[]{:S(2)}) copy-start(f32[1,384,512]{2,1,0:T(8,128)} %param.14) | copy-start | bytes 2359300
  109.3 4.1 %collective-permute-start.3 = (bf16[8,128,512]{2,1,0:T(8,128)(2,1)S(1)}, bf16[8,128,512]{2,1,0:T(8,128)(2,1)S(1)}, u32[]{:S(2)}, u32[]{:S(2)}) collective-permute-start(bf16[8,128,512]{2,1,0:T(8,128)(2,1)S(1)} %all_to_all.36.m_ref), channel_id=1, source_target_pairs={{0,1},{1,0},{2,3},{3,2},{4,5},{5,4},{6,7},{7,6},{8,9},{9,8},{10,11... | collective-permute-start | bytes 3145736 | tf_op jit(solution)/shard_map/ppermute | solution.py:367
  139.7 17.1 %all-to-all-start.5 = ((bf16[16,24,512]{2,1,0:T(8,128)(2,1)}), bf16[16,24,512]{2,1,0:T(8,128)(2,1)S(1)}, u32[]{:S(2)}, u32[]{:S(2)}) async-start(bf16[16,24,512]{2,1,0:T(8,128)(2,1)} %broadcast_in_dim.10), calls=%async_computation.5 | async-start | bytes 786432 | tf_op jit(solution)/shard_map/all_to_all | solution.py:381
  158.5 3.6 %collective-permute-start.4 = (f32[320,128]{1,0:T(8,128)S(1)}, f32[320,128]{1,0:T(8,128)S(1)}, u32[]{:S(2)}, u32[]{:S(2)}) collective-permute-start(f32[320,128]{1,0:T(8,128)S(1)} %pad_maximum_fusion), channel_id=1, source_target_pairs={{0,1},{1,0},{2,3},{3,2},{4,5},{5,4},{6,7},{7,6},{8,9},{9,8},{10,11... | collective-permute-start | bytes 491528 | tf_op jit(solution)/shard_map/ppermute | solution.py:367
  162.3 20.1 %copy-start.4 = (bf16[512,768]{1,0:T(8,128)(2,1)S(1)}, bf16[512,768]{1,0:T(8,128)(2,1)}, u32[]{:S(2)}) copy-start(bf16[512,768]{1,0:T(8,128)(2,1)} %copy-done.3) | copy-start | bytes 2359300
  180.4 9.2 %collective-permute-start.5 = (f32[448,128]{1,0:T(8,128)S(1)}, f32[448,128]{1,0:T(8,128)S(1)}, u32[]{:S(2)}, u32[]{:S(2)}) collective-permute-start(f32[448,128]{1,0:T(8,128)S(1)} %convert_reduce_fusion.m_ref), channel_id=1, source_target_pairs={{0,1},{1,0},{2,3},{3,2},{4,5},{5,4},{6,7},{7,6},{8,9},{9,8},{10,11... | collective-permute-start | bytes 688136 | tf_op jit(solution)/shard_map/ppermute | solution.py:367
  183.1 13.4 %collective-permute-start.6 = (bf16[128,768]{1,0:T(8,128)(2,1)S(1)}, bf16[128,768]{1,0:T(8,128)(2,1)S(1)}, u32[]{:S(2)}, u32[]{:S(2)}) collective-permute-start(bf16[128,768]{1,0:T(8,128)(2,1)S(1)} %get-tuple-element.48), channel_id=1, source_target_pairs={{0,1},{1,0},{2,3},{3,2},{4,5},{5,4},{6,7},{7,6},{8,9},{9,8},{10,11... | collective-permute-start | bytes 589832 | tf_op jit(solution)/shard_map/ppermute | solution.py:378
  183.2 13.4 %collective-permute-start.7 = (bf16[128,768]{1,0:T(8,128)(2,1)S(1)}, bf16[128,768]{1,0:T(8,128)(2,1)S(1)}, u32[]{:S(2)}, u32[]{:S(2)}) collective-permute-start(bf16[128,768]{1,0:T(8,128)(2,1)S(1)} %get-tuple-element.47), channel_id=1, source_target_pairs={{0,14},{1,15},{2,12},{3,13},{4,10},{5,11},{6,8},{7,9},{8,6},{9,7},... | collective-permute-start | bytes 589832 | tf_op jit(solution)/shard_map/ppermute | solution.py:378
  184.2 13.4 %collective-permute-start.8 = (bf16[128,768]{1,0:T(8,128)(2,1)S(1)}, bf16[128,768]{1,0:T(8,128)(2,1)S(1)}, u32[]{:S(2)}, u32[]{:S(2)}) collective-permute-start(bf16[128,768]{1,0:T(8,128)(2,1)S(1)} %get-tuple-element.46), channel_id=1, source_target_pairs={{0,15},{1,14},{2,13},{3,12},{4,11},{5,10},{6,9},{7,8},{8,7},{9,6},... | collective-permute-start | bytes 589832 | tf_op jit(solution)/shard_map/ppermute | solution.py:378
  196.6 1.0 copy-start.8
  196.6 1.0 copy-start.9
  197.6 0.7 copy-start.10

commit v8 on v6

--- a/solution.py
+++ b/solution.py
@@ -171,7 +171,7 @@
             jax.ShapeDtypeStruct((length, 2 * HEAD), jnp.bfloat16),
         ],
         compiler_params=pltpu.CompilerParams(
-            dimension_semantics=("arbitrary",), vmem_limit_bytes=58 * 1024 * 1024
+            dimension_semantics=("arbitrary",), vmem_limit_bytes=40 * 1024 * 1024
         ),
         cost_estimate=pl.CostEstimate(
             flops=8 * flops, bytes_accessed=8 * 1024 * 1024, transcendentals=0
@@ -411,14 +411,15 @@
     dk_theirs = swap(dk_mine)
     combined, low = gradient(where, feat, dk_mine, dk_theirs, error.reshape(rows, width_kv))
 
+    low, dq = lax.optimization_barrier((low, dq))
     shares = exchange(low.reshape(replicas, rows // replicas, width_kv), "dp")
-    share = jnp.sum(shares.astype(f32), axis=0).astype(bf16)
-    total = spread(share, "dp", replicas).reshape(rows, width_kv)
-
     back = [dq[:tokens]] + [
         move(dq[n * tokens : (n + 1) * tokens], *ways[n]) for n in range(1, 4)
     ]
+    share = jnp.sum(shares.astype(f32), axis=0).astype(bf16)
+    share, *back = lax.optimization_barrier((share, *back))
     d_query = unpack_queries(heads, back, group)
+    total = spread(share, "dp", replicas).reshape(rows, width_kv)
 
     total = total.astype(f32)
     p_sum = jnp.dot(total, q_init, precision=HIGHEST)
@@ -435,7 +436,9 @@
     mid = lax.reduce_precision(gram - high, 8, 7)
     low = gram - high - mid
     sums = jnp.concatenate([sums[:half], high, mid, low], axis=0).astype(bf16)
-    sums = jnp.sum(spread(sums, "chip", chips).astype(f32), axis=0)
+    sums = spread(sums, "chip", chips)
+    sums, d_query, d_value = lax.optimization_barrier((sums, d_query, d_value))
+    sums = jnp.sum(sums.astype(f32), axis=0)
     compressed, q_factor, new_error = finish(where, p_sum, sums, swap(sums), combined, replicas)
     return (d_query, d_key, d_value, compressed, q_factor, new_error)
 

time: 204 us -> 204 us (level)
  blocking collectives: 65.4 us -> 41.8 us
  waiting for transfers between devices: 55.8 us -> 70.3 us
  starting transfers between devices: 41.1 us -> 54.2 us
  Pallas kernels: 29.4 us -> 24.3 us
  local copies, waits for them, and re-layouts: 5.93 us -> 8.29 us
    all_to_all x3 -> x2, blocking collectives: 65.4 us -> 41.8 us  [exchange(): return lax.all_to_all(x, axis, 0, 0)]
    all_to_all x4 -> x5, starting transfers between devices: 23.1 us -> 36.3 us  [exchange(): return lax.all_to_all(x, axis, 0, 0)]
    all_to_all x4 -> x5, waiting for transfers between devices: 29.6 us -> 42.2 us  [exchange(): return lax.all_to_all(x, axis, 0, 0)]
    pallas_call x1, Pallas kernels: 13.1 us -> 7.99 us  [attention(): pl.pallas_call(kernel, grid_spec=pltpu.PrefetchScalarGridSpec(num_scalar_...]
  transfers between devices with their start and end apart: 13 -> 14, of which waited for: 10 -> 12; matrix products, arithmetic and copies ran while one was open for 2% -> 2% of each run, Pallas kernels for 9% -> 6%
where the time goes in v8:
time: 204 us; the launch traced here: 203 us
  waiting for transfers between devices  70.3 us (34%)
  starting transfers between devices  54.2 us (27%)
  blocking collectives  41.8 us (20%)
  Pallas kernels  24.3 us (12%)
  local copies, waits for them, and re-layouts  8.29 us (4%)
    all_to_all x5, waiting for transfers between devices, exchange(): return lax.all_to_all(x, axis, 0, 0)  42.2 us
    all_to_all x2, blocking collectives, exchange(): return lax.all_to_all(x, axis, 0, 0)  41.8 us
    all_to_all x5, starting transfers between devices, exchange(): return lax.all_to_all(x, axis, 0, 0)  36.3 us
    ppermute x6, waiting for transfers between devices, move(): return lax.ppermute(x, ctx, pairs)  23.7 us
    ppermute x6, starting transfers between devices, move(): return lax.ppermute(x, ctx, pairs)  11.7 us
    pallas_call x1, Pallas kernels, attention(): pl.pallas_call(kernel, grid_spec=pltpu.PrefetchScalarGridSpec(num_scalar_...  7.99 us
    pallas_call x1, Pallas kernels, finish(): pl.pallas_call(kernel, out_shape=[jax.ShapeDtypeStruct((rows, width), jnp...  7.01 us
    ppermute x3, starting transfers between devices, swap(): return lax.ppermute(x, 'core', [(0, 1), (1, 0)])  6.27 us
  transfers between devices with their start and end apart: 14, of which 12 were waited for; matrix products, arithmetic and copies ran while one was open for 2% of the time, Pallas kernels for 6%

profile of v8, /device:TPU:1, one launch (start us, length us, event | category | flops | bytes accessed | tf_op | source)
XLA Modules:
  0.0 203.2 jit_solution(5773531149759753435)
XLA Ops:
  0.6 0.0 copy-start
  0.6 2.2 %pack_keys.1 = bf16[16,144,256]{2,1,0:T(8,128)(2,1)} custom-call(bf16[128,512]{1,0:T(8,128)(2,1)} %k_ref.1, bf16[128,512]{1,0:T(8,128)(2,1)} %v_ref.1, s32[1,128]{1,0:T(1,128)} %bitcast.37), custom_call_target="tpu_custom_call" | custom-call | tf_op jit(solution)/shard_map/pack_keys/pallas_call | solution.py:203
  2.8 8.6 %all-to-all-start = ((bf16[16,144,256]{2,1,0:T(8,128)(2,1)}), bf16[16,144,256]{2,1,0:T(8,128)(2,1)S(1)}, u32[]{:S(2)}, u32[]{:S(2)}) async-start(bf16[16,144,256]{2,1,0:T(8,128)(2,1)} %pack_keys.1), calls=%async_computation | async-start | bytes 2359296 | tf_op jit(solution)/shard_map/all_to_all | solution.py:381
  11.4 0.6 pad_add_fusion.1.h_ref
  12.0 2.6 %pack_queries.1 = (bf16[128,1536]{1,0:T(8,128)(2,1)}, bf16[128,1536]{1,0:T(8,128)(2,1)}, bf16[128,1536]{1,0:T(8,128)(2,1)}, bf16[128,1536]{1,0:T(8,128)(2,1)}) custom-call(s32[4]{0:T(128)} %pad_add_fusion.1.h_ref, bf16[128,3072]{1,0:T(8,128)(2,1)} %q_ref.1, bf16[128,3072]{1,0:T(8,128)(2,1)} %g_ref.1), custom_call_target="tpu_custom_call" | custom-call | tf_op jit(solution)/shard_map/pack_queries/pallas_call | solution.py:221
  14.7 0.1 collective-permute-start
  14.8 5.3 %collective-permute-start.1 = (bf16[128,1536]{1,0:T(8,128)(2,1)}, bf16[128,1536]{1,0:T(8,128)(2,1)}, u32[]{:S(2)}, u32[]{:S(2)}) collective-permute-start(bf16[128,1536]{1,0:T(8,128)(2,1)} %get-tuple-element.33), channel_id=1, source_target_pairs={{0,14},{1,15},{2,12},{3,13},{4,10},{5,11},{6,8},{7,9},{8,6},{9,7},... | collective-permute-start | bytes 1179656 | tf_op jit(solution)/shard_map/ppermute | solution.py:378
  20.0 0.4 collective-permute-start.2
  20.4 0.0 copy-done.7
  20.4 1.6 copy.15
  22.0 0.1 pad_add_fusion.at
  22.1 8.0 %all-to-all-done.k_ref.v_ref = bf16[16,144,256]{2,1,0:T(8,128)(2,1)S(1)} async-done(((bf16[16,144,256]{2,1,0:T(8,128)(2,1)}), bf16[16,144,256]{2,1,0:T(8,128)(2,1)S(1)}, u32[]{:S(2)}, u32[]{:S(2)}) %all-to-all-start) | async-done | bytes 1179680 | tf_op jit(solution)/shard_map/all_to_all | solution.py:381
  30.1 5.0 %all-to-all-start.1 = ((bf16[16,384,128]{2,1,0:T(8,128)(2,1)}), bf16[16,384,128]{2,1,0:T(8,128)(2,1)S(1)}, u32[]{:S(2)}, u32[]{:S(2)}) async-start(bf16[16,384,128]{2,1,0:T(8,128)(2,1)} %bitcast.32), calls=%async_computation.1 | async-start | bytes 3145728 | tf_op jit(solution)/shard_map/all_to_all | solution.py:381
  35.1 0.0 collective-permute-done.q1.g1
  35.1 3.5 %collective-permute-done.1.q2.g2 = bf16[128,1536]{1,0:T(8,128)(2,1)} collective-permute-done((bf16[128,1536]{1,0:T(8,128)(2,1)}, bf16[128,1536]{1,0:T(8,128)(2,1)}, u32[]{:S(2)}, u32[]{:S(2)}) %collective-permute-start.1) | collective-permute-done | bytes 393248 | tf_op jit(solution)/shard_map/ppermute | solution.py:378
  38.6 12.7 %collective-permute-done.2.q3.g3 = bf16[128,1536]{1,0:T(8,128)(2,1)} collective-permute-done((bf16[128,1536]{1,0:T(8,128)(2,1)}, bf16[128,1536]{1,0:T(8,128)(2,1)}, u32[]{:S(2)}, u32[]{:S(2)}) %collective-permute-start.2) | collective-permute-done | bytes 393248 | tf_op jit(solution)/shard_map/ppermute | solution.py:378
  51.3 0.0 copy-done.6
  51.3 8.0 %attention.1 = (bf16[512,768]{1,0:T(8,128)(2,1)S(1)}, bf16[2048,256]{1,0:T(8,128)(2,1)S(1)}) custom-call(s32[3]{0:T(128)S(1)} %pad_add_fusion.at, bf16[128,1536]{1,0:T(8,128)(2,1)S(1)} %copy-done.6, bf16[128,1536]{1,0:T(8,128)(2,1)} %collective-permute-done.q1.g1, bf16[128,1536]{1,0:T(8,128)(2,1)} %collective-permute-done.1.q2.g2, ...), custom_call_target="tpu_custom_call" | custom-call | flops 32212254720 | bytes 8388608 | tf_op jit(solution)/shard_map/attention/pallas_call | solution.py:147
  59.3 1.0 copy-done.1
  60.3 0.9 copy-done.3
  61.2 6.1 %all-to-all-done.1.f_ref = bf16[16,384,128]{2,1,0:T(8,128)(2,1)S(1)} async-done(((bf16[16,384,128]{2,1,0:T(8,128)(2,1)}), bf16[16,384,128]{2,1,0:T(8,128)(2,1)S(1)}, u32[]{:S(2)}, u32[]{:S(2)}) %all-to-all-start.1) | async-done | bytes 1572896 | tf_op jit(solution)/shard_map/all_to_all | solution.py:381
  67.3 22.6 %all_to_all.35 = bf16[16,128,256]{2,1,0:T(8,128)(2,1)S(1)} all-to-all(bf16[16,128,256]{2,1,0:T(8,128)(2,1)} %bitcast.29), channel_id=1, replica_groups=mesh['dp'=16,'chip'=8,'core'=2] {'chip','core'}, dimensions={0} | all-to-all | bytes 2097152 | tf_op jit(solution)/shard_map/all_to_all | solution.py:381
  89.9 0.2 reduce_sum.33
  90.1 0.6 fusion.2
  90.7 0.6 fusion.4
  91.4 0.0 copy-start.8
  91.4 0.0 copy-start.2
  91.4 0.1 broadcast_in_dim.9
  91.5 19.2 %all_to_all.36.m_ref = bf16[8,128,512]{2,1,0:T(8,128)(2,1)S(1)} all-to-all(bf16[8,128,512]{2,1,0:T(8,128)(2,1)S(1)} %broadcast_in_dim.9), channel_id=1, replica_groups=mesh['dp'=16,'chip'=8,'core'=2] {'chip'}, dimensions={0} | all-to-all | bytes 2097152 | tf_op jit(solution)/shard_map/all_to_all | solution.py:381
  110.7 1.8 collective-permute-start.3
  112.6 2.3 %collective-permute-done.3.t_ref = bf16[8,128,512]{2,1,0:T(8,128)(2,1)S(1)} collective-permute-done((bf16[8,128,512]{2,1,0:T(8,128)(2,1)S(1)}, bf16[8,128,512]{2,1,0:T(8,128)(2,1)S(1)}, u32[]{:S(2)}, u32[]{:S(2)}) %collective-permute-start.3) | collective-permute-done | bytes 1048608 | tf_op jit(solution)/shard_map/ppermute | solution.py:367
  114.8 2.3 %gradient.1 = (f32[384,512]{1,0:T(8,128)S(1)}, bf16[384,512]{1,0:T(8,128)(2,1)S(1)}) custom-call(s32[3]{0:T(128)S(1)} %pad_add_fusion.at, bf16[16,384,128]{2,1,0:T(8,128)(2,1)S(1)} %all-to-all-done.1.f_ref, bf16[8,128,512]{2,1,0:T(8,128)(2,1)S(1)} %all_to_all.36.m_ref, bf16[8,128,512]{2,1,0:T(8,128)(2,1)S(1)} %collective-permute-done.3.t_ref, ...), custom_call_target="tpu_custom_call" | custom-call | tf_op jit(solution)/shard_map/gradient/pallas_call | solution.py:264
  117.2 0.0 copy-start.5
  117.2 0.7 copy-done.5
  117.9 12.0 %all-to-all-start.4 = ((bf16[16,24,512]{2,1,0:T(8,128)(2,1)}), bf16[16,24,512]{2,1,0:T(8,128)(2,1)S(1)}, u32[]{:S(2)}, u32[]{:S(2)}) async-start(bf16[16,24,512]{2,1,0:T(8,128)(2,1)} %bitcast.31), calls=%async_computation.4 | async-start | bytes 786432 | tf_op jit(solution)/shard_map/all_to_all | solution.py:381
  129.9 0.7 fusion.1
  130.6 0.7 collective-permute-start.4
  131.3 1.8 collective-permute-start.5
  133.1 3.4 %collective-permute-start.6 = (bf16[128,768]{1,0:T(8,128)(2,1)S(1)}, bf16[128,768]{1,0:T(8,128)(2,1)S(1)}, u32[]{:S(2)}, u32[]{:S(2)}) collective-permute-start(bf16[128,768]{1,0:T(8,128)(2,1)S(1)} %get-tuple-element.56), channel_id=1, source_target_pairs={{0,15},{1,14},{2,13},{3,12},{4,11},{5,10},{6,9},{7,8},{8,7},{9,6},... | collective-permute-start | bytes 589832 | tf_op jit(solution)/shard_map/ppermute | solution.py:378
  136.5 4.7 %all-to-all-done.4 = bf16[16,24,512]{2,1,0:T(8,128)(2,1)S(1)} async-done(((bf16[16,24,512]{2,1,0:T(8,128)(2,1)}), bf16[16,24,512]{2,1,0:T(8,128)(2,1)S(1)}, u32[]{:S(2)}, u32[]{:S(2)}) %all-to-all-start.4) | async-done | bytes 393248 | tf_op jit(solution)/shard_map/all_to_all | solution.py:381
  141.3 0.1 reduce_sum.34
  141.3 0.0 collective-permute-done.4.refs_1_
  141.3 0.0 copy-start.9
  141.4 3.2 %collective-permute-done.5.refs_2_ = bf16[128,768]{1,0:T(8,128)(2,1)S(1)} collective-permute-done((bf16[128,768]{1,0:T(8,128)(2,1)S(1)}, bf16[128,768]{1,0:T(8,128)(2,1)S(1)}, u32[]{:S(2)}, u32[]{:S(2)}) %collective-permute-start.5) | collective-permute-done | bytes 196640 | tf_op jit(solution)/shard_map/ppermute | solution.py:378
  144.6 4.2 %collective-permute-done.6.refs_3_ = bf16[128,768]{1,0:T(8,128)(2,1)S(1)} collective-permute-done((bf16[128,768]{1,0:T(8,128)(2,1)S(1)}, bf16[128,768]{1,0:T(8,128)(2,1)S(1)}, u32[]{:S(2)}, u32[]{:S(2)}) %collective-permute-start.6) | collective-permute-done | bytes 196640 | tf_op jit(solution)/shard_map/ppermute | solution.py:378
  148.8 0.8 broadcast_in_dim.10
  149.6 6.1 %all-to-all-start.5 = ((bf16[16,24,512]{2,1,0:T(8,128)(2,1)}), bf16[16,24,512]{2,1,0:T(8,128)(2,1)S(1)}, u32[]{:S(2)}, u32[]{:S(2)}) async-start(bf16[16,24,512]{2,1,0:T(8,128)(2,1)} %broadcast_in_dim.10), calls=%async_computation.5 | async-start | bytes 786432 | tf_op jit(solution)/shard_map/all_to_all | solution.py:381
  155.8 11.1 %all-to-all-done.5 = bf16[16,24,512]{2,1,0:T(8,128)(2,1)S(1)} async-done(((bf16[16,24,512]{2,1,0:T(8,128)(2,1)}), bf16[16,24,512]{2,1,0:T(8,128)(2,1)S(1)}, u32[]{:S(2)}, u32[]{:S(2)}) %all-to-all-start.5) | async-done | bytes 393248 | tf_op jit(solution)/shard_map/all_to_all | solution.py:381
  166.8 0.5 fusion.6.p_ref
  167.3 0.6 fusion.7
  167.9 0.5 fusion.8
  168.6 2.8 %collective-permute-start.7 = (f32[320,128]{1,0:T(8,128)S(1)}, f32[320,128]{1,0:T(8,128)S(1)}, u32[]{:S(2)}, u32[]{:S(2)}) collective-permute-start(f32[320,128]{1,0:T(8,128)S(1)} %pad_maximum_fusion), channel_id=1, source_target_pairs={{0,1},{1,0},{2,3},{3,2},{4,5},{5,4},{6,7},{7,6},{8,9},{9,8},{10,11... | collective-permute-start | bytes 491528 | tf_op jit(solution)/shard_map/ppermute | solution.py:367
  171.4 1.0 collective-permute-done.7
  172.5 0.0 copy-start.14
  172.5 0.0 copy-start.15
  172.5 1.1 broadcast_in_dim.11
  173.6 4.5 %all-to-all-start.6 = ((bf16[8,448,128]{2,1,0:T(8,128)(2,1)}), bf16[8,448,128]{2,1,0:T(8,128)(2,1)S(1)}, u32[]{:S(2)}, u32[]{:S(2)}) async-start(bf16[8,448,128]{2,1,0:T(8,128)(2,1)} %broadcast_in_dim.11), calls=%async_computation.6 | async-start | bytes 1835008 | tf_op jit(solution)/shard_map/all_to_all | solution.py:381
  178.2 0.7 pad_maximum_fusion.2
  178.8 2.2 %unpack_queries.1 = bf16[128,3072]{1,0:T(8,128)(2,1)} custom-call(s32[4]{0:T(128)} %pad_add_fusion.1.h_ref, bf16[128,768]{1,0:T(8,128)(2,1)} %get-tuple-element.45.refs_0_, bf16[128,768]{1,0:T(8,128)(2,1)} %copy-done.9, bf16[128,768]{1,0:T(8,128)(2,1)} %copy-done.10, bf16[128,768]{1,0:T(8,128)(2,1)} %copy-done.11), custom_call_target="tpu_custom_call" | custom-call | tf_op jit(solution)/shard_map/unpack_queries/pallas_call | solution.py:238
  181.0 12.4 %all-to-all-done.6 = bf16[8,448,128]{2,1,0:T(8,128)(2,1)S(1)} async-done(((bf16[8,448,128]{2,1,0:T(8,128)(2,1)}), bf16[8,448,128]{2,1,0:T(8,128)(2,1)S(1)}, u32[]{:S(2)}, u32[]{:S(2)}) %all-to-all-start.6) | async-done | bytes 917536 | tf_op jit(solution)/shard_map/all_to_all | solution.py:381
  193.4 0.1 convert_reduce_fusion.m_ref
  193.5 1.6 collective-permute-start.8
  195.1 1.1 collective-permute-done.8.t_ref
  196.2 7.0 %finish.1 = (f32[384,512]{1,0:T(8,128)}, f32[512,128]{1,0:T(8,128)}, f32[1,384,512]{2,1,0:T(8,128)}) custom-call(s32[3]{0:T(128)S(1)} %pad_add_fusion.at, f32[384,128]{1,0:T(8,128)S(1)} %fusion.6.p_ref, f32[448,128]{1,0:T(8,128)S(1)} %convert_reduce_fusion.m_ref, f32[448,128]{1,0:T(8,128)S(1)} %collective-permute-done.8.t_ref, ...), custom_call_target="tpu_custom_call" | custom-call | tf_op jit(solution)/shard_map/finish/pallas_call | solution.py:334
  (29 shorter events, 0.2 us)
Async XLA Ops:
  0.6 166.2 %copy-start = (f32[512,128]{1,0:T(8,128)S(1)}, f32[512,128]{1,0:T(8,128)}, u32[]{:S(2)}) copy-start(f32[512,128]{1,0:T(8,128)} %param.15) | copy-start | bytes 786436
  2.8 17.6 %copy-start.7 = (bf16[128,6144]{1,0:T(8,128)(2,1)S(1)}, bf16[128,6144]{1,0:T(8,128)(2,1)}, u32[]{:S(2)}) copy-start(bf16[128,6144]{1,0:T(8,128)(2,1)} %param.12) | copy-start | bytes 4718596
  2.8 27.2 %all-to-all-start = ((bf16[16,144,256]{2,1,0:T(8,128)(2,1)}), bf16[16,144,256]{2,1,0:T(8,128)(2,1)S(1)}, u32[]{:S(2)}, u32[]{:S(2)}) async-start(bf16[16,144,256]{2,1,0:T(8,128)(2,1)} %pack_keys.1), calls=%async_computation | async-start | bytes 2359296 | tf_op jit(solution)/shard_map/all_to_all | solution.py:381
  14.7 20.4 %collective-permute-start = (bf16[128,1536]{1,0:T(8,128)(2,1)}, bf16[128,1536]{1,0:T(8,128)(2,1)}, u32[]{:S(2)}, u32[]{:S(2)}) collective-permute-start(bf16[128,1536]{1,0:T(8,128)(2,1)} %get-tuple-element.32), channel_id=1, source_target_pairs={{0,1},{1,0},{2,3},{3,2},{4,5},{5,4},{6,7},{7,6},{8,9},{9,8},{10,11... | collective-permute-start | bytes 1179656 | tf_op jit(solution)/shard_map/ppermute | solution.py:378
  14.8 23.8 %collective-permute-start.1 = (bf16[128,1536]{1,0:T(8,128)(2,1)}, bf16[128,1536]{1,0:T(8,128)(2,1)}, u32[]{:S(2)}, u32[]{:S(2)}) collective-permute-start(bf16[128,1536]{1,0:T(8,128)(2,1)} %get-tuple-element.33), channel_id=1, source_target_pairs={{0,14},{1,15},{2,12},{3,13},{4,10},{5,11},{6,8},{7,9},{8,6},{9,7},... | collective-permute-start | bytes 1179656 | tf_op jit(solution)/shard_map/ppermute | solution.py:378
  20.0 31.3 %collective-permute-start.2 = (bf16[128,1536]{1,0:T(8,128)(2,1)}, bf16[128,1536]{1,0:T(8,128)(2,1)}, u32[]{:S(2)}, u32[]{:S(2)}) collective-permute-start(bf16[128,1536]{1,0:T(8,128)(2,1)} %get-tuple-element.34), channel_id=1, source_target_pairs={{0,15},{1,14},{2,13},{3,12},{4,11},{5,10},{6,9},{7,8},{8,7},{9,6},... | collective-permute-start | bytes 1179656 | tf_op jit(solution)/shard_map/ppermute | solution.py:378
  30.1 21.3 %copy-start.6 = (bf16[128,1536]{1,0:T(8,128)(2,1)S(1)}, bf16[128,1536]{1,0:T(8,128)(2,1)}, u32[]{:S(2)}) copy-start(bf16[128,1536]{1,0:T(8,128)(2,1)} %get-tuple-element.31.q0.g0) | copy-start | bytes 1179652
  30.1 37.2 %all-to-all-start.1 = ((bf16[16,384,128]{2,1,0:T(8,128)(2,1)}), bf16[16,384,128]{2,1,0:T(8,128)(2,1)S(1)}, u32[]{:S(2)}, u32[]{:S(2)}) async-start(bf16[16,384,128]{2,1,0:T(8,128)(2,1)} %bitcast.32), calls=%async_computation.1 | async-start | bytes 3145728 | tf_op jit(solution)/shard_map/all_to_all | solution.py:381
  59.3 1.0 copy-start.1
  60.3 0.9 copy-start.3
  91.4 19.3 %copy-start.8 = (bf16[128,512]{1,0:T(8,128)(2,1)}, bf16[128,512]{1,0:T(8,128)(2,1)S(1)}, u32[]{:S(2)}) copy-start(bf16[128,512]{1,0:T(8,128)(2,1)S(1)} %pad_maximum_fusion.1) | copy-start | bytes 393220
  91.4 23.4 %copy-start.2 = (f32[1,384,512]{2,1,0:T(8,128)S(1)}, f32[1,384,512]{2,1,0:T(8,128)}, u32[]{:S(2)}) copy-start(f32[1,384,512]{2,1,0:T(8,128)} %param.14) | copy-start | bytes 2359300
  110.7 4.1 %collective-permute-start.3 = (bf16[8,128,512]{2,1,0:T(8,128)(2,1)S(1)}, bf16[8,128,512]{2,1,0:T(8,128)(2,1)S(1)}, u32[]{:S(2)}, u32[]{:S(2)}) collective-permute-start(bf16[8,128,512]{2,1,0:T(8,128)(2,1)S(1)} %all_to_all.36.m_ref), channel_id=1, source_target_pairs={{0,1},{1,0},{2,3},{3,2},{4,5},{5,4},{6,7},{7,6},{8,9},{9,8},{10,11... | collective-permute-start | bytes 3145736 | tf_op jit(solution)/shard_map/ppermute | solution.py:367
  114.8 15.1 %copy-start.4 = (bf16[512,768]{1,0:T(8,128)(2,1)S(1)}, bf16[512,768]{1,0:T(8,128)(2,1)}, u32[]{:S(2)}) copy-start(bf16[512,768]{1,0:T(8,128)(2,1)} %copy-done.3) | copy-start | bytes 2359300
  117.2 0.7 copy-start.5
  117.9 23.4 %all-to-all-start.4 = ((bf16[16,24,512]{2,1,0:T(8,128)(2,1)}), bf16[16,24,512]{2,1,0:T(8,128)(2,1)S(1)}, u32[]{:S(2)}, u32[]{:S(2)}) async-start(bf16[16,24,512]{2,1,0:T(8,128)(2,1)} %bitcast.31), calls=%async_computation.4 | async-start | bytes 786432 | tf_op jit(solution)/shard_map/all_to_all | solution.py:381
  130.6 10.7 %collective-permute-start.4 = (bf16[128,768]{1,0:T(8,128)(2,1)S(1)}, bf16[128,768]{1,0:T(8,128)(2,1)S(1)}, u32[]{:S(2)}, u32[]{:S(2)}) collective-permute-start(bf16[128,768]{1,0:T(8,128)(2,1)S(1)} %get-tuple-element.58), channel_id=1, source_target_pairs={{0,1},{1,0},{2,3},{3,2},{4,5},{5,4},{6,7},{7,6},{8,9},{9,8},{10,11... | collective-permute-start | bytes 589832 | tf_op jit(solution)/shard_map/ppermute | solution.py:378
  131.3 13.3 %collective-permute-start.5 = (bf16[128,768]{1,0:T(8,128)(2,1)S(1)}, bf16[128,768]{1,0:T(8,128)(2,1)S(1)}, u32[]{:S(2)}, u32[]{:S(2)}) collective-permute-start(bf16[128,768]{1,0:T(8,128)(2,1)S(1)} %get-tuple-element.57), channel_id=1, source_target_pairs={{0,14},{1,15},{2,12},{3,13},{4,10},{5,11},{6,8},{7,9},{8,6},{9,7},... | collective-permute-start | bytes 589832 | tf_op jit(solution)/shard_map/ppermute | solution.py:378
  133.1 15.7 %collective-permute-start.6 = (bf16[128,768]{1,0:T(8,128)(2,1)S(1)}, bf16[128,768]{1,0:T(8,128)(2,1)S(1)}, u32[]{:S(2)}, u32[]{:S(2)}) collective-permute-start(bf16[128,768]{1,0:T(8,128)(2,1)S(1)} %get-tuple-element.56), channel_id=1, source_target_pairs={{0,15},{1,14},{2,13},{3,12},{4,11},{5,10},{6,9},{7,8},{8,7},{9,6},... | collective-permute-start | bytes 589832 | tf_op jit(solution)/shard_map/ppermute | solution.py:378
  141.3 27.1 %copy-start.9 = (bf16[128,768]{1,0:T(8,128)(2,1)}, bf16[128,768]{1,0:T(8,128)(2,1)S(1)}, u32[]{:S(2)}) copy-start(bf16[128,768]{1,0:T(8,128)(2,1)S(1)} %collective-permute-done.4.refs_1_) | copy-start | bytes 589828
  144.6 23.9 %copy-start.10 = (bf16[128,768]{1,0:T(8,128)(2,1)}, bf16[128,768]{1,0:T(8,128)(2,1)S(1)}, u32[]{:S(2)}) copy-start(bf16[128,768]{1,0:T(8,128)(2,1)S(1)} %collective-permute-done.5.refs_2_) | copy-start | bytes 589828
  148.8 19.7 %copy-start.11 = (bf16[128,768]{1,0:T(8,128)(2,1)}, bf16[128,768]{1,0:T(8,128)(2,1)S(1)}, u32[]{:S(2)}) copy-start(bf16[128,768]{1,0:T(8,128)(2,1)S(1)} %collective-permute-done.6.refs_3_) | copy-start | bytes 589828
  149.6 17.3 %all-to-all-start.5 = ((bf16[16,24,512]{2,1,0:T(8,128)(2,1)}), bf16[16,24,512]{2,1,0:T(8,128)(2,1)S(1)}, u32[]{:S(2)}, u32[]{:S(2)}) async-start(bf16[16,24,512]{2,1,0:T(8,128)(2,1)} %broadcast_in_dim.10), calls=%async_computation.5 | async-start | bytes 786432 | tf_op jit(solution)/shard_map/all_to_all | solution.py:381
  168.6 3.9 %collective-permute-start.7 = (f32[320,128]{1,0:T(8,128)S(1)}, f32[320,128]{1,0:T(8,128)S(1)}, u32[]{:S(2)}, u32[]{:S(2)}) collective-permute-start(f32[320,128]{1,0:T(8,128)S(1)} %pad_maximum_fusion), channel_id=1, source_target_pairs={{0,1},{1,0},{2,3},{3,2},{4,5},{5,4},{6,7},{7,6},{8,9},{9,8},{10,11... | collective-permute-start | bytes 491528 | tf_op jit(solution)/shard_map/ppermute | solution.py:367
  172.5 5.7 %copy-start.12 = (bf16[128,128]{1,0:T(8,128)(2,1)S(1)}, bf16[128,128]{1,0:T(8,128)(2,1)}, u32[]{:S(2)}) copy-start(bf16[128,128]{1,0:T(8,128)(2,1)} %get-tuple-element.69) | copy-start | bytes 98308
  172.5 5.6 %copy-start.13 = (bf16[128,128]{1,0:T(8,128)(2,1)S(1)}, bf16[128,128]{1,0:T(8,128)(2,1)}, u32[]{:S(2)}) copy-start(bf16[128,128]{1,0:T(8,128)(2,1)} %get-tuple-element.80) | copy-start | bytes 98308
  172.5 5.6 %copy-start.14 = (bf16[128,128]{1,0:T(8,128)(2,1)S(1)}, bf16[128,128]{1,0:T(8,128)(2,1)}, u32[]{:S(2)}) copy-start(bf16[128,128]{1,0:T(8,128)(2,1)} %get-tuple-element.73) | copy-start | bytes 98308
  172.5 5.6 %copy-start.15 = (bf16[128,128]{1,0:T(8,128)(2,1)S(1)}, bf16[128,128]{1,0:T(8,128)(2,1)}, u32[]{:S(2)}) copy-start(bf16[128,128]{1,0:T(8,128)(2,1)} %get-tuple-element.82) | copy-start | bytes 98308
  173.6 19.8 %all-to-all-start.6 = ((bf16[8,448,128]{2,1,0:T(8,128)(2,1)}), bf16[8,448,128]{2,1,0:T(8,128)(2,1)S(1)}, u32[]{:S(2)}, u32[]{:S(2)}) async-start(bf16[8,448,128]{2,1,0:T(8,128)(2,1)} %broadcast_in_dim.11), calls=%async_computation.6 | async-start | bytes 1835008 | tf_op jit(solution)/shard_map/all_to_all | solution.py:381
  193.5 2.7 %collective-permute-start.8 = (f32[448,128]{1,0:T(8,128)S(1)}, f32[448,128]{1,0:T(8,128)S(1)}, u32[]{:S(2)}, u32[]{:S(2)}) collective-permute-start(f32[448,128]{1,0:T(8,128)S(1)} %convert_reduce_fusion.m_ref), channel_id=1, source_target_pairs={{0,1},{1,0},{2,3},{3,2},{4,5},{5,4},{6,7},{7,6},{8,9},{9,8},{10,11... | collective-permute-start | bytes 688136 | tf_op jit(solution)/shard_map/ppermute | solution.py:367

commit v9 on v8

--- a/solution.py
+++ b/solution.py
@@ -417,8 +417,6 @@
         move(dq[n * tokens : (n + 1) * tokens], *ways[n]) for n in range(1, 4)
     ]
     share = jnp.sum(shares.astype(f32), axis=0).astype(bf16)
-    share, *back = lax.optimization_barrier((share, *back))
-    d_query = unpack_queries(heads, back, group)
     total = spread(share, "dp", replicas).reshape(rows, width_kv)
 
     total = total.astype(f32)
@@ -436,7 +434,9 @@
     mid = lax.reduce_precision(gram - high, 8, 7)
     low = gram - high - mid
     sums = jnp.concatenate([sums[:half], high, mid, low], axis=0).astype(bf16)
+    sums, *back = lax.optimization_barrier((sums, *back))
     sums = spread(sums, "chip", chips)
+    d_query = unpack_queries(heads, back, group)
     sums, d_query, d_value = lax.optimization_barrier((sums, d_query, d_value))
     sums = jnp.sum(sums.astype(f32), axis=0)
     compressed, q_factor, new_error = finish(where, p_sum, sums, swap(sums), combined, replicas)

time: 204 us -> 207 us (1.015)
  blocking collectives: 41.8 us -> 64.7 us
  starting transfers between devices: 54.2 us -> 40.4 us
  waiting for transfers between devices: 70.3 us -> 62.6 us
  Pallas kernels: 24.3 us -> 27.7 us
    all_to_all x2 -> x3, blocking collectives: 41.8 us -> 64.7 us  [exchange(): return lax.all_to_all(x, axis, 0, 0)]
    all_to_all x5 -> x4, starting transfers between devices: 36.3 us -> 23.2 us  [exchange(): return lax.all_to_all(x, axis, 0, 0)]
    all_to_all x5 -> x4, waiting for transfers between devices: 42.2 us -> 34.4 us  [exchange(): return lax.all_to_all(x, axis, 0, 0)]
    pallas_call x1, Pallas kernels: 7.99 us -> 11.4 us  [attention(): pl.pallas_call(kernel, grid_spec=pltpu.PrefetchScalarGridSpec(num_scalar_...]
  transfers between devices with their start and end apart: 14 -> 13, of which waited for: 12 -> 10; matrix products, arithmetic and copies ran while one was open for 2% -> 2% of each run, Pallas kernels for 6% -> 8%
where the time goes in v9:
time: 207 us; the launch traced here: 206 us
  blocking collectives  64.7 us (31%)
  waiting for transfers between devices  62.6 us (30%)
  starting transfers between devices  40.4 us (20%)
  Pallas kernels  27.7 us (13%)
  local copies, waits for them, and re-layouts  6.31 us (3%)
    all_to_all x3, blocking collectives, exchange(): return lax.all_to_all(x, axis, 0, 0)  64.7 us
    all_to_all x4, waiting for transfers between devices, exchange(): return lax.all_to_all(x, axis, 0, 0)  34.4 us
    ppermute x6, waiting for transfers between devices, move(): return lax.ppermute(x, ctx, pairs)  24.8 us
    all_to_all x4, starting transfers between devices, exchange(): return lax.all_to_all(x, axis, 0, 0)  23.2 us
    ppermute x6, starting transfers between devices, move(): return lax.ppermute(x, ctx, pairs)  11.5 us
    pallas_call x1, Pallas kernels, attention(): pl.pallas_call(kernel, grid_spec=pltpu.PrefetchScalarGridSpec(num_scalar_...  11.4 us
    pallas_call x1, Pallas kernels, finish(): pl.pallas_call(kernel, out_shape=[jax.ShapeDtypeStruct((rows, width), jnp...  7.01 us
    ppermute x3, starting transfers between devices, swap(): return lax.ppermute(x, 'core', [(0, 1), (1, 0)])  5.62 us
  transfers between devices with their start and end apart: 13, of which 10 were waited for; matrix products, arithmetic and copies ran while one was open for 2% of the time, Pallas kernels for 8%

profile of v9, /device:TPU:1, one launch (start us, length us, event | category | flops | bytes accessed | tf_op | source)
XLA Modules:
  0.0 205.9 jit_solution(4576312178157270287)
XLA Ops:
  0.6 0.0 copy-start
  0.6 2.2 %pack_keys.1 = bf16[16,144,256]{2,1,0:T(8,128)(2,1)} custom-call(bf16[128,512]{1,0:T(8,128)(2,1)} %k_ref.1, bf16[128,512]{1,0:T(8,128)(2,1)} %v_ref.1, s32[1,128]{1,0:T(1,128)} %bitcast.37), custom_call_target="tpu_custom_call" | custom-call | tf_op jit(solution)/shard_map/pack_keys/pallas_call | solution.py:203
  2.8 8.6 %all-to-all-start = ((bf16[16,144,256]{2,1,0:T(8,128)(2,1)}), bf16[16,144,256]{2,1,0:T(8,128)(2,1)S(1)}, u32[]{:S(2)}, u32[]{:S(2)}) async-start(bf16[16,144,256]{2,1,0:T(8,128)(2,1)} %pack_keys.1), calls=%async_computation | async-start | bytes 2359296 | tf_op jit(solution)/shard_map/all_to_all | solution.py:381
  11.4 0.7 pad_add_fusion.1.h_ref
  12.1 2.6 %pack_queries.1 = (bf16[128,1536]{1,0:T(8,128)(2,1)}, bf16[128,1536]{1,0:T(8,128)(2,1)}, bf16[128,1536]{1,0:T(8,128)(2,1)}, bf16[128,1536]{1,0:T(8,128)(2,1)}) custom-call(s32[4]{0:T(128)} %pad_add_fusion.1.h_ref, bf16[128,3072]{1,0:T(8,128)(2,1)} %q_ref.1, bf16[128,3072]{1,0:T(8,128)(2,1)} %g_ref.1), custom_call_target="tpu_custom_call" | custom-call | tf_op jit(solution)/shard_map/pack_queries/pallas_call | solution.py:221
  14.7 0.1 collective-permute-start
  14.8 5.3 %collective-permute-start.1 = (bf16[128,1536]{1,0:T(8,128)(2,1)}, bf16[128,1536]{1,0:T(8,128)(2,1)}, u32[]{:S(2)}, u32[]{:S(2)}) collective-permute-start(bf16[128,1536]{1,0:T(8,128)(2,1)} %get-tuple-element.33), channel_id=1, source_target_pairs={{0,14},{1,15},{2,12},{3,13},{4,10},{5,11},{6,8},{7,9},{8,6},{9,7},... | collective-permute-start | bytes 1179656 | tf_op jit(solution)/shard_map/ppermute | solution.py:378
  20.1 0.4 collective-permute-start.2
  20.4 0.0 copy-done.6
  20.5 1.6 copy.15
  22.1 0.1 pad_add_fusion.at
  22.1 7.9 %all-to-all-done.k_ref.v_ref = bf16[16,144,256]{2,1,0:T(8,128)(2,1)S(1)} async-done(((bf16[16,144,256]{2,1,0:T(8,128)(2,1)}), bf16[16,144,256]{2,1,0:T(8,128)(2,1)S(1)}, u32[]{:S(2)}, u32[]{:S(2)}) %all-to-all-start) | async-done | bytes 1179680 | tf_op jit(solution)/shard_map/all_to_all | solution.py:381
  30.1 5.0 %all-to-all-start.1 = ((bf16[16,384,128]{2,1,0:T(8,128)(2,1)}), bf16[16,384,128]{2,1,0:T(8,128)(2,1)S(1)}, u32[]{:S(2)}, u32[]{:S(2)}) async-start(bf16[16,384,128]{2,1,0:T(8,128)(2,1)} %bitcast.32), calls=%async_computation.1 | async-start | bytes 3145728 | tf_op jit(solution)/shard_map/all_to_all | solution.py:381
  35.1 0.0 collective-permute-done.q1.g1
  35.1 3.5 %collective-permute-done.1.q2.g2 = bf16[128,1536]{1,0:T(8,128)(2,1)} collective-permute-done((bf16[128,1536]{1,0:T(8,128)(2,1)}, bf16[128,1536]{1,0:T(8,128)(2,1)}, u32[]{:S(2)}, u32[]{:S(2)}) %collective-permute-start.1) | collective-permute-done | bytes 393248 | tf_op jit(solution)/shard_map/ppermute | solution.py:378
  38.6 12.7 %collective-permute-done.2.q3.g3 = bf16[128,1536]{1,0:T(8,128)(2,1)} collective-permute-done((bf16[128,1536]{1,0:T(8,128)(2,1)}, bf16[128,1536]{1,0:T(8,128)(2,1)}, u32[]{:S(2)}, u32[]{:S(2)}) %collective-permute-start.2) | collective-permute-done | bytes 393248 | tf_op jit(solution)/shard_map/ppermute | solution.py:378
  51.3 0.0 copy-done.5
  51.3 11.4 %attention.1 = (bf16[512,768]{1,0:T(8,128)(2,1)S(1)}, bf16[2048,256]{1,0:T(8,128)(2,1)S(1)}) custom-call(s32[3]{0:T(128)S(1)} %pad_add_fusion.at, bf16[128,1536]{1,0:T(8,128)(2,1)S(1)} %copy-done.5, bf16[128,1536]{1,0:T(8,128)(2,1)} %collective-permute-done.q1.g1, bf16[128,1536]{1,0:T(8,128)(2,1)} %collective-permute-done.1.q2.g2, ...), custom_call_target="tpu_custom_call" | custom-call | flops 32212254720 | bytes 8388608 | tf_op jit(solution)/shard_map/attention/pallas_call | solution.py:147
  62.7 0.0 copy-start.1
  62.7 1.0 copy-done.1
  63.7 0.9 copy-done.3
  64.6 2.7 %all-to-all-done.1.f_ref = bf16[16,384,128]{2,1,0:T(8,128)(2,1)S(1)} async-done(((bf16[16,384,128]{2,1,0:T(8,128)(2,1)}), bf16[16,384,128]{2,1,0:T(8,128)(2,1)S(1)}, u32[]{:S(2)}, u32[]{:S(2)}) %all-to-all-start.1) | async-done | bytes 1572896 | tf_op jit(solution)/shard_map/all_to_all | solution.py:381
  67.3 22.9 %all_to_all.35 = bf16[16,128,256]{2,1,0:T(8,128)(2,1)S(1)} all-to-all(bf16[16,128,256]{2,1,0:T(8,128)(2,1)} %bitcast.29), channel_id=1, replica_groups=mesh['dp'=16,'chip'=8,'core'=2] {'chip','core'}, dimensions={0} | all-to-all | bytes 2097152 | tf_op jit(solution)/shard_map/all_to_all | solution.py:381
  90.2 0.2 reduce_sum.33
  90.5 0.0 copy-start.7
  90.5 0.0 copy-start.2
  90.5 0.1 broadcast_in_dim.9
  90.6 19.2 %all_to_all.36.m_ref = bf16[8,128,512]{2,1,0:T(8,128)(2,1)S(1)} all-to-all(bf16[8,128,512]{2,1,0:T(8,128)(2,1)S(1)} %broadcast_in_dim.9), channel_id=1, replica_groups=mesh['dp'=16,'chip'=8,'core'=2] {'chip'}, dimensions={0} | all-to-all | bytes 2097152 | tf_op jit(solution)/shard_map/all_to_all | solution.py:381
  109.8 0.0 copy-done.7
  109.8 1.8 collective-permute-start.3
  111.7 2.3 %collective-permute-done.3.t_ref = bf16[8,128,512]{2,1,0:T(8,128)(2,1)S(1)} collective-permute-done((bf16[8,128,512]{2,1,0:T(8,128)(2,1)S(1)}, bf16[8,128,512]{2,1,0:T(8,128)(2,1)S(1)}, u32[]{:S(2)}, u32[]{:S(2)}) %collective-permute-start.3) | collective-permute-done | bytes 1048608 | tf_op jit(solution)/shard_map/ppermute | solution.py:367
  113.9 0.0 copy-done.2
  113.9 2.3 %gradient.1 = (f32[384,512]{1,0:T(8,128)S(1)}, bf16[384,512]{1,0:T(8,128)(2,1)S(1)}) custom-call(s32[3]{0:T(128)S(1)} %pad_add_fusion.at, bf16[16,384,128]{2,1,0:T(8,128)(2,1)S(1)} %all-to-all-done.1.f_ref, bf16[8,128,512]{2,1,0:T(8,128)(2,1)S(1)} %all_to_all.36.m_ref, bf16[8,128,512]{2,1,0:T(8,128)(2,1)S(1)} %collective-permute-done.3.t_ref, ...), custom_call_target="tpu_custom_call" | custom-call | tf_op jit(solution)/shard_map/gradient/pallas_call | solution.py:264
  116.3 22.6 %all_to_all.37 = bf16[16,24,512]{2,1,0:T(8,128)(2,1)S(1)} all-to-all(bf16[16,24,512]{2,1,0:T(8,128)(2,1)S(1)} %bitcast.31), channel_id=1, replica_groups=mesh['dp'=16,'chip'=8,'core'=2] {'dp'}, dimensions={0} | all-to-all | bytes 786432 | tf_op jit(solution)/shard_map/all_to_all | solution.py:381
  138.8 0.1 reduce_sum.34
  138.9 0.8 broadcast_in_dim.10
  139.7 6.1 %all-to-all-start.5 = ((bf16[16,24,512]{2,1,0:T(8,128)(2,1)}), bf16[16,24,512]{2,1,0:T(8,128)(2,1)S(1)}, u32[]{:S(2)}, u32[]{:S(2)}) async-start(bf16[16,24,512]{2,1,0:T(8,128)(2,1)} %broadcast_in_dim.10), calls=%async_computation.5 | async-start | bytes 786432 | tf_op jit(solution)/shard_map/all_to_all | solution.py:381
  145.8 11.1 %all-to-all-done.5 = bf16[16,24,512]{2,1,0:T(8,128)(2,1)S(1)} async-done(((bf16[16,24,512]{2,1,0:T(8,128)(2,1)}), bf16[16,24,512]{2,1,0:T(8,128)(2,1)S(1)}, u32[]{:S(2)}, u32[]{:S(2)}) %all-to-all-start.5) | async-done | bytes 393248 | tf_op jit(solution)/shard_map/all_to_all | solution.py:381
  156.8 0.0 copy-done
  156.8 0.5 fusion.6.p_ref
  157.3 0.6 fusion.7
  157.9 0.5 fusion.8
  158.5 2.5 %collective-permute-start.4 = (f32[320,128]{1,0:T(8,128)S(1)}, f32[320,128]{1,0:T(8,128)S(1)}, u32[]{:S(2)}, u32[]{:S(2)}) collective-permute-start(f32[320,128]{1,0:T(8,128)S(1)} %pad_maximum_fusion), channel_id=1, source_target_pairs={{0,1},{1,0},{2,3},{3,2},{4,5},{5,4},{6,7},{7,6},{8,9},{9,8},{10,11... | collective-permute-start | bytes 491528 | tf_op jit(solution)/shard_map/ppermute | solution.py:367
  161.1 0.0 copy-done.4
  161.1 0.7 fusion.1
  161.8 0.0 collective-permute-start.5
  161.8 1.8 collective-permute-start.6
  163.6 3.9 %collective-permute-start.7 = (bf16[128,768]{1,0:T(8,128)(2,1)S(1)}, bf16[128,768]{1,0:T(8,128)(2,1)S(1)}, u32[]{:S(2)}, u32[]{:S(2)}) collective-permute-start(bf16[128,768]{1,0:T(8,128)(2,1)S(1)} %get-tuple-element.56), channel_id=1, source_target_pairs={{0,15},{1,14},{2,13},{3,12},{4,11},{5,10},{6,9},{7,8},{8,7},{9,6},... | collective-permute-start | bytes 589832 | tf_op jit(solution)/shard_map/ppermute | solution.py:378
  167.5 0.0 collective-permute-done.4
  167.6 0.0 collective-permute-done.5.refs_1_
  167.6 0.0 copy-start.8
  167.7 3.8 %collective-permute-done.6.refs_2_ = bf16[128,768]{1,0:T(8,128)(2,1)S(1)} collective-permute-done((bf16[128,768]{1,0:T(8,128)(2,1)S(1)}, bf16[128,768]{1,0:T(8,128)(2,1)S(1)}, u32[]{:S(2)}, u32[]{:S(2)}) %collective-permute-start.6) | collective-permute-done | bytes 196640 | tf_op jit(solution)/shard_map/ppermute | solution.py:378
  171.4 4.9 %collective-permute-done.7.refs_3_ = bf16[128,768]{1,0:T(8,128)(2,1)S(1)} collective-permute-done((bf16[128,768]{1,0:T(8,128)(2,1)S(1)}, bf16[128,768]{1,0:T(8,128)(2,1)S(1)}, u32[]{:S(2)}, u32[]{:S(2)}) %collective-permute-start.7) | collective-permute-done | bytes 196640 | tf_op jit(solution)/shard_map/ppermute | solution.py:378
  176.3 1.1 broadcast_in_dim.11
  177.3 3.6 %all-to-all-start.6 = ((bf16[8,448,128]{2,1,0:T(8,128)(2,1)}), bf16[8,448,128]{2,1,0:T(8,128)(2,1)S(1)}, u32[]{:S(2)}, u32[]{:S(2)}) async-start(bf16[8,448,128]{2,1,0:T(8,128)(2,1)} %broadcast_in_dim.11), calls=%async_computation.6 | async-start | bytes 1835008 | tf_op jit(solution)/shard_map/all_to_all | solution.py:381
  180.9 0.7 pad_maximum_fusion.2
  181.6 0.0 copy-done.8
  181.6 0.0 copy-done.9
  181.6 2.2 %unpack_queries.1 = bf16[128,3072]{1,0:T(8,128)(2,1)} custom-call(s32[4]{0:T(128)} %pad_add_fusion.1.h_ref, bf16[128,768]{1,0:T(8,128)(2,1)} %get-tuple-element.45.refs_0_, bf16[128,768]{1,0:T(8,128)(2,1)} %copy-done.8, bf16[128,768]{1,0:T(8,128)(2,1)} %copy-done.9, bf16[128,768]{1,0:T(8,128)(2,1)} %copy-done.10), custom_call_target="tpu_custom_call" | custom-call | tf_op jit(solution)/shard_map/unpack_queries/pallas_call | solution.py:238
  183.7 12.7 %all-to-all-done.6 = bf16[8,448,128]{2,1,0:T(8,128)(2,1)S(1)} async-done(((bf16[8,448,128]{2,1,0:T(8,128)(2,1)}), bf16[8,448,128]{2,1,0:T(8,128)(2,1)S(1)}, u32[]{:S(2)}, u32[]{:S(2)}) %all-to-all-start.6) | async-done | bytes 917536 | tf_op jit(solution)/shard_map/all_to_all | solution.py:381
  196.4 0.1 convert_reduce_fusion.m_ref
  196.6 1.2 collective-permute-start.8
  197.8 1.1 collective-permute-done.8.t_ref
  198.9 7.0 %finish.1 = (f32[384,512]{1,0:T(8,128)}, f32[512,128]{1,0:T(8,128)}, f32[1,384,512]{2,1,0:T(8,128)}) custom-call(s32[3]{0:T(128)S(1)} %pad_add_fusion.at, f32[384,128]{1,0:T(8,128)S(1)} %fusion.6.p_ref, f32[448,128]{1,0:T(8,128)S(1)} %convert_reduce_fusion.m_ref, f32[448,128]{1,0:T(8,128)S(1)} %collective-permute-done.8.t_ref, ...), custom_call_target="tpu_custom_call" | custom-call | tf_op jit(solution)/shard_map/finish/pallas_call | solution.py:334
  (18 shorter events, 0.2 us)
Async XLA Ops:
  0.6 156.2 %copy-start = (f32[512,128]{1,0:T(8,128)S(1)}, f32[512,128]{1,0:T(8,128)}, u32[]{:S(2)}) copy-start(f32[512,128]{1,0:T(8,128)} %param.15) | copy-start | bytes 786436
  2.8 17.6 %copy-start.6 = (bf16[128,6144]{1,0:T(8,128)(2,1)S(1)}, bf16[128,6144]{1,0:T(8,128)(2,1)}, u32[]{:S(2)}) copy-start(bf16[128,6144]{1,0:T(8,128)(2,1)} %param.12) | copy-start | bytes 4718596
  2.8 27.2 %all-to-all-start = ((bf16[16,144,256]{2,1,0:T(8,128)(2,1)}), bf16[16,144,256]{2,1,0:T(8,128)(2,1)S(1)}, u32[]{:S(2)}, u32[]{:S(2)}) async-start(bf16[16,144,256]{2,1,0:T(8,128)(2,1)} %pack_keys.1), calls=%async_computation | async-start | bytes 2359296 | tf_op jit(solution)/shard_map/all_to_all | solution.py:381
  14.7 20.4 %collective-permute-start = (bf16[128,1536]{1,0:T(8,128)(2,1)}, bf16[128,1536]{1,0:T(8,128)(2,1)}, u32[]{:S(2)}, u32[]{:S(2)}) collective-permute-start(bf16[128,1536]{1,0:T(8,128)(2,1)} %get-tuple-element.32), channel_id=1, source_target_pairs={{0,1},{1,0},{2,3},{3,2},{4,5},{5,4},{6,7},{7,6},{8,9},{9,8},{10,11... | collective-permute-start | bytes 1179656 | tf_op jit(solution)/shard_map/ppermute | solution.py:378
  14.8 23.8 %collective-permute-start.1 = (bf16[128,1536]{1,0:T(8,128)(2,1)}, bf16[128,1536]{1,0:T(8,128)(2,1)}, u32[]{:S(2)}, u32[]{:S(2)}) collective-permute-start(bf16[128,1536]{1,0:T(8,128)(2,1)} %get-tuple-element.33), channel_id=1, source_target_pairs={{0,14},{1,15},{2,12},{3,13},{4,10},{5,11},{6,8},{7,9},{8,6},{9,7},... | collective-permute-start | bytes 1179656 | tf_op jit(solution)/shard_map/ppermute | solution.py:378
  20.1 31.3 %collective-permute-start.2 = (bf16[128,1536]{1,0:T(8,128)(2,1)}, bf16[128,1536]{1,0:T(8,128)(2,1)}, u32[]{:S(2)}, u32[]{:S(2)}) collective-permute-start(bf16[128,1536]{1,0:T(8,128)(2,1)} %get-tuple-element.34), channel_id=1, source_target_pairs={{0,15},{1,14},{2,13},{3,12},{4,11},{5,10},{6,9},{7,8},{8,7},{9,6},... | collective-permute-start | bytes 1179656 | tf_op jit(solution)/shard_map/ppermute | solution.py:378
  30.1 21.3 %copy-start.5 = (bf16[128,1536]{1,0:T(8,128)(2,1)S(1)}, bf16[128,1536]{1,0:T(8,128)(2,1)}, u32[]{:S(2)}) copy-start(bf16[128,1536]{1,0:T(8,128)(2,1)} %get-tuple-element.31.q0.g0) | copy-start | bytes 1179652
  30.1 37.2 %all-to-all-start.1 = ((bf16[16,384,128]{2,1,0:T(8,128)(2,1)}), bf16[16,384,128]{2,1,0:T(8,128)(2,1)S(1)}, u32[]{:S(2)}, u32[]{:S(2)}) async-start(bf16[16,384,128]{2,1,0:T(8,128)(2,1)} %bitcast.32), calls=%async_computation.1 | async-start | bytes 3145728 | tf_op jit(solution)/shard_map/all_to_all | solution.py:381
  62.7 1.0 copy-start.1
  63.7 0.9 copy-start.3
  90.5 19.3 %copy-start.7 = (bf16[128,512]{1,0:T(8,128)(2,1)}, bf16[128,512]{1,0:T(8,128)(2,1)S(1)}, u32[]{:S(2)}) copy-start(bf16[128,512]{1,0:T(8,128)(2,1)S(1)} %pad_maximum_fusion.1) | copy-start | bytes 393220
  90.5 23.4 %copy-start.2 = (f32[1,384,512]{2,1,0:T(8,128)S(1)}, f32[1,384,512]{2,1,0:T(8,128)}, u32[]{:S(2)}) copy-start(f32[1,384,512]{2,1,0:T(8,128)} %param.14) | copy-start | bytes 2359300
  109.8 4.1 %collective-permute-start.3 = (bf16[8,128,512]{2,1,0:T(8,128)(2,1)S(1)}, bf16[8,128,512]{2,1,0:T(8,128)(2,1)S(1)}, u32[]{:S(2)}, u32[]{:S(2)}) collective-permute-start(bf16[8,128,512]{2,1,0:T(8,128)(2,1)S(1)} %all_to_all.36.m_ref), channel_id=1, source_target_pairs={{0,1},{1,0},{2,3},{3,2},{4,5},{5,4},{6,7},{7,6},{8,9},{9,8},{10,11... | collective-permute-start | bytes 3145736 | tf_op jit(solution)/shard_map/ppermute | solution.py:367
  139.7 17.2 %all-to-all-start.5 = ((bf16[16,24,512]{2,1,0:T(8,128)(2,1)}), bf16[16,24,512]{2,1,0:T(8,128)(2,1)S(1)}, u32[]{:S(2)}, u32[]{:S(2)}) async-start(bf16[16,24,512]{2,1,0:T(8,128)(2,1)} %broadcast_in_dim.10), calls=%async_computation.5 | async-start | bytes 786432 | tf_op jit(solution)/shard_map/all_to_all | solution.py:381
  156.8 4.2 %copy-start.4 = (bf16[512,768]{1,0:T(8,128)(2,1)S(1)}, bf16[512,768]{1,0:T(8,128)(2,1)}, u32[]{:S(2)}) copy-start(bf16[512,768]{1,0:T(8,128)(2,1)} %copy-done.3) | copy-start | bytes 2359300
  158.5 9.0 %collective-permute-start.4 = (f32[320,128]{1,0:T(8,128)S(1)}, f32[320,128]{1,0:T(8,128)S(1)}, u32[]{:S(2)}, u32[]{:S(2)}) collective-permute-start(f32[320,128]{1,0:T(8,128)S(1)} %pad_maximum_fusion), channel_id=1, source_target_pairs={{0,1},{1,0},{2,3},{3,2},{4,5},{5,4},{6,7},{7,6},{8,9},{9,8},{10,11... | collective-permute-start | bytes 491528 | tf_op jit(solution)/shard_map/ppermute | solution.py:367
  161.8 5.8 %collective-permute-start.5 = (bf16[128,768]{1,0:T(8,128)(2,1)S(1)}, bf16[128,768]{1,0:T(8,128)(2,1)S(1)}, u32[]{:S(2)}, u32[]{:S(2)}) collective-permute-start(bf16[128,768]{1,0:T(8,128)(2,1)S(1)} %get-tuple-element.58), channel_id=1, source_target_pairs={{0,1},{1,0},{2,3},{3,2},{4,5},{5,4},{6,7},{7,6},{8,9},{9,8},{10,11... | collective-permute-start | bytes 589832 | tf_op jit(solution)/shard_map/ppermute | solution.py:378
  161.8 9.6 %collective-permute-start.6 = (bf16[128,768]{1,0:T(8,128)(2,1)S(1)}, bf16[128,768]{1,0:T(8,128)(2,1)S(1)}, u32[]{:S(2)}, u32[]{:S(2)}) collective-permute-start(bf16[128,768]{1,0:T(8,128)(2,1)S(1)} %get-tuple-element.57), channel_id=1, source_target_pairs={{0,14},{1,15},{2,12},{3,13},{4,10},{5,11},{6,8},{7,9},{8,6},{9,7},... | collective-permute-start | bytes 589832 | tf_op jit(solution)/shard_map/ppermute | solution.py:378
  163.6 12.6 %collective-permute-start.7 = (bf16[128,768]{1,0:T(8,128)(2,1)S(1)}, bf16[128,768]{1,0:T(8,128)(2,1)S(1)}, u32[]{:S(2)}, u32[]{:S(2)}) collective-permute-start(bf16[128,768]{1,0:T(8,128)(2,1)S(1)} %get-tuple-element.56), channel_id=1, source_target_pairs={{0,15},{1,14},{2,13},{3,12},{4,11},{5,10},{6,9},{7,8},{8,7},{9,6},... | collective-permute-start | bytes 589832 | tf_op jit(solution)/shard_map/ppermute | solution.py:378
  167.6 13.9 %copy-start.8 = (bf16[128,768]{1,0:T(8,128)(2,1)}, bf16[128,768]{1,0:T(8,128)(2,1)S(1)}, u32[]{:S(2)}) copy-start(bf16[128,768]{1,0:T(8,128)(2,1)S(1)} %collective-permute-done.5.refs_1_) | copy-start | bytes 589828
  171.4 10.2 %copy-start.9 = (bf16[128,768]{1,0:T(8,128)(2,1)}, bf16[128,768]{1,0:T(8,128)(2,1)S(1)}, u32[]{:S(2)}) copy-start(bf16[128,768]{1,0:T(8,128)(2,1)S(1)} %collective-permute-done.6.refs_2_) | copy-start | bytes 589828
  176.3 5.3 %copy-start.10 = (bf16[128,768]{1,0:T(8,128)(2,1)}, bf16[128,768]{1,0:T(8,128)(2,1)S(1)}, u32[]{:S(2)}) copy-start(bf16[128,768]{1,0:T(8,128)(2,1)S(1)} %collective-permute-done.7.refs_3_) | copy-start | bytes 589828
  177.3 19.1 %all-to-all-start.6 = ((bf16[8,448,128]{2,1,0:T(8,128)(2,1)}), bf16[8,448,128]{2,1,0:T(8,128)(2,1)S(1)}, u32[]{:S(2)}, u32[]{:S(2)}) async-start(bf16[8,448,128]{2,1,0:T(8,128)(2,1)} %broadcast_in_dim.11), calls=%async_computation.6 | async-start | bytes 1835008 | tf_op jit(solution)/shard_map/all_to_all | solution.py:381
  196.6 2.4 %collective-permute-start.8 = (f32[448,128]{1,0:T(8,128)S(1)}, f32[448,128]{1,0:T(8,128)S(1)}, u32[]{:S(2)}, u32[]{:S(2)}) collective-permute-start(f32[448,128]{1,0:T(8,128)S(1)} %convert_reduce_fusion.m_ref), channel_id=1, source_target_pairs={{0,1},{1,0},{2,3},{3,2},{4,5},{5,4},{6,7},{7,6},{8,9},{9,8},{10,11... | collective-permute-start | bytes 688136 | tf_op jit(solution)/shard_map/ppermute | solution.py:367

commit v10 on v9

--- a/solution.py
+++ b/solution.py
@@ -413,11 +413,13 @@
 
     low, dq = lax.optimization_barrier((low, dq))
     shares = exchange(low.reshape(replicas, rows // replicas, width_kv), "dp")
-    back = [dq[:tokens]] + [
-        move(dq[n * tokens : (n + 1) * tokens], *ways[n]) for n in range(1, 4)
-    ]
+    near = [move(dq[n * tokens : (n + 1) * tokens], *ways[n]) for n in (1, 2)]
     share = jnp.sum(shares.astype(f32), axis=0).astype(bf16)
+    share, last, *near = lax.optimization_barrier((share, dq[3 * tokens :], *near))
     total = spread(share, "dp", replicas).reshape(rows, width_kv)
+    last = move(last, *ways[3])
+    total, last = lax.optimization_barrier((total, last))
+    back = [dq[:tokens], *near, last]
 
     total = total.astype(f32)
     p_sum = jnp.dot(total, q_init, precision=HIGHEST)
@@ -434,7 +436,6 @@
     mid = lax.reduce_precision(gram - high, 8, 7)
     low = gram - high - mid
     sums = jnp.concatenate([sums[:half], high, mid, low], axis=0).astype(bf16)
-    sums, *back = lax.optimization_barrier((sums, *back))
     sums = spread(sums, "chip", chips)
     d_query = unpack_queries(heads, back, group)
     sums, d_query, d_value = lax.optimization_barrier((sums, d_query, d_value))

time: 207 us -> 201 us (0.971)
  blocking collectives: 64.7 us -> 41.6 us
  starting transfers between devices: 40.4 us -> 53.1 us
  waiting for transfers between devices: 62.6 us -> 67 us
    all_to_all x3 -> x2, blocking collectives: 64.7 us -> 41.6 us  [exchange(): return lax.all_to_all(x, axis, 0, 0)]
    all_to_all x4 -> x5, starting transfers between devices: 23.2 us -> 36.6 us  [exchange(): return lax.all_to_all(x, axis, 0, 0)]
    ppermute x6, waiting for transfers between devices: 24.8 us -> 29.5 us  [move(): return lax.ppermute(x, ctx, pairs)]
    all_to_all x4 -> x5, waiting for transfers between devices: 34.4 us -> 33.1 us  [exchange(): return lax.all_to_all(x, axis, 0, 0)]
  transfers between devices with their start and end apart: 13 -> 14, of which waited for: 10 -> 11; matrix products, arithmetic and copies ran while one was open for 2% -> 2% of each run, Pallas kernels for 8% -> 7%
where the time goes in v10:
time: 201 us; the launch traced here: 200 us
  waiting for transfers between devices  67 us (33%)
  starting transfers between devices  53.1 us (26%)
  blocking collectives  41.6 us (21%)
  Pallas kernels  25.8 us (13%)
  local copies, waits for them, and re-layouts  8.3 us (4%)
    all_to_all x2, blocking collectives, exchange(): return lax.all_to_all(x, axis, 0, 0)  41.6 us
    all_to_all x5, starting transfers between devices, exchange(): return lax.all_to_all(x, axis, 0, 0)  36.6 us
    all_to_all x5, waiting for transfers between devices, exchange(): return lax.all_to_all(x, axis, 0, 0)  33.1 us
    ppermute x6, waiting for transfers between devices, move(): return lax.ppermute(x, ctx, pairs)  29.5 us
    ppermute x6, starting transfers between devices, move(): return lax.ppermute(x, ctx, pairs)  12.3 us
    pallas_call x1, Pallas kernels, attention(): pl.pallas_call(kernel, grid_spec=pltpu.PrefetchScalarGridSpec(num_scalar_...  9.51 us
    pallas_call x1, Pallas kernels, finish(): pl.pallas_call(kernel, out_shape=[jax.ShapeDtypeStruct((rows, width), jnp...  7.01 us
    ppermute x3, waiting for transfers between devices, swap(): return lax.ppermute(x, 'core', [(0, 1), (1, 0)])  4.43 us
  transfers between devices with their start and end apart: 14, of which 11 were waited for; matrix products, arithmetic and copies ran while one was open for 2% of the time, Pallas kernels for 7%

profile of v10, /device:TPU:1, one launch (start us, length us, event | category | flops | bytes accessed | tf_op | source)
XLA Modules:
  0.0 200.1 jit_solution(9267365825640703796)
XLA Ops:
  0.6 0.0 copy-start
  0.6 2.2 %pack_keys.1 = bf16[16,144,256]{2,1,0:T(8,128)(2,1)} custom-call(bf16[128,512]{1,0:T(8,128)(2,1)} %k_ref.1, bf16[128,512]{1,0:T(8,128)(2,1)} %v_ref.1, s32[1,128]{1,0:T(1,128)} %bitcast.37), custom_call_target="tpu_custom_call" | custom-call | tf_op jit(solution)/shard_map/pack_keys/pallas_call | solution.py:203
  2.8 8.6 %all-to-all-start = ((bf16[16,144,256]{2,1,0:T(8,128)(2,1)}), bf16[16,144,256]{2,1,0:T(8,128)(2,1)S(1)}, u32[]{:S(2)}, u32[]{:S(2)}) async-start(bf16[16,144,256]{2,1,0:T(8,128)(2,1)} %pack_keys.1), calls=%async_computation | async-start | bytes 2359296 | tf_op jit(solution)/shard_map/all_to_all | solution.py:381
  11.4 0.6 pad_add_fusion.1.h_ref
  12.0 2.6 %pack_queries.1 = (bf16[128,1536]{1,0:T(8,128)(2,1)}, bf16[128,1536]{1,0:T(8,128)(2,1)}, bf16[128,1536]{1,0:T(8,128)(2,1)}, bf16[128,1536]{1,0:T(8,128)(2,1)}) custom-call(s32[4]{0:T(128)} %pad_add_fusion.1.h_ref, bf16[128,3072]{1,0:T(8,128)(2,1)} %q_ref.1, bf16[128,3072]{1,0:T(8,128)(2,1)} %g_ref.1), custom_call_target="tpu_custom_call" | custom-call | tf_op jit(solution)/shard_map/pack_queries/pallas_call | solution.py:221
  14.7 0.1 collective-permute-start
  14.8 5.3 %collective-permute-start.1 = (bf16[128,1536]{1,0:T(8,128)(2,1)}, bf16[128,1536]{1,0:T(8,128)(2,1)}, u32[]{:S(2)}, u32[]{:S(2)}) collective-permute-start(bf16[128,1536]{1,0:T(8,128)(2,1)} %get-tuple-element.34), channel_id=1, source_target_pairs={{0,14},{1,15},{2,12},{3,13},{4,10},{5,11},{6,8},{7,9},{8,6},{9,7},... | collective-permute-start | bytes 1179656 | tf_op jit(solution)/shard_map/ppermute | solution.py:378
  20.0 0.4 collective-permute-start.2
  20.4 1.6 copy.15
  22.0 0.1 pad_add_fusion.at
  22.1 8.0 %all-to-all-done.k_ref.v_ref = bf16[16,144,256]{2,1,0:T(8,128)(2,1)S(1)} async-done(((bf16[16,144,256]{2,1,0:T(8,128)(2,1)}), bf16[16,144,256]{2,1,0:T(8,128)(2,1)S(1)}, u32[]{:S(2)}, u32[]{:S(2)}) %all-to-all-start) | async-done | bytes 1179680 | tf_op jit(solution)/shard_map/all_to_all | solution.py:381
  30.1 5.0 %all-to-all-start.1 = ((bf16[16,384,128]{2,1,0:T(8,128)(2,1)}), bf16[16,384,128]{2,1,0:T(8,128)(2,1)S(1)}, u32[]{:S(2)}, u32[]{:S(2)}) async-start(bf16[16,384,128]{2,1,0:T(8,128)(2,1)} %bitcast.32), calls=%async_computation.1 | async-start | bytes 3145728 | tf_op jit(solution)/shard_map/all_to_all | solution.py:381
  35.1 0.0 collective-permute-done.q1.g1
  35.1 3.5 %collective-permute-done.1.q2.g2 = bf16[128,1536]{1,0:T(8,128)(2,1)} collective-permute-done((bf16[128,1536]{1,0:T(8,128)(2,1)}, bf16[128,1536]{1,0:T(8,128)(2,1)}, u32[]{:S(2)}, u32[]{:S(2)}) %collective-permute-start.1) | collective-permute-done | bytes 393248 | tf_op jit(solution)/shard_map/ppermute | solution.py:378
  38.6 12.7 %collective-permute-done.2.q3.g3 = bf16[128,1536]{1,0:T(8,128)(2,1)} collective-permute-done((bf16[128,1536]{1,0:T(8,128)(2,1)}, bf16[128,1536]{1,0:T(8,128)(2,1)}, u32[]{:S(2)}, u32[]{:S(2)}) %collective-permute-start.2) | collective-permute-done | bytes 393248 | tf_op jit(solution)/shard_map/ppermute | solution.py:378
  51.3 9.5 %attention.1 = (bf16[512,768]{1,0:T(8,128)(2,1)S(1)}, bf16[2048,256]{1,0:T(8,128)(2,1)S(1)}) custom-call(s32[3]{0:T(128)S(1)} %pad_add_fusion.at, bf16[128,1536]{1,0:T(8,128)(2,1)S(1)} %copy-done.6, bf16[128,1536]{1,0:T(8,128)(2,1)} %collective-permute-done.q1.g1, bf16[128,1536]{1,0:T(8,128)(2,1)} %collective-permute-done.1.q2.g2, ...), custom_call_target="tpu_custom_call" | custom-call | flops 32212254720 | bytes 8388608 | tf_op jit(solution)/shard_map/attention/pallas_call | solution.py:147
  60.9 1.0 copy-done.1
  61.8 0.9 copy-done.3
  62.7 4.6 %all-to-all-done.1.f_ref = bf16[16,384,128]{2,1,0:T(8,128)(2,1)S(1)} async-done(((bf16[16,384,128]{2,1,0:T(8,128)(2,1)}), bf16[16,384,128]{2,1,0:T(8,128)(2,1)S(1)}, u32[]{:S(2)}, u32[]{:S(2)}) %all-to-all-start.1) | async-done | bytes 1572896 | tf_op jit(solution)/shard_map/all_to_all | solution.py:381
  67.3 22.4 %all_to_all.35 = bf16[16,128,256]{2,1,0:T(8,128)(2,1)S(1)} all-to-all(bf16[16,128,256]{2,1,0:T(8,128)(2,1)} %bitcast.29), channel_id=1, replica_groups=mesh['dp'=16,'chip'=8,'core'=2] {'chip','core'}, dimensions={0} | all-to-all | bytes 2097152 | tf_op jit(solution)/shard_map/all_to_all | solution.py:381
  89.6 0.2 reduce_sum.33
  89.9 0.6 fusion.2
  90.5 0.6 fusion.4
  91.2 0.0 copy-start.8
  91.2 0.0 copy-start.2
  91.2 0.1 broadcast_in_dim.9
  91.3 19.2 %all_to_all.36.m_ref = bf16[8,128,512]{2,1,0:T(8,128)(2,1)S(1)} all-to-all(bf16[8,128,512]{2,1,0:T(8,128)(2,1)S(1)} %broadcast_in_dim.9), channel_id=1, replica_groups=mesh['dp'=16,'chip'=8,'core'=2] {'chip'}, dimensions={0} | all-to-all | bytes 2097152 | tf_op jit(solution)/shard_map/all_to_all | solution.py:381
  110.5 0.0 copy-done.8
  110.5 1.8 collective-permute-start.3
  112.4 2.3 %collective-permute-done.3.t_ref = bf16[8,128,512]{2,1,0:T(8,128)(2,1)S(1)} collective-permute-done((bf16[8,128,512]{2,1,0:T(8,128)(2,1)S(1)}, bf16[8,128,512]{2,1,0:T(8,128)(2,1)S(1)}, u32[]{:S(2)}, u32[]{:S(2)}) %collective-permute-start.3) | collective-permute-done | bytes 1048608 | tf_op jit(solution)/shard_map/ppermute | solution.py:367
  114.6 2.3 %gradient.1 = (f32[384,512]{1,0:T(8,128)S(1)}, bf16[384,512]{1,0:T(8,128)(2,1)S(1)}) custom-call(s32[3]{0:T(128)S(1)} %pad_add_fusion.at, bf16[16,384,128]{2,1,0:T(8,128)(2,1)S(1)} %all-to-all-done.1.f_ref, bf16[8,128,512]{2,1,0:T(8,128)(2,1)S(1)} %all_to_all.36.m_ref, bf16[8,128,512]{2,1,0:T(8,128)(2,1)S(1)} %collective-permute-done.3.t_ref, ...), custom_call_target="tpu_custom_call" | custom-call | tf_op jit(solution)/shard_map/gradient/pallas_call | solution.py:264
  117.0 0.0 copy-start.5
  117.0 0.7 copy-done.5
  117.7 12.2 %all-to-all-start.4 = ((bf16[16,24,512]{2,1,0:T(8,128)(2,1)}), bf16[16,24,512]{2,1,0:T(8,128)(2,1)S(1)}, u32[]{:S(2)}, u32[]{:S(2)}) async-start(bf16[16,24,512]{2,1,0:T(8,128)(2,1)} %bitcast.31), calls=%async_computation.4 | async-start | bytes 786432 | tf_op jit(solution)/shard_map/all_to_all | solution.py:381
  129.9 0.0 copy-done.4
  129.9 0.7 fusion.1
  130.6 0.7 collective-permute-start.4
  131.3 1.8 collective-permute-start.5
  133.1 8.2 %all-to-all-done.4 = bf16[16,24,512]{2,1,0:T(8,128)(2,1)S(1)} async-done(((bf16[16,24,512]{2,1,0:T(8,128)(2,1)}), bf16[16,24,512]{2,1,0:T(8,128)(2,1)S(1)}, u32[]{:S(2)}, u32[]{:S(2)}) %all-to-all-start.4) | async-done | bytes 393248 | tf_op jit(solution)/shard_map/all_to_all | solution.py:381
  141.3 0.1 reduce_sum.34
  141.3 0.0 collective-permute-done.4.refs_1_
  141.3 0.0 copy-start.9
  141.4 3.2 %collective-permute-done.5.refs_2_ = bf16[128,768]{1,0:T(8,128)(2,1)S(1)} collective-permute-done((bf16[128,768]{1,0:T(8,128)(2,1)S(1)}, bf16[128,768]{1,0:T(8,128)(2,1)S(1)}, u32[]{:S(2)}, u32[]{:S(2)}) %collective-permute-start.5) | collective-permute-done | bytes 196640 | tf_op jit(solution)/shard_map/ppermute | solution.py:378
  144.6 0.8 broadcast_in_dim.10
  145.4 6.1 %all-to-all-start.5 = ((bf16[16,24,512]{2,1,0:T(8,128)(2,1)}), bf16[16,24,512]{2,1,0:T(8,128)(2,1)S(1)}, u32[]{:S(2)}, u32[]{:S(2)}) async-start(bf16[16,24,512]{2,1,0:T(8,128)(2,1)} %broadcast_in_dim.10), calls=%async_computation.5 | async-start | bytes 786432 | tf_op jit(solution)/shard_map/all_to_all | solution.py:381
  151.5 4.1 %collective-permute-start.6 = (bf16[128,768]{1,0:T(8,128)(2,1)S(1)}, bf16[128,768]{1,0:T(8,128)(2,1)S(1)}, u32[]{:S(2)}, u32[]{:S(2)}) collective-permute-start(bf16[128,768]{1,0:T(8,128)(2,1)S(1)} %get-tuple-element.46), channel_id=1, source_target_pairs={{0,15},{1,14},{2,13},{3,12},{4,11},{5,10},{6,9},{7,8},{8,7},{9,6},... | collective-permute-start | bytes 589832 | tf_op jit(solution)/shard_map/ppermute | solution.py:378
  155.6 10.1 %collective-permute-done.6.refs_3_ = bf16[128,768]{1,0:T(8,128)(2,1)S(1)} collective-permute-done((bf16[128,768]{1,0:T(8,128)(2,1)S(1)}, bf16[128,768]{1,0:T(8,128)(2,1)S(1)}, u32[]{:S(2)}, u32[]{:S(2)}) %collective-permute-start.6) | collective-permute-done | bytes 196640 | tf_op jit(solution)/shard_map/ppermute | solution.py:378
  165.7 0.0 all-to-all-done.5
  165.7 0.5 fusion.6.p_ref
  166.2 0.6 fusion.7
  166.8 0.5 fusion.8
  167.4 0.8 collective-permute-start.7
  168.2 1.0 collective-permute-done.7
  169.3 0.0 copy-start.14
  169.3 0.0 copy-start.15
  169.3 1.1 broadcast_in_dim.11
  170.4 4.6 %all-to-all-start.6 = ((bf16[8,448,128]{2,1,0:T(8,128)(2,1)}), bf16[8,448,128]{2,1,0:T(8,128)(2,1)S(1)}, u32[]{:S(2)}, u32[]{:S(2)}) async-start(bf16[8,448,128]{2,1,0:T(8,128)(2,1)} %broadcast_in_dim.11), calls=%async_computation.6 | async-start | bytes 1835008 | tf_op jit(solution)/shard_map/all_to_all | solution.py:381
  175.1 0.7 pad_maximum_fusion.2
  175.7 2.2 %unpack_queries.1 = bf16[128,3072]{1,0:T(8,128)(2,1)} custom-call(s32[4]{0:T(128)} %pad_add_fusion.1.h_ref, bf16[128,768]{1,0:T(8,128)(2,1)} %get-tuple-element.58.refs_0_, bf16[128,768]{1,0:T(8,128)(2,1)} %copy-done.9, bf16[128,768]{1,0:T(8,128)(2,1)} %copy-done.10, bf16[128,768]{1,0:T(8,128)(2,1)} %copy-done.11), custom_call_target="tpu_custom_call" | custom-call | tf_op jit(solution)/shard_map/unpack_queries/pallas_call | solution.py:238
  177.9 12.4 %all-to-all-done.6 = bf16[8,448,128]{2,1,0:T(8,128)(2,1)S(1)} async-done(((bf16[8,448,128]{2,1,0:T(8,128)(2,1)}), bf16[8,448,128]{2,1,0:T(8,128)(2,1)S(1)}, u32[]{:S(2)}, u32[]{:S(2)}) %all-to-all-start.6) | async-done | bytes 917536 | tf_op jit(solution)/shard_map/all_to_all | solution.py:381
  190.3 0.1 convert_reduce_fusion.m_ref
  190.4 1.6 collective-permute-start.8
  192.0 1.1 collective-permute-done.8.t_ref
  193.1 7.0 %finish.1 = (f32[384,512]{1,0:T(8,128)}, f32[512,128]{1,0:T(8,128)}, f32[1,384,512]{2,1,0:T(8,128)}) custom-call(s32[3]{0:T(128)S(1)} %pad_add_fusion.at, f32[384,128]{1,0:T(8,128)S(1)} %fusion.6.p_ref, f32[448,128]{1,0:T(8,128)S(1)} %convert_reduce_fusion.m_ref, f32[448,128]{1,0:T(8,128)S(1)} %collective-permute-done.8.t_ref, ...), custom_call_target="tpu_custom_call" | custom-call | tf_op jit(solution)/shard_map/finish/pallas_call | solution.py:334
  (29 shorter events, 0.2 us)
Async XLA Ops:
  0.6 165.1 %copy-start = (f32[512,128]{1,0:T(8,128)S(1)}, f32[512,128]{1,0:T(8,128)}, u32[]{:S(2)}) copy-start(f32[512,128]{1,0:T(8,128)} %param.15) | copy-start | bytes 786436
  2.8 17.6 %copy-start.7 = (bf16[128,6144]{1,0:T(8,128)(2,1)S(1)}, bf16[128,6144]{1,0:T(8,128)(2,1)}, u32[]{:S(2)}) copy-start(bf16[128,6144]{1,0:T(8,128)(2,1)} %param.12) | copy-start | bytes 4718596
  2.8 27.2 %all-to-all-start = ((bf16[16,144,256]{2,1,0:T(8,128)(2,1)}), bf16[16,144,256]{2,1,0:T(8,128)(2,1)S(1)}, u32[]{:S(2)}, u32[]{:S(2)}) async-start(bf16[16,144,256]{2,1,0:T(8,128)(2,1)} %pack_keys.1), calls=%async_computation | async-start | bytes 2359296 | tf_op jit(solution)/shard_map/all_to_all | solution.py:381
  14.7 20.4 %collective-permute-start = (bf16[128,1536]{1,0:T(8,128)(2,1)}, bf16[128,1536]{1,0:T(8,128)(2,1)}, u32[]{:S(2)}, u32[]{:S(2)}) collective-permute-start(bf16[128,1536]{1,0:T(8,128)(2,1)} %get-tuple-element.33), channel_id=1, source_target_pairs={{0,1},{1,0},{2,3},{3,2},{4,5},{5,4},{6,7},{7,6},{8,9},{9,8},{10,11... | collective-permute-start | bytes 1179656 | tf_op jit(solution)/shard_map/ppermute | solution.py:378
  14.8 23.8 %collective-permute-start.1 = (bf16[128,1536]{1,0:T(8,128)(2,1)}, bf16[128,1536]{1,0:T(8,128)(2,1)}, u32[]{:S(2)}, u32[]{:S(2)}) collective-permute-start(bf16[128,1536]{1,0:T(8,128)(2,1)} %get-tuple-element.34), channel_id=1, source_target_pairs={{0,14},{1,15},{2,12},{3,13},{4,10},{5,11},{6,8},{7,9},{8,6},{9,7},... | collective-permute-start | bytes 1179656 | tf_op jit(solution)/shard_map/ppermute | solution.py:378
  20.0 31.3 %collective-permute-start.2 = (bf16[128,1536]{1,0:T(8,128)(2,1)}, bf16[128,1536]{1,0:T(8,128)(2,1)}, u32[]{:S(2)}, u32[]{:S(2)}) collective-permute-start(bf16[128,1536]{1,0:T(8,128)(2,1)} %get-tuple-element.35), channel_id=1, source_target_pairs={{0,15},{1,14},{2,13},{3,12},{4,11},{5,10},{6,9},{7,8},{8,7},{9,6},... | collective-permute-start | bytes 1179656 | tf_op jit(solution)/shard_map/ppermute | solution.py:378
  30.1 21.3 %copy-start.6 = (bf16[128,1536]{1,0:T(8,128)(2,1)S(1)}, bf16[128,1536]{1,0:T(8,128)(2,1)}, u32[]{:S(2)}) copy-start(bf16[128,1536]{1,0:T(8,128)(2,1)} %get-tuple-element.32.q0.g0) | copy-start | bytes 1179652
  30.1 37.2 %all-to-all-start.1 = ((bf16[16,384,128]{2,1,0:T(8,128)(2,1)}), bf16[16,384,128]{2,1,0:T(8,128)(2,1)S(1)}, u32[]{:S(2)}, u32[]{:S(2)}) async-start(bf16[16,384,128]{2,1,0:T(8,128)(2,1)} %bitcast.32), calls=%async_computation.1 | async-start | bytes 3145728 | tf_op jit(solution)/shard_map/all_to_all | solution.py:381
  60.8 1.0 copy-start.1
  61.8 0.9 copy-start.3
  91.2 19.3 %copy-start.8 = (bf16[128,512]{1,0:T(8,128)(2,1)}, bf16[128,512]{1,0:T(8,128)(2,1)S(1)}, u32[]{:S(2)}) copy-start(bf16[128,512]{1,0:T(8,128)(2,1)S(1)} %pad_maximum_fusion.1) | copy-start | bytes 393220
  91.2 23.4 %copy-start.2 = (f32[1,384,512]{2,1,0:T(8,128)S(1)}, f32[1,384,512]{2,1,0:T(8,128)}, u32[]{:S(2)}) copy-start(f32[1,384,512]{2,1,0:T(8,128)} %param.14) | copy-start | bytes 2359300
  110.5 4.1 %collective-permute-start.3 = (bf16[8,128,512]{2,1,0:T(8,128)(2,1)S(1)}, bf16[8,128,512]{2,1,0:T(8,128)(2,1)S(1)}, u32[]{:S(2)}, u32[]{:S(2)}) collective-permute-start(bf16[8,128,512]{2,1,0:T(8,128)(2,1)S(1)} %all_to_all.36.m_ref), channel_id=1, source_target_pairs={{0,1},{1,0},{2,3},{3,2},{4,5},{5,4},{6,7},{7,6},{8,9},{9,8},{10,11... | collective-permute-start | bytes 3145736 | tf_op jit(solution)/shard_map/ppermute | solution.py:367
  114.6 15.3 %copy-start.4 = (bf16[512,768]{1,0:T(8,128)(2,1)S(1)}, bf16[512,768]{1,0:T(8,128)(2,1)}, u32[]{:S(2)}) copy-start(bf16[512,768]{1,0:T(8,128)(2,1)} %copy-done.3) | copy-start | bytes 2359300
  117.0 0.7 copy-start.5
  117.7 23.6 %all-to-all-start.4 = ((bf16[16,24,512]{2,1,0:T(8,128)(2,1)}), bf16[16,24,512]{2,1,0:T(8,128)(2,1)S(1)}, u32[]{:S(2)}, u32[]{:S(2)}) async-start(bf16[16,24,512]{2,1,0:T(8,128)(2,1)} %bitcast.31), calls=%async_computation.4 | async-start | bytes 786432 | tf_op jit(solution)/shard_map/all_to_all | solution.py:381
  130.6 10.7 %collective-permute-start.4 = (bf16[128,768]{1,0:T(8,128)(2,1)S(1)}, bf16[128,768]{1,0:T(8,128)(2,1)S(1)}, u32[]{:S(2)}, u32[]{:S(2)}) collective-permute-start(bf16[128,768]{1,0:T(8,128)(2,1)S(1)} %get-tuple-element.60), channel_id=1, source_target_pairs={{0,1},{1,0},{2,3},{3,2},{4,5},{5,4},{6,7},{7,6},{8,9},{9,8},{10,11... | collective-permute-start | bytes 589832 | tf_op jit(solution)/shard_map/ppermute | solution.py:378
  131.3 13.3 %collective-permute-start.5 = (bf16[128,768]{1,0:T(8,128)(2,1)S(1)}, bf16[128,768]{1,0:T(8,128)(2,1)S(1)}, u32[]{:S(2)}, u32[]{:S(2)}) collective-permute-start(bf16[128,768]{1,0:T(8,128)(2,1)S(1)} %get-tuple-element.59), channel_id=1, source_target_pairs={{0,14},{1,15},{2,12},{3,13},{4,10},{5,11},{6,8},{7,9},{8,6},{9,7},... | collective-permute-start | bytes 589832 | tf_op jit(solution)/shard_map/ppermute | solution.py:378
  141.3 26.0 %copy-start.9 = (bf16[128,768]{1,0:T(8,128)(2,1)}, bf16[128,768]{1,0:T(8,128)(2,1)S(1)}, u32[]{:S(2)}) copy-start(bf16[128,768]{1,0:T(8,128)(2,1)S(1)} %collective-permute-done.4.refs_1_) | copy-start | bytes 589828
  144.6 22.8 %copy-start.10 = (bf16[128,768]{1,0:T(8,128)(2,1)}, bf16[128,768]{1,0:T(8,128)(2,1)S(1)}, u32[]{:S(2)}) copy-start(bf16[128,768]{1,0:T(8,128)(2,1)S(1)} %collective-permute-done.5.refs_2_) | copy-start | bytes 589828
  145.4 20.3 %all-to-all-start.5 = ((bf16[16,24,512]{2,1,0:T(8,128)(2,1)}), bf16[16,24,512]{2,1,0:T(8,128)(2,1)S(1)}, u32[]{:S(2)}, u32[]{:S(2)}) async-start(bf16[16,24,512]{2,1,0:T(8,128)(2,1)} %broadcast_in_dim.10), calls=%async_computation.5 | async-start | bytes 786432 | tf_op jit(solution)/shard_map/all_to_all | solution.py:381
  151.5 14.2 %collective-permute-start.6 = (bf16[128,768]{1,0:T(8,128)(2,1)S(1)}, bf16[128,768]{1,0:T(8,128)(2,1)S(1)}, u32[]{:S(2)}, u32[]{:S(2)}) collective-permute-start(bf16[128,768]{1,0:T(8,128)(2,1)S(1)} %get-tuple-element.46), channel_id=1, source_target_pairs={{0,15},{1,14},{2,13},{3,12},{4,11},{5,10},{6,9},{7,8},{8,7},{9,6},... | collective-permute-start | bytes 589832 | tf_op jit(solution)/shard_map/ppermute | solution.py:378
  165.7 1.7 copy-start.11
  167.4 1.8 collective-permute-start.7
  169.3 5.7 %copy-start.12 = (bf16[128,128]{1,0:T(8,128)(2,1)S(1)}, bf16[128,128]{1,0:T(8,128)(2,1)}, u32[]{:S(2)}) copy-start(bf16[128,128]{1,0:T(8,128)(2,1)} %get-tuple-element.71) | copy-start | bytes 98308
  169.3 5.7 %copy-start.13 = (bf16[128,128]{1,0:T(8,128)(2,1)S(1)}, bf16[128,128]{1,0:T(8,128)(2,1)}, u32[]{:S(2)}) copy-start(bf16[128,128]{1,0:T(8,128)(2,1)} %get-tuple-element.82) | copy-start | bytes 98308
  169.3 5.7 %copy-start.14 = (bf16[128,128]{1,0:T(8,128)(2,1)S(1)}, bf16[128,128]{1,0:T(8,128)(2,1)}, u32[]{:S(2)}) copy-start(bf16[128,128]{1,0:T(8,128)(2,1)} %get-tuple-element.75) | copy-start | bytes 98308
  169.3 5.7 %copy-start.15 = (bf16[128,128]{1,0:T(8,128)(2,1)S(1)}, bf16[128,128]{1,0:T(8,128)(2,1)}, u32[]{:S(2)}) copy-start(bf16[128,128]{1,0:T(8,128)(2,1)} %get-tuple-element.84) | copy-start | bytes 98308
  170.4 19.9 %all-to-all-start.6 = ((bf16[8,448,128]{2,1,0:T(8,128)(2,1)}), bf16[8,448,128]{2,1,0:T(8,128)(2,1)S(1)}, u32[]{:S(2)}, u32[]{:S(2)}) async-start(bf16[8,448,128]{2,1,0:T(8,128)(2,1)} %broadcast_in_dim.11), calls=%async_computation.6 | async-start | bytes 1835008 | tf_op jit(solution)/shard_map/all_to_all | solution.py:381
  190.4 2.7 %collective-permute-start.8 = (f32[448,128]{1,0:T(8,128)S(1)}, f32[448,128]{1,0:T(8,128)S(1)}, u32[]{:S(2)}, u32[]{:S(2)}) collective-permute-start(f32[448,128]{1,0:T(8,128)S(1)} %convert_reduce_fusion.m_ref), channel_id=1, source_target_pairs={{0,1},{1,0},{2,3},{3,2},{4,5},{5,4},{6,7},{7,6},{8,9},{9,8},{10,11... | collective-permute-start | bytes 688136 | tf_op jit(solution)/shard_map/ppermute | solution.py:367
